TPU v7x, 32 devices: a whole 2x2x4 slice. The times are simulated.
32 devices in a mesh: gx: 8 (over z, y), gy: 4 (over x, core).
Axes of the slice: x: 2, y: 2, z: 4, core: 2. Of those that a mesh axis runs over, the one named last changes fastest.
Arguments:
- tokens: bfloat16 [128, 9216], P(('gx', 'gy')), may hold values from -6 to 6
- gain: float32 [9216], replicated, may hold values from 0.1 to 1.9
- w_gate: bfloat16 [9216, 36864], P('gy', 'gx'), may hold values from -0.0625 to 0.0625
- w_up: bfloat16 [9216, 36864], P('gy', 'gx'), may hold values from -0.0625 to 0.0625
- w_down: bfloat16 [36864, 9216], P('gx', 'gy'), may hold values from -0.03125 to 0.03125
- w_kv: bfloat16 [4, 2304, 512], P('gy', 'gx'), may hold values from -0.0625 to 0.0625
- queries: bfloat16 [128, 12288], P(('gx', 'gy')), may hold values from -64 to 64
- key_cache: bfloat16 [128, 2048, 256], P(('gx', 'gy')), may hold values from -4 to 4
- value_cache: bfloat16 [128, 2048, 256], P(('gx', 'gy')), may hold values from -6 to 6
- lengths: int32 [128], P(('gx', 'gy')), may hold values from 2 to 2048, as said below
Outputs:
- mixed: bfloat16 [128, 9216], P(('gx', 'gy'))
- context: bfloat16 [128, 12288], P(('gx', 'gy'))
Inputs may be any that keep to these rules, and one draw needn't show every extreme that they name: `lengths`: each row has at least two live slots, and some row fills all 2048 slots.
All inputs are finite; a program needn't handle non-finite values.
Results may differ from a plain program's by a relative error of at most 0.0055.
Values may be sent and summed in bfloat16 or wider, within the bound.
No kernel may reach another device: no remote copies, remote signals or barrier semaphores. Data moves between devices by JAX's collectives and lax.ppermute only.
A program may use at most 128 MiB of HBM per device.

v0:
```python
import math

import jax
import jax.numpy as jnp
from jax import lax
from jax.sharding import PartitionSpec as P

HD = 256


def layer_norm(tokens, gain):
    values = tokens.astype(jnp.float32)
    centred = values - jnp.mean(values, axis=-1, keepdims=True)
    spread = jnp.mean(centred * centred, axis=-1, keepdims=True)
    return (centred * lax.rsqrt(spread + 1e-05) * gain).astype(jnp.bfloat16)


def gated(pair, hidden_cols):
    return (jax.nn.silu(pair[:, :hidden_cols]) * pair[:, hidden_cols:]).astype(jnp.bfloat16)


def attend(queries, key_cache, value_cache, lengths, key_new, value_new):
    batch = queries.shape[0]
    span = key_cache.shape[1]
    depth = key_cache.shape[2]
    grouped = queries.reshape(batch, -1, depth)
    scale = 1.0 / math.sqrt(depth)
    scores = (
        jnp.einsum("rhd,rcd->rhc", grouped, key_cache, preferred_element_type=jnp.float32) * scale
    )
    own = jnp.einsum("rhd,rd->rh", grouped, key_new, preferred_element_type=jnp.float32) * scale
    live = lax.broadcasted_iota(jnp.int32, (batch, span), 1) < lengths[:, None]
    scores = jnp.where(live[:, None, :], scores, -jnp.inf)
    top = jnp.maximum(jnp.max(scores, axis=-1), own)
    weights = jnp.exp(scores - top[:, :, None])
    own_weight = jnp.exp(own - top)
    total = jnp.sum(weights, axis=-1) + own_weight
    probs = (weights / total[:, :, None]).astype(jnp.bfloat16)
    own_prob = (own_weight / total).astype(jnp.bfloat16)
    context = jnp.einsum("rhc,rcd->rhd", probs, value_cache, preferred_element_type=jnp.float32)
    context = (
        context
        + own_prob.astype(jnp.float32)[:, :, None] * value_new.astype(jnp.float32)[:, None, :]
    )
    return context.reshape(batch, -1).astype(jnp.bfloat16)


def body(tokens, gain, w_gate, w_up, w_down, w_kv, queries, key_cache, value_cache, lengths):
    normed = layer_norm(tokens, gain)
    grid_in = lax.all_to_all(normed, "gy", split_axis=1, concat_axis=0, tiled=True)
    slab = w_kv.shape[1]
    offset = lax.axis_index("gx") * slab
    hidden_cols = w_gate.shape[1]
    piece = lax.all_gather(grid_in, "gx", axis=0, tiled=True)
    part_cols = lax.dynamic_slice_in_dim(piece, offset, slab, 1)
    partial_value = jnp.concatenate(
        (
            jnp.dot(piece, w_gate, preferred_element_type=jnp.float32),
            jnp.dot(piece, w_up, preferred_element_type=jnp.float32),
            jnp.dot(part_cols, w_kv[0], preferred_element_type=jnp.float32),
        ),
        axis=1,
    )
    pair = partial_value[:, : 2 * hidden_cols]
    kv_term = partial_value[:, 2 * hidden_cols :]
    summed = lax.psum(pair, "gy")
    hidden = gated(summed, hidden_cols)
    back = lax.psum_scatter(
        jnp.concatenate(
            (jnp.dot(hidden, w_down, preferred_element_type=jnp.float32), kv_term), axis=1
        ),
        "gx",
        scatter_dimension=0,
        tiled=True,
    )
    width_dev = w_down.shape[1]
    ffn, kv_sums = (
        lax.all_to_all(back[:, :width_dev], "gy", split_axis=0, concat_axis=1, tiled=True),
        lax.all_to_all(back[:, width_dev:], "gy", split_axis=0, concat_axis=1, tiled=True),
    )
    fresh = jnp.sum(kv_sums.reshape(kv_sums.shape[0], -1, 2 * HD), axis=1)
    mixed = (tokens.astype(jnp.float32) + ffn).astype(jnp.bfloat16)
    key_new = fresh[:, :HD].astype(jnp.bfloat16)
    value_new = fresh[:, HD:].astype(jnp.bfloat16)
    context = attend(queries, key_cache, value_cache, lengths, key_new, value_new)
    return (mixed, context)


def solution(mesh):
    return jax.shard_map(
        body,
        mesh=mesh,
        in_specs=(
            P(("gx", "gy"), None),
            P(),
            P("gy", "gx"),
            P("gy", "gx"),
            P("gx", "gy"),
            P("gy", "gx", None),
            P(("gx", "gy"), None),
            P(("gx", "gy"), None, None),
            P(("gx", "gy"), None, None),
            P(("gx", "gy")),
        ),
        out_specs=(P(("gx", "gy"), None), P(("gx", "gy"), None)),
        check_vma=False,
    )
```

profile of v0, /device:TPU:0, one launch (start us, length us, event | category | flops | bytes accessed | tf_op | source)
XLA Modules:
  0.0 266.4 jit_solution(11144670958850965390)
XLA Ops:
  7.2 0.0 copy-start
  7.2 0.0 all-reduce.2.cloned.1.call-start
  7.2 1.1 convert_reduce_fusion
  8.3 1.1 fusion.14
  9.5 1.0 fusion.16
  10.5 8.2 %all_to_all.51 = bf16[4,4,2304]{2,0,1:T(4,128)(2,1)S(1)} all-to-all(bf16[4,4,2304]{2,0,1:T(4,128)(2,1)S(1)} %bitcast.32), channel_id=1, replica_groups=mesh['gx'=8,'gy'=4] {'gy'}, dimensions={1} | all-to-all | bytes 147456 | tf_op jit(solution)/shard_map/all_to_all | solution.py:50
  18.7 31.9 %all_gather.3 = bf16[128,2304]{1,0:T(8,128)(2,1)S(1)} all-gather(bf16[16,2304]{1,0:T(8,128)(2,1)S(1)} %all_to_all.41), channel_id=1, replica_groups=mesh['gx'=8,'gy'=4] {'gx'}, dimensions={0}, use_global_device_ids=true | all-gather | bytes 663552 | tf_op jit(solution)/shard_map/all_gather | solution.py:54
  50.6 8.8 %fusion.30 = f32[128,4608]{1,0:T(8,128)S(1)} fusion(bf16[128,2304]{1,0:T(8,128)(2,1)S(1)} %all_gather.3, bf16[2304,4608]{1,0:T(8,128)(2,1)} %param.12), kind=kOutput, calls=%fused_computation.47 | convolution fusion | flops 2717908992 | bytes 24182784 | tf_op jit(solution)/shard_map/dot_general | solution.py:58
  59.4 4.3 %copy-done.2 = bf16[2304,4608]{1,0:T(8,128)(2,1)S(1)} copy-done((bf16[2304,4608]{1,0:T(8,128)(2,1)S(1)}, bf16[2304,4608]{1,0:T(8,128)(2,1)}, u32[]{:S(2)}) %copy-start.2) | copy-done | bytes 21233688
  63.7 2.9 %fusion.31 = f32[128,4608]{1,0:T(8,128)S(1)} fusion(bf16[128,2304]{1,0:T(8,128)(2,1)S(1)} %all_gather.3, bf16[2304,4608]{1,0:T(8,128)(2,1)S(1)} %copy-done.2), kind=kOutput, calls=%fused_computation.48 | convolution fusion | flops 2717908992 | bytes 24182784 | tf_op jit(solution)/shard_map/dot_general | solution.py:59
  66.6 2.5 pad_maximum_fusion
  69.1 0.0 all-reduce.2.cloned.1.call-update
  69.1 0.0 reduce-scatter.2.cloned.1.call-start
  69.2 0.3 fusion.10
  69.5 94.0 %all-reduce.2.cloned.1.call-done = f32[128,9216]{1,0:T(8,128)} async-done(((f32[128,9216]{1,0:T(8,128)}), f32[128,9216]{1,0:T(8,128)}) %all-reduce.2.cloned.1.call-update) | async-done | bytes 4718608 | tf_op jit(solution)/shard_map/psum | solution.py:66
  163.4 11.7 %fusion.3 = f32[128,2304]{1,0:T(8,128)S(1)} fusion(bf16[4608,2304]{1,0:T(8,128)(2,1)} %param.14, f32[128,9216]{1,0:T(8,128)} %all-reduce.2.cloned.1.call-done), kind=kOutput, calls=%fused_computation.9 | convolution fusion | flops 2721447936 | bytes 27131904 | tf_op jit(solution)/shard_map/dot_general | solution.py:70
  175.1 1.2 pad_maximum_fusion.1
  176.3 0.0 reduce-scatter.2.cloned.1.call-update
  176.4 0.1 iota_compare_fusion
  176.5 65.2 %reduce-scatter.2.cloned.1.call-done = f32[16,2816]{1,0:T(8,128)} async-done(((f32[128,2816]{1,0:T(8,128)}), f32[16,2816]{1,0:T(8,128)}) %reduce-scatter.2.cloned.1.call-update) | async-done | bytes 180240 | tf_op jit(solution)/shard_map/reduce_scatter | solution.py:68
  241.7 0.8 slice.29
  242.5 0.6 all_to_all.46
  243.1 3.3 %all-to-all-start.2 = ((f32[4,4,512]{2,1,0:T(4,128)}), f32[4,4,512]{2,1,0:T(4,128)S(1)}, u32[]{:S(2)}, u32[]{:S(2)}) async-start(f32[4,4,512]{2,1,0:T(4,128)} %all_to_all.46), calls=%async_computation.3 | async-start | bytes 65536 | tf_op jit(solution)/shard_map/all_to_all | solution.py:79
  246.4 3.7 %fusion.29 = (f32[4,48]{1,0:T(4,128)S(1)}, f32[4,48,2048]{2,1,0:T(8,128)S(1)}) fusion(bf16[4,2048,256]{2,1,0:T(8,128)(2,1)} %param.17, bf16[1,4,48,256]{3,1,2,0:T(4,128)(2,1)S(1)} %bitcast.34, pred[4,2048]{1,0:T(4,128)(4,1)S(1)} %iota_compare_fusion), kind=kOutput, calls=%fused_computation.46 | convolution fusion | flops 202506048 | bytes 5874432 | tf_op jit(solution)/shard_map/rhd,rcd->rhc/dot_general | solution.py:29
  250.1 0.7 all_to_all.42
  250.8 3.3 %all-to-all-start.1 = ((f32[4,4,2304]{2,1,0:T(4,128)}), f32[4,4,2304]{2,1,0:T(4,128)S(1)}, u32[]{:S(2)}, u32[]{:S(2)}) async-start(f32[4,4,2304]{2,1,0:T(4,128)} %all_to_all.42), calls=%async_computation.2 | async-start | bytes 294912 | tf_op jit(solution)/shard_map/all_to_all | solution.py:78
  254.1 0.1 fusion.18
  254.3 0.4 fusion.2
  254.7 3.1 %fusion.7 = bf16[1,4,48,256]{3,2,1,0:T(8,128)(2,1)S(1)} fusion(bf16[4,2048,256]{2,1,0:T(8,128)(2,1)} %param.18, f32[4,48,2048]{2,1,0:T(8,128)S(1)} %get-tuple-element.7, f32[4,48]{1,0:T(4,128)S(1)} %get-tuple-element.3, f32[4,48]{1,0:T(4,128)S(1)} %multiply_maximum_fusion, f32[4,256]{1,0:T(4,128)S(1)} %get-tuple-element.4, f32[4,48]{1,0:T(4,128)S(1)} %get-tuple-element.2), kind=kOutput, calls=%fused_computation.13 | convolution fusion | flops 202653696 | bytes 5871872 | tf_op jit(solution)/shard_map/rhc,rcd->rhd/dot_general | solution.py:40
  257.8 0.7 copy.18
  258.5 0.4 all-to-all-done.1
  258.9 0.7 fusion.17
  (20 shorter events, 0.1 us)
Async XLA Ops:
  7.2 62.0 %copy-start = (bf16[1,288,512]{2,1,0:T(8,128)(2,1)S(1)}, bf16[1,288,512]{2,1,0:T(8,128)(2,1)}, u32[]{:S(2)}) copy-start(bf16[1,288,512]{2,1,0:T(8,128)(2,1)} %param.15) | copy-start | bytes 884740
  7.2 156.2 %all-reduce.2.cloned.1.call-start = ((), (), s32[]{:S(2)}) async-start(), calls=%async_computation.4 | async-start | bytes 9437184 | tf_op jit(solution)/shard_map/psum | solution.py:66
  50.6 13.1 %copy-start.2 = (bf16[2304,4608]{1,0:T(8,128)(2,1)S(1)}, bf16[2304,4608]{1,0:T(8,128)(2,1)}, u32[]{:S(2)}) copy-start(bf16[2304,4608]{1,0:T(8,128)(2,1)} %param.13) | copy-start | bytes 63700996
  69.1 172.6 %reduce-scatter.2.cloned.1.call-start = ((), (), s32[]{:S(2)}) async-start(), calls=%async_computation.5 | async-start | bytes 1622016 | tf_op jit(solution)/shard_map/reduce_scatter | solution.py:68
  175.1 1.3 copy-start.5
  175.1 71.2 %copy-start.4 = (bf16[4,12288]{1,0:T(4,128)(2,1)S(1)}, bf16[4,12288]{1,0:T(4,128)(2,1)}, u32[]{:S(2)}) copy-start(bf16[4,12288]{1,0:T(4,128)(2,1)} %param.16) | copy-start | bytes 294916
  243.1 7.7 %all-to-all-start.2 = ((f32[4,4,512]{2,1,0:T(4,128)}), f32[4,4,512]{2,1,0:T(4,128)S(1)}, u32[]{:S(2)}, u32[]{:S(2)}) async-start(f32[4,4,512]{2,1,0:T(4,128)} %all_to_all.46), calls=%async_computation.3 | async-start | bytes 65536 | tf_op jit(solution)/shard_map/all_to_all | solution.py:79
  246.4 3.7 %slice-start = ((f32[16,2816]{1,0:T(8,128)}), f32[16,2304]{1,0:T(8,128)S(1)}, s32[]{:S(2)}) async-start(f32[16,2816]{1,0:T(8,128)} %reduce-scatter.2.cloned.1.call-done), calls=%async_computation.6 | async-start | bytes 294912 | tf_op jit(solution)/shard_map/slice | solution.py:78
  250.8 8.1 %all-to-all-start.1 = ((f32[4,4,2304]{2,1,0:T(4,128)}), f32[4,4,2304]{2,1,0:T(4,128)S(1)}, u32[]{:S(2)}, u32[]{:S(2)}) async-start(f32[4,4,2304]{2,1,0:T(4,128)} %all_to_all.42), calls=%async_computation.2 | async-start | bytes 294912 | tf_op jit(solution)/shard_map/all_to_all | solution.py:78
  254.7 4.2 %copy-start.3 = (bf16[4,9216]{1,0:T(4,128)(2,1)S(1)}, bf16[4,9216]{1,0:T(4,128)(2,1)}, u32[]{:S(2)}) copy-start(bf16[4,9216]{1,0:T(4,128)(2,1)} %param.10) | copy-start | bytes 221188
  254.7 4.9 %copy-start.1 = (bf16[1,288,512]{2,1,0:T(8,128)(2,1)S(1)}, bf16[1,288,512]{2,1,0:T(8,128)(2,1)}, u32[]{:S(2)}) copy-start(bf16[1,288,512]{2,1,0:T(8,128)(2,1)} %param.15) | copy-start | bytes 884740
Sparse Core Ops, SparseCore 0:
  69.2 94.1 all-reduce.1
  176.5 65.1 reduce-scatter.1
where the time goes:
time: 267 us; the launch traced here: 266 us
  waiting for transfers between devices  160 us (60%)
  blocking collectives  40.1 us (15%)
  matrix products  30.5 us (11%)
  between operations  14.2 us (5%)
  other arithmetic  8.14 us (3%)
  local copies, waits for them, and re-layouts  7.14 us (3%)
  starting transfers between devices  6.68 us (3%)
    psum x1, waiting for transfers between devices, body(): summed = lax.psum(pair, 'gy')  94 us
    reduce_scatter x1, waiting for transfers between devices, body(): lax.psum_scatter(jnp.concatenate((jnp.dot(hidden, w_down, preferred_eleme...  65.2 us
    all_gather x1, blocking collectives, body(): piece = lax.all_gather(grid_in, 'gx', axis=0, tiled=True)  31.9 us
    dot_general x1, matrix products, body(): jnp.dot(hidden, w_down, preferred_element_type=jnp.float32)  11.7 us
    dot_general x1, matrix products, body(): jnp.dot(piece, w_gate, preferred_element_type=jnp.float32)  8.77 us
    all_to_all x1, blocking collectives, body(): lax.all_to_all(normed, 'gy', split_axis=1, concat_axis=0, tiled=True)  8.17 us
  transfers between devices with their start and end apart: 4, of which 3 were waited for; matrix products, arithmetic and copies ran while one was open for 3% of the time, Pallas kernels for 0%

commit v1 on v0

v1 whole, which is shorter than its diff:
```python
import functools
import math

import jax
import jax.numpy as jnp
from jax import lax
from jax.experimental import pallas as pl
from jax.experimental.pallas import tpu as pltpu
from jax.sharding import PartitionSpec as P

HD = 256
F32 = jnp.float32
BF16 = jnp.bfloat16
VMEM_LIMIT = 40 * 1024 * 1024


def params():
    return pltpu.CompilerParams(vmem_limit_bytes=VMEM_LIMIT)


def tile_of(width, most):
    return max(t for t in range(128, most + 1, 128) if width % t == 0)


def swap(x, axis, size, bits):
    return lax.ppermute(x, axis, [(i, i ^ bits) for i in range(size)])


def layer_norm(tokens, gain):
    values = tokens.astype(F32)
    centred = values - jnp.mean(values, axis=-1, keepdims=True)
    spread = jnp.mean(centred * centred, axis=-1, keepdims=True)
    return (centred * lax.rsqrt(spread + 1e-05) * gain).astype(BF16)


def assemble_kernel(dest_ref, *refs):
    pieces, out_ref = refs[:-1], refs[-1]
    for q, piece in enumerate(pieces):
        out_ref[dest_ref[q]] = piece[...]


def assemble(dest, pieces):
    count = len(pieces)
    rows, width = pieces[0].shape
    size = count * rows * width
    return pl.pallas_call(
        assemble_kernel,
        grid_spec=pltpu.PrefetchScalarGridSpec(
            num_scalar_prefetch=1,
            grid=(1,),
            in_specs=[pl.BlockSpec((rows, width), lambda i, d: (0, 0))] * count,
            out_specs=pl.BlockSpec((count, rows, width), lambda i, d: (0, 0, 0)),
        ),
        out_shape=jax.ShapeDtypeStruct((count, rows, width), pieces[0].dtype),
        compiler_params=params(),
        cost_estimate=pl.CostEstimate(flops=size, bytes_accessed=4 * size, transcendentals=0),
    )(dest, *pieces)


def gate_up_kernel(x_ref, gate_ref, up_ref, keep_ref, send_ref):
    half = keep_ref.shape[1]
    x = x_ref[...]
    for at, weight in enumerate((gate_ref, up_ref)):
        value = jnp.dot(x, weight[...], preferred_element_type=F32)
        keep_ref[at] = value[:half]
        send_ref[at] = value[half:].astype(BF16)


def gate_up(x, w_gate, w_up, start, width):
    rows, depth = x.shape
    half = rows // 2
    tile = tile_of(width, 384)
    first = start // tile
    weight = pl.BlockSpec((depth, tile), lambda j: (0, first + j))
    part = pl.BlockSpec((2, half, tile), lambda j: (0, 0, j))
    return pl.pallas_call(
        gate_up_kernel,
        grid=(width // tile,),
        in_specs=[pl.BlockSpec((rows, depth), lambda j: (0, 0)), weight, weight],
        out_specs=[part, part],
        out_shape=[
            jax.ShapeDtypeStruct((2, half, width), F32),
            jax.ShapeDtypeStruct((2, half, width), BF16),
        ],
        compiler_params=params(),
        cost_estimate=pl.CostEstimate(
            flops=4 * rows * depth * width,
            bytes_accessed=4 * depth * width + 2 * rows * depth + 6 * rows * width,
            transcendentals=0,
        ),
    )(x, w_gate, w_up)


def down_kernel(has_sum, last, dest_ref, *refs):
    hidden, refs = refs[:4], refs[4:]
    weight_ref, refs = refs[0], refs[1:]
    x = jnp.concatenate([h[...] for h in hidden], axis=0)
    value = jnp.dot(x, weight_ref[...], preferred_element_type=F32)
    if has_sum:
        value = value + refs[0][...]
        refs = refs[1:]
    if not last:
        refs[0][...] = value
        return
    keep_ref, send_ref, scratch = refs
    groups = scratch.shape[0]
    scratch[...] = value.reshape(scratch.shape)
    for q in range(0, groups, 2):
        keep_ref[q // 2] = scratch[dest_ref[q]]
        send_ref[q // 2] = scratch[dest_ref[q + 1]].astype(BF16)


def down(dest, hidden, w_down, start, total, groups, last):
    part_rows, depth = hidden[0].shape
    rows = 4 * part_rows
    width = w_down.shape[1]
    tile = tile_of(width, 384)
    first = start // depth
    in_specs = [pl.BlockSpec((part_rows, depth), lambda j, d: (0, 0))] * 4
    in_specs.append(pl.BlockSpec((depth, tile), lambda j, d: (first, j)))
    args = [*hidden, w_down]
    block = pl.BlockSpec((rows, tile), lambda j, d: (0, j))
    if total is not None:
        in_specs.append(block)
        args.append(total)
    aliases = {}
    scratch = []
    if last:
        shape = (groups // 2, rows // groups, width)
        part = pl.BlockSpec((groups // 2, rows // groups, tile), lambda j, d: (0, 0, j))
        out_specs = [part, part]
        out_shape = [jax.ShapeDtypeStruct(shape, F32), jax.ShapeDtypeStruct(shape, BF16)]
        scratch = [pltpu.VMEM((groups, rows // groups, tile), F32)]
    else:
        out_specs = block
        out_shape = jax.ShapeDtypeStruct((rows, width), F32)
    return pl.pallas_call(
        functools.partial(down_kernel, total is not None, last),
        grid_spec=pltpu.PrefetchScalarGridSpec(
            num_scalar_prefetch=1,
            grid=(width // tile,),
            in_specs=in_specs,
            out_specs=out_specs,
            scratch_shapes=scratch,
        ),
        out_shape=out_shape,
        input_output_aliases=aliases,
        compiler_params=params(),
        cost_estimate=pl.CostEstimate(
            flops=2 * rows * depth * width,
            bytes_accessed=2 * depth * width + 8 * rows * width,
            transcendentals=0,
        ),
    )(dest, *args)


def cache_kernel(scale, lengths_ref, query_ref, key_ref, value_ref, acc_ref, top_ref, sum_ref):
    length = lengths_ref[pl.program_id(0)]
    scores = scale * lax.dot_general(
        query_ref[0], key_ref[0], (((1,), (1,)), ((), ())), preferred_element_type=F32
    )
    heads = scores.shape[0]
    live = lax.broadcasted_iota(jnp.int32, scores.shape, 1) < length
    scores = jnp.where(live, scores, -jnp.inf)
    top = jnp.max(scores, axis=1, keepdims=True)
    weights = jnp.exp(scores - top)
    high = weights.astype(BF16)
    low = (weights - high.astype(F32)).astype(BF16)
    both = jnp.dot(
        jnp.concatenate((high, low), axis=0), value_ref[0], preferred_element_type=F32
    )
    acc_ref[0] = both[:heads] + both[heads:]
    top_ref[0] = top
    sum_ref[0] = jnp.sum(weights, axis=1, keepdims=True)


def attend_cache(grouped, key_cache, value_cache, lengths):
    batch, heads, depth = grouped.shape
    span = key_cache.shape[1]
    row = lambda r, n: (r, 0, 0)
    cache = pl.BlockSpec((1, span, depth), row)
    return pl.pallas_call(
        functools.partial(cache_kernel, 1.0 / math.sqrt(depth)),
        grid_spec=pltpu.PrefetchScalarGridSpec(
            num_scalar_prefetch=1,
            grid=(batch,),
            in_specs=[pl.BlockSpec((1, heads, depth), row), cache, cache],
            out_specs=[
                pl.BlockSpec((1, heads, depth), row),
                pl.BlockSpec((1, heads, 1), row),
                pl.BlockSpec((1, heads, 1), row),
            ],
        ),
        out_shape=[
            jax.ShapeDtypeStruct((batch, heads, depth), F32),
            jax.ShapeDtypeStruct((batch, heads, 1), F32),
            jax.ShapeDtypeStruct((batch, heads, 1), F32),
        ],
        compiler_params=params(),
        cost_estimate=pl.CostEstimate(
            flops=6 * batch * heads * span * depth,
            bytes_accessed=4 * batch * span * depth,
            transcendentals=batch * heads * span,
        ),
    )(lengths, grouped, key_cache, value_cache)


def attend_new(grouped, cached, key_new, value_new):
    acc, top_cached, sum_cached = cached
    batch = grouped.shape[0]
    scale = 1.0 / math.sqrt(grouped.shape[2])
    own = jnp.einsum("rhd,rd->rh", grouped, key_new, preferred_element_type=F32)
    own = own[:, :, None] * scale
    top = jnp.maximum(top_cached, own)
    old = jnp.exp(top_cached - top)
    new = jnp.exp(own - top)
    total = sum_cached * old + new
    context = (acc * old + new * value_new.astype(F32)[:, None, :]) / total
    return context.astype(BF16).reshape(batch, -1)


def body(n_gx, n_gy, tokens, gain, w_gate, w_up, w_down, w_kv, queries, key_cache, value_cache, lengths):
    gx = lax.axis_index("gx")
    gy = lax.axis_index("gy")
    swap_x = lambda x, bits: swap(x, "gx", n_gx, bits)
    swap_y = lambda x, bits: swap(x, "gy", n_gy, bits)
    blocks = n_gx // n_gy

    group = gx ^ jnp.arange(n_gx, dtype=jnp.int32)
    turn = (group // blocks) ^ gy
    dest = (((turn & 1) << 1) | (turn >> 1)) * blocks + group % blocks

    normed = layer_norm(tokens, gain)
    grid_in = lax.all_to_all(normed, "gy", split_axis=1, concat_axis=0, tiled=True)
    group_rows = grid_in.shape[0]
    pieces = [None] * n_gx
    for q in range(0, n_gx, 2):
        pieces[q] = swap_x(grid_in, q) if q else grid_in
    for q in range(0, n_gx, 2):
        pieces[q + 1] = swap_x(pieces[q], 1)
    x = assemble(dest, pieces).reshape(n_gx * group_rows, -1)
    rows = x.shape[0]

    batch = tokens.shape[0]
    grouped = queries.reshape(batch, -1, HD)
    cached = attend_cache(grouped, key_cache, value_cache, lengths)

    slab = w_kv.shape[1]
    part = jnp.dot(
        lax.dynamic_slice_in_dim(x, gx * slab, slab, 1), w_kv[0], preferred_element_type=F32
    )
    order = jnp.arange(n_gx, dtype=jnp.int32)
    turn_abs = (order // blocks) ^ gy
    place = (((turn_abs & 1) << 1) | (turn_abs >> 1)) * blocks + order % blocks
    part = part.reshape(n_gx, group_rows, -1)[place].reshape(rows, -1)
    fresh = lax.psum_scatter(part, ("gx", "gy"), scatter_dimension=0, tiled=True)
    key_new = fresh[:, :HD].astype(BF16)
    value_new = fresh[:, HD:].astype(BF16)

    hidden_cols = w_gate.shape[1]
    chunks = max(c for c in (1, 2, 3, 4) if hidden_cols % (128 * c) == 0)
    width = hidden_cols // chunks
    quarter = rows // 4
    total = None
    for c in range(chunks):
        keep, send = gate_up(x, w_gate, w_up, c * width, width)
        near = keep + swap_y(send, 1).astype(F32)
        pair = near[:, :quarter] + swap_y(near[:, quarter:].astype(BF16), 2).astype(F32)
        own = (jax.nn.silu(pair[0]) * pair[1]).astype(BF16)
        across = swap_y(own, 2)
        hidden = (own, across, swap_y(own, 1), swap_y(across, 1))
        total = down(dest, hidden, w_down, c * width, total, n_gx, c == chunks - 1)

    keep, send = total
    near = keep + swap_x(send, 1).astype(F32)
    back = near[0]
    for t in range(1, n_gx // 2):
        back = back + swap_x(near[t].astype(BF16), 2 * t).astype(F32)
    ffn = lax.all_to_all(back, "gy", split_axis=0, concat_axis=1, tiled=True)
    mixed = (tokens.astype(F32) + ffn).astype(BF16)
    context = attend_new(grouped, cached, key_new, value_new)
    return (mixed, context)


def solution(mesh):
    sizes = dict(mesh.shape)
    return jax.shard_map(
        functools.partial(body, sizes["gx"], sizes["gy"]),
        mesh=mesh,
        in_specs=(
            P(("gx", "gy"), None),
            P(),
            P("gy", "gx"),
            P("gy", "gx"),
            P("gx", "gy"),
            P("gy", "gx", None),
            P(("gx", "gy"), None),
            P(("gx", "gy"), None, None),
            P(("gx", "gy"), None, None),
            P(("gx", "gy")),
        ),
        out_specs=(P(("gx", "gy"), None), P(("gx", "gy"), None)),
        check_vma=False,
    )
```

time: 267 us -> 182 us (0.68)
  waiting for transfers between devices: 160 us -> 30.9 us
  Pallas kernels: 0 us -> 52.8 us
  matrix products: 30.5 us -> 1.06 us
  starting transfers between devices: 6.68 us -> 34.8 us
  between operations: 14.2 us -> 1.04 us
  local copies, waits for them, and re-layouts: 7.14 us -> 9.91 us
    psum x1 -> x0, waiting for transfers between devices: 94 us -> none  [body(): summed = lax.psum(pair, 'gy')]
    reduce_scatter x1 -> x0, waiting for transfers between devices: 65.2 us -> none  [body(): lax.psum_scatter(jnp.concatenate((jnp.dot(hidden, w_down, preferred_eleme...]
    pallas_call x0 -> x10, Pallas kernels: none -> 52.8 us  [the longest x4 25.2 us: gate_up(): pl.pallas_call(gate_up_kernel, grid=(width // tile,), in_specs=[pl.BlockS...]
    unnamed x0 -> x1, blocking collectives: none -> 40.9 us
    all_gather x1 -> x0, blocking collectives: 31.9 us -> none  [body(): piece = lax.all_gather(grid_in, 'gx', axis=0, tiled=True)]
    dot_general x7 -> x2, matrix products: 30.5 us -> 1.06 us  [the longest x1 0.94 us: body(): jnp.dot(lax.dynamic_slice_in_dim(x, gx * slab, slab, 1), w_kv[0], preferr...]
    ppermute x0 -> x31, starting transfers between devices: none -> 27.3 us  [swap(): return lax.ppermute(x, axis, [(i, i ^ bits) for i in range(size)])]
    ppermute x0 -> x31, waiting for transfers between devices: none -> 22.8 us  [swap(): return lax.ppermute(x, axis, [(i, i ^ bits) for i in range(size)])]
  transfers between devices with their start and end apart: 4 -> 33, of which waited for: 3 -> 10; matrix products, arithmetic and copies ran while one was open for 3% -> 6% of each run, Pallas kernels for 0% -> 12%
where the time goes in v1:
time: 182 us; the launch traced here: 181 us
  Pallas kernels  52.8 us (29%)
  blocking collectives  40.9 us (22%)
  starting transfers between devices  34.8 us (19%)
  waiting for transfers between devices  30.9 us (17%)
  local copies, waits for them, and re-layouts  9.91 us (5%)
  other arithmetic  9.49 us (5%)
    unnamed x1, blocking collectives  40.9 us
    ppermute x31, starting transfers between devices, swap(): return lax.ppermute(x, axis, [(i, i ^ bits) for i in range(size)])  27.3 us
    pallas_call x4, Pallas kernels, gate_up(): pl.pallas_call(gate_up_kernel, grid=(width // tile,), in_specs=[pl.BlockS...  25.2 us
    ppermute x31, waiting for transfers between devices, swap(): return lax.ppermute(x, axis, [(i, i ^ bits) for i in range(size)])  22.8 us
    pallas_call x4, Pallas kernels, down(): pl.pallas_call(functools.partial(down_kernel, total is not None, last), g...  22.4 us
    unnamed x14, local copies, waits for them, and re-layouts  6.65 us
    pallas_call x1, Pallas kernels, attend_cache(): pl.pallas_call(functools.partial(cache_kernel, 1.0 / math.sqrt(depth)), g...  4.59 us
    all_to_all x1, starting transfers between devices, body(): lax.all_to_all(normed, 'gy', split_axis=1, concat_axis=0, tiled=True)  4.21 us
  transfers between devices with their start and end apart: 33, of which 10 were waited for; matrix products, arithmetic and copies ran while one was open for 6% of the time, Pallas kernels for 12%

profile of v1, /device:TPU:0, one launch (start us, length us, event | category | flops | bytes accessed | tf_op | source)
XLA Modules:
  0.0 180.9 jit_solution(1024837630669217504)
XLA Ops:
  2.9 1.6 fusion.6
  4.6 4.2 %all-to-all-start = ((bf16[4,4,2304]{2,0,1:T(4,128)(2,1)}), bf16[4,4,2304]{2,0,1:T(4,128)(2,1)S(1)}, u32[]{:S(2)}, u32[]{:S(2)}) async-start(bf16[4,4,2304]{2,0,1:T(4,128)(2,1)} %bitcast), calls=%async_computation | async-start | bytes 147456 | tf_op jit(solution)/shard_map/all_to_all | solution.py:234
  8.8 4.1 %all-to-all-done = bf16[4,4,2304]{2,0,1:T(4,128)(2,1)S(1)} async-done(((bf16[4,4,2304]{2,0,1:T(4,128)(2,1)}), bf16[4,4,2304]{2,0,1:T(4,128)(2,1)S(1)}, u32[]{:S(2)}, u32[]{:S(2)}) %all-to-all-start) | async-done | bytes 73760 | tf_op jit(solution)/shard_map/all_to_all | solution.py:234
  13.0 2.1 %collective-permute-start.1 = (bf16[16,2304]{1,0:T(8,128)(2,1)S(1)}, bf16[16,2304]{1,0:T(8,128)(2,1)S(1)}, u32[]{:S(2)}, u32[]{:S(2)}) collective-permute-start(bf16[16,2304]{1,0:T(8,128)(2,1)S(1)} %all_to_all.31.refs_0_), channel_id=1, source_target_pairs={{0,8},{4,12},{8,0},{12,4},{16,24},{20,28},{24,16},{28,20},{1,9},{5... | collective-permute-start | bytes 221192 | tf_op jit(solution)/shard_map/ppermute | solution.py:26
  15.1 2.6 %collective-permute-start.3 = (bf16[16,2304]{1,0:T(8,128)(2,1)S(1)}, bf16[16,2304]{1,0:T(8,128)(2,1)S(1)}, u32[]{:S(2)}, u32[]{:S(2)}) collective-permute-start(bf16[16,2304]{1,0:T(8,128)(2,1)S(1)} %all_to_all.31.refs_0_), channel_id=1, source_target_pairs={{0,16},{4,20},{8,24},{12,28},{16,0},{20,4},{24,8},{28,12},{1,17},{... | collective-permute-start | bytes 221192 | tf_op jit(solution)/shard_map/ppermute | solution.py:26
  17.7 1.7 collective-permute-start
  19.8 2.9 %collective-permute-done.3.refs_4_ = bf16[16,2304]{1,0:T(8,128)(2,1)S(1)} collective-permute-done((bf16[16,2304]{1,0:T(8,128)(2,1)S(1)}, bf16[16,2304]{1,0:T(8,128)(2,1)S(1)}, u32[]{:S(2)}, u32[]{:S(2)}) %collective-permute-start.3) | collective-permute-done | bytes 73760 | tf_op jit(solution)/shard_map/ppermute | solution.py:26
  22.7 1.5 collective-permute-start.4
  26.4 2.2 %copy-done.1 = bf16[4,2048,256]{2,1,0:T(8,128)(2,1)S(1)} copy-done((bf16[4,2048,256]{2,1,0:T(8,128)(2,1)S(1)}, bf16[4,2048,256]{2,1,0:T(8,128)(2,1)}, u32[]{:S(2)}) %copy-start.1) | copy-done | bytes 4194328
  28.6 2.2 %copy-done.2 = bf16[4,2048,256]{2,1,0:T(8,128)(2,1)S(1)} copy-done((bf16[4,2048,256]{2,1,0:T(8,128)(2,1)S(1)}, bf16[4,2048,256]{2,1,0:T(8,128)(2,1)}, u32[]{:S(2)}) %copy-start.2) | copy-done | bytes 4194328
  31.4 4.6 %shard_map.122 = (f32[4,48,256]{2,1,0:T(8,128)S(1)}, f32[4,48,1]{2,1,0:T(8,128)S(1)}, f32[4,48,1]{2,1,0:T(8,128)S(1)}) custom-call(s32[4]{0:T(128)S(1)} %copy-done.3, bf16[4,48,256]{2,1,0:T(8,128)(2,1)S(1)} %bitcast.88, bf16[4,2048,256]{2,1,0:T(8,128)(2,1)S(1)} %copy-done.1, bf16[4,2048,256]{2,1,0:T(8,128)(2,1)S(1)} %copy-done.2), custom_call_target="tpu_custom_call" | custom-call | flops 603979776 | bytes 8388608 | tf_op jit(solution)/shard_map/pallas_call | solution.py:182
  36.7 6.5 %shard_map.117 = (f32[2,64,1152]{2,1,0:T(8,128)S(1)}, bf16[2,64,1152]{2,1,0:T(8,128)(2,1)}) custom-call(bf16[128,2304]{1,0:T(8,128)(2,1)S(1)} %bitcast.83, bf16[2304,4608]{1,0:T(8,128)(2,1)} %gate_ref.7, bf16[2304,4608]{1,0:T(8,128)(2,1)} %up_ref.7), custom_call_target="tpu_custom_call" | custom-call | flops 1358954496 | bytes 12091392 | tf_op jit(solution)/shard_map/pallas_call | solution.py:76
  43.1 6.5 %shard_map.116 = (f32[2,64,1152]{2,1,0:T(8,128)S(1)}, bf16[2,64,1152]{2,1,0:T(8,128)(2,1)}) custom-call(bf16[128,2304]{1,0:T(8,128)(2,1)S(1)} %bitcast.84, bf16[2304,4608]{1,0:T(8,128)(2,1)} %gate_ref.7, bf16[2304,4608]{1,0:T(8,128)(2,1)} %up_ref.7), custom_call_target="tpu_custom_call" | custom-call | flops 1358954496 | bytes 12091392 | tf_op jit(solution)/shard_map/pallas_call | solution.py:76
  49.6 6.5 %shard_map.115 = (f32[2,64,1152]{2,1,0:T(8,128)S(1)}, bf16[2,64,1152]{2,1,0:T(8,128)(2,1)}) custom-call(bf16[128,2304]{1,0:T(8,128)(2,1)S(1)} %bitcast.85, bf16[2304,4608]{1,0:T(8,128)(2,1)} %gate_ref.7, bf16[2304,4608]{1,0:T(8,128)(2,1)} %up_ref.7), custom_call_target="tpu_custom_call" | custom-call | flops 1358954496 | bytes 12091392 | tf_op jit(solution)/shard_map/pallas_call | solution.py:76
  56.1 5.8 %shard_map.114 = (f32[2,64,1152]{2,1,0:T(8,128)S(1)}, bf16[2,64,1152]{2,1,0:T(8,128)(2,1)S(1)}) custom-call(bf16[128,2304]{1,0:T(8,128)(2,1)S(1)} %bitcast.86, bf16[2304,4608]{1,0:T(8,128)(2,1)} %gate_ref.7, bf16[2304,4608]{1,0:T(8,128)(2,1)} %up_ref.7), custom_call_target="tpu_custom_call" | custom-call | flops 1358954496 | bytes 12091392 | tf_op jit(solution)/shard_map/pallas_call | solution.py:76
  64.0 2.2 %gather_fusion = f32[8,16,512]{2,1,0:T(8,128)} fusion(f32[8,16,512]{2,1,0:T(8,128)} %fusion, s32[1024]{0:T(1024)S(1)} %pad_clamp_fusion), kind=kCustom, calls=%fused_computation | custom fusion | bytes 524320 | tf_op jit(solution)/shard_map/gather | solution.py:255
  66.2 40.9 %all-reduce.2 = bf16[128,512]{1,0:T(8,128)(2,1)S(1)} all-reduce(f32[128,512]{1,0:T(8,128)} %bitcast.89), channel_id=2, replica_groups=mesh['gx'=8,'gy'=4] {'gx','gy'}, use_global_device_ids=true, to_apply=%region_2.3.clone | all-reduce | flops 65536 | bytes 393216
  108.3 1.5 collective-permute-start.23
  115.9 1.5 collective-permute-start.24
  119.8 1.7 collective-permute-done.13
  121.5 2.6 %collective-permute-done.8 = bf16[2,32,1152]{2,1,0:T(8,128)(2,1)S(1)} collective-permute-done((bf16[2,32,1152]{2,1,0:T(8,128)(2,1)S(1)}, bf16[2,32,1152]{2,1,0:T(8,128)(2,1)S(1)}, u32[]{:S(2)}, u32[]{:S(2)}) %collective-permute-start.8) | collective-permute-done | bytes 147488 | tf_op jit(solution)/shard_map/ppermute | solution.py:26
  126.9 1.6 collective-permute-done.14.refs_1_
  129.0 5.6 %shard_map.118.refs_5_ = f32[128,2304]{1,0:T(8,128)S(1)} custom-call(s32[8]{0:T(128)S(1)} %fusion.27.dest_ref, bf16[32,1152]{1,0:T(8,128)(2,1)S(1)} %fusion.12.refs_0_, bf16[32,1152]{1,0:T(8,128)(2,1)S(1)} %collective-permute-done.24.refs_1_, bf16[32,1152]{1,0:T(8,128)(2,1)S(1)} %collective-permute-done.25.refs_2_, ...), custom_call_target="tpu_custom_call" | custom-call | flops 679477248 | bytes 7667712 | tf_op jit(solution)/shard_map/pallas_call | solution.py:137
  135.2 5.6 %shard_map.119.refs_5_ = f32[128,2304]{1,0:T(8,128)S(1)} custom-call(s32[8]{0:T(128)S(1)} %fusion.27.dest_ref, bf16[32,1152]{1,0:T(8,128)(2,1)S(1)} %fusion.14.refs_0_, bf16[32,1152]{1,0:T(8,128)(2,1)S(1)} %collective-permute-done.19.refs_1_, bf16[32,1152]{1,0:T(8,128)(2,1)S(1)} %collective-permute-done.20.refs_2_, ...), custom_call_target="tpu_custom_call" | custom-call | flops 679477248 | bytes 7667712 | tf_op jit(solution)/shard_map/pallas_call | solution.py:137
  140.8 5.6 %shard_map.120.refs_5_ = f32[128,2304]{1,0:T(8,128)S(1)} custom-call(s32[8]{0:T(128)S(1)} %fusion.27.dest_ref, bf16[32,1152]{1,0:T(8,128)(2,1)S(1)} %fusion.16.refs_0_, bf16[32,1152]{1,0:T(8,128)(2,1)S(1)} %collective-permute-done.14.refs_1_, bf16[32,1152]{1,0:T(8,128)(2,1)S(1)} %collective-permute-done.15.refs_2_, ...), custom_call_target="tpu_custom_call" | custom-call | flops 679477248 | bytes 7667712 | tf_op jit(solution)/shard_map/pallas_call | solution.py:137
  146.5 5.7 %shard_map.121 = (f32[4,16,2304]{2,1,0:T(8,128)S(1)}, bf16[4,16,2304]{2,1,0:T(8,128)(2,1)S(1)}) custom-call(s32[8]{0:T(128)S(1)} %fusion.27.dest_ref, bf16[32,1152]{1,0:T(8,128)(2,1)S(1)} %fusion.18.refs_0_, bf16[32,1152]{1,0:T(8,128)(2,1)S(1)} %collective-permute-done.9.refs_1_, bf16[32,1152]{1,0:T(8,128)(2,1)S(1)} %collective-permute-done.10.refs_2_, ...), custom_call_target="tpu_custom_call" | custom-call | flops 679477248 | bytes 7667712 | tf_op jit(solution)/shard_map/pallas_call | solution.py:137
  153.8 7.4 %collective-permute-done.27 = bf16[4,16,2304]{2,1,0:T(8,128)(2,1)S(1)} collective-permute-done((bf16[4,16,2304]{2,1,0:T(8,128)(2,1)S(1)}, bf16[4,16,2304]{2,1,0:T(8,128)(2,1)S(1)}, u32[]{:S(2)}, u32[]{:S(2)}) %collective-permute-start.27) | collective-permute-done | bytes 294944 | tf_op jit(solution)/shard_map/ppermute | solution.py:26
  161.3 2.1 %collective-permute-start.28 = (bf16[16,2304]{1,0:T(8,128)(2,1)S(1)}, bf16[16,2304]{1,0:T(8,128)(2,1)S(1)}, u32[]{:S(2)}, u32[]{:S(2)}) collective-permute-start(bf16[16,2304]{1,0:T(8,128)(2,1)S(1)} %get-tuple-element.33), channel_id=1, source_target_pairs={{0,8},{4,12},{8,0},{12,4},{16,24},{20,28},{24,16},{28,20},{1,9},{5... | collective-permute-start | bytes 221192 | tf_op jit(solution)/shard_map/ppermute | solution.py:26
  164.3 1.5 collective-permute-start.30
  166.0 5.4 %collective-permute-done.29 = bf16[16,2304]{1,0:T(8,128)(2,1)S(1)} collective-permute-done((bf16[16,2304]{1,0:T(8,128)(2,1)S(1)}, bf16[16,2304]{1,0:T(8,128)(2,1)S(1)}, u32[]{:S(2)}, u32[]{:S(2)}) %collective-permute-start.29) | collective-permute-done | bytes 73760 | tf_op jit(solution)/shard_map/ppermute | solution.py:26
  172.1 3.3 %all-to-all-start.1 = ((f32[4,4,2304]{2,1,0:T(4,128)}), f32[4,4,2304]{2,1,0:T(4,128)S(1)}, u32[]{:S(2)}, u32[]{:S(2)}) async-start(f32[4,4,2304]{2,1,0:T(4,128)} %all_to_all.32), calls=%async_computation.1 | async-start | bytes 294912 | tf_op jit(solution)/shard_map/all_to_all | solution.py:279
  176.3 3.9 %all-to-all-done.1 = f32[4,4,2304]{2,1,0:T(4,128)S(1)} async-done(((f32[4,4,2304]{2,1,0:T(4,128)}), f32[4,4,2304]{2,1,0:T(4,128)S(1)}, u32[]{:S(2)}, u32[]{:S(2)}) %all-to-all-start.1) | async-done | bytes 147488 | tf_op jit(solution)/shard_map/all_to_all | solution.py:279
  (99 shorter events, 26.7 us)
Async XLA Ops:
  4.6 8.4 %all-to-all-start = ((bf16[4,4,2304]{2,0,1:T(4,128)(2,1)}), bf16[4,4,2304]{2,0,1:T(4,128)(2,1)S(1)}, u32[]{:S(2)}, u32[]{:S(2)}) async-start(bf16[4,4,2304]{2,0,1:T(4,128)(2,1)} %bitcast), calls=%async_computation | async-start | bytes 147456 | tf_op jit(solution)/shard_map/all_to_all | solution.py:234
  13.0 6.5 %collective-permute-start.1 = (bf16[16,2304]{1,0:T(8,128)(2,1)S(1)}, bf16[16,2304]{1,0:T(8,128)(2,1)S(1)}, u32[]{:S(2)}, u32[]{:S(2)}) collective-permute-start(bf16[16,2304]{1,0:T(8,128)(2,1)S(1)} %all_to_all.31.refs_0_), channel_id=1, source_target_pairs={{0,8},{4,12},{8,0},{12,4},{16,24},{20,28},{24,16},{28,20},{1,9},{5... | collective-permute-start | bytes 221192 | tf_op jit(solution)/shard_map/ppermute | solution.py:26
  15.1 7.6 %collective-permute-start.3 = (bf16[16,2304]{1,0:T(8,128)(2,1)S(1)}, bf16[16,2304]{1,0:T(8,128)(2,1)S(1)}, u32[]{:S(2)}, u32[]{:S(2)}) collective-permute-start(bf16[16,2304]{1,0:T(8,128)(2,1)S(1)} %all_to_all.31.refs_0_), channel_id=1, source_target_pairs={{0,16},{4,20},{8,24},{12,28},{16,0},{20,4},{24,8},{28,12},{1,17},{... | collective-permute-start | bytes 221192 | tf_op jit(solution)/shard_map/ppermute | solution.py:26
  17.7 6.5 %collective-permute-start.5 = (bf16[16,2304]{1,0:T(8,128)(2,1)S(1)}, bf16[16,2304]{1,0:T(8,128)(2,1)S(1)}, u32[]{:S(2)}, u32[]{:S(2)}) collective-permute-start(bf16[16,2304]{1,0:T(8,128)(2,1)S(1)} %all_to_all.31.refs_0_), channel_id=1, source_target_pairs={{0,24},{4,28},{8,16},{12,20},{16,8},{20,12},{24,0},{28,4},{1,25},{... | collective-permute-start | bytes 221192 | tf_op jit(solution)/shard_map/ppermute | solution.py:26
  17.7 18.3 %collective-permute-start = (bf16[16,2304]{1,0:T(8,128)(2,1)S(1)}, bf16[16,2304]{1,0:T(8,128)(2,1)S(1)}, u32[]{:S(2)}, u32[]{:S(2)}) collective-permute-start(bf16[16,2304]{1,0:T(8,128)(2,1)S(1)} %all_to_all.31.refs_0_), channel_id=1, source_target_pairs={{0,4},{4,0},{8,12},{12,8},{16,20},{20,16},{24,28},{28,24},{1,5},{5... | collective-permute-start | bytes 221192 | tf_op jit(solution)/shard_map/ppermute | solution.py:26
  19.4 16.6 %collective-permute-start.2 = (bf16[16,2304]{1,0:T(8,128)(2,1)S(1)}, bf16[16,2304]{1,0:T(8,128)(2,1)S(1)}, u32[]{:S(2)}, u32[]{:S(2)}) collective-permute-start(bf16[16,2304]{1,0:T(8,128)(2,1)S(1)} %collective-permute-done.1.refs_2_), channel_id=1, source_target_pairs={{0,4},{4,0},{8,12},{12,8},{16,20},{20,16},{24,28},{28,24},{1,5},{5... | collective-permute-start | bytes 221192 | tf_op jit(solution)/shard_map/ppermute | solution.py:26
  22.7 13.4 %collective-permute-start.4 = (bf16[16,2304]{1,0:T(8,128)(2,1)S(1)}, bf16[16,2304]{1,0:T(8,128)(2,1)S(1)}, u32[]{:S(2)}, u32[]{:S(2)}) collective-permute-start(bf16[16,2304]{1,0:T(8,128)(2,1)S(1)} %collective-permute-done.3.refs_4_), channel_id=1, source_target_pairs={{0,4},{4,0},{8,12},{12,8},{16,20},{20,16},{24,28},{28,24},{1,5},{5... | collective-permute-start | bytes 221192 | tf_op jit(solution)/shard_map/ppermute | solution.py:26
  24.2 11.9 %collective-permute-start.6 = (bf16[16,2304]{1,0:T(8,128)(2,1)S(1)}, bf16[16,2304]{1,0:T(8,128)(2,1)S(1)}, u32[]{:S(2)}, u32[]{:S(2)}) collective-permute-start(bf16[16,2304]{1,0:T(8,128)(2,1)S(1)} %collective-permute-done.5.refs_6_), channel_id=1, source_target_pairs={{0,4},{4,0},{8,12},{12,8},{16,20},{20,16},{24,28},{28,24},{1,5},{5... | collective-permute-start | bytes 221192 | tf_op jit(solution)/shard_map/ppermute | solution.py:26
  61.9 45.3 %collective-permute-start.22 = (bf16[2,64,1152]{2,1,0:T(8,128)(2,1)}, bf16[2,64,1152]{2,1,0:T(8,128)(2,1)}, u32[]{:S(2)}, u32[]{:S(2)}) collective-permute-start(bf16[2,64,1152]{2,1,0:T(8,128)(2,1)} %get-tuple-element.22), channel_id=1, source_target_pairs={{0,1},{1,0},{2,3},{3,2},{4,5},{5,4},{6,7},{7,6},{8,9},{9,8},{10,11... | collective-permute-start | bytes 884744 | tf_op jit(solution)/shard_map/ppermute | solution.py:26
  61.9 47.8 %collective-permute-start.17 = (bf16[2,64,1152]{2,1,0:T(8,128)(2,1)}, bf16[2,64,1152]{2,1,0:T(8,128)(2,1)}, u32[]{:S(2)}, u32[]{:S(2)}) collective-permute-start(bf16[2,64,1152]{2,1,0:T(8,128)(2,1)} %get-tuple-element.20), channel_id=1, source_target_pairs={{0,1},{1,0},{2,3},{3,2},{4,5},{5,4},{6,7},{7,6},{8,9},{9,8},{10,11... | collective-permute-start | bytes 884744 | tf_op jit(solution)/shard_map/ppermute | solution.py:26
  62.4 49.1 %collective-permute-start.12 = (bf16[2,64,1152]{2,1,0:T(8,128)(2,1)}, bf16[2,64,1152]{2,1,0:T(8,128)(2,1)}, u32[]{:S(2)}, u32[]{:S(2)}) collective-permute-start(bf16[2,64,1152]{2,1,0:T(8,128)(2,1)} %get-tuple-element.18), channel_id=1, source_target_pairs={{0,1},{1,0},{2,3},{3,2},{4,5},{5,4},{6,7},{7,6},{8,9},{9,8},{10,11... | collective-permute-start | bytes 884744 | tf_op jit(solution)/shard_map/ppermute | solution.py:26
  62.5 51.6 %collective-permute-start.7 = (bf16[2,64,1152]{2,1,0:T(8,128)(2,1)S(1)}, bf16[2,64,1152]{2,1,0:T(8,128)(2,1)}, u32[]{:S(2)}, u32[]{:S(2)}) collective-permute-start(bf16[2,64,1152]{2,1,0:T(8,128)(2,1)S(1)} %get-tuple-element.16), channel_id=1, source_target_pairs={{0,1},{1,0},{2,3},{3,2},{4,5},{5,4},{6,7},{7,6},{8,9},{9,8},{10,11... | collective-permute-start | bytes 884744 | tf_op jit(solution)/shard_map/ppermute | solution.py:26
  108.3 7.5 %collective-permute-start.23 = (bf16[2,32,1152]{2,1,0:T(8,128)(2,1)S(1)}, bf16[2,32,1152]{2,1,0:T(8,128)(2,1)S(1)}, u32[]{:S(2)}, u32[]{:S(2)}) collective-permute-start(bf16[2,32,1152]{2,1,0:T(8,128)(2,1)S(1)} %slice.173), channel_id=1, source_target_pairs={{0,2},{1,3},{2,0},{3,1},{4,6},{5,7},{6,4},{7,5},{8,10},{9,11},{10,... | collective-permute-start | bytes 442376 | tf_op jit(solution)/shard_map/ppermute | solution.py:26
  110.9 7.4 %collective-permute-start.18 = (bf16[2,32,1152]{2,1,0:T(8,128)(2,1)S(1)}, bf16[2,32,1152]{2,1,0:T(8,128)(2,1)S(1)}, u32[]{:S(2)}, u32[]{:S(2)}) collective-permute-start(bf16[2,32,1152]{2,1,0:T(8,128)(2,1)S(1)} %slice.174), channel_id=1, source_target_pairs={{0,2},{1,3},{2,0},{3,1},{4,6},{5,7},{6,4},{7,5},{8,10},{9,11},{10,... | collective-permute-start | bytes 442376 | tf_op jit(solution)/shard_map/ppermute | solution.py:26
  112.6 8.9 %collective-permute-start.13 = (bf16[2,32,1152]{2,1,0:T(8,128)(2,1)S(1)}, bf16[2,32,1152]{2,1,0:T(8,128)(2,1)S(1)}, u32[]{:S(2)}, u32[]{:S(2)}) collective-permute-start(bf16[2,32,1152]{2,1,0:T(8,128)(2,1)S(1)} %slice.175), channel_id=1, source_target_pairs={{0,2},{1,3},{2,0},{3,1},{4,6},{5,7},{6,4},{7,5},{8,10},{9,11},{10,... | collective-permute-start | bytes 442376 | tf_op jit(solution)/shard_map/ppermute | solution.py:26
  115.1 9.0 %collective-permute-start.8 = (bf16[2,32,1152]{2,1,0:T(8,128)(2,1)S(1)}, bf16[2,32,1152]{2,1,0:T(8,128)(2,1)S(1)}, u32[]{:S(2)}, u32[]{:S(2)}) collective-permute-start(bf16[2,32,1152]{2,1,0:T(8,128)(2,1)S(1)} %slice.176), channel_id=1, source_target_pairs={{0,2},{1,3},{2,0},{3,1},{4,6},{5,7},{6,4},{7,5},{8,10},{9,11},{10,... | collective-permute-start | bytes 442376 | tf_op jit(solution)/shard_map/ppermute | solution.py:26
  115.9 9.7 %collective-permute-start.24 = (bf16[32,1152]{1,0:T(8,128)(2,1)S(1)}, bf16[32,1152]{1,0:T(8,128)(2,1)S(1)}, u32[]{:S(2)}, u32[]{:S(2)}) collective-permute-start(bf16[32,1152]{1,0:T(8,128)(2,1)S(1)} %fusion.12.refs_0_), channel_id=1, source_target_pairs={{0,2},{1,3},{2,0},{3,1},{4,6},{5,7},{6,4},{7,5},{8,10},{9,11},{10,... | collective-permute-start | bytes 221192 | tf_op jit(solution)/shard_map/ppermute | solution.py:26
  117.4 9.0 %collective-permute-start.25 = (bf16[32,1152]{1,0:T(8,128)(2,1)S(1)}, bf16[32,1152]{1,0:T(8,128)(2,1)S(1)}, u32[]{:S(2)}, u32[]{:S(2)}) collective-permute-start(bf16[32,1152]{1,0:T(8,128)(2,1)S(1)} %fusion.12.refs_0_), channel_id=1, source_target_pairs={{0,1},{1,0},{2,3},{3,2},{4,5},{5,4},{6,7},{7,6},{8,9},{9,8},{10,11... | collective-permute-start | bytes 221192 | tf_op jit(solution)/shard_map/ppermute | solution.py:26
  118.4 8.3 %collective-permute-start.19 = (bf16[32,1152]{1,0:T(8,128)(2,1)S(1)}, bf16[32,1152]{1,0:T(8,128)(2,1)S(1)}, u32[]{:S(2)}, u32[]{:S(2)}) collective-permute-start(bf16[32,1152]{1,0:T(8,128)(2,1)S(1)} %fusion.14.refs_0_), channel_id=1, source_target_pairs={{0,2},{1,3},{2,0},{3,1},{4,6},{5,7},{6,4},{7,5},{8,10},{9,11},{10,... | collective-permute-start | bytes 221192 | tf_op jit(solution)/shard_map/ppermute | solution.py:26
  121.4 13.2 %collective-permute-start.20 = (bf16[32,1152]{1,0:T(8,128)(2,1)S(1)}, bf16[32,1152]{1,0:T(8,128)(2,1)S(1)}, u32[]{:S(2)}, u32[]{:S(2)}) collective-permute-start(bf16[32,1152]{1,0:T(8,128)(2,1)S(1)} %fusion.14.refs_0_), channel_id=1, source_target_pairs={{0,1},{1,0},{2,3},{3,2},{4,5},{5,4},{6,7},{7,6},{8,9},{9,8},{10,11... | collective-permute-start | bytes 221192 | tf_op jit(solution)/shard_map/ppermute | solution.py:26
  124.2 4.4 %collective-permute-start.14 = (bf16[32,1152]{1,0:T(8,128)(2,1)S(1)}, bf16[32,1152]{1,0:T(8,128)(2,1)S(1)}, u32[]{:S(2)}, u32[]{:S(2)}) collective-permute-start(bf16[32,1152]{1,0:T(8,128)(2,1)S(1)} %fusion.16.refs_0_), channel_id=1, source_target_pairs={{0,2},{1,3},{2,0},{3,1},{4,6},{5,7},{6,4},{7,5},{8,10},{9,11},{10,... | collective-permute-start | bytes 221192 | tf_op jit(solution)/shard_map/ppermute | solution.py:26
  125.6 9.1 %collective-permute-start.9 = (bf16[32,1152]{1,0:T(8,128)(2,1)S(1)}, bf16[32,1152]{1,0:T(8,128)(2,1)S(1)}, u32[]{:S(2)}, u32[]{:S(2)}) collective-permute-start(bf16[32,1152]{1,0:T(8,128)(2,1)S(1)} %fusion.18.refs_0_), channel_id=1, source_target_pairs={{0,2},{1,3},{2,0},{3,1},{4,6},{5,7},{6,4},{7,5},{8,10},{9,11},{10,... | collective-permute-start | bytes 221192 | tf_op jit(solution)/shard_map/ppermute | solution.py:26
  126.7 8.5 %collective-permute-start.21 = (bf16[32,1152]{1,0:T(8,128)(2,1)S(1)}, bf16[32,1152]{1,0:T(8,128)(2,1)S(1)}, u32[]{:S(2)}, u32[]{:S(2)}) collective-permute-start(bf16[32,1152]{1,0:T(8,128)(2,1)S(1)} %collective-permute-done.19.refs_1_), channel_id=1, source_target_pairs={{0,1},{1,0},{2,3},{3,2},{4,5},{5,4},{6,7},{7,6},{8,9},{9,8},{10,11... | collective-permute-start | bytes 221192 | tf_op jit(solution)/shard_map/ppermute | solution.py:26
  128.5 12.3 %collective-permute-start.15 = (bf16[32,1152]{1,0:T(8,128)(2,1)S(1)}, bf16[32,1152]{1,0:T(8,128)(2,1)S(1)}, u32[]{:S(2)}, u32[]{:S(2)}) collective-permute-start(bf16[32,1152]{1,0:T(8,128)(2,1)S(1)} %fusion.16.refs_0_), channel_id=1, source_target_pairs={{0,1},{1,0},{2,3},{3,2},{4,5},{5,4},{6,7},{7,6},{8,9},{9,8},{10,11... | collective-permute-start | bytes 221192 | tf_op jit(solution)/shard_map/ppermute | solution.py:26
  128.5 12.3 %collective-permute-start.16 = (bf16[32,1152]{1,0:T(8,128)(2,1)S(1)}, bf16[32,1152]{1,0:T(8,128)(2,1)S(1)}, u32[]{:S(2)}, u32[]{:S(2)}) collective-permute-start(bf16[32,1152]{1,0:T(8,128)(2,1)S(1)} %collective-permute-done.14.refs_1_), channel_id=1, source_target_pairs={{0,1},{1,0},{2,3},{3,2},{4,5},{5,4},{6,7},{7,6},{8,9},{9,8},{10,11... | collective-permute-start | bytes 221192 | tf_op jit(solution)/shard_map/ppermute | solution.py:26
  134.6 11.8 %collective-permute-start.10 = (bf16[32,1152]{1,0:T(8,128)(2,1)S(1)}, bf16[32,1152]{1,0:T(8,128)(2,1)S(1)}, u32[]{:S(2)}, u32[]{:S(2)}) collective-permute-start(bf16[32,1152]{1,0:T(8,128)(2,1)S(1)} %fusion.18.refs_0_), channel_id=1, source_target_pairs={{0,1},{1,0},{2,3},{3,2},{4,5},{5,4},{6,7},{7,6},{8,9},{9,8},{10,11... | collective-permute-start | bytes 221192 | tf_op jit(solution)/shard_map/ppermute | solution.py:26
  134.7 11.8 %collective-permute-start.11 = (bf16[32,1152]{1,0:T(8,128)(2,1)S(1)}, bf16[32,1152]{1,0:T(8,128)(2,1)S(1)}, u32[]{:S(2)}, u32[]{:S(2)}) collective-permute-start(bf16[32,1152]{1,0:T(8,128)(2,1)S(1)} %collective-permute-done.9.refs_1_), channel_id=1, source_target_pairs={{0,1},{1,0},{2,3},{3,2},{4,5},{5,4},{6,7},{7,6},{8,9},{9,8},{10,11... | collective-permute-start | bytes 221192 | tf_op jit(solution)/shard_map/ppermute | solution.py:26
  152.1 9.1 %collective-permute-start.27 = (bf16[4,16,2304]{2,1,0:T(8,128)(2,1)S(1)}, bf16[4,16,2304]{2,1,0:T(8,128)(2,1)S(1)}, u32[]{:S(2)}, u32[]{:S(2)}) collective-permute-start(bf16[4,16,2304]{2,1,0:T(8,128)(2,1)S(1)} %get-tuple-element.24), channel_id=1, source_target_pairs={{0,4},{4,0},{8,12},{12,8},{16,20},{20,16},{24,28},{28,24},{1,5},{5... | collective-permute-start | bytes 884744 | tf_op jit(solution)/shard_map/ppermute | solution.py:26
  161.3 4.7 %collective-permute-start.28 = (bf16[16,2304]{1,0:T(8,128)(2,1)S(1)}, bf16[16,2304]{1,0:T(8,128)(2,1)S(1)}, u32[]{:S(2)}, u32[]{:S(2)}) collective-permute-start(bf16[16,2304]{1,0:T(8,128)(2,1)S(1)} %get-tuple-element.33), channel_id=1, source_target_pairs={{0,8},{4,12},{8,0},{12,4},{16,24},{20,28},{24,16},{28,20},{1,9},{5... | collective-permute-start | bytes 221192 | tf_op jit(solution)/shard_map/ppermute | solution.py:26
  163.4 8.0 %collective-permute-start.29 = (bf16[16,2304]{1,0:T(8,128)(2,1)S(1)}, bf16[16,2304]{1,0:T(8,128)(2,1)S(1)}, u32[]{:S(2)}, u32[]{:S(2)}) collective-permute-start(bf16[16,2304]{1,0:T(8,128)(2,1)S(1)} %get-tuple-element.35), channel_id=1, source_target_pairs={{0,16},{4,20},{8,24},{12,28},{16,0},{20,4},{24,8},{28,12},{1,17},{... | collective-permute-start | bytes 221192 | tf_op jit(solution)/shard_map/ppermute | solution.py:26
  164.3 7.1 %collective-permute-start.30 = (bf16[16,2304]{1,0:T(8,128)(2,1)S(1)}, bf16[16,2304]{1,0:T(8,128)(2,1)S(1)}, u32[]{:S(2)}, u32[]{:S(2)}) collective-permute-start(bf16[16,2304]{1,0:T(8,128)(2,1)S(1)} %get-tuple-element.34), channel_id=1, source_target_pairs={{0,24},{4,28},{8,16},{12,20},{16,8},{20,12},{24,0},{28,4},{1,25},{... | collective-permute-start | bytes 221192 | tf_op jit(solution)/shard_map/ppermute | solution.py:26
  172.1 8.1 %all-to-all-start.1 = ((f32[4,4,2304]{2,1,0:T(4,128)}), f32[4,4,2304]{2,1,0:T(4,128)S(1)}, u32[]{:S(2)}, u32[]{:S(2)}) async-start(f32[4,4,2304]{2,1,0:T(4,128)} %all_to_all.32), calls=%async_computation.1 | async-start | bytes 294912 | tf_op jit(solution)/shard_map/all_to_all | solution.py:279
  (7 other events, 104.7 us)

commit v2 on v0

v2 whole, which is shorter than its diff:
```python
import functools
import math

import jax
import jax.numpy as jnp
from jax import lax
from jax.experimental import pallas as pl
from jax.experimental.pallas import tpu as pltpu
from jax.sharding import PartitionSpec as P

HD = 256
F32 = jnp.float32
BF16 = jnp.bfloat16
MIB = 1024 * 1024
WHOLE = pl.BlockSpec(memory_space=pltpu.VMEM)
SCALARS = pl.BlockSpec(memory_space=pltpu.SMEM)
ANYWHERE = pl.BlockSpec(memory_space=pl.ANY)
ORDER = (0, 2, 1, 3)


def params(mib):
    return pltpu.CompilerParams(vmem_limit_bytes=mib * MIB)


def cost(flops, moved, transcendentals=0):
    return pl.CostEstimate(flops=flops, bytes_accessed=moved, transcendentals=transcendentals)


def tile_of(width, most):
    return max(t for t in range(128, most + 1, 128) if width % t == 0)


def swap(x, axis, size, bits):
    return lax.ppermute(x, axis, [(i, i ^ bits) for i in range(size)])


def norm_kernel(tokens_ref, gain_ref, out_ref):
    copies, blocks, _, width = out_ref.shape
    values = tokens_ref[...].astype(F32)
    centred = values - jnp.mean(values, axis=-1, keepdims=True)
    spread = jnp.mean(centred * centred, axis=-1, keepdims=True)
    normed = (centred * lax.rsqrt(spread + 1e-05) * gain_ref[...]).astype(BF16)
    for b in range(blocks):
        part = normed[:, b * width : (b + 1) * width]
        for c in range(copies):
            out_ref[c, b] = part


def norm(tokens, gain, n_gx, n_gy):
    batch, channels = tokens.shape
    return pl.pallas_call(
        norm_kernel,
        in_specs=[WHOLE, WHOLE],
        out_specs=WHOLE,
        out_shape=jax.ShapeDtypeStruct((n_gx, n_gy, batch, channels // n_gy), BF16),
        compiler_params=params(8),
        cost_estimate=cost(10 * tokens.size, 2 * n_gx * tokens.size),
    )(tokens, gain.reshape(1, -1))


def assemble_kernel(gy_ref, rows_ref, out_ref):
    devices, batch, _ = rows_ref.shape
    quarter = devices // 4
    pack = 16 // batch
    for at, turn in enumerate(ORDER):
        base = (gy_ref[0] ^ turn) * quarter
        for i in range(0, quarter, pack):
            tall = jnp.concatenate(
                [rows_ref[base + i + k].astype(F32) for k in range(pack)], axis=0
            )
            start = (at * quarter + i) * batch
            out_ref[start : start + 16] = tall.astype(BF16)


def assemble(gy, rows):
    devices, batch, width = rows.shape
    return pl.pallas_call(
        assemble_kernel,
        in_specs=[SCALARS, WHOLE],
        out_specs=WHOLE,
        out_shape=jax.ShapeDtypeStruct((devices * batch, width), BF16),
        compiler_params=params(12),
        cost_estimate=cost(2 * rows.size, 4 * rows.size),
    )(gy, rows)


def spread_rows(out_ref, value, gy, columns=slice(None)):
    devices, batch, _ = out_ref.shape
    quarter = devices // 4
    for at, turn in enumerate(ORDER):
        base = (gy ^ turn) * quarter
        for i in range(quarter):
            start = (at * quarter + i) * batch
            out_ref[base + i, :, columns] = value[start : start + batch].astype(out_ref.dtype)


def gate_up_tile(x, weights, at, tile, keep_ref, send_ref):
    half = keep_ref.shape[1]
    for k, weight in enumerate(weights):
        value = jnp.dot(x, weight, preferred_element_type=F32)
        keep_ref[k, :, at : at + tile] = value[:half]
        send_ref[k, :, at : at + tile] = value[half:].astype(BF16)


def gate_up_kernel(start, tile, x_ref, gate_ref, up_ref, after_ref, keep_ref, send_ref, slots, sems):
    del after_ref
    width = keep_ref.shape[2]
    depth = x_ref.shape[1]
    copies = []
    for at in range(0, width, tile):
        for k, source in enumerate((gate_ref, up_ref)):
            copies.append(
                pltpu.make_async_copy(
                    source.at[:, pl.ds(start + at, tile)],
                    slots.at[k, at // tile],
                    sems.at[k, at // tile],
                )
            )
    for copy in copies:
        copy.start()
    x = x_ref[...]
    for n in range(width // tile):
        for k in range(2):
            copies[2 * n + k].wait()
        gate_up_tile(x, [slots[k, n] for k in range(2)], n * tile, tile, keep_ref, send_ref)


def gate_up_ready_kernel(tile, x_ref, gate_ref, up_ref, keep_ref, send_ref):
    x = x_ref[...]
    for at in range(0, keep_ref.shape[2], tile):
        weights = [ref[:, at : at + tile] for ref in (gate_ref, up_ref)]
        gate_up_tile(x, weights, at, tile, keep_ref, send_ref)


def gate_up_shapes(rows, width):
    half = rows // 2
    return [
        jax.ShapeDtypeStruct((2, half, width), F32),
        jax.ShapeDtypeStruct((2, half, width), BF16),
    ]


def gate_up_ready(x, gate, up):
    rows, depth = x.shape
    width = gate.shape[1]
    return pl.pallas_call(
        functools.partial(gate_up_ready_kernel, tile_of(width, 384)),
        in_specs=[WHOLE, WHOLE, WHOLE],
        out_specs=[WHOLE, WHOLE],
        out_shape=gate_up_shapes(rows, width),
        compiler_params=params(16),
        cost_estimate=cost(4 * rows * depth * width, 2 * rows * depth),
    )(x, gate, up)


def gate_up(x, w_gate, w_up, start, width, after):
    rows, depth = x.shape
    tile = tile_of(width, 384)
    count = width // tile
    return pl.pallas_call(
        functools.partial(gate_up_kernel, start, tile),
        in_specs=[WHOLE, ANYWHERE, ANYWHERE, ANYWHERE],
        out_specs=[WHOLE, WHOLE],
        out_shape=gate_up_shapes(rows, width),
        scratch_shapes=[
            pltpu.VMEM((2, count, depth, tile), BF16),
            pltpu.SemaphoreType.DMA((2, count)),
        ],
        compiler_params=params(20),
        cost_estimate=cost(4 * rows * depth * width, 4 * depth * width),
    )(x, w_gate, w_up, after)


def down_kernel(start, tile, has_sum, last, gy_ref, *refs):
    hidden, (weight_ref, *refs) = refs[:4], refs[4:]
    sum_ref = refs.pop(0) if has_sum else None
    out_ref, slots, sems = refs
    depth = hidden[0].shape[1]
    width = weight_ref.shape[1]
    copies = [
        pltpu.make_async_copy(
            weight_ref.at[pl.ds(start, depth), pl.ds(at, tile)],
            slots.at[at // tile],
            sems.at[at // tile],
        )
        for at in range(0, width, tile)
    ]
    for copy in copies:
        copy.start()
    x = jnp.concatenate([h[...] for h in hidden], axis=0)
    gy = gy_ref[0]
    for n, copy in enumerate(copies):
        columns = slice(n * tile, (n + 1) * tile)
        copy.wait()
        value = jnp.dot(x, slots[n], preferred_element_type=F32)
        if has_sum:
            value = value + sum_ref[:, columns]
        if last:
            spread_rows(out_ref, value, gy, columns)
        else:
            out_ref[:, columns] = value


def down(gy, hidden, w_down, start, total, devices, last):
    part_rows, depth = hidden[0].shape
    rows = 4 * part_rows
    width = w_down.shape[1]
    tile = tile_of(width, 384)
    count = width // tile
    args = [gy, *hidden, w_down]
    in_specs = [SCALARS] + [WHOLE] * 4 + [ANYWHERE]
    if total is not None:
        args.append(total)
        in_specs.append(WHOLE)
    shape = (devices, rows // devices, width) if last else (rows, width)
    return pl.pallas_call(
        functools.partial(down_kernel, start, tile, total is not None, last),
        in_specs=in_specs,
        out_specs=WHOLE,
        out_shape=jax.ShapeDtypeStruct(shape, BF16 if last else F32),
        scratch_shapes=[
            pltpu.VMEM((count, depth, tile), BF16),
            pltpu.SemaphoreType.DMA((count,)),
        ],
        compiler_params=params(20),
        cost_estimate=cost(2 * rows * depth * width, 2 * depth * width),
    )(*args)


def finish_kernel(tokens_ref, sums_ref, out_ref):
    sources, blocks, _, width = sums_ref.shape
    for b in range(blocks):
        columns = slice(b * width, (b + 1) * width)
        ffn = sums_ref[0, b].astype(F32)
        for s in range(1, sources):
            ffn = ffn + sums_ref[s, b].astype(F32)
        out_ref[:, columns] = (tokens_ref[:, columns].astype(F32) + ffn).astype(BF16)


def finish(tokens, sums):
    return pl.pallas_call(
        finish_kernel,
        in_specs=[WHOLE, WHOLE],
        out_specs=WHOLE,
        out_shape=jax.ShapeDtypeStruct(tokens.shape, BF16),
        compiler_params=params(8),
        cost_estimate=cost(sums.size, 2 * sums.size),
    )(tokens, sums)


def fresh_kernel(gy_ref, x_ref, weight_ref, out_ref):
    value = jnp.dot(x_ref[...], weight_ref[0], preferred_element_type=F32)
    spread_rows(out_ref, value, gy_ref[0])


def fresh_part(gy, x, w_kv, devices):
    rows, depth = x.shape
    columns = w_kv.shape[2]
    return pl.pallas_call(
        fresh_kernel,
        in_specs=[SCALARS, WHOLE, WHOLE],
        out_specs=WHOLE,
        out_shape=jax.ShapeDtypeStruct((devices, rows // devices, columns), F32),
        compiler_params=params(8),
        cost_estimate=cost(2 * rows * depth * columns, 2 * depth * columns),
    )(gy, x, w_kv)


def cache_kernel(
    scale, tile, lengths_ref, query_ref, key_ref, value_ref, gate_ref, up_ref, after_ref,
    acc_ref, top_ref, sum_ref, gate_out, up_out, keys, values, cache_sems, weight_sems,
):
    del after_ref
    batch = query_ref.shape[0]
    caches = [
        [
            pltpu.make_async_copy(source.at[r], slots.at[r], cache_sems.at[k, r])
            for k, (source, slots) in enumerate(((key_ref, keys), (value_ref, values)))
        ]
        for r in range(batch)
    ]
    weights = [
        pltpu.make_async_copy(
            source.at[:, pl.ds(at, tile)],
            target.at[:, pl.ds(at, tile)],
            weight_sems.at[k, at // tile],
        )
        for at in range(0, gate_out.shape[1], tile)
        for k, (source, target) in enumerate(((gate_ref, gate_out), (up_ref, up_out)))
    ]
    for pair in caches:
        for copy in pair:
            copy.start()
    for copy in weights:
        copy.start()
    for r in range(batch):
        caches[r][0].wait()
        scores = scale * lax.dot_general(
            query_ref[r], keys[r], (((1,), (1,)), ((), ())), preferred_element_type=F32
        )
        heads = scores.shape[0]
        live = lax.broadcasted_iota(jnp.int32, scores.shape, 1) < lengths_ref[r]
        scores = jnp.where(live, scores, -jnp.inf)
        top = jnp.max(scores, axis=1, keepdims=True)
        chance = jnp.exp(scores - top)
        high = chance.astype(BF16)
        low = (chance - high.astype(F32)).astype(BF16)
        caches[r][1].wait()
        both = jnp.dot(
            jnp.concatenate((high, low), axis=0), values[r], preferred_element_type=F32
        )
        acc_ref[r] = both[:heads] + both[heads:]
        top_ref[r] = top
        sum_ref[r] = jnp.sum(chance, axis=1, keepdims=True)
    for copy in weights:
        copy.wait()


def attend_cache(grouped, key_cache, value_cache, lengths, w_gate, w_up, width, after):
    batch, heads, depth = grouped.shape
    span = key_cache.shape[1]
    tall = w_gate.shape[0]
    tile = tile_of(width, 384)
    *cached, gate, up = pl.pallas_call(
        functools.partial(cache_kernel, 1.0 / math.sqrt(depth), tile),
        in_specs=[SCALARS, WHOLE] + [ANYWHERE] * 5,
        out_specs=[WHOLE] * 5,
        out_shape=[
            jax.ShapeDtypeStruct((batch, heads, depth), F32),
            jax.ShapeDtypeStruct((batch, heads, 1), F32),
            jax.ShapeDtypeStruct((batch, heads, 1), F32),
            pltpu.VMEM((tall, width), BF16),
            pltpu.VMEM((tall, width), BF16),
        ],
        scratch_shapes=[
            pltpu.VMEM((batch, span, depth), BF16),
            pltpu.VMEM((batch, span, depth), BF16),
            pltpu.SemaphoreType.DMA((2, batch)),
            pltpu.SemaphoreType.DMA((2, width // tile)),
        ],
        compiler_params=params(24),
        cost_estimate=cost(
            6 * batch * heads * span * depth,
            4 * batch * span * depth + 4 * tall * width,
            batch * heads * span,
        ),
    )(lengths, grouped, key_cache, value_cache, w_gate, w_up, after)
    return cached, gate, up


def attend_new(grouped, cached, key_new, value_new):
    acc, top_cached, sum_cached = cached
    batch = grouped.shape[0]
    scale = 1.0 / math.sqrt(grouped.shape[2])
    own = jnp.einsum("rhd,rd->rh", grouped, key_new, preferred_element_type=F32)
    own = own[:, :, None] * scale
    top = jnp.maximum(top_cached, own)
    old = jnp.exp(top_cached - top)
    new = jnp.exp(own - top)
    total = sum_cached * old + new
    context = (acc * old + new * value_new.astype(F32)[:, None, :]) / total
    return context.astype(BF16).reshape(batch, -1)


def chunk_widths(columns):
    units = columns // 128
    first = units // 2
    second = (units - first) // 2
    return [128 * u for u in (first, second, units - first - second)]


def body(n_gx, n_gy, tokens, gain, w_gate, w_up, w_down, w_kv, queries, key_cache, value_cache, lengths):
    gx = lax.axis_index("gx")
    gy = lax.axis_index("gy").astype(jnp.int32).reshape(1)
    swap_gy = lambda x, bits: swap(x, "gy", n_gy, bits)
    exchange = lambda x: lax.all_to_all(x, ("gx", "gy"), split_axis=0, concat_axis=0, tiled=True)
    devices = n_gx * n_gy
    batch = tokens.shape[0]
    widths = chunk_widths(w_gate.shape[1])

    normed = norm(tokens, gain, n_gx, n_gy)
    gathered = exchange(normed.reshape(devices, batch, -1))
    grouped = queries.reshape(batch, -1, HD)
    cached, gate, up = attend_cache(
        grouped, key_cache, value_cache, lengths, w_gate, w_up, widths[0], normed
    )
    x = assemble(gy, gathered)
    rows = x.shape[0]
    quarter = rows // 4

    sums = []
    start = 0
    for c, width in enumerate(widths):
        if c == 0:
            keep, send = gate_up_ready(x, gate, up)
        else:
            keep, send = gate_up(x, w_gate, w_up, start, width, sums[0][2] if c == 1 else send)
        core = swap_gy(send, 1)
        across = (keep[:, quarter:] + core[:, quarter:].astype(F32)).astype(BF16)
        sums.append((keep, core, across))
        start += width

    slab = w_kv.shape[1]
    part = fresh_part(gy, lax.dynamic_slice_in_dim(x, gx * slab, slab, 1), w_kv, devices)
    fresh = jnp.sum(exchange(part), axis=0)
    key_new = fresh[:, :HD].astype(BF16)
    value_new = fresh[:, HD:].astype(BF16)

    start = 0
    total = None
    for c, (keep, core, across) in enumerate(sums):
        pair = keep[:, :quarter] + core[:, :quarter].astype(F32) + swap_gy(across, 2).astype(F32)
        own = (jax.nn.silu(pair[0]) * pair[1]).astype(BF16)
        far = swap_gy(own, 2)
        hidden = (own, far, swap_gy(own, 1), swap_gy(far, 1))
        total = down(gy, hidden, w_down, start, total, devices, c == len(sums) - 1)
        start += widths[c]

    ffn = exchange(total)
    mixed = finish(tokens, ffn.reshape(n_gx, n_gy, batch, -1))
    context = attend_new(grouped, cached, key_new, value_new)
    return (mixed, context)


def solution(mesh):
    sizes = dict(mesh.shape)
    return jax.shard_map(
        functools.partial(body, sizes["gx"], sizes["gy"]),
        mesh=mesh,
        in_specs=(
            P(("gx", "gy"), None),
            P(),
            P("gy", "gx"),
            P("gy", "gx"),
            P("gx", "gy"),
            P("gy", "gx", None),
            P(("gx", "gy"), None),
            P(("gx", "gy"), None, None),
            P(("gx", "gy"), None, None),
            P(("gx", "gy")),
        ),
        out_specs=(P(("gx", "gy"), None), P(("gx", "gy"), None)),
        check_vma=False,
    )
```

time: 267 us -> 129 us (0.48)
  waiting for transfers between devices: 160 us -> 24 us
  blocking collectives: 40.1 us -> 0 us
  Pallas kernels: 0 us -> 34.9 us
  matrix products: 30.5 us -> 0.13 us
  local copies, waits for them, and re-layouts: 7.14 us -> 33 us
  starting transfers between devices: 6.68 us -> 28 us
  between operations: 14.2 us -> 1.01 us
    psum x1 -> x0, waiting for transfers between devices: 94 us -> none  [body(): summed = lax.psum(pair, 'gy')]
    reduce_scatter x1 -> x0, waiting for transfers between devices: 65.2 us -> none  [body(): lax.psum_scatter(jnp.concatenate((jnp.dot(hidden, w_down, preferred_eleme...]
    pallas_call x0 -> x11, Pallas kernels: none -> 34.9 us  [the longest x3 10.3 us: down(): pl.pallas_call(functools.partial(down_kernel, start, tile, total is not N...]
    all_gather x1 -> x0, blocking collectives: 31.9 us -> none  [body(): piece = lax.all_gather(grid_in, 'gx', axis=0, tiled=True)]
    dot_general x7 -> x1, matrix products: 30.5 us -> 0.13 us  [attend_new(): own = jnp.einsum('rhd,rd->rh', grouped, key_new, preferred_element_type=F32)]
    unnamed x13 -> x46, local copies, waits for them, and re-layouts: 5.03 us -> 32.8 us
    all_to_all x2 -> x3, waiting for transfers between devices: 0.4 us -> 14.4 us  [body(): lax.all_to_all(x, ('gx', 'gy'), split_axis=0, concat_axis=0, tiled=True)]
    all_to_all x2 -> x3, starting transfers between devices: 6.6 us -> 17.5 us  [body(): lax.all_to_all(x, ('gx', 'gy'), split_axis=0, concat_axis=0, tiled=True)]
  transfers between devices with their start and end apart: 4 -> 18, of which waited for: 3 -> 5; matrix products, arithmetic and copies ran while one was open for 3% -> 6% of each run, Pallas kernels for 0% -> 22%
where the time goes in v2:
time: 129 us; the launch traced here: 128 us
  Pallas kernels  34.9 us (27%)
  local copies, waits for them, and re-layouts  33 us (26%)
  starting transfers between devices  28 us (22%)
  waiting for transfers between devices  24 us (19%)
  other arithmetic  6.66 us (5%)
    unnamed x46, local copies, waits for them, and re-layouts  32.8 us
    all_to_all x3, starting transfers between devices, body(): lax.all_to_all(x, ('gx', 'gy'), split_axis=0, concat_axis=0, tiled=True)  17.5 us
    all_to_all x3, waiting for transfers between devices, body(): lax.all_to_all(x, ('gx', 'gy'), split_axis=0, concat_axis=0, tiled=True)  14.4 us
    ppermute x15, starting transfers between devices, swap(): return lax.ppermute(x, axis, [(i, i ^ bits) for i in range(size)])  10.6 us
    pallas_call x3, Pallas kernels, down(): pl.pallas_call(functools.partial(down_kernel, start, tile, total is not N...  10.3 us
    ppermute x15, waiting for transfers between devices, swap(): return lax.ppermute(x, axis, [(i, i ^ bits) for i in range(size)])  9.62 us
    pallas_call x1, Pallas kernels, attend_cache(): pl.pallas_call(functools.partial(cache_kernel, 1.0 / math.sqrt(depth), ti...  8.56 us
    pallas_call x2, Pallas kernels, gate_up(): pl.pallas_call(functools.partial(gate_up_kernel, start, tile), in_specs=[...  8.29 us
  transfers between devices with their start and end apart: 18, of which 5 were waited for; matrix products, arithmetic and copies ran while one was open for 6% of the time, Pallas kernels for 22%

profile of v2, /device:TPU:0, one launch (start us, length us, event | category | flops | bytes accessed | tf_op | source)
XLA Modules:
  0.0 127.8 jit_solution(6658041530870922081)
XLA Ops:
  2.3 1.2 shard_map.113.after_ref
  3.5 7.3 %all-to-all-start = ((bf16[32,4,2304]{2,1,0:T(4,128)(2,1)}), bf16[32,4,2304]{2,1,0:T(4,128)(2,1)S(1)}, u32[]{:S(2)}, u32[]{:S(2)}) async-start(bf16[32,4,2304]{2,1,0:T(4,128)(2,1)} %bitcast.2), calls=%async_computation | async-start | bytes 1179648 | tf_op jit(solution)/shard_map/all_to_all | solution.py:376
  11.7 2.2 %copy-done.5 = bf16[4,2048,256]{2,1,0:T(8,128)(2,1)S(1)} copy-done((bf16[4,2048,256]{2,1,0:T(8,128)(2,1)S(1)}, bf16[4,2048,256]{2,1,0:T(8,128)(2,1)}, u32[]{:S(2)}) %copy-start.5) | copy-done | bytes 4194328
  13.9 2.2 %copy-done.6 = bf16[4,2048,256]{2,1,0:T(8,128)(2,1)S(1)} copy-done((bf16[4,2048,256]{2,1,0:T(8,128)(2,1)S(1)}, bf16[4,2048,256]{2,1,0:T(8,128)(2,1)}, u32[]{:S(2)}) %copy-start.6) | copy-done | bytes 4194328
  16.8 8.6 %shard_map.115 = (f32[4,48,256]{2,1,0:T(8,128)S(1)}, f32[4,48,1]{2,1,0:T(8,128)S(1)}, f32[4,48,1]{2,1,0:T(8,128)S(1)}, bf16[2304,2304]{1,0:T(8,128)(2,1)S(1)}, bf16[2304,2304]{1,0:T(8,128)(2,1)S(1)}) custom-call(s32[4]{0:T(128)S(1)} %copy-done.14, bf16[4,48,256]{2,1,0:T(8,128)(2,1)S(1)} %bitcast.51, bf16[4,2048,256]{2,1,0:T(8,128)(2,1)S(1)} %copy-done.5, ...), custom_call_target="tpu_custom_call" | custom-call | flops 603979776 | bytes 29622272 | tf_op jit(solution)/shard_map/pallas_call | solution.py:324
  25.3 4.1 %copy-done.1 = bf16[2304,2304]{1,0:T(8,128)(2,1)} copy-done((bf16[2304,2304]{1,0:T(8,128)(2,1)}, bf16[2304,2304]{1,0:T(8,128)(2,1)S(1)}, u32[]{:S(2)}) %copy-start.1) | copy-done | bytes 10616856
  29.4 3.9 %copy-done.3 = bf16[2304,2304]{1,0:T(8,128)(2,1)} copy-done((bf16[2304,2304]{1,0:T(8,128)(2,1)}, bf16[2304,2304]{1,0:T(8,128)(2,1)S(1)}, u32[]{:S(2)}) %copy-start.3) | copy-done | bytes 10616856
  34.1 4.0 %copy-done.2 = bf16[2304,2304]{1,0:T(8,128)(2,1)S(1)} copy-done((bf16[2304,2304]{1,0:T(8,128)(2,1)S(1)}, bf16[2304,2304]{1,0:T(8,128)(2,1)}, u32[]{:S(2)}) %copy-start.2) | copy-done | bytes 10616856
  38.1 4.0 %copy-done.4 = bf16[2304,2304]{1,0:T(8,128)(2,1)S(1)} copy-done((bf16[2304,2304]{1,0:T(8,128)(2,1)S(1)}, bf16[2304,2304]{1,0:T(8,128)(2,1)}, u32[]{:S(2)}) %copy-start.4) | copy-done | bytes 10616856
  42.1 4.7 %shard_map.116 = (f32[2,64,2304]{2,1,0:T(8,128)S(1)}, bf16[2,64,2304]{2,1,0:T(8,128)(2,1)}) custom-call(bf16[128,2304]{1,0:T(8,128)(2,1)S(1)} %shard_map.114.x_ref, bf16[2304,2304]{1,0:T(8,128)(2,1)S(1)} %copy-done.2, bf16[2304,2304]{1,0:T(8,128)(2,1)S(1)} %copy-done.4), custom_call_target="tpu_custom_call" | custom-call | flops 2717908992 | bytes 589824 | tf_op jit(solution)/shard_map/pallas_call | solution.py:146
  47.1 2.1 %collective-permute-done = bf16[2,64,2304]{2,1,0:T(8,128)(2,1)} collective-permute-done((bf16[2,64,2304]{2,1,0:T(8,128)(2,1)}, bf16[2,64,2304]{2,1,0:T(8,128)(2,1)}, u32[]{:S(2)}, u32[]{:S(2)}) %collective-permute-start) | collective-permute-done | bytes 589856 | tf_op jit(solution)/shard_map/ppermute | solution.py:34
  49.2 1.0 add_convert_fusion.after_ref
  50.2 1.8 %collective-permute-start.11 = (bf16[2,32,2304]{2,1,0:T(8,128)(2,1)S(1)}, bf16[2,32,2304]{2,1,0:T(8,128)(2,1)}, u32[]{:S(2)}, u32[]{:S(2)}) collective-permute-start(bf16[2,32,2304]{2,1,0:T(8,128)(2,1)S(1)} %add_convert_fusion.after_ref), channel_id=1, source_target_pairs={{0,2},{1,3},{2,0},{3,1},{4,6},{5,7},{6,4},{7,5},{8,10},{9,11},{10,... | collective-permute-start | bytes 884744 | tf_op jit(solution)/shard_map/ppermute | solution.py:34
  53.1 4.9 %all-to-all-start.2 = ((f32[32,4,512]{2,1,0:T(4,128)}), f32[32,4,512]{2,1,0:T(4,128)}, u32[]{:S(2)}, u32[]{:S(2)}) async-start(f32[32,4,512]{2,1,0:T(4,128)} %shard_map.123), calls=%async_computation.2 | async-start | bytes 524288 | tf_op jit(solution)/shard_map/all_to_all | solution.py:376
  58.0 7.0 %copy-done = bf16[2304,4608]{1,0:T(8,128)(2,1)S(1)} copy-done((bf16[2304,4608]{1,0:T(8,128)(2,1)S(1)}, bf16[2304,4608]{1,0:T(8,128)(2,1)}, u32[]{:S(2)}) %copy-start) | copy-done | bytes 21233688
  65.0 4.1 %shard_map.117 = (f32[2,64,1152]{2,1,0:T(8,128)S(1)}, bf16[2,64,1152]{2,1,0:T(8,128)(2,1)S(1)}) custom-call(bf16[128,2304]{1,0:T(8,128)(2,1)S(1)} %shard_map.114.x_ref, bf16[2304,4608]{1,0:T(8,128)(2,1)S(1)} %copy-done, bf16[2304,4608]{1,0:T(8,128)(2,1)} %up_ref.5, bf16[2,32,2304]{2,1,0:T(8,128)(2,1)S(1)} %add_convert_fusion.after_ref), custom_call_target="tpu_custom_call" | custom-call | flops 1358954496 | bytes 10616832 | tf_op jit(solution)/shard_map/pallas_call | solution.py:160
  70.1 4.2 %shard_map.118 = (f32[2,64,1152]{2,1,0:T(8,128)S(1)}, bf16[2,64,1152]{2,1,0:T(8,128)(2,1)S(1)}) custom-call(bf16[128,2304]{1,0:T(8,128)(2,1)S(1)} %shard_map.114.x_ref, bf16[2304,4608]{1,0:T(8,128)(2,1)S(1)} %copy-done, bf16[2304,4608]{1,0:T(8,128)(2,1)} %up_ref.5, bf16[2,64,1152]{2,1,0:T(8,128)(2,1)S(1)} %get-tuple-element.17.after_ref), custom_call_target="tpu_custom_call" | custom-call | flops 1358954496 | bytes 10616832 | tf_op jit(solution)/shard_map/pallas_call | solution.py:160
  75.1 1.9 %convert_add_fusion = f32[2,32,2304]{2,1,0:T(8,128)S(1)} fusion(bf16[2,32,2304]{2,1,0:T(8,128)(2,1)} %collective-permute-done.11, f32[2,64,2304]{2,1,0:T(8,128)S(1)} %get-tuple-element.15, bf16[2,64,2304]{2,1,0:T(8,128)(2,1)} %collective-permute-done), kind=kLoop, calls=%fused_computation | loop fusion | flops 589824 | bytes 1769472 | tf_op jit(solution)/shard_map/add | solution.py:412
  77.1 1.5 %collective-permute-start.12 = (bf16[32,2304]{1,0:T(8,128)(2,1)S(1)}, bf16[32,2304]{1,0:T(8,128)(2,1)S(1)}, u32[]{:S(2)}, u32[]{:S(2)}) collective-permute-start(bf16[32,2304]{1,0:T(8,128)(2,1)S(1)} %fusion.1.refs_0_), channel_id=1, source_target_pairs={{0,2},{1,3},{2,0},{3,1},{4,6},{5,7},{6,4},{7,5},{8,10},{9,11},{10,... | collective-permute-start | bytes 442376 | tf_op jit(solution)/shard_map/ppermute | solution.py:34
  78.7 1.0 add_convert_fusion.1
  80.6 1.4 %collective-permute-start.2 = (bf16[2,32,1152]{2,1,0:T(8,128)(2,1)S(1)}, bf16[2,32,1152]{2,1,0:T(8,128)(2,1)S(1)}, u32[]{:S(2)}, u32[]{:S(2)}) collective-permute-start(bf16[2,32,1152]{2,1,0:T(8,128)(2,1)S(1)} %add_convert_fusion.2), channel_id=1, source_target_pairs={{0,2},{1,3},{2,0},{3,1},{4,6},{5,7},{6,4},{7,5},{8,10},{9,11},{10,... | collective-permute-start | bytes 442376 | tf_op jit(solution)/shard_map/ppermute | solution.py:34
  81.9 4.5 %collective-permute-done.7 = bf16[2,32,1152]{2,1,0:T(8,128)(2,1)S(1)} collective-permute-done((bf16[2,32,1152]{2,1,0:T(8,128)(2,1)S(1)}, bf16[2,32,1152]{2,1,0:T(8,128)(2,1)S(1)}, u32[]{:S(2)}, u32[]{:S(2)}) %collective-permute-start.7) | collective-permute-done | bytes 147488 | tf_op jit(solution)/shard_map/ppermute | solution.py:34
  86.4 1.1 convert_add_fusion.1
  87.5 2.2 %collective-permute-start.8 = (bf16[32,1152]{1,0:T(8,128)(2,1)S(1)}, bf16[32,1152]{1,0:T(8,128)(2,1)S(1)}, u32[]{:S(2)}, u32[]{:S(2)}) collective-permute-start(bf16[32,1152]{1,0:T(8,128)(2,1)S(1)} %fusion.3.refs_0_), channel_id=1, source_target_pairs={{0,2},{1,3},{2,0},{3,1},{4,6},{5,7},{6,4},{7,5},{8,10},{9,11},{10,... | collective-permute-start | bytes 221192 | tf_op jit(solution)/shard_map/ppermute | solution.py:34
  89.8 1.2 collective-permute-start.3
  92.4 2.2 %collective-permute-done.3.refs_1_ = bf16[32,1152]{1,0:T(8,128)(2,1)S(1)} collective-permute-done((bf16[32,1152]{1,0:T(8,128)(2,1)S(1)}, bf16[32,1152]{1,0:T(8,128)(2,1)S(1)}, u32[]{:S(2)}, u32[]{:S(2)}) %collective-permute-start.3) | collective-permute-done | bytes 73760 | tf_op jit(solution)/shard_map/ppermute | solution.py:34
  94.7 4.0 %shard_map.119.refs_5_ = f32[128,2304]{1,0:T(8,128)S(1)} custom-call(s32[1]{0:T(128)} %bitcast.gy_ref, bf16[32,2304]{1,0:T(8,128)(2,1)S(1)} %fusion.1.refs_0_, bf16[32,2304]{1,0:T(8,128)(2,1)S(1)} %collective-permute-done.12.refs_1_, bf16[32,2304]{1,0:T(8,128)(2,1)S(1)} %collective-permute-done.13.refs_2_, ...), custom_call_target="tpu_custom_call" | custom-call | flops 1358954496 | bytes 10616832 | tf_op jit(solution)/shard_map/pallas_call | solution.py:216
  98.7 2.9 %shard_map.120.refs_5_ = f32[128,2304]{1,0:T(8,128)S(1)} custom-call(s32[1]{0:T(128)} %bitcast.gy_ref, bf16[32,1152]{1,0:T(8,128)(2,1)S(1)} %fusion.3.refs_0_, bf16[32,1152]{1,0:T(8,128)(2,1)S(1)} %collective-permute-done.8.refs_1_, bf16[32,1152]{1,0:T(8,128)(2,1)S(1)} %collective-permute-done.9.refs_2_, ...), custom_call_target="tpu_custom_call" | custom-call | flops 679477248 | bytes 5308416 | tf_op jit(solution)/shard_map/pallas_call | solution.py:216
  101.6 3.5 %shard_map.121 = bf16[32,4,2304]{2,1,0:T(4,128)(2,1)} custom-call(s32[1]{0:T(128)} %bitcast.gy_ref, bf16[32,1152]{1,0:T(8,128)(2,1)S(1)} %fusion.5.refs_0_, bf16[32,1152]{1,0:T(8,128)(2,1)S(1)} %collective-permute-done.3.refs_1_, bf16[32,1152]{1,0:T(8,128)(2,1)S(1)} %collective-permute-done.4.refs_2_, bf16[32,1152]{1,0:T(8,128)(2,1)S(1)} %collective-permute-done.5.refs_3_, ...), custom_call_target="tpu_custom_call" | custom-call | flops 679477248 | bytes 5308416 | tf_op jit(solution)/shard_map/pallas_call | solution.py:216
  105.1 5.2 %all-to-all-start.1 = ((bf16[32,4,2304]{2,1,0:T(4,128)(2,1)}), bf16[32,4,2304]{2,1,0:T(4,128)(2,1)S(1)}, u32[]{:S(2)}, u32[]{:S(2)}) async-start(bf16[32,4,2304]{2,1,0:T(4,128)(2,1)} %shard_map.121), calls=%async_computation.1 | async-start | bytes 1179648 | tf_op jit(solution)/shard_map/all_to_all | solution.py:376
  110.3 1.0 reduce_sum.9
  112.7 14.4 %all-to-all-done.1 = bf16[32,4,2304]{2,1,0:T(4,128)(2,1)S(1)} async-done(((bf16[32,4,2304]{2,1,0:T(4,128)(2,1)}), bf16[32,4,2304]{2,1,0:T(4,128)(2,1)S(1)}, u32[]{:S(2)}, u32[]{:S(2)}) %all-to-all-start.1) | async-done | bytes 589856 | tf_op jit(solution)/shard_map/all_to_all | solution.py:376
  (79 shorter events, 11.4 us)
Async XLA Ops:
  3.5 30.4 %all-to-all-start = ((bf16[32,4,2304]{2,1,0:T(4,128)(2,1)}), bf16[32,4,2304]{2,1,0:T(4,128)(2,1)S(1)}, u32[]{:S(2)}, u32[]{:S(2)}) async-start(bf16[32,4,2304]{2,1,0:T(4,128)(2,1)} %bitcast.2), calls=%async_computation | async-start | bytes 1179648 | tf_op jit(solution)/shard_map/all_to_all | solution.py:376
  25.3 4.1 %copy-start.1 = (bf16[2304,2304]{1,0:T(8,128)(2,1)}, bf16[2304,2304]{1,0:T(8,128)(2,1)S(1)}, u32[]{:S(2)}) copy-start(bf16[2304,2304]{1,0:T(8,128)(2,1)S(1)} %get-tuple-element.13.gate_ref) | copy-start | bytes 31850500
  34.1 4.0 %copy-start.2 = (bf16[2304,2304]{1,0:T(8,128)(2,1)S(1)}, bf16[2304,2304]{1,0:T(8,128)(2,1)}, u32[]{:S(2)}) copy-start(bf16[2304,2304]{1,0:T(8,128)(2,1)} %copy-done.1) | copy-start | bytes 31850500
  38.1 4.0 %copy-start.4 = (bf16[2304,2304]{1,0:T(8,128)(2,1)S(1)}, bf16[2304,2304]{1,0:T(8,128)(2,1)}, u32[]{:S(2)}) copy-start(bf16[2304,2304]{1,0:T(8,128)(2,1)} %copy-done.3) | copy-start | bytes 31850500
  42.1 10.0 %copy-start.10 = (bf16[1,288,512]{2,1,0:T(8,128)(2,1)S(1)}, bf16[1,288,512]{2,1,0:T(8,128)(2,1)}, u32[]{:S(2)}) copy-start(bf16[1,288,512]{2,1,0:T(8,128)(2,1)} %weight_ref.1) | copy-start | bytes 884740
  46.8 2.3 %collective-permute-start = (bf16[2,64,2304]{2,1,0:T(8,128)(2,1)}, bf16[2,64,2304]{2,1,0:T(8,128)(2,1)}, u32[]{:S(2)}, u32[]{:S(2)}) collective-permute-start(bf16[2,64,2304]{2,1,0:T(8,128)(2,1)} %get-tuple-element.16), channel_id=1, source_target_pairs={{0,1},{1,0},{2,3},{3,2},{4,5},{5,4},{6,7},{7,6},{8,9},{9,8},{10,11... | collective-permute-start | bytes 1769480 | tf_op jit(solution)/shard_map/ppermute | solution.py:34
  50.2 24.9 %collective-permute-start.11 = (bf16[2,32,2304]{2,1,0:T(8,128)(2,1)S(1)}, bf16[2,32,2304]{2,1,0:T(8,128)(2,1)}, u32[]{:S(2)}, u32[]{:S(2)}) collective-permute-start(bf16[2,32,2304]{2,1,0:T(8,128)(2,1)S(1)} %add_convert_fusion.after_ref), channel_id=1, source_target_pairs={{0,2},{1,3},{2,0},{3,1},{4,6},{5,7},{6,4},{7,5},{8,10},{9,11},{10,... | collective-permute-start | bytes 884744 | tf_op jit(solution)/shard_map/ppermute | solution.py:34
  53.1 52.1 %all-to-all-start.2 = ((f32[32,4,512]{2,1,0:T(4,128)}), f32[32,4,512]{2,1,0:T(4,128)}, u32[]{:S(2)}, u32[]{:S(2)}) async-start(f32[32,4,512]{2,1,0:T(4,128)} %shard_map.123), calls=%async_computation.2 | async-start | bytes 524288 | tf_op jit(solution)/shard_map/all_to_all | solution.py:376
  58.0 7.0 %copy-start = (bf16[2304,4608]{1,0:T(8,128)(2,1)S(1)}, bf16[2304,4608]{1,0:T(8,128)(2,1)}, u32[]{:S(2)}) copy-start(bf16[2304,4608]{1,0:T(8,128)(2,1)} %gate_ref.5) | copy-start | bytes 63700996
  70.0 24.6 %slice-start = ((s8[21233664]{0:T(1024)(128)(4,1)}), s8[4194304]{0:T(1024)(128)(4,1)S(1)}, s32[]{:S(2)}) async-start(s8[21233664]{0:T(1024)(128)(4,1)} %bitcast.48), calls=%async_computation.3 | async-start | bytes 8388608
  70.0 24.6 %slice-start.1 = ((s8[21233664]{0:T(1024)(128)(4,1)}), s8[4194304]{0:T(1024)(128)(4,1)S(1)}, s32[]{:S(2)}) async-start(s8[21233664]{0:T(1024)(128)(4,1)} %bitcast.48), calls=%async_computation.4 | async-start | bytes 8388608
  70.0 24.6 %slice-start.2 = ((s8[21233664]{0:T(1024)(128)(4,1)}), s8[4194304]{0:T(1024)(128)(4,1)S(1)}, s32[]{:S(2)}) async-start(s8[21233664]{0:T(1024)(128)(4,1)} %bitcast.48), calls=%async_computation.5 | async-start | bytes 8388608
  70.0 24.7 %slice-start.3 = ((s8[21233664]{0:T(1024)(128)(4,1)}), s8[4194304]{0:T(1024)(128)(4,1)S(1)}, s32[]{:S(2)}) async-start(s8[21233664]{0:T(1024)(128)(4,1)} %bitcast.48), calls=%async_computation.6 | async-start | bytes 8388608
  70.0 24.7 %slice-start.4 = ((s8[21233664]{0:T(1024)(128)(4,1)}), s8[4194304]{0:T(1024)(128)(4,1)S(1)}, s32[]{:S(2)}) async-start(s8[21233664]{0:T(1024)(128)(4,1)} %bitcast.48), calls=%async_computation.7 | async-start | bytes 8388608
  70.0 24.7 %slice-start.5 = ((s8[21233664]{0:T(1024)(128)(4,1)}), s8[262144]{0:T(1024)(128)(4,1)S(1)}, s32[]{:S(2)}) async-start(s8[21233664]{0:T(1024)(128)(4,1)} %bitcast.48), calls=%async_computation.8 | async-start | bytes 524288
  70.0 8.7 %collective-permute-start.6 = (bf16[2,64,1152]{2,1,0:T(8,128)(2,1)S(1)}, bf16[2,64,1152]{2,1,0:T(8,128)(2,1)}, u32[]{:S(2)}, u32[]{:S(2)}) collective-permute-start(bf16[2,64,1152]{2,1,0:T(8,128)(2,1)S(1)} %get-tuple-element.17.after_ref), channel_id=1, source_target_pairs={{0,1},{1,0},{2,3},{3,2},{4,5},{5,4},{6,7},{7,6},{8,9},{9,8},{10,11... | collective-permute-start | bytes 884744 | tf_op jit(solution)/shard_map/ppermute | solution.py:34
  74.3 6.2 %collective-permute-start.1 = (bf16[2,64,1152]{2,1,0:T(8,128)(2,1)S(1)}, bf16[2,64,1152]{2,1,0:T(8,128)(2,1)S(1)}, u32[]{:S(2)}, u32[]{:S(2)}) collective-permute-start(bf16[2,64,1152]{2,1,0:T(8,128)(2,1)S(1)} %get-tuple-element.19), channel_id=1, source_target_pairs={{0,1},{1,0},{2,3},{3,2},{4,5},{5,4},{6,7},{7,6},{8,9},{9,8},{10,11... | collective-permute-start | bytes 884744 | tf_op jit(solution)/shard_map/ppermute | solution.py:34
  77.1 12.6 %collective-permute-start.12 = (bf16[32,2304]{1,0:T(8,128)(2,1)S(1)}, bf16[32,2304]{1,0:T(8,128)(2,1)S(1)}, u32[]{:S(2)}, u32[]{:S(2)}) collective-permute-start(bf16[32,2304]{1,0:T(8,128)(2,1)S(1)} %fusion.1.refs_0_), channel_id=1, source_target_pairs={{0,2},{1,3},{2,0},{3,1},{4,6},{5,7},{6,4},{7,5},{8,10},{9,11},{10,... | collective-permute-start | bytes 442376 | tf_op jit(solution)/shard_map/ppermute | solution.py:34
  78.7 12.4 %collective-permute-start.13 = (bf16[32,2304]{1,0:T(8,128)(2,1)S(1)}, bf16[32,2304]{1,0:T(8,128)(2,1)S(1)}, u32[]{:S(2)}, u32[]{:S(2)}) collective-permute-start(bf16[32,2304]{1,0:T(8,128)(2,1)S(1)} %fusion.1.refs_0_), channel_id=1, source_target_pairs={{0,1},{1,0},{2,3},{3,2},{4,5},{5,4},{6,7},{7,6},{8,9},{9,8},{10,11... | collective-permute-start | bytes 442376 | tf_op jit(solution)/shard_map/ppermute | solution.py:34
  79.7 6.7 %collective-permute-start.7 = (bf16[2,32,1152]{2,1,0:T(8,128)(2,1)S(1)}, bf16[2,32,1152]{2,1,0:T(8,128)(2,1)S(1)}, u32[]{:S(2)}, u32[]{:S(2)}) collective-permute-start(bf16[2,32,1152]{2,1,0:T(8,128)(2,1)S(1)} %add_convert_fusion.1), channel_id=1, source_target_pairs={{0,2},{1,3},{2,0},{3,1},{4,6},{5,7},{6,4},{7,5},{8,10},{9,11},{10,... | collective-permute-start | bytes 442376 | tf_op jit(solution)/shard_map/ppermute | solution.py:34
  80.6 9.2 %collective-permute-start.2 = (bf16[2,32,1152]{2,1,0:T(8,128)(2,1)S(1)}, bf16[2,32,1152]{2,1,0:T(8,128)(2,1)S(1)}, u32[]{:S(2)}, u32[]{:S(2)}) collective-permute-start(bf16[2,32,1152]{2,1,0:T(8,128)(2,1)S(1)} %add_convert_fusion.2), channel_id=1, source_target_pairs={{0,2},{1,3},{2,0},{3,1},{4,6},{5,7},{6,4},{7,5},{8,10},{9,11},{10,... | collective-permute-start | bytes 442376 | tf_op jit(solution)/shard_map/ppermute | solution.py:34
  87.5 4.8 %collective-permute-start.8 = (bf16[32,1152]{1,0:T(8,128)(2,1)S(1)}, bf16[32,1152]{1,0:T(8,128)(2,1)S(1)}, u32[]{:S(2)}, u32[]{:S(2)}) collective-permute-start(bf16[32,1152]{1,0:T(8,128)(2,1)S(1)} %fusion.3.refs_0_), channel_id=1, source_target_pairs={{0,2},{1,3},{2,0},{3,1},{4,6},{5,7},{6,4},{7,5},{8,10},{9,11},{10,... | collective-permute-start | bytes 221192 | tf_op jit(solution)/shard_map/ppermute | solution.py:34
  89.7 4.9 %collective-permute-start.14 = (bf16[32,2304]{1,0:T(8,128)(2,1)S(1)}, bf16[32,2304]{1,0:T(8,128)(2,1)S(1)}, u32[]{:S(2)}, u32[]{:S(2)}) collective-permute-start(bf16[32,2304]{1,0:T(8,128)(2,1)S(1)} %collective-permute-done.12.refs_1_), channel_id=1, source_target_pairs={{0,1},{1,0},{2,3},{3,2},{4,5},{5,4},{6,7},{7,6},{8,9},{9,8},{10,11... | collective-permute-start | bytes 442376 | tf_op jit(solution)/shard_map/ppermute | solution.py:34
  89.8 4.7 %collective-permute-start.3 = (bf16[32,1152]{1,0:T(8,128)(2,1)S(1)}, bf16[32,1152]{1,0:T(8,128)(2,1)S(1)}, u32[]{:S(2)}, u32[]{:S(2)}) collective-permute-start(bf16[32,1152]{1,0:T(8,128)(2,1)S(1)} %fusion.5.refs_0_), channel_id=1, source_target_pairs={{0,2},{1,3},{2,0},{3,1},{4,6},{5,7},{6,4},{7,5},{8,10},{9,11},{10,... | collective-permute-start | bytes 221192 | tf_op jit(solution)/shard_map/ppermute | solution.py:34
  91.1 7.6 %collective-permute-start.9 = (bf16[32,1152]{1,0:T(8,128)(2,1)S(1)}, bf16[32,1152]{1,0:T(8,128)(2,1)S(1)}, u32[]{:S(2)}, u32[]{:S(2)}) collective-permute-start(bf16[32,1152]{1,0:T(8,128)(2,1)S(1)} %fusion.3.refs_0_), channel_id=1, source_target_pairs={{0,1},{1,0},{2,3},{3,2},{4,5},{5,4},{6,7},{7,6},{8,9},{9,8},{10,11... | collective-permute-start | bytes 221192 | tf_op jit(solution)/shard_map/ppermute | solution.py:34
  91.1 10.5 %collective-permute-start.4 = (bf16[32,1152]{1,0:T(8,128)(2,1)S(1)}, bf16[32,1152]{1,0:T(8,128)(2,1)S(1)}, u32[]{:S(2)}, u32[]{:S(2)}) collective-permute-start(bf16[32,1152]{1,0:T(8,128)(2,1)S(1)} %fusion.5.refs_0_), channel_id=1, source_target_pairs={{0,1},{1,0},{2,3},{3,2},{4,5},{5,4},{6,7},{7,6},{8,9},{9,8},{10,11... | collective-permute-start | bytes 221192 | tf_op jit(solution)/shard_map/ppermute | solution.py:34
  92.4 6.3 %collective-permute-start.10 = (bf16[32,1152]{1,0:T(8,128)(2,1)S(1)}, bf16[32,1152]{1,0:T(8,128)(2,1)S(1)}, u32[]{:S(2)}, u32[]{:S(2)}) collective-permute-start(bf16[32,1152]{1,0:T(8,128)(2,1)S(1)} %collective-permute-done.8.refs_1_), channel_id=1, source_target_pairs={{0,1},{1,0},{2,3},{3,2},{4,5},{5,4},{6,7},{7,6},{8,9},{9,8},{10,11... | collective-permute-start | bytes 221192 | tf_op jit(solution)/shard_map/ppermute | solution.py:34
  94.6 7.0 %collective-permute-start.5 = (bf16[32,1152]{1,0:T(8,128)(2,1)S(1)}, bf16[32,1152]{1,0:T(8,128)(2,1)S(1)}, u32[]{:S(2)}, u32[]{:S(2)}) collective-permute-start(bf16[32,1152]{1,0:T(8,128)(2,1)S(1)} %collective-permute-done.3.refs_1_), channel_id=1, source_target_pairs={{0,1},{1,0},{2,3},{3,2},{4,5},{5,4},{6,7},{7,6},{8,9},{9,8},{10,11... | collective-permute-start | bytes 221192 | tf_op jit(solution)/shard_map/ppermute | solution.py:34
  101.6 9.8 %copy-start.15 = (bf16[4,12288]{1,0:T(4,128)(2,1)S(1)}, bf16[4,12288]{1,0:T(4,128)(2,1)}, u32[]{:S(2)}) copy-start(bf16[4,12288]{1,0:T(4,128)(2,1)} %param.16) | copy-start | bytes 294916
  101.6 10.1 %copy-start.12 = (f32[4,48,1]{2,1,0:T(8,128)S(1)}, f32[4,48,1]{2,1,0:T(8,128)}, u32[]{:S(2)}) copy-start(f32[4,48,1]{2,1,0:T(8,128)} %copy-done.11) | copy-start | bytes 2308
  101.6 25.5 %copy-start.9 = (bf16[4,9216]{1,0:T(4,128)(2,1)S(1)}, bf16[4,9216]{1,0:T(4,128)(2,1)}, u32[]{:S(2)}) copy-start(bf16[4,9216]{1,0:T(4,128)(2,1)} %tokens_ref.3) | copy-start | bytes 221188
  105.1 22.0 %all-to-all-start.1 = ((bf16[32,4,2304]{2,1,0:T(4,128)(2,1)}), bf16[32,4,2304]{2,1,0:T(4,128)(2,1)S(1)}, u32[]{:S(2)}, u32[]{:S(2)}) async-start(bf16[32,4,2304]{2,1,0:T(4,128)(2,1)} %shard_map.121), calls=%async_computation.1 | async-start | bytes 1179648 | tf_op jit(solution)/shard_map/all_to_all | solution.py:376
  (8 other events, 12.1 us)

commit v3 on v2

--- a/solution.py
+++ b/solution.py
@@ -30,12 +30,24 @@
     return max(t for t in range(128, most + 1, 128) if width % t == 0)
 
 
+def in_hbm(x):
+    return pltpu.with_memory_space_constraint(x, pltpu.HBM)
+
+
 def swap(x, axis, size, bits):
     return lax.ppermute(x, axis, [(i, i ^ bits) for i in range(size)])
 
 
-def norm_kernel(tokens_ref, gain_ref, out_ref):
+def norm_kernel(tokens_hbm, gain_hbm, out_ref, tokens_ref, gain_ref, sems):
     copies, blocks, _, width = out_ref.shape
+    moves = [
+        pltpu.make_async_copy(source, target, sems.at[k])
+        for k, (source, target) in enumerate(((tokens_hbm, tokens_ref), (gain_hbm, gain_ref)))
+    ]
+    for move in moves:
+        move.start()
+    for move in moves:
+        move.wait()
     values = tokens_ref[...].astype(F32)
     centred = values - jnp.mean(values, axis=-1, keepdims=True)
     spread = jnp.mean(centred * centred, axis=-1, keepdims=True)
@@ -50,12 +62,17 @@
     batch, channels = tokens.shape
     return pl.pallas_call(
         norm_kernel,
-        in_specs=[WHOLE, WHOLE],
+        in_specs=[ANYWHERE, ANYWHERE],
         out_specs=WHOLE,
         out_shape=jax.ShapeDtypeStruct((n_gx, n_gy, batch, channels // n_gy), BF16),
+        scratch_shapes=[
+            pltpu.VMEM((batch, channels), BF16),
+            pltpu.VMEM((1, channels), F32),
+            pltpu.SemaphoreType.DMA((2,)),
+        ],
         compiler_params=params(8),
         cost_estimate=cost(10 * tokens.size, 2 * n_gx * tokens.size),
-    )(tokens, gain.reshape(1, -1))
+    )(in_hbm(tokens), in_hbm(gain.reshape(1, -1)))
 
 
 def assemble_kernel(gy_ref, rows_ref, out_ref):
@@ -79,7 +96,7 @@
         in_specs=[SCALARS, WHOLE],
         out_specs=WHOLE,
         out_shape=jax.ShapeDtypeStruct((devices * batch, width), BF16),
-        compiler_params=params(12),
+        compiler_params=params(4),
         cost_estimate=cost(2 * rows.size, 4 * rows.size),
     )(gy, rows)
 
@@ -144,18 +161,18 @@
     rows, depth = x.shape
     width = gate.shape[1]
     return pl.pallas_call(
-        functools.partial(gate_up_ready_kernel, tile_of(width, 384)),
+        functools.partial(gate_up_ready_kernel, tile_of(width, 256)),
         in_specs=[WHOLE, WHOLE, WHOLE],
         out_specs=[WHOLE, WHOLE],
         out_shape=gate_up_shapes(rows, width),
-        compiler_params=params(16),
+        compiler_params=params(8),
         cost_estimate=cost(4 * rows * depth * width, 2 * rows * depth),
     )(x, gate, up)
 
 
 def gate_up(x, w_gate, w_up, start, width, after):
     rows, depth = x.shape
-    tile = tile_of(width, 384)
+    tile = tile_of(width, 256)
     count = width // tile
     return pl.pallas_call(
         functools.partial(gate_up_kernel, start, tile),
@@ -166,9 +183,9 @@
             pltpu.VMEM((2, count, depth, tile), BF16),
             pltpu.SemaphoreType.DMA((2, count)),
         ],
-        compiler_params=params(20),
+        compiler_params=params(14),
         cost_estimate=cost(4 * rows * depth * width, 4 * depth * width),
-    )(x, w_gate, w_up, after)
+    )(x, in_hbm(w_gate), in_hbm(w_up), after)
 
 
 def down_kernel(start, tile, has_sum, last, gy_ref, *refs):
@@ -205,9 +222,9 @@
     part_rows, depth = hidden[0].shape
     rows = 4 * part_rows
     width = w_down.shape[1]
-    tile = tile_of(width, 384)
+    tile = tile_of(width, 256)
     count = width // tile
-    args = [gy, *hidden, w_down]
+    args = [gy, *hidden, in_hbm(w_down)]
     in_specs = [SCALARS] + [WHOLE] * 4 + [ANYWHERE]
     if total is not None:
         args.append(total)
@@ -222,7 +239,7 @@
             pltpu.VMEM((count, depth, tile), BF16),
             pltpu.SemaphoreType.DMA((count,)),
         ],
-        compiler_params=params(20),
+        compiler_params=params(14),
         cost_estimate=cost(2 * rows * depth * width, 2 * depth * width),
     )(*args)
 
@@ -264,6 +281,25 @@
         compiler_params=params(8),
         cost_estimate=cost(2 * rows * depth * columns, 2 * depth * columns),
     )(gy, x, w_kv)
+
+
+def own_first_kernel(gx_ref, gy_ref, sums_ref, after_ref, near_ref, far_ref):
+    del after_ref
+    for at, turn in enumerate(ORDER):
+        device = gx_ref[0] * len(ORDER) + (gy_ref[0] ^ turn)
+        (near_ref, far_ref)[at // 2][at % 2] = sums_ref[device]
+
+
+def own_first(gx, gy, sums, after):
+    shape = jax.ShapeDtypeStruct((2, *sums.shape[1:]), sums.dtype)
+    return pl.pallas_call(
+        own_first_kernel,
+        in_specs=[SCALARS, SCALARS, WHOLE, ANYWHERE],
+        out_specs=[WHOLE, WHOLE],
+        out_shape=[shape, shape],
+        compiler_params=params(4),
+        cost_estimate=cost(sums.size, 8 * sums.size),
+    )(gx, gy, sums, after)
 
 
 def cache_kernel(
@@ -320,7 +356,7 @@
     batch, heads, depth = grouped.shape
     span = key_cache.shape[1]
     tall = w_gate.shape[0]
-    tile = tile_of(width, 384)
+    tile = tile_of(width, 256)
     *cached, gate, up = pl.pallas_call(
         functools.partial(cache_kernel, 1.0 / math.sqrt(depth), tile),
         in_specs=[SCALARS, WHOLE] + [ANYWHERE] * 5,
@@ -338,13 +374,13 @@
             pltpu.SemaphoreType.DMA((2, batch)),
             pltpu.SemaphoreType.DMA((2, width // tile)),
         ],
-        compiler_params=params(24),
+        compiler_params=params(14),
         cost_estimate=cost(
             6 * batch * heads * span * depth,
             4 * batch * span * depth + 4 * tall * width,
             batch * heads * span,
         ),
-    )(lengths, grouped, key_cache, value_cache, w_gate, w_up, after)
+    )(lengths, grouped, in_hbm(key_cache), in_hbm(value_cache), in_hbm(w_gate), in_hbm(w_up), after)
     return cached, gate, up
 
 
@@ -363,10 +399,11 @@
 
 
 def chunk_widths(columns):
-    units = columns // 128
+    unit = 256 if columns % 256 == 0 else 128
+    units = columns // unit
     first = units // 2
     second = (units - first) // 2
-    return [128 * u for u in (first, second, units - first - second)]
+    return [unit * u for u in (first, second, units - first - second)]
 
 
 def body(n_gx, n_gy, tokens, gain, w_gate, w_up, w_down, w_kv, queries, key_cache, value_cache, lengths):
@@ -402,9 +439,7 @@
 
     slab = w_kv.shape[1]
     part = fresh_part(gy, lax.dynamic_slice_in_dim(x, gx * slab, slab, 1), w_kv, devices)
-    fresh = jnp.sum(exchange(part), axis=0)
-    key_new = fresh[:, :HD].astype(BF16)
-    value_new = fresh[:, HD:].astype(BF16)
+    over_gx = lax.psum(part, "gx")
 
     start = 0
     total = None
@@ -415,6 +450,12 @@
         hidden = (own, far, swap_gy(own, 1), swap_gy(far, 1))
         total = down(gy, hidden, w_down, start, total, devices, c == len(sums) - 1)
         start += widths[c]
+        if c == 0:
+            near, far = own_first(gx.astype(jnp.int32).reshape(1), gy, over_gx, total)
+            near = near + swap_gy(far, 1)
+            fresh = near[0] + swap_gy(near[1], 2)
+            key_new = fresh[:, :HD].astype(BF16)
+            value_new = fresh[:, HD:].astype(BF16)
 
     ffn = exchange(total)
     mixed = finish(tokens, ffn.reshape(n_gx, n_gy, batch, -1))

time: 129 us -> 168 us (1.30)
  waiting for transfers between devices: 24 us -> 69 us
  between operations: 1.01 us -> 14.3 us
  local copies, waits for them, and re-layouts: 33 us -> 20.2 us
  starting transfers between devices: 28 us -> 19.7 us
  Pallas kernels: 34.9 us -> 41 us
  other arithmetic: 6.66 us -> 2.63 us
    psum x0 -> x1, waiting for transfers between devices: none -> 39.7 us  [body(): over_gx = lax.psum(part, 'gx')]
    unnamed x46 -> x24, local copies, waits for them, and re-layouts: 32.8 us -> 20 us
    all_to_all x3 -> x2, starting transfers between devices: 17.5 us -> 10.3 us  [body(): lax.all_to_all(x, ('gx', 'gy'), split_axis=0, concat_axis=0, tiled=True)]
    ppermute x15 -> x17, waiting for transfers between devices: 9.62 us -> 13.9 us  [swap(): return lax.ppermute(x, axis, [(i, i ^ bits) for i in range(size)])]
    pallas_call x3, Pallas kernels: 10.3 us -> 14 us  [down(): pl.pallas_call(functools.partial(down_kernel, start, tile, total is not N...]
    pallas_call x1, Pallas kernels: 8.56 us -> 10.7 us  [attend_cache(): pl.pallas_call(functools.partial(cache_kernel, 1.0 / math.sqrt(depth), ti...]
    add x3, other arithmetic: 3.04 us -> 1.07 us  [body(): keep[:, :quarter] + core[:, :quarter].astype(F32)]
    ppermute x15 -> x17, starting transfers between devices: 10.6 us -> 9.36 us  [swap(): return lax.ppermute(x, axis, [(i, i ^ bits) for i in range(size)])]
  transfers between devices with their start and end apart: 18 -> 20, of which waited for: 5 -> 8; matrix products, arithmetic and copies ran while one was open for 6% -> 3% of each run, Pallas kernels for 22% -> 18%
where the time goes in v3:
time: 168 us; the launch traced here: 167 us
  waiting for transfers between devices  69 us (41%)
  Pallas kernels  41 us (24%)
  local copies, waits for them, and re-layouts  20.2 us (12%)
  starting transfers between devices  19.7 us (12%)
  between operations  14.3 us (9%)
  other arithmetic  2.63 us (2%)
    psum x1, waiting for transfers between devices, body(): over_gx = lax.psum(part, 'gx')  39.7 us
    unnamed x24, local copies, waits for them, and re-layouts  20 us
    all_to_all x2, waiting for transfers between devices, body(): lax.all_to_all(x, ('gx', 'gy'), split_axis=0, concat_axis=0, tiled=True)  15.4 us
    pallas_call x3, Pallas kernels, down(): pl.pallas_call(functools.partial(down_kernel, start, tile, total is not N...  14 us
    ppermute x17, waiting for transfers between devices, swap(): return lax.ppermute(x, axis, [(i, i ^ bits) for i in range(size)])  13.9 us
    pallas_call x1, Pallas kernels, attend_cache(): pl.pallas_call(functools.partial(cache_kernel, 1.0 / math.sqrt(depth), ti...  10.7 us
    all_to_all x2, starting transfers between devices, body(): lax.all_to_all(x, ('gx', 'gy'), split_axis=0, concat_axis=0, tiled=True)  10.3 us
    pallas_call x2, Pallas kernels, gate_up(): pl.pallas_call(functools.partial(gate_up_kernel, start, tile), in_specs=[...  9.52 us
  transfers between devices with their start and end apart: 20, of which 8 were waited for; matrix products, arithmetic and copies ran while one was open for 3% of the time, Pallas kernels for 18%

profile of v3, /device:TPU:0, one launch (start us, length us, event | category | flops | bytes accessed | tf_op | source)
XLA Modules:
  0.0 167.1 jit_solution(7119204711133487901)
XLA Ops:
  7.2 2.1 %shard_map.113.after_ref = bf16[8,4,4,2304]{3,2,1,0:T(4,128)(2,1)} custom-call(bf16[4,9216]{1,0:T(4,128)(2,1)} %tokens_ref.1, f32[1,9216]{1,0:T(1,128)} %bitcast.62), custom_call_target="tpu_custom_call" | custom-call | flops 368640 | bytes 589824 | tf_op jit(solution)/shard_map/pallas_call | solution.py:63
  9.3 7.3 %all-to-all-start = ((bf16[32,4,2304]{2,1,0:T(4,128)(2,1)}), bf16[32,4,2304]{2,1,0:T(4,128)(2,1)S(1)}, u32[]{:S(2)}, u32[]{:S(2)}) async-start(bf16[32,4,2304]{2,1,0:T(4,128)(2,1)} %bitcast.2), calls=%async_computation | async-start | bytes 1179648 | tf_op jit(solution)/shard_map/all_to_all | solution.py:413
  16.6 0.9 copy.22
  18.2 10.7 %shard_map.115 = (f32[4,48,256]{2,1,0:T(8,128)S(1)}, f32[4,48,1]{2,1,0:T(8,128)S(1)}, f32[4,48,1]{2,1,0:T(8,128)S(1)}, bf16[2304,2304]{1,0:T(8,128)(2,1)S(1)}, bf16[2304,2304]{1,0:T(8,128)(2,1)S(1)}) custom-call(s32[4]{0:T(128)S(1)} %copy-done.7, bf16[4,48,256]{2,1,0:T(8,128)(2,1)S(1)} %bitcast.58, bf16[4,2048,256]{2,1,0:T(8,128)(2,1)} %key_ref.1, ...), custom_call_target="tpu_custom_call" | custom-call | flops 603979776 | bytes 29622272 | tf_op jit(solution)/shard_map/pallas_call | solution.py:360
  28.9 4.1 %copy-done = bf16[2304,2304]{1,0:T(8,128)(2,1)} copy-done((bf16[2304,2304]{1,0:T(8,128)(2,1)}, bf16[2304,2304]{1,0:T(8,128)(2,1)S(1)}, u32[]{:S(2)}) %copy-start) | copy-done | bytes 10616856
  33.0 3.9 %copy-done.2 = bf16[2304,2304]{1,0:T(8,128)(2,1)} copy-done((bf16[2304,2304]{1,0:T(8,128)(2,1)}, bf16[2304,2304]{1,0:T(8,128)(2,1)S(1)}, u32[]{:S(2)}) %copy-start.2) | copy-done | bytes 10616856
  37.0 4.0 %copy-done.1 = bf16[2304,2304]{1,0:T(8,128)(2,1)S(1)} copy-done((bf16[2304,2304]{1,0:T(8,128)(2,1)S(1)}, bf16[2304,2304]{1,0:T(8,128)(2,1)}, u32[]{:S(2)}) %copy-start.1) | copy-done | bytes 10616856
  41.0 4.0 %copy-done.3 = bf16[2304,2304]{1,0:T(8,128)(2,1)S(1)} copy-done((bf16[2304,2304]{1,0:T(8,128)(2,1)S(1)}, bf16[2304,2304]{1,0:T(8,128)(2,1)}, u32[]{:S(2)}) %copy-start.3) | copy-done | bytes 10616856
  45.0 2.9 %shard_map.116 = (f32[2,64,2304]{2,1,0:T(8,128)S(1)}, bf16[2,64,2304]{2,1,0:T(8,128)(2,1)S(1)}) custom-call(bf16[128,2304]{1,0:T(8,128)(2,1)S(1)} %shard_map.114.x_ref, bf16[2304,2304]{1,0:T(8,128)(2,1)S(1)} %copy-done.1, bf16[2304,2304]{1,0:T(8,128)(2,1)S(1)} %copy-done.3), custom_call_target="tpu_custom_call" | custom-call | flops 2717908992 | bytes 589824 | tf_op jit(solution)/shard_map/pallas_call | solution.py:163
  48.3 1.8 %collective-permute-done = bf16[2,64,2304]{2,1,0:T(8,128)(2,1)S(1)} collective-permute-done((bf16[2,64,2304]{2,1,0:T(8,128)(2,1)S(1)}, bf16[2,64,2304]{2,1,0:T(8,128)(2,1)S(1)}, u32[]{:S(2)}, u32[]{:S(2)}) %collective-permute-start) | collective-permute-done | bytes 589856 | tf_op jit(solution)/shard_map/ppermute | solution.py:38
  50.0 0.8 copy-done.8
  50.9 4.4 %shard_map.117 = (f32[2,64,1024]{2,1,0:T(8,128)S(1)}, bf16[2,64,1024]{2,1,0:T(8,128)(2,1)S(1)}) custom-call(bf16[128,2304]{1,0:T(8,128)(2,1)S(1)} %shard_map.114.x_ref, bf16[2304,4608]{1,0:T(8,128)(2,1)} %gate_ref.5, bf16[2304,4608]{1,0:T(8,128)(2,1)} %up_ref.5, bf16[2,32,2304]{2,1,0:T(8,128)(2,1)S(1)} %add_convert_fusion.after_ref), custom_call_target="tpu_custom_call" | custom-call | flops 1207959552 | bytes 9437184 | tf_op jit(solution)/shard_map/pallas_call | solution.py:177
  55.8 0.9 shard_map.123
  56.7 1.7 %collective-permute-start.11 = (bf16[2,32,2304]{2,1,0:T(8,128)(2,1)S(1)}, bf16[2,32,2304]{2,1,0:T(8,128)(2,1)S(1)}, u32[]{:S(2)}, u32[]{:S(2)}) collective-permute-start(bf16[2,32,2304]{2,1,0:T(8,128)(2,1)S(1)} %add_convert_fusion.after_ref), channel_id=1, source_target_pairs={{0,2},{1,3},{2,0},{3,1},{4,6},{5,7},{6,4},{7,5},{8,10},{9,11},{10,... | collective-permute-start | bytes 884744 | tf_op jit(solution)/shard_map/ppermute | solution.py:38
  58.5 5.1 %shard_map.118 = (f32[2,64,1280]{2,1,0:T(8,128)S(1)}, bf16[2,64,1280]{2,1,0:T(8,128)(2,1)S(1)}) custom-call(bf16[128,2304]{1,0:T(8,128)(2,1)S(1)} %shard_map.114.x_ref, bf16[2304,4608]{1,0:T(8,128)(2,1)} %gate_ref.5, bf16[2304,4608]{1,0:T(8,128)(2,1)} %up_ref.5, bf16[2,64,1024]{2,1,0:T(8,128)(2,1)S(1)} %get-tuple-element.19.after_ref), custom_call_target="tpu_custom_call" | custom-call | flops 1509949440 | bytes 11796480 | tf_op jit(solution)/shard_map/pallas_call | solution.py:177
  63.7 0.9 add_convert_fusion.2
  65.1 0.9 collective-permute-done.11
  66.2 1.8 %collective-permute-start.12 = (bf16[32,2304]{1,0:T(8,128)(2,1)S(1)}, bf16[32,2304]{1,0:T(8,128)(2,1)S(1)}, u32[]{:S(2)}, u32[]{:S(2)}) collective-permute-start(bf16[32,2304]{1,0:T(8,128)(2,1)S(1)} %fusion.1.refs_0_), channel_id=1, source_target_pairs={{0,2},{1,3},{2,0},{3,1},{4,6},{5,7},{6,4},{7,5},{8,10},{9,11},{10,... | collective-permute-start | bytes 442376 | tf_op jit(solution)/shard_map/ppermute | solution.py:38
  68.4 2.6 %collective-permute-done.7 = bf16[2,32,1024]{2,1,0:T(8,128)(2,1)S(1)} collective-permute-done((bf16[2,32,1024]{2,1,0:T(8,128)(2,1)S(1)}, bf16[2,32,1024]{2,1,0:T(8,128)(2,1)S(1)}, u32[]{:S(2)}, u32[]{:S(2)}) %collective-permute-start.7) | collective-permute-done | bytes 131104 | tf_op jit(solution)/shard_map/ppermute | solution.py:38
  71.0 0.9 convert_add_fusion.2
  72.0 2.2 %collective-permute-done.12.refs_1_ = bf16[32,2304]{1,0:T(8,128)(2,1)S(1)} collective-permute-done((bf16[32,2304]{1,0:T(8,128)(2,1)S(1)}, bf16[32,2304]{1,0:T(8,128)(2,1)S(1)}, u32[]{:S(2)}, u32[]{:S(2)}) %collective-permute-start.12) | collective-permute-done | bytes 147488 | tf_op jit(solution)/shard_map/ppermute | solution.py:38
  74.2 3.1 %collective-permute-done.2 = bf16[2,32,1280]{2,1,0:T(8,128)(2,1)S(1)} collective-permute-done((bf16[2,32,1280]{2,1,0:T(8,128)(2,1)S(1)}, bf16[2,32,1280]{2,1,0:T(8,128)(2,1)S(1)}, u32[]{:S(2)}, u32[]{:S(2)}) %collective-permute-start.2) | collective-permute-done | bytes 163872 | tf_op jit(solution)/shard_map/ppermute | solution.py:38
  77.8 1.8 %collective-permute-start.8 = (bf16[32,1024]{1,0:T(8,128)(2,1)S(1)}, bf16[32,1024]{1,0:T(8,128)(2,1)S(1)}, u32[]{:S(2)}, u32[]{:S(2)}) collective-permute-start(bf16[32,1024]{1,0:T(8,128)(2,1)S(1)} %fusion.5.refs_0_), channel_id=1, source_target_pairs={{0,2},{1,3},{2,0},{3,1},{4,6},{5,7},{6,4},{7,5},{8,10},{9,11},{10,... | collective-permute-start | bytes 196616 | tf_op jit(solution)/shard_map/ppermute | solution.py:38
  79.6 3.3 %collective-permute-done.8.refs_1_ = bf16[32,1024]{1,0:T(8,128)(2,1)S(1)} collective-permute-done((bf16[32,1024]{1,0:T(8,128)(2,1)S(1)}, bf16[32,1024]{1,0:T(8,128)(2,1)S(1)}, u32[]{:S(2)}, u32[]{:S(2)}) %collective-permute-start.8) | collective-permute-done | bytes 65568 | tf_op jit(solution)/shard_map/ppermute | solution.py:38
  83.4 5.5 %shard_map.119.refs_5_.after_ref = f32[128,2304]{1,0:T(8,128)S(1)} custom-call(s32[1]{0:T(128)} %bitcast.gy_ref, bf16[32,2304]{1,0:T(8,128)(2,1)S(1)} %fusion.1.refs_0_, bf16[32,2304]{1,0:T(8,128)(2,1)S(1)} %collective-permute-done.12.refs_1_, bf16[32,2304]{1,0:T(8,128)(2,1)S(1)} %collective-permute-done.13.refs_2_, ...), custom_call_target="tpu_custom_call" | custom-call | flops 1358954496 | bytes 10616832 | tf_op jit(solution)/shard_map/pallas_call | solution.py:233
  89.0 39.7 %all-reduce.2.cloned.1.call-done.sums_ref = f32[32,4,512]{2,1,0:T(4,128)} async-done(((f32[32,4,512]{2,1,0:T(4,128)}), f32[32,4,512]{2,1,0:T(4,128)}) %all-reduce.2.cloned.1.call-update) | async-done | bytes 262160 | tf_op jit(solution)/shard_map/psum | solution.py:442
  128.7 0.9 copy-done.6
  129.6 3.7 %shard_map.120.refs_5_ = f32[128,2304]{1,0:T(8,128)S(1)} custom-call(s32[1]{0:T(128)} %bitcast.gy_ref, bf16[32,1024]{1,0:T(8,128)(2,1)S(1)} %fusion.5.refs_0_, bf16[32,1024]{1,0:T(8,128)(2,1)S(1)} %collective-permute-done.8.refs_1_, bf16[32,1024]{1,0:T(8,128)(2,1)S(1)} %collective-permute-done.9.refs_2_, ...), custom_call_target="tpu_custom_call" | custom-call | flops 603979776 | bytes 4718592 | tf_op jit(solution)/shard_map/pallas_call | solution.py:233
  133.4 1.5 collective-permute-start.16
  134.9 4.8 %shard_map.121 = bf16[32,4,2304]{2,1,0:T(4,128)(2,1)} custom-call(s32[1]{0:T(128)} %bitcast.gy_ref, bf16[32,1280]{1,0:T(8,128)(2,1)S(1)} %fusion.3.refs_0_, bf16[32,1280]{1,0:T(8,128)(2,1)S(1)} %collective-permute-done.3.refs_1_, bf16[32,1280]{1,0:T(8,128)(2,1)S(1)} %collective-permute-done.4.refs_2_, bf16[32,1280]{1,0:T(8,128)(2,1)S(1)} %collective-permute-done.5.refs_3_, ...), custom_call_target="tpu_custom_call" | custom-call | flops 754974720 | bytes 5898240 | tf_op jit(solution)/shard_map/pallas_call | solution.py:233
  139.7 3.0 %all-to-all-start.1 = ((bf16[32,4,2304]{2,1,0:T(4,128)(2,1)}), bf16[32,4,2304]{2,1,0:T(4,128)(2,1)S(1)}, u32[]{:S(2)}, u32[]{:S(2)}) async-start(bf16[32,4,2304]{2,1,0:T(4,128)(2,1)} %shard_map.121), calls=%async_computation.1 | async-start | bytes 1179648 | tf_op jit(solution)/shard_map/all_to_all | solution.py:413
  144.1 15.4 %all-to-all-done.1 = bf16[32,4,2304]{2,1,0:T(4,128)(2,1)S(1)} async-done(((bf16[32,4,2304]{2,1,0:T(4,128)(2,1)}), bf16[32,4,2304]{2,1,0:T(4,128)(2,1)S(1)}, u32[]{:S(2)}, u32[]{:S(2)}) %all-to-all-start.1) | async-done | bytes 589856 | tf_op jit(solution)/shard_map/all_to_all | solution.py:413
  (64 shorter events, 6.0 us)
Async XLA Ops:
  9.3 27.6 %all-to-all-start = ((bf16[32,4,2304]{2,1,0:T(4,128)(2,1)}), bf16[32,4,2304]{2,1,0:T(4,128)(2,1)S(1)}, u32[]{:S(2)}, u32[]{:S(2)}) async-start(bf16[32,4,2304]{2,1,0:T(4,128)(2,1)} %bitcast.2), calls=%async_computation | async-start | bytes 1179648 | tf_op jit(solution)/shard_map/all_to_all | solution.py:413
  16.6 112.1 %all-reduce.2.cloned.1.call-start = ((), (), s32[]{:S(2)}) async-start(), calls=%async_computation.2 | async-start | bytes 524288 | tf_op jit(solution)/shard_map/psum | solution.py:442
  17.5 0.7 copy-start.7
  28.9 4.1 %copy-start = (bf16[2304,2304]{1,0:T(8,128)(2,1)}, bf16[2304,2304]{1,0:T(8,128)(2,1)S(1)}, u32[]{:S(2)}) copy-start(bf16[2304,2304]{1,0:T(8,128)(2,1)S(1)} %get-tuple-element.15.gate_ref) | copy-start | bytes 31850500
  33.0 3.9 %copy-start.2 = (bf16[2304,2304]{1,0:T(8,128)(2,1)}, bf16[2304,2304]{1,0:T(8,128)(2,1)S(1)}, u32[]{:S(2)}) copy-start(bf16[2304,2304]{1,0:T(8,128)(2,1)S(1)} %get-tuple-element.16.up_ref) | copy-start | bytes 31850500
  37.0 4.0 %copy-start.1 = (bf16[2304,2304]{1,0:T(8,128)(2,1)S(1)}, bf16[2304,2304]{1,0:T(8,128)(2,1)}, u32[]{:S(2)}) copy-start(bf16[2304,2304]{1,0:T(8,128)(2,1)} %copy-done) | copy-start | bytes 31850500
  41.0 4.0 %copy-start.3 = (bf16[2304,2304]{1,0:T(8,128)(2,1)S(1)}, bf16[2304,2304]{1,0:T(8,128)(2,1)}, u32[]{:S(2)}) copy-start(bf16[2304,2304]{1,0:T(8,128)(2,1)} %copy-done.2) | copy-start | bytes 31850500
  47.9 2.1 %collective-permute-start = (bf16[2,64,2304]{2,1,0:T(8,128)(2,1)S(1)}, bf16[2,64,2304]{2,1,0:T(8,128)(2,1)S(1)}, u32[]{:S(2)}, u32[]{:S(2)}) collective-permute-start(bf16[2,64,2304]{2,1,0:T(8,128)(2,1)S(1)} %get-tuple-element.18), channel_id=1, source_target_pairs={{0,1},{1,0},{2,3},{3,2},{4,5},{5,4},{6,7},{7,6},{8,9},{9,8},{10,11... | collective-permute-start | bytes 1769480 | tf_op jit(solution)/shard_map/ppermute | solution.py:38
  50.0 0.8 copy-start.8
  50.9 4.9 %copy-start.5 = (bf16[1,288,512]{2,1,0:T(8,128)(2,1)S(1)}, bf16[1,288,512]{2,1,0:T(8,128)(2,1)}, u32[]{:S(2)}) copy-start(bf16[1,288,512]{2,1,0:T(8,128)(2,1)} %weight_ref.1) | copy-start | bytes 884740
  55.3 8.4 %collective-permute-start.6 = (bf16[2,64,1024]{2,1,0:T(8,128)(2,1)S(1)}, bf16[2,64,1024]{2,1,0:T(8,128)(2,1)}, u32[]{:S(2)}, u32[]{:S(2)}) collective-permute-start(bf16[2,64,1024]{2,1,0:T(8,128)(2,1)S(1)} %get-tuple-element.19.after_ref), channel_id=1, source_target_pairs={{0,1},{1,0},{2,3},{3,2},{4,5},{5,4},{6,7},{7,6},{8,9},{9,8},{10,11... | collective-permute-start | bytes 786440 | tf_op jit(solution)/shard_map/ppermute | solution.py:38
  56.7 9.3 %copy-start.9 = (bf16[2,64,2304]{2,1,0:T(8,128)(2,1)S(1)}, bf16[2,64,2304]{2,1,0:T(8,128)(2,1)}, u32[]{:S(2)}) copy-start(bf16[2,64,2304]{2,1,0:T(8,128)(2,1)} %copy-done.8) | copy-start | bytes 1769476
  56.7 9.3 %collective-permute-start.11 = (bf16[2,32,2304]{2,1,0:T(8,128)(2,1)S(1)}, bf16[2,32,2304]{2,1,0:T(8,128)(2,1)S(1)}, u32[]{:S(2)}, u32[]{:S(2)}) collective-permute-start(bf16[2,32,2304]{2,1,0:T(8,128)(2,1)S(1)} %add_convert_fusion.after_ref), channel_id=1, source_target_pairs={{0,2},{1,3},{2,0},{3,1},{4,6},{5,7},{6,4},{7,5},{8,10},{9,11},{10,... | collective-permute-start | bytes 884744 | tf_op jit(solution)/shard_map/ppermute | solution.py:38
  63.6 4.4 %collective-permute-start.1 = (bf16[2,64,1280]{2,1,0:T(8,128)(2,1)S(1)}, bf16[2,64,1280]{2,1,0:T(8,128)(2,1)S(1)}, u32[]{:S(2)}, u32[]{:S(2)}) collective-permute-start(bf16[2,64,1280]{2,1,0:T(8,128)(2,1)S(1)} %get-tuple-element.21), channel_id=1, source_target_pairs={{0,1},{1,0},{2,3},{3,2},{4,5},{5,4},{6,7},{7,6},{8,9},{9,8},{10,11... | collective-permute-start | bytes 983048 | tf_op jit(solution)/shard_map/ppermute | solution.py:38
  64.7 6.4 %collective-permute-start.7 = (bf16[2,32,1024]{2,1,0:T(8,128)(2,1)S(1)}, bf16[2,32,1024]{2,1,0:T(8,128)(2,1)S(1)}, u32[]{:S(2)}, u32[]{:S(2)}) collective-permute-start(bf16[2,32,1024]{2,1,0:T(8,128)(2,1)S(1)} %add_convert_fusion.2), channel_id=1, source_target_pairs={{0,2},{1,3},{2,0},{3,1},{4,6},{5,7},{6,4},{7,5},{8,10},{9,11},{10,... | collective-permute-start | bytes 393224 | tf_op jit(solution)/shard_map/ppermute | solution.py:38
  66.2 8.0 %collective-permute-start.12 = (bf16[32,2304]{1,0:T(8,128)(2,1)S(1)}, bf16[32,2304]{1,0:T(8,128)(2,1)S(1)}, u32[]{:S(2)}, u32[]{:S(2)}) collective-permute-start(bf16[32,2304]{1,0:T(8,128)(2,1)S(1)} %fusion.1.refs_0_), channel_id=1, source_target_pairs={{0,2},{1,3},{2,0},{3,1},{4,6},{5,7},{6,4},{7,5},{8,10},{9,11},{10,... | collective-permute-start | bytes 442376 | tf_op jit(solution)/shard_map/ppermute | solution.py:38
  68.0 14.9 %collective-permute-start.13 = (bf16[32,2304]{1,0:T(8,128)(2,1)S(1)}, bf16[32,2304]{1,0:T(8,128)(2,1)S(1)}, u32[]{:S(2)}, u32[]{:S(2)}) collective-permute-start(bf16[32,2304]{1,0:T(8,128)(2,1)S(1)} %fusion.1.refs_0_), channel_id=1, source_target_pairs={{0,1},{1,0},{2,3},{3,2},{4,5},{5,4},{6,7},{7,6},{8,9},{9,8},{10,11... | collective-permute-start | bytes 442376 | tf_op jit(solution)/shard_map/ppermute | solution.py:38
  68.0 9.2 %collective-permute-start.2 = (bf16[2,32,1280]{2,1,0:T(8,128)(2,1)S(1)}, bf16[2,32,1280]{2,1,0:T(8,128)(2,1)S(1)}, u32[]{:S(2)}, u32[]{:S(2)}) collective-permute-start(bf16[2,32,1280]{2,1,0:T(8,128)(2,1)S(1)} %add_convert_fusion.1), channel_id=1, source_target_pairs={{0,2},{1,3},{2,0},{3,1},{4,6},{5,7},{6,4},{7,5},{8,10},{9,11},{10,... | collective-permute-start | bytes 491528 | tf_op jit(solution)/shard_map/ppermute | solution.py:38
  74.2 9.2 %collective-permute-start.14 = (bf16[32,2304]{1,0:T(8,128)(2,1)S(1)}, bf16[32,2304]{1,0:T(8,128)(2,1)S(1)}, u32[]{:S(2)}, u32[]{:S(2)}) collective-permute-start(bf16[32,2304]{1,0:T(8,128)(2,1)S(1)} %collective-permute-done.12.refs_1_), channel_id=1, source_target_pairs={{0,1},{1,0},{2,3},{3,2},{4,5},{5,4},{6,7},{7,6},{8,9},{9,8},{10,11... | collective-permute-start | bytes 442376 | tf_op jit(solution)/shard_map/ppermute | solution.py:38
  77.4 6.0 %collective-permute-start.3 = (bf16[32,1280]{1,0:T(8,128)(2,1)S(1)}, bf16[32,1280]{1,0:T(8,128)(2,1)S(1)}, u32[]{:S(2)}, u32[]{:S(2)}) collective-permute-start(bf16[32,1280]{1,0:T(8,128)(2,1)S(1)} %fusion.3.refs_0_), channel_id=1, source_target_pairs={{0,2},{1,3},{2,0},{3,1},{4,6},{5,7},{6,4},{7,5},{8,10},{9,11},{10,... | collective-permute-start | bytes 245768 | tf_op jit(solution)/shard_map/ppermute | solution.py:38
  77.8 5.0 %collective-permute-start.8 = (bf16[32,1024]{1,0:T(8,128)(2,1)S(1)}, bf16[32,1024]{1,0:T(8,128)(2,1)S(1)}, u32[]{:S(2)}, u32[]{:S(2)}) collective-permute-start(bf16[32,1024]{1,0:T(8,128)(2,1)S(1)} %fusion.5.refs_0_), channel_id=1, source_target_pairs={{0,2},{1,3},{2,0},{3,1},{4,6},{5,7},{6,4},{7,5},{8,10},{9,11},{10,... | collective-permute-start | bytes 196616 | tf_op jit(solution)/shard_map/ppermute | solution.py:38
  79.6 50.1 %collective-permute-start.9 = (bf16[32,1024]{1,0:T(8,128)(2,1)S(1)}, bf16[32,1024]{1,0:T(8,128)(2,1)S(1)}, u32[]{:S(2)}, u32[]{:S(2)}) collective-permute-start(bf16[32,1024]{1,0:T(8,128)(2,1)S(1)} %fusion.5.refs_0_), channel_id=1, source_target_pairs={{0,1},{1,0},{2,3},{3,2},{4,5},{5,4},{6,7},{7,6},{8,9},{9,8},{10,11... | collective-permute-start | bytes 196616 | tf_op jit(solution)/shard_map/ppermute | solution.py:38
  82.8 46.8 %collective-permute-start.10 = (bf16[32,1024]{1,0:T(8,128)(2,1)S(1)}, bf16[32,1024]{1,0:T(8,128)(2,1)S(1)}, u32[]{:S(2)}, u32[]{:S(2)}) collective-permute-start(bf16[32,1024]{1,0:T(8,128)(2,1)S(1)} %collective-permute-done.8.refs_1_), channel_id=1, source_target_pairs={{0,1},{1,0},{2,3},{3,2},{4,5},{5,4},{6,7},{7,6},{8,9},{9,8},{10,11... | collective-permute-start | bytes 196616 | tf_op jit(solution)/shard_map/ppermute | solution.py:38
  82.8 52.1 %collective-permute-start.4 = (bf16[32,1280]{1,0:T(8,128)(2,1)S(1)}, bf16[32,1280]{1,0:T(8,128)(2,1)S(1)}, u32[]{:S(2)}, u32[]{:S(2)}) collective-permute-start(bf16[32,1280]{1,0:T(8,128)(2,1)S(1)} %fusion.3.refs_0_), channel_id=1, source_target_pairs={{0,1},{1,0},{2,3},{3,2},{4,5},{5,4},{6,7},{7,6},{8,9},{9,8},{10,11... | collective-permute-start | bytes 245768 | tf_op jit(solution)/shard_map/ppermute | solution.py:38
  83.3 51.5 %collective-permute-start.5 = (bf16[32,1280]{1,0:T(8,128)(2,1)S(1)}, bf16[32,1280]{1,0:T(8,128)(2,1)S(1)}, u32[]{:S(2)}, u32[]{:S(2)}) collective-permute-start(bf16[32,1280]{1,0:T(8,128)(2,1)S(1)} %collective-permute-done.3.refs_1_), channel_id=1, source_target_pairs={{0,1},{1,0},{2,3},{3,2},{4,5},{5,4},{6,7},{7,6},{8,9},{9,8},{10,11... | collective-permute-start | bytes 245768 | tf_op jit(solution)/shard_map/ppermute | solution.py:38
  128.7 0.9 copy-start.6
  129.6 3.7 %collective-permute-start.15 = (f32[2,4,512]{2,1,0:T(4,128)S(1)}, f32[2,4,512]{2,1,0:T(4,128)S(1)}, u32[]{:S(2)}, u32[]{:S(2)}) collective-permute-start(f32[2,4,512]{2,1,0:T(4,128)S(1)} %get-tuple-element.26), channel_id=1, source_target_pairs={{0,1},{1,0},{2,3},{3,2},{4,5},{5,4},{6,7},{7,6},{8,9},{9,8},{10,11... | collective-permute-start | bytes 49160 | tf_op jit(solution)/shard_map/ppermute | solution.py:38
  133.3 9.4 %copy-start.10 = (bf16[4,12288]{1,0:T(4,128)(2,1)S(1)}, bf16[4,12288]{1,0:T(4,128)(2,1)}, u32[]{:S(2)}) copy-start(bf16[4,12288]{1,0:T(4,128)(2,1)} %param.16) | copy-start | bytes 294916
  133.3 26.1 %copy-start.4 = (bf16[4,9216]{1,0:T(4,128)(2,1)S(1)}, bf16[4,9216]{1,0:T(4,128)(2,1)}, u32[]{:S(2)}) copy-start(bf16[4,9216]{1,0:T(4,128)(2,1)} %tokens_ref.1) | copy-start | bytes 221188
  133.4 9.4 %collective-permute-start.16 = (f32[4,512]{1,0:T(4,128)S(1)}, f32[4,512]{1,0:T(4,128)S(1)}, u32[]{:S(2)}, u32[]{:S(2)}) collective-permute-start(f32[4,512]{1,0:T(4,128)S(1)} %slice_bitcast_fusion.6), channel_id=1, source_target_pairs={{0,2},{1,3},{2,0},{3,1},{4,6},{5,7},{6,4},{7,5},{8,10},{9,11},{10,... | collective-permute-start | bytes 24584 | tf_op jit(solution)/shard_map/ppermute | solution.py:38
  139.7 19.7 %all-to-all-start.1 = ((bf16[32,4,2304]{2,1,0:T(4,128)(2,1)}), bf16[32,4,2304]{2,1,0:T(4,128)(2,1)S(1)}, u32[]{:S(2)}, u32[]{:S(2)}) async-start(bf16[32,4,2304]{2,1,0:T(4,128)(2,1)} %shard_map.121), calls=%async_computation.1 | async-start | bytes 1179648 | tf_op jit(solution)/shard_map/all_to_all | solution.py:413
Sparse Core Ops, SparseCore 0:
  56.8 71.7 all-reduce.1

commit v4 on v3

--- a/solution.py
+++ b/solution.py
@@ -32,6 +32,14 @@
 
 def in_hbm(x):
     return pltpu.with_memory_space_constraint(x, pltpu.HBM)
+
+
+def vmem_out(shape, dtype):
+    return pltpu.VMEM(shape, dtype)
+
+
+def in_vmem(x):
+    return pltpu.with_memory_space_constraint(x, pltpu.VMEM)
 
 
 def swap(x, axis, size, bits):
@@ -64,7 +72,7 @@
         norm_kernel,
         in_specs=[ANYWHERE, ANYWHERE],
         out_specs=WHOLE,
-        out_shape=jax.ShapeDtypeStruct((n_gx, n_gy, batch, channels // n_gy), BF16),
+        out_shape=vmem_out((n_gx, n_gy, batch, channels // n_gy), BF16),
         scratch_shapes=[
             pltpu.VMEM((batch, channels), BF16),
             pltpu.VMEM((1, channels), F32),
@@ -75,7 +83,8 @@
     )(in_hbm(tokens), in_hbm(gain.reshape(1, -1)))
 
 
-def assemble_kernel(gy_ref, rows_ref, out_ref):
+def assemble_kernel(gy_ref, rows_ref, after_ref, out_ref):
+    del after_ref
     devices, batch, _ = rows_ref.shape
     quarter = devices // 4
     pack = 16 // batch
@@ -89,16 +98,16 @@
             out_ref[start : start + 16] = tall.astype(BF16)
 
 
-def assemble(gy, rows):
+def assemble(gy, rows, after):
     devices, batch, width = rows.shape
     return pl.pallas_call(
         assemble_kernel,
-        in_specs=[SCALARS, WHOLE],
+        in_specs=[SCALARS, WHOLE, ANYWHERE],
         out_specs=WHOLE,
-        out_shape=jax.ShapeDtypeStruct((devices * batch, width), BF16),
+        out_shape=vmem_out((devices * batch, width), BF16),
         compiler_params=params(4),
         cost_estimate=cost(2 * rows.size, 4 * rows.size),
-    )(gy, rows)
+    )(gy, in_vmem(rows), after)
 
 
 def spread_rows(out_ref, value, gy, columns=slice(None)):
@@ -142,32 +151,12 @@
         gate_up_tile(x, [slots[k, n] for k in range(2)], n * tile, tile, keep_ref, send_ref)
 
 
-def gate_up_ready_kernel(tile, x_ref, gate_ref, up_ref, keep_ref, send_ref):
-    x = x_ref[...]
-    for at in range(0, keep_ref.shape[2], tile):
-        weights = [ref[:, at : at + tile] for ref in (gate_ref, up_ref)]
-        gate_up_tile(x, weights, at, tile, keep_ref, send_ref)
-
-
 def gate_up_shapes(rows, width):
     half = rows // 2
     return [
-        jax.ShapeDtypeStruct((2, half, width), F32),
-        jax.ShapeDtypeStruct((2, half, width), BF16),
+        vmem_out((2, half, width), F32),
+        vmem_out((2, half, width), BF16),
     ]
-
-
-def gate_up_ready(x, gate, up):
-    rows, depth = x.shape
-    width = gate.shape[1]
-    return pl.pallas_call(
-        functools.partial(gate_up_ready_kernel, tile_of(width, 256)),
-        in_specs=[WHOLE, WHOLE, WHOLE],
-        out_specs=[WHOLE, WHOLE],
-        out_shape=gate_up_shapes(rows, width),
-        compiler_params=params(8),
-        cost_estimate=cost(4 * rows * depth * width, 2 * rows * depth),
-    )(x, gate, up)
 
 
 def gate_up(x, w_gate, w_up, start, width, after):
@@ -183,9 +172,9 @@
             pltpu.VMEM((2, count, depth, tile), BF16),
             pltpu.SemaphoreType.DMA((2, count)),
         ],
-        compiler_params=params(14),
-        cost_estimate=cost(4 * rows * depth * width, 4 * depth * width),
-    )(x, in_hbm(w_gate), in_hbm(w_up), after)
+        compiler_params=params(22),
+        cost_estimate=cost(rows * depth * width, depth * width),
+    )(in_vmem(x), in_hbm(w_gate), in_hbm(w_up), after)
 
 
 def down_kernel(start, tile, has_sum, last, gy_ref, *refs):
@@ -224,23 +213,23 @@
     width = w_down.shape[1]
     tile = tile_of(width, 256)
     count = width // tile
-    args = [gy, *hidden, in_hbm(w_down)]
+    args = [gy, *[in_vmem(h) for h in hidden], in_hbm(w_down)]
     in_specs = [SCALARS] + [WHOLE] * 4 + [ANYWHERE]
     if total is not None:
-        args.append(total)
+        args.append(in_vmem(total))
         in_specs.append(WHOLE)
     shape = (devices, rows // devices, width) if last else (rows, width)
     return pl.pallas_call(
         functools.partial(down_kernel, start, tile, total is not None, last),
         in_specs=in_specs,
         out_specs=WHOLE,
-        out_shape=jax.ShapeDtypeStruct(shape, BF16 if last else F32),
+        out_shape=vmem_out(shape, BF16 if last else F32),
         scratch_shapes=[
             pltpu.VMEM((count, depth, tile), BF16),
             pltpu.SemaphoreType.DMA((count,)),
         ],
-        compiler_params=params(14),
-        cost_estimate=cost(2 * rows * depth * width, 2 * depth * width),
+        compiler_params=params(22),
+        cost_estimate=cost(rows * depth * width, depth * width),
     )(*args)
 
 
@@ -262,49 +251,31 @@
         out_shape=jax.ShapeDtypeStruct(tokens.shape, BF16),
         compiler_params=params(8),
         cost_estimate=cost(sums.size, 2 * sums.size),
-    )(tokens, sums)
-
-
-def fresh_kernel(gy_ref, x_ref, weight_ref, out_ref):
+    )(in_vmem(tokens), in_vmem(sums))
+
+
+def fresh_kernel(gy_ref, x_ref, weight_ref, after_ref, out_ref):
+    del after_ref
     value = jnp.dot(x_ref[...], weight_ref[0], preferred_element_type=F32)
     spread_rows(out_ref, value, gy_ref[0])
 
 
-def fresh_part(gy, x, w_kv, devices):
+def fresh_part(gy, x, w_kv, devices, after):
     rows, depth = x.shape
     columns = w_kv.shape[2]
     return pl.pallas_call(
         fresh_kernel,
-        in_specs=[SCALARS, WHOLE, WHOLE],
+        in_specs=[SCALARS, WHOLE, WHOLE, ANYWHERE],
         out_specs=WHOLE,
-        out_shape=jax.ShapeDtypeStruct((devices, rows // devices, columns), F32),
+        out_shape=vmem_out((devices, rows // devices, columns), F32),
         compiler_params=params(8),
         cost_estimate=cost(2 * rows * depth * columns, 2 * depth * columns),
-    )(gy, x, w_kv)
-
-
-def own_first_kernel(gx_ref, gy_ref, sums_ref, after_ref, near_ref, far_ref):
-    del after_ref
-    for at, turn in enumerate(ORDER):
-        device = gx_ref[0] * len(ORDER) + (gy_ref[0] ^ turn)
-        (near_ref, far_ref)[at // 2][at % 2] = sums_ref[device]
-
-
-def own_first(gx, gy, sums, after):
-    shape = jax.ShapeDtypeStruct((2, *sums.shape[1:]), sums.dtype)
-    return pl.pallas_call(
-        own_first_kernel,
-        in_specs=[SCALARS, SCALARS, WHOLE, ANYWHERE],
-        out_specs=[WHOLE, WHOLE],
-        out_shape=[shape, shape],
-        compiler_params=params(4),
-        cost_estimate=cost(sums.size, 8 * sums.size),
-    )(gx, gy, sums, after)
+    )(gy, in_vmem(x), in_vmem(w_kv), after)
 
 
 def cache_kernel(
-    scale, tile, lengths_ref, query_ref, key_ref, value_ref, gate_ref, up_ref, after_ref,
-    acc_ref, top_ref, sum_ref, gate_out, up_out, keys, values, cache_sems, weight_sems,
+    scale, lengths_ref, query_ref, key_ref, value_ref, after_ref,
+    acc_ref, top_ref, sum_ref, keys, values, cache_sems,
 ):
     del after_ref
     batch = query_ref.shape[0]
@@ -315,20 +286,9 @@
         ]
         for r in range(batch)
     ]
-    weights = [
-        pltpu.make_async_copy(
-            source.at[:, pl.ds(at, tile)],
-            target.at[:, pl.ds(at, tile)],
-            weight_sems.at[k, at // tile],
-        )
-        for at in range(0, gate_out.shape[1], tile)
-        for k, (source, target) in enumerate(((gate_ref, gate_out), (up_ref, up_out)))
-    ]
     for pair in caches:
         for copy in pair:
             copy.start()
-    for copy in weights:
-        copy.start()
     for r in range(batch):
         caches[r][0].wait()
         scores = scale * lax.dot_general(
@@ -348,40 +308,30 @@
         acc_ref[r] = both[:heads] + both[heads:]
         top_ref[r] = top
         sum_ref[r] = jnp.sum(chance, axis=1, keepdims=True)
-    for copy in weights:
-        copy.wait()
-
-
-def attend_cache(grouped, key_cache, value_cache, lengths, w_gate, w_up, width, after):
+
+
+def attend_cache(grouped, key_cache, value_cache, lengths, after):
     batch, heads, depth = grouped.shape
     span = key_cache.shape[1]
-    tall = w_gate.shape[0]
-    tile = tile_of(width, 256)
-    *cached, gate, up = pl.pallas_call(
-        functools.partial(cache_kernel, 1.0 / math.sqrt(depth), tile),
-        in_specs=[SCALARS, WHOLE] + [ANYWHERE] * 5,
-        out_specs=[WHOLE] * 5,
+    return pl.pallas_call(
+        functools.partial(cache_kernel, 1.0 / math.sqrt(depth)),
+        in_specs=[SCALARS, WHOLE] + [ANYWHERE] * 3,
+        out_specs=[WHOLE] * 3,
         out_shape=[
-            jax.ShapeDtypeStruct((batch, heads, depth), F32),
-            jax.ShapeDtypeStruct((batch, heads, 1), F32),
-            jax.ShapeDtypeStruct((batch, heads, 1), F32),
-            pltpu.VMEM((tall, width), BF16),
-            pltpu.VMEM((tall, width), BF16),
+            vmem_out((batch, heads, depth), F32),
+            vmem_out((batch, heads, 1), F32),
+            vmem_out((batch, heads, 1), F32),
         ],
         scratch_shapes=[
             pltpu.VMEM((batch, span, depth), BF16),
             pltpu.VMEM((batch, span, depth), BF16),
             pltpu.SemaphoreType.DMA((2, batch)),
-            pltpu.SemaphoreType.DMA((2, width // tile)),
         ],
-        compiler_params=params(14),
+        compiler_params=params(16),
         cost_estimate=cost(
-            6 * batch * heads * span * depth,
-            4 * batch * span * depth + 4 * tall * width,
-            batch * heads * span,
+            6 * batch * heads * span * depth, 4 * batch * span * depth, batch * heads * span
         ),
-    )(lengths, grouped, in_hbm(key_cache), in_hbm(value_cache), in_hbm(w_gate), in_hbm(w_up), after)
-    return cached, gate, up
+    )(lengths, in_vmem(grouped), in_hbm(key_cache), in_hbm(value_cache), after)
 
 
 def attend_new(grouped, cached, key_new, value_new):
@@ -401,9 +351,8 @@
 def chunk_widths(columns):
     unit = 256 if columns % 256 == 0 else 128
     units = columns // unit
-    first = units // 2
-    second = (units - first) // 2
-    return [unit * u for u in (first, second, units - first - second)]
+    side = max(1, 5 * units // 18)
+    return [unit * u for u in (side, units - 2 * side, side)]
 
 
 def body(n_gx, n_gy, tokens, gain, w_gate, w_up, w_down, w_kv, queries, key_cache, value_cache, lengths):
@@ -418,28 +367,25 @@
     normed = norm(tokens, gain, n_gx, n_gy)
     gathered = exchange(normed.reshape(devices, batch, -1))
     grouped = queries.reshape(batch, -1, HD)
-    cached, gate, up = attend_cache(
-        grouped, key_cache, value_cache, lengths, w_gate, w_up, widths[0], normed
-    )
-    x = assemble(gy, gathered)
+    cached = attend_cache(grouped, key_cache, value_cache, lengths, normed)
+    x = assemble(gy, gathered, cached[0])
     rows = x.shape[0]
     quarter = rows // 4
 
     sums = []
     start = 0
     for c, width in enumerate(widths):
-        if c == 0:
-            keep, send = gate_up_ready(x, gate, up)
-        else:
-            keep, send = gate_up(x, w_gate, w_up, start, width, sums[0][2] if c == 1 else send)
+        keep, send = gate_up(x, w_gate, w_up, start, width, sums[-1][2] if c else gy)
         core = swap_gy(send, 1)
         across = (keep[:, quarter:] + core[:, quarter:].astype(F32)).astype(BF16)
         sums.append((keep, core, across))
         start += width
 
     slab = w_kv.shape[1]
-    part = fresh_part(gy, lax.dynamic_slice_in_dim(x, gx * slab, slab, 1), w_kv, devices)
-    over_gx = lax.psum(part, "gx")
+    part = fresh_part(gy, lax.dynamic_slice_in_dim(x, gx * slab, slab, 1), w_kv, devices, send)
+    fresh = jnp.sum(exchange(part), axis=0)
+    key_new = fresh[:, :HD].astype(BF16)
+    value_new = fresh[:, HD:].astype(BF16)
 
     start = 0
     total = None
@@ -450,12 +396,6 @@
         hidden = (own, far, swap_gy(own, 1), swap_gy(far, 1))
         total = down(gy, hidden, w_down, start, total, devices, c == len(sums) - 1)
         start += widths[c]
-        if c == 0:
-            near, far = own_first(gx.astype(jnp.int32).reshape(1), gy, over_gx, total)
-            near = near + swap_gy(far, 1)
-            fresh = near[0] + swap_gy(near[1], 2)
-            key_new = fresh[:, :HD].astype(BF16)
-            value_new = fresh[:, HD:].astype(BF16)
 
     ffn = exchange(total)
     mixed = finish(tokens, ffn.reshape(n_gx, n_gy, batch, -1))

time: 168 us -> 108 us (0.64)
  waiting for transfers between devices: 69 us -> 34.8 us
  local copies, waits for them, and re-layouts: 20.2 us -> 3.21 us
  between operations: 14.3 us -> 0.92 us
  starting transfers between devices: 19.7 us -> 22.8 us
    psum x1 -> x0, waiting for transfers between devices: 39.7 us -> none  [body(): over_gx = lax.psum(part, 'gx')]
    unnamed x24 -> x12, local copies, waits for them, and re-layouts: 20 us -> 2.99 us
    all_to_all x2 -> x3, waiting for transfers between devices: 15.4 us -> 24.2 us  [body(): lax.all_to_all(x, ('gx', 'gy'), split_axis=0, concat_axis=0, tiled=True)]
    pallas_call x2 -> x3, Pallas kernels: 9.52 us -> 17.5 us  [gate_up(): pl.pallas_call(functools.partial(gate_up_kernel, start, tile), in_specs=[...]
    pallas_call x5 -> x3, Pallas kernels: 14.7 us -> 7.39 us  [the longest x1 6.31 us: attend_cache(): pl.pallas_call(functools.partial(cache_kernel, 1.0 / math.sqrt(depth)), i...]
    all_to_all x2 -> x3, starting transfers between devices: 10.3 us -> 13.9 us  [body(): lax.all_to_all(x, ('gx', 'gy'), split_axis=0, concat_axis=0, tiled=True)]
    ppermute x17 -> x15, waiting for transfers between devices: 13.9 us -> 10.6 us  [swap(): return lax.ppermute(x, axis, [(i, i ^ bits) for i in range(size)])]
    ppermute x17 -> x15, starting transfers between devices: 9.36 us -> 8.9 us  [swap(): return lax.ppermute(x, axis, [(i, i ^ bits) for i in range(size)])]
  transfers between devices with their start and end apart: 20 -> 18, of which waited for: 8 -> 8; matrix products, arithmetic and copies ran while one was open for 3% -> 5% of each run, Pallas kernels for 18% -> 25%
where the time goes in v4:
time: 108 us; the launch traced here: 107 us
  Pallas kernels  41.6 us (39%)
  waiting for transfers between devices  34.8 us (32%)
  starting transfers between devices  22.8 us (21%)
  other arithmetic  3.69 us (3%)
  local copies, waits for them, and re-layouts  3.21 us (3%)
    all_to_all x3, waiting for transfers between devices, body(): lax.all_to_all(x, ('gx', 'gy'), split_axis=0, concat_axis=0, tiled=True)  24.2 us
    pallas_call x3, Pallas kernels, gate_up(): pl.pallas_call(functools.partial(gate_up_kernel, start, tile), in_specs=[...  17.5 us
    pallas_call x3, Pallas kernels, down(): pl.pallas_call(functools.partial(down_kernel, start, tile, total is not N...  13.9 us
    all_to_all x3, starting transfers between devices, body(): lax.all_to_all(x, ('gx', 'gy'), split_axis=0, concat_axis=0, tiled=True)  13.9 us
    ppermute x15, waiting for transfers between devices, swap(): return lax.ppermute(x, axis, [(i, i ^ bits) for i in range(size)])  10.6 us
    ppermute x15, starting transfers between devices, swap(): return lax.ppermute(x, axis, [(i, i ^ bits) for i in range(size)])  8.9 us
    pallas_call x1, Pallas kernels, attend_cache(): pl.pallas_call(functools.partial(cache_kernel, 1.0 / math.sqrt(depth)), i...  6.31 us
    unnamed x12, local copies, waits for them, and re-layouts  2.99 us
  transfers between devices with their start and end apart: 18, of which 8 were waited for; matrix products, arithmetic and copies ran while one was open for 5% of the time, Pallas kernels for 25%

profile of v4, /device:TPU:0, one launch (start us, length us, event | category | flops | bytes accessed | tf_op | source)
XLA Modules:
  0.0 107.1 jit_solution(12964880788588000731)
XLA Ops:
  0.6 2.1 %shard_map.113.after_ref = bf16[8,4,4,2304]{3,2,1,0:T(4,128)(2,1)} custom-call(bf16[4,9216]{1,0:T(4,128)(2,1)} %tokens_ref.1, f32[1,9216]{1,0:T(1,128)} %bitcast.53), custom_call_target="tpu_custom_call" | custom-call | flops 368640 | bytes 589824 | tf_op jit(solution)/shard_map/pallas_call | solution.py:71
  2.7 7.3 %all-to-all-start = ((bf16[32,4,2304]{2,1,0:T(4,128)(2,1)}), bf16[32,4,2304]{2,1,0:T(4,128)(2,1)S(1)}, u32[]{:S(2)}, u32[]{:S(2)}) async-start(bf16[32,4,2304]{2,1,0:T(4,128)(2,1)} %bitcast.2), calls=%async_computation | async-start | bytes 1179648 | tf_op jit(solution)/shard_map/all_to_all | solution.py:362
  10.1 0.9 copy.22
  11.6 6.3 %shard_map.114 = (f32[4,48,256]{2,1,0:T(8,128)S(1)}, f32[4,48,1]{2,1,0:T(8,128)S(1)}, f32[4,48,1]{2,1,0:T(8,128)S(1)}) custom-call(s32[4]{0:T(128)S(1)} %copy-done.2, bf16[4,48,256]{2,1,0:T(8,128)(2,1)S(1)} %bitcast.49, bf16[4,2048,256]{2,1,0:T(8,128)(2,1)} %key_ref.1, bf16[4,2048,256]{2,1,0:T(8,128)(2,1)} %value_ref.1, ...), custom_call_target="tpu_custom_call" | custom-call | flops 603979776 | bytes 8388608 | tf_op jit(solution)/shard_map/pallas_call | solution.py:316
  17.9 8.8 %all-to-all-done.rows_ref = bf16[32,4,2304]{2,1,0:T(4,128)(2,1)S(1)} async-done(((bf16[32,4,2304]{2,1,0:T(4,128)(2,1)}), bf16[32,4,2304]{2,1,0:T(4,128)(2,1)S(1)}, u32[]{:S(2)}, u32[]{:S(2)}) %all-to-all-start) | async-done | bytes 589856 | tf_op jit(solution)/shard_map/all_to_all | solution.py:362
  26.9 5.1 %shard_map.116 = (f32[2,64,1280]{2,1,0:T(8,128)S(1)}, bf16[2,64,1280]{2,1,0:T(8,128)(2,1)S(1)}) custom-call(bf16[128,2304]{1,0:T(8,128)(2,1)S(1)} %shard_map.115.x_ref, bf16[2304,4608]{1,0:T(8,128)(2,1)} %gate_ref.5, bf16[2304,4608]{1,0:T(8,128)(2,1)} %up_ref.5, s32[1]{0:T(128)} %bitcast.gy_ref.after_ref), custom_call_target="tpu_custom_call" | custom-call | flops 377487360 | bytes 2949120 | tf_op jit(solution)/shard_map/pallas_call | solution.py:166
  32.1 1.6 %collective-permute-done = bf16[2,64,1280]{2,1,0:T(8,128)(2,1)S(1)} collective-permute-done((bf16[2,64,1280]{2,1,0:T(8,128)(2,1)S(1)}, bf16[2,64,1280]{2,1,0:T(8,128)(2,1)S(1)}, u32[]{:S(2)}, u32[]{:S(2)}) %collective-permute-start) | collective-permute-done | bytes 327712 | tf_op jit(solution)/shard_map/ppermute | solution.py:46
  33.7 0.7 copy-done.3
  34.5 7.3 %shard_map.117 = (f32[2,64,2048]{2,1,0:T(8,128)S(1)}, bf16[2,64,2048]{2,1,0:T(8,128)(2,1)S(1)}) custom-call(bf16[128,2304]{1,0:T(8,128)(2,1)S(1)} %shard_map.115.x_ref, bf16[2304,4608]{1,0:T(8,128)(2,1)} %gate_ref.5, bf16[2304,4608]{1,0:T(8,128)(2,1)} %up_ref.5, bf16[2,32,1280]{2,1,0:T(8,128)(2,1)S(1)} %add_convert_fusion.2.after_ref), custom_call_target="tpu_custom_call" | custom-call | flops 603979776 | bytes 4718592 | tf_op jit(solution)/shard_map/pallas_call | solution.py:166
  42.1 1.4 %collective-permute-start.11 = (bf16[2,32,1280]{2,1,0:T(8,128)(2,1)S(1)}, bf16[2,32,1280]{2,1,0:T(8,128)(2,1)S(1)}, u32[]{:S(2)}, u32[]{:S(2)}) collective-permute-start(bf16[2,32,1280]{2,1,0:T(8,128)(2,1)S(1)} %add_convert_fusion.2.after_ref), channel_id=1, source_target_pairs={{0,2},{1,3},{2,0},{3,1},{4,6},{5,7},{6,4},{7,5},{8,10},{9,11},{10,... | collective-permute-start | bytes 491528 | tf_op jit(solution)/shard_map/ppermute | solution.py:46
  43.9 1.0 add_convert_fusion.after_ref
  44.9 1.2 %collective-permute-start.7 = (bf16[2,32,2048]{2,1,0:T(8,128)(2,1)S(1)}, bf16[2,32,2048]{2,1,0:T(8,128)(2,1)S(1)}, u32[]{:S(2)}, u32[]{:S(2)}) collective-permute-start(bf16[2,32,2048]{2,1,0:T(8,128)(2,1)S(1)} %add_convert_fusion.after_ref), channel_id=1, source_target_pairs={{0,2},{1,3},{2,0},{3,1},{4,6},{5,7},{6,4},{7,5},{8,10},{9,11},{10,... | collective-permute-start | bytes 786440 | tf_op jit(solution)/shard_map/ppermute | solution.py:46
  46.1 3.1 %collective-permute-done.11 = bf16[2,32,1280]{2,1,0:T(8,128)(2,1)S(1)} collective-permute-done((bf16[2,32,1280]{2,1,0:T(8,128)(2,1)S(1)}, bf16[2,32,1280]{2,1,0:T(8,128)(2,1)S(1)}, u32[]{:S(2)}, u32[]{:S(2)}) %collective-permute-start.11) | collective-permute-done | bytes 163872 | tf_op jit(solution)/shard_map/ppermute | solution.py:46
  49.2 1.0 convert_add_fusion.1
  50.1 5.1 %shard_map.118 = (f32[2,64,1280]{2,1,0:T(8,128)S(1)}, bf16[2,64,1280]{2,1,0:T(8,128)(2,1)S(1)}) custom-call(bf16[128,2304]{1,0:T(8,128)(2,1)S(1)} %shard_map.115.x_ref, bf16[2304,4608]{1,0:T(8,128)(2,1)} %gate_ref.5, bf16[2304,4608]{1,0:T(8,128)(2,1)} %up_ref.5, bf16[2,32,2048]{2,1,0:T(8,128)(2,1)S(1)} %add_convert_fusion.after_ref), custom_call_target="tpu_custom_call" | custom-call | flops 377487360 | bytes 2949120 | tf_op jit(solution)/shard_map/pallas_call | solution.py:166
  55.4 1.0 convert_add_fusion
  56.5 1.3 %collective-permute-start.8 = (bf16[32,2048]{1,0:T(8,128)(2,1)S(1)}, bf16[32,2048]{1,0:T(8,128)(2,1)S(1)}, u32[]{:S(2)}, u32[]{:S(2)}) collective-permute-start(bf16[32,2048]{1,0:T(8,128)(2,1)S(1)} %fusion.1.refs_0_), channel_id=1, source_target_pairs={{0,2},{1,3},{2,0},{3,1},{4,6},{5,7},{6,4},{7,5},{8,10},{9,11},{10,... | collective-permute-start | bytes 393224 | tf_op jit(solution)/shard_map/ppermute | solution.py:46
  57.9 0.8 collective-permute-start.3
  58.8 1.3 %collective-permute-start.12 = (bf16[32,1280]{1,0:T(8,128)(2,1)S(1)}, bf16[32,1280]{1,0:T(8,128)(2,1)S(1)}, u32[]{:S(2)}, u32[]{:S(2)}) collective-permute-start(bf16[32,1280]{1,0:T(8,128)(2,1)S(1)} %fusion.3.refs_0_), channel_id=1, source_target_pairs={{0,2},{1,3},{2,0},{3,1},{4,6},{5,7},{6,4},{7,5},{8,10},{9,11},{10,... | collective-permute-start | bytes 245768 | tf_op jit(solution)/shard_map/ppermute | solution.py:46
  60.2 0.9 shard_map.123
  61.1 2.8 %all-to-all-start.2 = ((f32[32,4,512]{2,1,0:T(4,128)}), f32[32,4,512]{2,1,0:T(4,128)S(1)}, u32[]{:S(2)}, u32[]{:S(2)}) async-start(f32[32,4,512]{2,1,0:T(4,128)} %shard_map.123), calls=%async_computation.2 | async-start | bytes 524288 | tf_op jit(solution)/shard_map/all_to_all | solution.py:362
  64.5 1.9 %collective-permute-done.3 = bf16[2,32,1280]{2,1,0:T(8,128)(2,1)S(1)} collective-permute-done((bf16[2,32,1280]{2,1,0:T(8,128)(2,1)S(1)}, bf16[2,32,1280]{2,1,0:T(8,128)(2,1)S(1)}, u32[]{:S(2)}, u32[]{:S(2)}) %collective-permute-start.3) | collective-permute-done | bytes 163872 | tf_op jit(solution)/shard_map/ppermute | solution.py:46
  66.5 1.3 %collective-permute-start.4 = (bf16[32,1280]{1,0:T(8,128)(2,1)S(1)}, bf16[32,1280]{1,0:T(8,128)(2,1)S(1)}, u32[]{:S(2)}, u32[]{:S(2)}) collective-permute-start(bf16[32,1280]{1,0:T(8,128)(2,1)S(1)} %fusion.5.refs_0_), channel_id=1, source_target_pairs={{0,2},{1,3},{2,0},{3,1},{4,6},{5,7},{6,4},{7,5},{8,10},{9,11},{10,... | collective-permute-start | bytes 245768 | tf_op jit(solution)/shard_map/ppermute | solution.py:46
  67.8 0.9 collective-permute-done.12.refs_1_
  69.2 2.6 %collective-permute-done.4.refs_1_ = bf16[32,1280]{1,0:T(8,128)(2,1)S(1)} collective-permute-done((bf16[32,1280]{1,0:T(8,128)(2,1)S(1)}, bf16[32,1280]{1,0:T(8,128)(2,1)S(1)}, u32[]{:S(2)}, u32[]{:S(2)}) %collective-permute-start.4) | collective-permute-done | bytes 81952 | tf_op jit(solution)/shard_map/ppermute | solution.py:46
  71.9 4.0 %shard_map.119.refs_5_ = f32[128,2304]{1,0:T(8,128)S(1)} custom-call(s32[1]{0:T(128)} %bitcast.gy_ref.after_ref, bf16[32,1280]{1,0:T(8,128)(2,1)S(1)} %fusion.3.refs_0_, bf16[32,1280]{1,0:T(8,128)(2,1)S(1)} %collective-permute-done.12.refs_1_, bf16[32,1280]{1,0:T(8,128)(2,1)S(1)} %collective-permute-done.13.refs_2_, ...), custom_call_target="tpu_custom_call" | custom-call | flops 377487360 | bytes 2949120 | tf_op jit(solution)/shard_map/pallas_call | solution.py:222
  75.9 5.0 %shard_map.120.refs_5_ = f32[128,2304]{1,0:T(8,128)S(1)} custom-call(s32[1]{0:T(128)} %bitcast.gy_ref.after_ref, bf16[32,2048]{1,0:T(8,128)(2,1)S(1)} %fusion.1.refs_0_, bf16[32,2048]{1,0:T(8,128)(2,1)S(1)} %collective-permute-done.8.refs_1_, bf16[32,2048]{1,0:T(8,128)(2,1)S(1)} %collective-permute-done.9.refs_2_, ...), custom_call_target="tpu_custom_call" | custom-call | flops 603979776 | bytes 4718592 | tf_op jit(solution)/shard_map/pallas_call | solution.py:222
  80.9 4.9 %shard_map.121 = bf16[32,4,2304]{2,1,0:T(4,128)(2,1)} custom-call(s32[1]{0:T(128)} %bitcast.gy_ref.after_ref, bf16[32,1280]{1,0:T(8,128)(2,1)S(1)} %fusion.5.refs_0_, bf16[32,1280]{1,0:T(8,128)(2,1)S(1)} %collective-permute-done.4.refs_1_, bf16[32,1280]{1,0:T(8,128)(2,1)S(1)} %collective-permute-done.5.refs_2_, ...), custom_call_target="tpu_custom_call" | custom-call | flops 377487360 | bytes 2949120 | tf_op jit(solution)/shard_map/pallas_call | solution.py:222
  85.8 3.8 %all-to-all-start.1 = ((bf16[32,4,2304]{2,1,0:T(4,128)(2,1)}), bf16[32,4,2304]{2,1,0:T(4,128)(2,1)S(1)}, u32[]{:S(2)}, u32[]{:S(2)}) async-start(bf16[32,4,2304]{2,1,0:T(4,128)(2,1)} %shard_map.121), calls=%async_computation.1 | async-start | bytes 1179648 | tf_op jit(solution)/shard_map/all_to_all | solution.py:362
  90.3 0.7 copy.17
  91.0 15.4 %all-to-all-done.1 = bf16[32,4,2304]{2,1,0:T(4,128)(2,1)S(1)} async-done(((bf16[32,4,2304]{2,1,0:T(4,128)(2,1)}), bf16[32,4,2304]{2,1,0:T(4,128)(2,1)S(1)}, u32[]{:S(2)}, u32[]{:S(2)}) %all-to-all-start.1) | async-done | bytes 589856 | tf_op jit(solution)/shard_map/all_to_all | solution.py:362
  106.4 0.7 shard_map.122
  (44 shorter events, 3.8 us)
Async XLA Ops:
  2.7 24.0 %all-to-all-start = ((bf16[32,4,2304]{2,1,0:T(4,128)(2,1)}), bf16[32,4,2304]{2,1,0:T(4,128)(2,1)S(1)}, u32[]{:S(2)}, u32[]{:S(2)}) async-start(bf16[32,4,2304]{2,1,0:T(4,128)(2,1)} %bitcast.2), calls=%async_computation | async-start | bytes 1179648 | tf_op jit(solution)/shard_map/all_to_all | solution.py:362
  11.0 0.7 copy-start.2
  32.0 1.7 %collective-permute-start = (bf16[2,64,1280]{2,1,0:T(8,128)(2,1)S(1)}, bf16[2,64,1280]{2,1,0:T(8,128)(2,1)S(1)}, u32[]{:S(2)}, u32[]{:S(2)}) collective-permute-start(bf16[2,64,1280]{2,1,0:T(8,128)(2,1)S(1)} %get-tuple-element.13), channel_id=1, source_target_pairs={{0,1},{1,0},{2,3},{3,2},{4,5},{5,4},{6,7},{7,6},{8,9},{9,8},{10,11... | collective-permute-start | bytes 983048 | tf_op jit(solution)/shard_map/ppermute | solution.py:46
  33.7 0.7 copy-start.3
  41.8 2.1 %collective-permute-start.1 = (bf16[2,64,2048]{2,1,0:T(8,128)(2,1)S(1)}, bf16[2,64,2048]{2,1,0:T(8,128)(2,1)}, u32[]{:S(2)}, u32[]{:S(2)}) collective-permute-start(bf16[2,64,2048]{2,1,0:T(8,128)(2,1)S(1)} %get-tuple-element.15), channel_id=1, source_target_pairs={{0,1},{1,0},{2,3},{3,2},{4,5},{5,4},{6,7},{7,6},{8,9},{9,8},{10,11... | collective-permute-start | bytes 1572872 | tf_op jit(solution)/shard_map/ppermute | solution.py:46
  42.1 7.1 %collective-permute-start.11 = (bf16[2,32,1280]{2,1,0:T(8,128)(2,1)S(1)}, bf16[2,32,1280]{2,1,0:T(8,128)(2,1)S(1)}, u32[]{:S(2)}, u32[]{:S(2)}) collective-permute-start(bf16[2,32,1280]{2,1,0:T(8,128)(2,1)S(1)} %add_convert_fusion.2.after_ref), channel_id=1, source_target_pairs={{0,2},{1,3},{2,0},{3,1},{4,6},{5,7},{6,4},{7,5},{8,10},{9,11},{10,... | collective-permute-start | bytes 491528 | tf_op jit(solution)/shard_map/ppermute | solution.py:46
  44.9 10.5 %collective-permute-start.7 = (bf16[2,32,2048]{2,1,0:T(8,128)(2,1)S(1)}, bf16[2,32,2048]{2,1,0:T(8,128)(2,1)S(1)}, u32[]{:S(2)}, u32[]{:S(2)}) collective-permute-start(bf16[2,32,2048]{2,1,0:T(8,128)(2,1)S(1)} %add_convert_fusion.after_ref), channel_id=1, source_target_pairs={{0,2},{1,3},{2,0},{3,1},{4,6},{5,7},{6,4},{7,5},{8,10},{9,11},{10,... | collective-permute-start | bytes 786440 | tf_op jit(solution)/shard_map/ppermute | solution.py:46
  50.1 10.0 %copy-start = (bf16[1,288,512]{2,1,0:T(8,128)(2,1)S(1)}, bf16[1,288,512]{2,1,0:T(8,128)(2,1)}, u32[]{:S(2)}) copy-start(bf16[1,288,512]{2,1,0:T(8,128)(2,1)} %weight_ref.1) | copy-start | bytes 884740
  55.3 2.5 %collective-permute-start.2 = (bf16[2,64,1280]{2,1,0:T(8,128)(2,1)S(1)}, bf16[2,64,1280]{2,1,0:T(8,128)(2,1)S(1)}, u32[]{:S(2)}, u32[]{:S(2)}) collective-permute-start(bf16[2,64,1280]{2,1,0:T(8,128)(2,1)S(1)} %get-tuple-element.17.after_ref), channel_id=1, source_target_pairs={{0,1},{1,0},{2,3},{3,2},{4,5},{5,4},{6,7},{7,6},{8,9},{9,8},{10,11... | collective-permute-start | bytes 983048 | tf_op jit(solution)/shard_map/ppermute | solution.py:46
  56.5 7.5 %collective-permute-start.8 = (bf16[32,2048]{1,0:T(8,128)(2,1)S(1)}, bf16[32,2048]{1,0:T(8,128)(2,1)S(1)}, u32[]{:S(2)}, u32[]{:S(2)}) collective-permute-start(bf16[32,2048]{1,0:T(8,128)(2,1)S(1)} %fusion.1.refs_0_), channel_id=1, source_target_pairs={{0,2},{1,3},{2,0},{3,1},{4,6},{5,7},{6,4},{7,5},{8,10},{9,11},{10,... | collective-permute-start | bytes 393224 | tf_op jit(solution)/shard_map/ppermute | solution.py:46
  57.9 8.5 %collective-permute-start.3 = (bf16[2,32,1280]{2,1,0:T(8,128)(2,1)S(1)}, bf16[2,32,1280]{2,1,0:T(8,128)(2,1)S(1)}, u32[]{:S(2)}, u32[]{:S(2)}) collective-permute-start(bf16[2,32,1280]{2,1,0:T(8,128)(2,1)S(1)} %add_convert_fusion.1), channel_id=1, source_target_pairs={{0,2},{1,3},{2,0},{3,1},{4,6},{5,7},{6,4},{7,5},{8,10},{9,11},{10,... | collective-permute-start | bytes 491528 | tf_op jit(solution)/shard_map/ppermute | solution.py:46
  58.8 10.0 %collective-permute-start.13 = (bf16[32,1280]{1,0:T(8,128)(2,1)S(1)}, bf16[32,1280]{1,0:T(8,128)(2,1)S(1)}, u32[]{:S(2)}, u32[]{:S(2)}) collective-permute-start(bf16[32,1280]{1,0:T(8,128)(2,1)S(1)} %fusion.3.refs_0_), channel_id=1, source_target_pairs={{0,1},{1,0},{2,3},{3,2},{4,5},{5,4},{6,7},{7,6},{8,9},{9,8},{10,11... | collective-permute-start | bytes 245768 | tf_op jit(solution)/shard_map/ppermute | solution.py:46
  58.8 9.9 %collective-permute-start.12 = (bf16[32,1280]{1,0:T(8,128)(2,1)S(1)}, bf16[32,1280]{1,0:T(8,128)(2,1)S(1)}, u32[]{:S(2)}, u32[]{:S(2)}) collective-permute-start(bf16[32,1280]{1,0:T(8,128)(2,1)S(1)} %fusion.3.refs_0_), channel_id=1, source_target_pairs={{0,2},{1,3},{2,0},{3,1},{4,6},{5,7},{6,4},{7,5},{8,10},{9,11},{10,... | collective-permute-start | bytes 245768 | tf_op jit(solution)/shard_map/ppermute | solution.py:46
  61.1 24.7 %all-to-all-start.2 = ((f32[32,4,512]{2,1,0:T(4,128)}), f32[32,4,512]{2,1,0:T(4,128)S(1)}, u32[]{:S(2)}, u32[]{:S(2)}) async-start(f32[32,4,512]{2,1,0:T(4,128)} %shard_map.123), calls=%async_computation.2 | async-start | bytes 524288 | tf_op jit(solution)/shard_map/all_to_all | solution.py:362
  63.9 12.0 %collective-permute-start.9 = (bf16[32,2048]{1,0:T(8,128)(2,1)S(1)}, bf16[32,2048]{1,0:T(8,128)(2,1)S(1)}, u32[]{:S(2)}, u32[]{:S(2)}) collective-permute-start(bf16[32,2048]{1,0:T(8,128)(2,1)S(1)} %fusion.1.refs_0_), channel_id=1, source_target_pairs={{0,1},{1,0},{2,3},{3,2},{4,5},{5,4},{6,7},{7,6},{8,9},{9,8},{10,11... | collective-permute-start | bytes 393224 | tf_op jit(solution)/shard_map/ppermute | solution.py:46
  64.0 11.8 %collective-permute-start.10 = (bf16[32,2048]{1,0:T(8,128)(2,1)S(1)}, bf16[32,2048]{1,0:T(8,128)(2,1)S(1)}, u32[]{:S(2)}, u32[]{:S(2)}) collective-permute-start(bf16[32,2048]{1,0:T(8,128)(2,1)S(1)} %collective-permute-done.8.refs_1_), channel_id=1, source_target_pairs={{0,1},{1,0},{2,3},{3,2},{4,5},{5,4},{6,7},{7,6},{8,9},{9,8},{10,11... | collective-permute-start | bytes 393224 | tf_op jit(solution)/shard_map/ppermute | solution.py:46
  66.5 5.4 %collective-permute-start.4 = (bf16[32,1280]{1,0:T(8,128)(2,1)S(1)}, bf16[32,1280]{1,0:T(8,128)(2,1)S(1)}, u32[]{:S(2)}, u32[]{:S(2)}) collective-permute-start(bf16[32,1280]{1,0:T(8,128)(2,1)S(1)} %fusion.5.refs_0_), channel_id=1, source_target_pairs={{0,2},{1,3},{2,0},{3,1},{4,6},{5,7},{6,4},{7,5},{8,10},{9,11},{10,... | collective-permute-start | bytes 245768 | tf_op jit(solution)/shard_map/ppermute | solution.py:46
  68.7 3.1 %collective-permute-start.14 = (bf16[32,1280]{1,0:T(8,128)(2,1)S(1)}, bf16[32,1280]{1,0:T(8,128)(2,1)S(1)}, u32[]{:S(2)}, u32[]{:S(2)}) collective-permute-start(bf16[32,1280]{1,0:T(8,128)(2,1)S(1)} %collective-permute-done.12.refs_1_), channel_id=1, source_target_pairs={{0,1},{1,0},{2,3},{3,2},{4,5},{5,4},{6,7},{7,6},{8,9},{9,8},{10,11... | collective-permute-start | bytes 245768 | tf_op jit(solution)/shard_map/ppermute | solution.py:46
  68.7 12.2 %collective-permute-start.5 = (bf16[32,1280]{1,0:T(8,128)(2,1)S(1)}, bf16[32,1280]{1,0:T(8,128)(2,1)S(1)}, u32[]{:S(2)}, u32[]{:S(2)}) collective-permute-start(bf16[32,1280]{1,0:T(8,128)(2,1)S(1)} %fusion.5.refs_0_), channel_id=1, source_target_pairs={{0,1},{1,0},{2,3},{3,2},{4,5},{5,4},{6,7},{7,6},{8,9},{9,8},{10,11... | collective-permute-start | bytes 245768 | tf_op jit(solution)/shard_map/ppermute | solution.py:46
  71.9 9.1 %collective-permute-start.6 = (bf16[32,1280]{1,0:T(8,128)(2,1)S(1)}, bf16[32,1280]{1,0:T(8,128)(2,1)S(1)}, u32[]{:S(2)}, u32[]{:S(2)}) collective-permute-start(bf16[32,1280]{1,0:T(8,128)(2,1)S(1)} %collective-permute-done.4.refs_1_), channel_id=1, source_target_pairs={{0,1},{1,0},{2,3},{3,2},{4,5},{5,4},{6,7},{7,6},{8,9},{9,8},{10,11... | collective-permute-start | bytes 245768 | tf_op jit(solution)/shard_map/ppermute | solution.py:46
  80.9 8.8 %copy-start.4 = (bf16[4,12288]{1,0:T(4,128)(2,1)S(1)}, bf16[4,12288]{1,0:T(4,128)(2,1)}, u32[]{:S(2)}) copy-start(bf16[4,12288]{1,0:T(4,128)(2,1)} %param.16) | copy-start | bytes 294916
  80.9 25.5 %copy-start.1 = (bf16[4,9216]{1,0:T(4,128)(2,1)S(1)}, bf16[4,9216]{1,0:T(4,128)(2,1)}, u32[]{:S(2)}) copy-start(bf16[4,9216]{1,0:T(4,128)(2,1)} %tokens_ref.1) | copy-start | bytes 221188
  85.8 20.5 %all-to-all-start.1 = ((bf16[32,4,2304]{2,1,0:T(4,128)(2,1)}), bf16[32,4,2304]{2,1,0:T(4,128)(2,1)S(1)}, u32[]{:S(2)}, u32[]{:S(2)}) async-start(bf16[32,4,2304]{2,1,0:T(4,128)(2,1)} %shard_map.121), calls=%async_computation.1 | async-start | bytes 1179648 | tf_op jit(solution)/shard_map/all_to_all | solution.py:362

commit v5 on v4

--- a/solution.py
+++ b/solution.py
@@ -34,6 +34,10 @@
     return pltpu.with_memory_space_constraint(x, pltpu.HBM)
 
 
+def hbm_out(shape, dtype):
+    return pltpu.HBM(shape, dtype)
+
+
 def vmem_out(shape, dtype):
     return pltpu.VMEM(shape, dtype)
 
@@ -46,8 +50,10 @@
     return lax.ppermute(x, axis, [(i, i ^ bits) for i in range(size)])
 
 
-def norm_kernel(tokens_hbm, gain_hbm, out_ref, tokens_ref, gain_ref, sems):
-    copies, blocks, _, width = out_ref.shape
+def norm_kernel(tokens_hbm, gain_hbm, *refs):
+    *out_refs, tokens_ref, gain_ref, sems = refs
+    copies, blocks = out_refs[0].shape[:2]
+    width = sum(ref.shape[3] for ref in out_refs)
     moves = [
         pltpu.make_async_copy(source, target, sems.at[k])
         for k, (source, target) in enumerate(((tokens_hbm, tokens_ref), (gain_hbm, gain_ref)))
@@ -61,18 +67,21 @@
     spread = jnp.mean(centred * centred, axis=-1, keepdims=True)
     normed = (centred * lax.rsqrt(spread + 1e-05) * gain_ref[...]).astype(BF16)
     for b in range(blocks):
-        part = normed[:, b * width : (b + 1) * width]
-        for c in range(copies):
-            out_ref[c, b] = part
-
-
-def norm(tokens, gain, n_gx, n_gy):
+        start = b * width
+        for out_ref in out_refs:
+            part = normed[:, start : start + out_ref.shape[3]]
+            start += out_ref.shape[3]
+            for c in range(copies):
+                out_ref[c, b] = part
+
+
+def norm(tokens, gain, n_gx, n_gy, widths):
     batch, channels = tokens.shape
     return pl.pallas_call(
         norm_kernel,
         in_specs=[ANYWHERE, ANYWHERE],
-        out_specs=WHOLE,
-        out_shape=vmem_out((n_gx, n_gy, batch, channels // n_gy), BF16),
+        out_specs=[WHOLE] * len(widths),
+        out_shape=[vmem_out((n_gx, n_gy, batch, width), BF16) for width in widths],
         scratch_shapes=[
             pltpu.VMEM((batch, channels), BF16),
             pltpu.VMEM((1, channels), F32),
@@ -83,8 +92,12 @@
     )(in_hbm(tokens), in_hbm(gain.reshape(1, -1)))
 
 
-def assemble_kernel(gy_ref, rows_ref, after_ref, out_ref):
-    del after_ref
+def assemble_kernel(gy_ref, rows_ref, *refs):
+    out_ref = refs[-1]
+    first = 0
+    if len(refs) > 1:
+        first = refs[0].shape[1]
+        out_ref[:, :first] = refs[0][...]
     devices, batch, _ = rows_ref.shape
     quarter = devices // 4
     pack = 16 // batch
@@ -95,19 +108,20 @@
                 [rows_ref[base + i + k].astype(F32) for k in range(pack)], axis=0
             )
             start = (at * quarter + i) * batch
-            out_ref[start : start + 16] = tall.astype(BF16)
-
-
-def assemble(gy, rows, after):
+            out_ref[start : start + 16, first:] = tall.astype(BF16)
+
+
+def assemble(gy, rows, before=(), after=()):
     devices, batch, width = rows.shape
+    width += sum(x.shape[1] for x in before)
     return pl.pallas_call(
         assemble_kernel,
-        in_specs=[SCALARS, WHOLE, ANYWHERE],
+        in_specs=[SCALARS, WHOLE] + [WHOLE] * len(before) + [ANYWHERE] * len(after),
         out_specs=WHOLE,
         out_shape=vmem_out((devices * batch, width), BF16),
         compiler_params=params(4),
         cost_estimate=cost(2 * rows.size, 4 * rows.size),
-    )(gy, in_vmem(rows), after)
+    )(gy, in_vmem(rows), *[in_vmem(x) for x in before], *after)
 
 
 def spread_rows(out_ref, value, gy, columns=slice(None)):
@@ -120,84 +134,168 @@
             out_ref[base + i, :, columns] = value[start : start + batch].astype(out_ref.dtype)
 
 
-def gate_up_tile(x, weights, at, tile, keep_ref, send_ref):
-    half = keep_ref.shape[1]
-    for k, weight in enumerate(weights):
-        value = jnp.dot(x, weight, preferred_element_type=F32)
-        keep_ref[k, :, at : at + tile] = value[:half]
-        send_ref[k, :, at : at + tile] = value[half:].astype(BF16)
-
-
-def gate_up_kernel(start, tile, x_ref, gate_ref, up_ref, after_ref, keep_ref, send_ref, slots, sems):
-    del after_ref
-    width = keep_ref.shape[2]
+def in_turn(groups, ahead):
+    for group in groups[:ahead]:
+        for copy in group:
+            copy.start()
+    for n, group in enumerate(groups):
+        for copy in group:
+            copy.wait()
+        if n + ahead < len(groups):
+            for copy in groups[n + ahead]:
+                copy.start()
+        yield n
+
+
+def gate_up_first_kernel(tile, x_ref, gate_ref, up_ref, out_ref, slots, sums, sems, out_sems):
     depth = x_ref.shape[1]
-    copies = []
-    for at in range(0, width, tile):
-        for k, source in enumerate((gate_ref, up_ref)):
-            copies.append(
+    groups = []
+    outs = []
+    for n in range(slots.shape[1]):
+        columns = pl.ds(n * tile, tile)
+        groups.append(
+            [
                 pltpu.make_async_copy(
-                    source.at[:, pl.ds(start + at, tile)],
-                    slots.at[k, at // tile],
-                    sems.at[k, at // tile],
+                    source.at[pl.ds(0, depth), columns], slots.at[k, n], sems.at[k, n]
                 )
-            )
-    for copy in copies:
-        copy.start()
+                for k, source in enumerate((gate_ref, up_ref))
+            ]
+        )
+        outs.append(
+            pltpu.make_async_copy(sums.at[n], out_ref.at[:, :, columns], out_sems.at[n])
+        )
     x = x_ref[...]
-    for n in range(width // tile):
+    for n in in_turn(groups, 3):
         for k in range(2):
-            copies[2 * n + k].wait()
-        gate_up_tile(x, [slots[k, n] for k in range(2)], n * tile, tile, keep_ref, send_ref)
-
-
-def gate_up_shapes(rows, width):
-    half = rows // 2
-    return [
-        vmem_out((2, half, width), F32),
-        vmem_out((2, half, width), BF16),
-    ]
-
-
-def gate_up(x, w_gate, w_up, start, width, after):
+            sums[n, k] = jnp.dot(x, slots[k, n], preferred_element_type=F32)
+        outs[n].start()
+    for out in outs:
+        out.wait()
+
+
+def gate_up_first(x, w_gate, w_up):
     rows, depth = x.shape
+    width = w_gate.shape[1]
     tile = tile_of(width, 256)
     count = width // tile
     return pl.pallas_call(
-        functools.partial(gate_up_kernel, start, tile),
-        in_specs=[WHOLE, ANYWHERE, ANYWHERE, ANYWHERE],
-        out_specs=[WHOLE, WHOLE],
-        out_shape=gate_up_shapes(rows, width),
+        functools.partial(gate_up_first_kernel, tile),
+        in_specs=[WHOLE, ANYWHERE, ANYWHERE],
+        out_specs=ANYWHERE,
+        out_shape=hbm_out((2, rows, width), F32),
         scratch_shapes=[
             pltpu.VMEM((2, count, depth, tile), BF16),
+            pltpu.VMEM((count, 2, rows, tile), F32),
             pltpu.SemaphoreType.DMA((2, count)),
+            pltpu.SemaphoreType.DMA((count,)),
         ],
-        compiler_params=params(22),
+        compiler_params=params(28),
+        cost_estimate=cost(4 * rows * depth * width, 4 * depth * width),
+    )(in_vmem(x), in_hbm(w_gate), in_hbm(w_up))
+
+
+def gate_up_kernel(start, tile, first, count_after, x_ref, gate_ref, up_ref, sums_ref, *refs):
+    keep_ref, send_ref, slots, sum_slots, sems = refs[count_after:]
+    _, half, width = keep_ref.shape
+    depth = slots.shape[2]
+    groups = []
+    for n in range(width // tile):
+        columns = pl.ds(start + n * tile, tile)
+        groups.append(
+            [
+                pltpu.make_async_copy(
+                    source.at[pl.ds(first, depth), columns], slots.at[k, n], sems.at[k, n]
+                )
+                for k, source in enumerate((gate_ref, up_ref))
+            ]
+            + [pltpu.make_async_copy(sums_ref.at[:, :, columns], sum_slots.at[n], sems.at[2, n])]
+        )
+    x = x_ref[:, first:]
+    for n in in_turn(groups, 3):
+        columns = slice(n * tile, (n + 1) * tile)
+        for k in range(2):
+            value = jnp.dot(x, slots[k, n], preferred_element_type=F32) + sum_slots[n, k]
+            keep_ref[k, :, columns] = value[:half]
+            send_ref[k, :, columns] = value[half:].astype(BF16)
+
+
+def gate_up(x, w_gate, w_up, sums, first, start, width, after):
+    rows = x.shape[0]
+    depth = x.shape[1] - first
+    half = rows // 2
+    tile = tile_of(width, 256)
+    count = width // tile
+    return pl.pallas_call(
+        functools.partial(gate_up_kernel, start, tile, first, len(after)),
+        in_specs=[WHOLE] + [ANYWHERE] * (3 + len(after)),
+        out_specs=[WHOLE, WHOLE],
+        out_shape=[vmem_out((2, half, width), F32), vmem_out((2, half, width), BF16)],
+        scratch_shapes=[
+            pltpu.VMEM((2, count, depth, tile), BF16),
+            pltpu.VMEM((count, 2, rows, tile), F32),
+            pltpu.SemaphoreType.DMA((3, count)),
+        ],
+        compiler_params=params(20),
         cost_estimate=cost(rows * depth * width, depth * width),
-    )(in_vmem(x), in_hbm(w_gate), in_hbm(w_up), after)
+    )(in_vmem(x), in_hbm(w_gate), in_hbm(w_up), in_hbm(sums), *after)
+
+
+def combine_kernel(keep_ref, core_ref, own_ref, across_ref):
+    half = own_ref.shape[1]
+    own_ref[...] = keep_ref[:, :half] + core_ref[:, :half].astype(F32)
+    across_ref[...] = (keep_ref[:, half:] + core_ref[:, half:].astype(F32)).astype(BF16)
+
+
+def combine(keep, core):
+    _, half, width = keep.shape
+    shape = (2, half // 2, width)
+    return pl.pallas_call(
+        combine_kernel,
+        in_specs=[WHOLE, WHOLE],
+        out_specs=[WHOLE, WHOLE],
+        out_shape=[vmem_out(shape, F32), vmem_out(shape, BF16)],
+        compiler_params=params(4),
+        cost_estimate=cost(keep.size, keep.size),
+    )(in_vmem(keep), in_vmem(core))
+
+
+def activate_kernel(own_ref, far_ref, *refs):
+    gate = own_ref[0] + far_ref[0].astype(F32)
+    up = own_ref[1] + far_ref[1].astype(F32)
+    refs[-1][...] = (jax.nn.silu(gate) * up).astype(BF16)
+
+
+def activate(own, far, after):
+    return pl.pallas_call(
+        activate_kernel,
+        in_specs=[WHOLE, WHOLE] + [ANYWHERE] * len(after),
+        out_specs=WHOLE,
+        out_shape=vmem_out(own.shape[1:], BF16),
+        compiler_params=params(4),
+        cost_estimate=cost(own.size, own.size),
+    )(in_vmem(own), in_vmem(far), *after)
 
 
 def down_kernel(start, tile, has_sum, last, gy_ref, *refs):
     hidden, (weight_ref, *refs) = refs[:4], refs[4:]
     sum_ref = refs.pop(0) if has_sum else None
-    out_ref, slots, sems = refs
+    out_ref, slots, sems = refs[-3:]
     depth = hidden[0].shape[1]
     width = weight_ref.shape[1]
-    copies = [
-        pltpu.make_async_copy(
-            weight_ref.at[pl.ds(start, depth), pl.ds(at, tile)],
-            slots.at[at // tile],
-            sems.at[at // tile],
-        )
-        for at in range(0, width, tile)
+    groups = [
+        [
+            pltpu.make_async_copy(
+                weight_ref.at[pl.ds(start, depth), pl.ds(n * tile, tile)],
+                slots.at[n],
+                sems.at[n],
+            )
+        ]
+        for n in range(width // tile)
     ]
-    for copy in copies:
-        copy.start()
     x = jnp.concatenate([h[...] for h in hidden], axis=0)
     gy = gy_ref[0]
-    for n, copy in enumerate(copies):
+    for n in in_turn(groups, 5):
         columns = slice(n * tile, (n + 1) * tile)
-        copy.wait()
         value = jnp.dot(x, slots[n], preferred_element_type=F32)
         if has_sum:
             value = value + sum_ref[:, columns]
@@ -207,7 +305,7 @@
             out_ref[:, columns] = value
 
 
-def down(gy, hidden, w_down, start, total, devices, last):
+def down(gy, hidden, w_down, start, total, devices, last, after):
     part_rows, depth = hidden[0].shape
     rows = 4 * part_rows
     width = w_down.shape[1]
@@ -218,6 +316,8 @@
     if total is not None:
         args.append(in_vmem(total))
         in_specs.append(WHOLE)
+    args.extend(after)
+    in_specs.extend([ANYWHERE] * len(after))
     shape = (devices, rows // devices, width) if last else (rows, width)
     return pl.pallas_call(
         functools.partial(down_kernel, start, tile, total is not None, last),
@@ -364,42 +464,54 @@
     batch = tokens.shape[0]
     widths = chunk_widths(w_gate.shape[1])
 
-    normed = norm(tokens, gain, n_gx, n_gy)
-    gathered = exchange(normed.reshape(devices, batch, -1))
-    grouped = queries.reshape(batch, -1, HD)
-    cached = attend_cache(grouped, key_cache, value_cache, lengths, normed)
-    x = assemble(gy, gathered, cached[0])
-    rows = x.shape[0]
-    quarter = rows // 4
-
-    sums = []
+    depth = w_gate.shape[0]
+    unit = 256 if depth % 256 == 0 else 128
+    first = depth // unit // 2 * unit
+
+    normed = norm(tokens, gain, n_gx, n_gy, (first, depth - first))
+    parts = [exchange(part.reshape(devices, batch, -1)) for part in normed]
+    x_first = assemble(gy, parts[0])
+    sums = gate_up_first(x_first, w_gate, w_up)
+    x = assemble(gy, parts[1], [x_first], [sums])
+
+    owns, far, hidden = [], [], []
     start = 0
+    after = []
     for c, width in enumerate(widths):
-        keep, send = gate_up(x, w_gate, w_up, start, width, sums[-1][2] if c else gy)
-        core = swap_gy(send, 1)
-        across = (keep[:, quarter:] + core[:, quarter:].astype(F32)).astype(BF16)
-        sums.append((keep, core, across))
+        keep, send = gate_up(x, w_gate, w_up, sums, first, start, width, after)
+        own, across = combine(keep, swap_gy(send, 1))
+        owns.append(own)
+        far.append(swap_gy(across, 2))
+        after = [across]
+        if c == 1:
+            hidden.append(activate(owns[0], far[0], []))
+            after.append(hidden[0])
         start += width
+    hidden.append(activate(owns[1], far[1], [across]))
 
     slab = w_kv.shape[1]
-    part = fresh_part(gy, lax.dynamic_slice_in_dim(x, gx * slab, slab, 1), w_kv, devices, send)
+    part = fresh_part(gy, lax.dynamic_slice_in_dim(x, gx * slab, slab, 1), w_kv, devices, across)
     fresh = jnp.sum(exchange(part), axis=0)
     key_new = fresh[:, :HD].astype(BF16)
     value_new = fresh[:, HD:].astype(BF16)
 
+    total = None
     start = 0
-    total = None
-    for c, (keep, core, across) in enumerate(sums):
-        pair = keep[:, :quarter] + core[:, :quarter].astype(F32) + swap_gy(across, 2).astype(F32)
-        own = (jax.nn.silu(pair[0]) * pair[1]).astype(BF16)
-        far = swap_gy(own, 2)
-        hidden = (own, far, swap_gy(own, 1), swap_gy(far, 1))
-        total = down(gy, hidden, w_down, start, total, devices, c == len(sums) - 1)
-        start += widths[c]
+    for c, width in enumerate(widths):
+        if c == 1:
+            hidden.append(activate(owns[2], far[2], [total]))
+        own = hidden[c]
+        other = swap_gy(own, 2)
+        pieces = (own, other, swap_gy(own, 1), swap_gy(other, 1))
+        last = c == len(widths) - 1
+        total = down(gy, pieces, w_down, start, total, devices, last, [] if last else [hidden[c + 1]])
+        start += width
 
     ffn = exchange(total)
+    grouped = queries.reshape(batch, -1, HD)
+    cached = attend_cache(grouped, key_cache, value_cache, lengths, total)
+    context = attend_new(grouped, cached, key_new, value_new)
     mixed = finish(tokens, ffn.reshape(n_gx, n_gy, batch, -1))
-    context = attend_new(grouped, cached, key_new, value_new)
     return (mixed, context)
 
 

time: 108 us -> 119 us (1.10)
  blocking collectives: 0 us -> 17.7 us
  Pallas kernels: 41.6 us -> 48.6 us
  waiting for transfers between devices: 34.8 us -> 28.9 us
  starting transfers between devices: 22.8 us -> 18.5 us
  other arithmetic: 3.69 us -> 0.4 us
    all_to_all x0 -> x1, blocking collectives: none -> 17.7 us  [body(): lax.all_to_all(x, ('gx', 'gy'), split_axis=0, concat_axis=0, tiled=True)]
    all_to_all x3, waiting for transfers between devices: 24.2 us -> 10.5 us  [body(): lax.all_to_all(x, ('gx', 'gy'), split_axis=0, concat_axis=0, tiled=True)]
    ppermute x15, waiting for transfers between devices: 10.6 us -> 18.4 us  [swap(): return lax.ppermute(x, axis, [(i, i ^ bits) for i in range(size)])]
    pallas_call x5 -> x13, Pallas kernels: 19.8 us -> 26.7 us  [the longest x3 13.7 us: gate_up(): pl.pallas_call(functools.partial(gate_up_kernel, start, tile, first, len(...]
    all_to_all x3, starting transfers between devices: 13.9 us -> 11.6 us  [body(): lax.all_to_all(x, ('gx', 'gy'), split_axis=0, concat_axis=0, tiled=True)]
    add x3 -> x0, other arithmetic: 2.04 us -> none  [body(): keep[:, :quarter] + core[:, :quarter].astype(F32)]
    ppermute x15, starting transfers between devices: 8.9 us -> 6.89 us  [swap(): return lax.ppermute(x, axis, [(i, i ^ bits) for i in range(size)])]
    convert_element_type x6 -> x0, other arithmetic: 1.25 us -> none  [the longest x3 1.06 us: body(): across = (keep[:, quarter:] + core[:, quarter:].astype(F32)).astype(BF16)]
  transfers between devices with their start and end apart: 18 -> 18, of which waited for: 8 -> 8; matrix products, arithmetic and copies ran while one was open for 5% -> 1% of each run, Pallas kernels for 25% -> 27%
where the time goes in v5:
time: 119 us
  Pallas kernels  48.6 us (41%)
  waiting for transfers between devices  28.9 us (24%)
  starting transfers between devices  18.5 us (16%)
  blocking collectives  17.7 us (15%)
  local copies, waits for them, and re-layouts  3.28 us (3%)
    ppermute x15, waiting for transfers between devices, swap(): return lax.ppermute(x, axis, [(i, i ^ bits) for i in range(size)])  18.4 us
    all_to_all x1, blocking collectives, body(): lax.all_to_all(x, ('gx', 'gy'), split_axis=0, concat_axis=0, tiled=True)  17.7 us
    pallas_call x3, Pallas kernels, down(): pl.pallas_call(functools.partial(down_kernel, start, tile, total is not N...  13.9 us
    pallas_call x3, Pallas kernels, gate_up(): pl.pallas_call(functools.partial(gate_up_kernel, start, tile, first, len(...  13.7 us
    all_to_all x3, starting transfers between devices, body(): lax.all_to_all(x, ('gx', 'gy'), split_axis=0, concat_axis=0, tiled=True)  11.6 us
    all_to_all x3, waiting for transfers between devices, body(): lax.all_to_all(x, ('gx', 'gy'), split_axis=0, concat_axis=0, tiled=True)  10.5 us
    pallas_call x1, Pallas kernels, gate_up_first(): pl.pallas_call(functools.partial(gate_up_first_kernel, tile), in_specs=[W...  10.4 us
    ppermute x15, starting transfers between devices, swap(): return lax.ppermute(x, axis, [(i, i ^ bits) for i in range(size)])  6.89 us
  transfers between devices with their start and end apart: 18, of which 8 were waited for; matrix products, arithmetic and copies ran while one was open for 1% of the time, Pallas kernels for 27%

profile of v5, /device:TPU:0, one launch (start us, length us, event | category | flops | bytes accessed | tf_op | source)
XLA Modules:
  0.0 118.5 jit_solution(2657684293749073926)
XLA Ops:
  0.6 2.0 %shard_map.113 = (bf16[8,4,4,1024]{3,2,1,0:T(4,128)(2,1)S(1)}, bf16[8,4,4,1280]{3,2,1,0:T(4,128)(2,1)}) custom-call(bf16[4,9216]{1,0:T(4,128)(2,1)} %tokens_ref.1, f32[1,9216]{1,0:T(1,128)} %bitcast.25), custom_call_target="tpu_custom_call" | custom-call | flops 368640 | bytes 589824 | tf_op jit(solution)/shard_map/pallas_call | solution.py:80
  2.6 17.7 %all_to_all.20.rows_ref = bf16[32,4,1024]{2,1,0:T(4,128)(2,1)S(1)} all-to-all(bf16[32,4,1024]{2,1,0:T(4,128)(2,1)S(1)} %bitcast.21), channel_id=1, replica_groups=mesh['gx'=8,'gy'=4] {'gx','gy'}, dimensions={0} | all-to-all | bytes 524288 | tf_op jit(solution)/shard_map/all_to_all | solution.py:462
  20.3 2.6 %all-to-all-start = ((bf16[32,4,1280]{2,1,0:T(4,128)(2,1)}), bf16[32,4,1280]{2,1,0:T(4,128)(2,1)S(1)}, u32[]{:S(2)}, u32[]{:S(2)}) async-start(bf16[32,4,1280]{2,1,0:T(4,128)(2,1)} %bitcast.2), calls=%async_computation | async-start | bytes 655360 | tf_op jit(solution)/shard_map/all_to_all | solution.py:462
  23.0 10.4 %shard_map.115.refs_1_.sums_ref = f32[2,128,4608]{2,1,0:T(8,128)} custom-call(bf16[128,1024]{1,0:T(8,128)(2,1)S(1)} %shard_map.114.x_ref.refs_0_, bf16[2304,4608]{1,0:T(8,128)(2,1)} %gate_ref.7, bf16[2304,4608]{1,0:T(8,128)(2,1)} %up_ref.7), custom_call_target="tpu_custom_call" | custom-call | flops 2415919104 | bytes 18874368 | tf_op jit(solution)/shard_map/pallas_call | solution.py:181
  33.4 1.5 %all-to-all-done.rows_ref = bf16[32,4,1280]{2,1,0:T(4,128)(2,1)S(1)} async-done(((bf16[32,4,1280]{2,1,0:T(4,128)(2,1)}), bf16[32,4,1280]{2,1,0:T(4,128)(2,1)S(1)}, u32[]{:S(2)}, u32[]{:S(2)}) %all-to-all-start) | async-done | bytes 327712 | tf_op jit(solution)/shard_map/all_to_all | solution.py:462
  34.9 2.3 %copy-done = f32[2,128,4608]{2,1,0:T(8,128)S(1)} copy-done((f32[2,128,4608]{2,1,0:T(8,128)S(1)}, f32[2,128,4608]{2,1,0:T(8,128)}, u32[]{:S(2)}) %copy-start) | copy-done | bytes 4718616
  37.4 4.0 %shard_map.117 = (f32[2,64,1280]{2,1,0:T(8,128)S(1)}, bf16[2,64,1280]{2,1,0:T(8,128)(2,1)S(1)}) custom-call(bf16[128,2304]{1,0:T(8,128)(2,1)S(1)} %shard_map.116.x_ref, bf16[2304,4608]{1,0:T(8,128)(2,1)} %gate_ref.7, bf16[2304,4608]{1,0:T(8,128)(2,1)} %up_ref.7, f32[2,128,4608]{2,1,0:T(8,128)} %shard_map.115.refs_1_.sums_ref), custom_call_target="tpu_custom_call" | custom-call | flops 209715200 | bytes 1638400 | tf_op jit(solution)/shard_map/pallas_call | solution.py:228
  41.4 1.6 %collective-permute-done.core_ref = bf16[2,64,1280]{2,1,0:T(8,128)(2,1)S(1)} collective-permute-done((bf16[2,64,1280]{2,1,0:T(8,128)(2,1)S(1)}, bf16[2,64,1280]{2,1,0:T(8,128)(2,1)S(1)}, u32[]{:S(2)}, u32[]{:S(2)}) %collective-permute-start) | collective-permute-done | bytes 327712 | tf_op jit(solution)/shard_map/ppermute | solution.py:50
  43.1 5.7 %shard_map.119 = (f32[2,64,2048]{2,1,0:T(8,128)S(1)}, bf16[2,64,2048]{2,1,0:T(8,128)(2,1)S(1)}) custom-call(bf16[128,2304]{1,0:T(8,128)(2,1)S(1)} %shard_map.116.x_ref, bf16[2304,4608]{1,0:T(8,128)(2,1)} %gate_ref.7, bf16[2304,4608]{1,0:T(8,128)(2,1)} %up_ref.7, f32[2,128,4608]{2,1,0:T(8,128)} %shard_map.115.refs_1_.sums_ref, ...), custom_call_target="tpu_custom_call" | custom-call | flops 335544320 | bytes 2621440 | tf_op jit(solution)/shard_map/pallas_call | solution.py:228
  49.0 0.7 collective-permute-start.2
  49.7 5.8 %collective-permute-done.2.far_ref = bf16[2,32,1280]{2,1,0:T(8,128)(2,1)S(1)} collective-permute-done((bf16[2,32,1280]{2,1,0:T(8,128)(2,1)S(1)}, bf16[2,32,1280]{2,1,0:T(8,128)(2,1)S(1)}, u32[]{:S(2)}, u32[]{:S(2)}) %collective-permute-start.2) | collective-permute-done | bytes 163872 | tf_op jit(solution)/shard_map/ppermute | solution.py:50
  55.7 4.0 %shard_map.122 = (f32[2,64,1280]{2,1,0:T(8,128)S(1)}, bf16[2,64,1280]{2,1,0:T(8,128)(2,1)S(1)}) custom-call(bf16[128,2304]{1,0:T(8,128)(2,1)S(1)} %shard_map.116.x_ref, bf16[2304,4608]{1,0:T(8,128)(2,1)} %gate_ref.7, bf16[2304,4608]{1,0:T(8,128)(2,1)} %up_ref.7, f32[2,128,4608]{2,1,0:T(8,128)} %shard_map.115.refs_1_.sums_ref, ...), custom_call_target="tpu_custom_call" | custom-call | flops 209715200 | bytes 1638400 | tf_op jit(solution)/shard_map/pallas_call | solution.py:228
  59.8 0.5 collective-permute-start.8
  60.4 1.0 collective-permute-done.3.core_ref
  61.5 1.0 shard_map.131
  62.4 4.5 %all-to-all-start.3 = ((f32[32,4,512]{2,1,0:T(4,128)}), f32[32,4,512]{2,1,0:T(4,128)S(1)}, u32[]{:S(2)}, u32[]{:S(2)}) async-start(f32[32,4,512]{2,1,0:T(4,128)} %shard_map.131), calls=%async_computation.3 | async-start | bytes 524288 | tf_op jit(solution)/shard_map/all_to_all | solution.py:462
  67.0 1.7 %collective-permute-start.5 = (bf16[32,1280]{1,0:T(8,128)(2,1)S(1)}, bf16[32,1280]{1,0:T(8,128)(2,1)S(1)}, u32[]{:S(2)}, u32[]{:S(2)}) collective-permute-start(bf16[32,1280]{1,0:T(8,128)(2,1)S(1)} %shard_map.121.refs_1_.refs_0_), channel_id=1, source_target_pairs={{0,2},{1,3},{2,0},{3,1},{4,6},{5,7},{6,4},{7,5},{8,10},{9,11},{10,... | collective-permute-start | bytes 245768 | tf_op jit(solution)/shard_map/ppermute | solution.py:50
  68.7 0.5 collective-permute-start.12
  69.2 1.6 %collective-permute-start.4 = (bf16[2,32,1280]{2,1,0:T(8,128)(2,1)S(1)}, bf16[2,32,1280]{2,1,0:T(8,128)(2,1)S(1)}, u32[]{:S(2)}, u32[]{:S(2)}) collective-permute-start(bf16[2,32,1280]{2,1,0:T(8,128)(2,1)S(1)} %get-tuple-element.31.refs_0_.after_ref), channel_id=1, source_target_pairs={{0,2},{1,3},{2,0},{3,1},{4,6},{5,7},{6,4},{7,5},{8,10},{9,11},{10,... | collective-permute-start | bytes 491528 | tf_op jit(solution)/shard_map/ppermute | solution.py:50
  70.8 3.2 %collective-permute-done.5.refs_1_ = bf16[32,1280]{1,0:T(8,128)(2,1)S(1)} collective-permute-done((bf16[32,1280]{1,0:T(8,128)(2,1)S(1)}, bf16[32,1280]{1,0:T(8,128)(2,1)S(1)}, u32[]{:S(2)}, u32[]{:S(2)}) %collective-permute-start.5) | collective-permute-done | bytes 81952 | tf_op jit(solution)/shard_map/ppermute | solution.py:50
  74.0 0.5 collective-permute-start.13
  74.5 3.0 %collective-permute-done.12.refs_1_ = bf16[32,2048]{1,0:T(8,128)(2,1)S(1)} collective-permute-done((bf16[32,2048]{1,0:T(8,128)(2,1)S(1)}, bf16[32,2048]{1,0:T(8,128)(2,1)S(1)}, u32[]{:S(2)}, u32[]{:S(2)}) %collective-permute-start.12) | collective-permute-done | bytes 131104 | tf_op jit(solution)/shard_map/ppermute | solution.py:50
  77.5 4.0 %shard_map.125.refs_0_.refs_5_ = f32[128,2304]{1,0:T(8,128)S(1)} custom-call(s32[1]{0:T(128)} %bitcast.gy_ref, bf16[32,1280]{1,0:T(8,128)(2,1)S(1)} %shard_map.121.refs_1_.refs_0_, bf16[32,1280]{1,0:T(8,128)(2,1)S(1)} %collective-permute-done.5.refs_1_, bf16[32,1280]{1,0:T(8,128)(2,1)S(1)} %collective-permute-done.6.refs_2_, ...), custom_call_target="tpu_custom_call" | custom-call | flops 377487360 | bytes 2949120 | tf_op jit(solution)/shard_map/pallas_call | solution.py:322
  81.6 0.9 collective-permute-start.9
  82.7 3.8 %collective-permute-done.9.refs_1_ = bf16[32,1280]{1,0:T(8,128)(2,1)S(1)} collective-permute-done((bf16[32,1280]{1,0:T(8,128)(2,1)S(1)}, bf16[32,1280]{1,0:T(8,128)(2,1)S(1)}, u32[]{:S(2)}, u32[]{:S(2)}) %collective-permute-start.9) | collective-permute-done | bytes 81952 | tf_op jit(solution)/shard_map/ppermute | solution.py:50
  86.5 5.0 %shard_map.127.refs_5_ = f32[128,2304]{1,0:T(8,128)S(1)} custom-call(s32[1]{0:T(128)} %bitcast.gy_ref, bf16[32,2048]{1,0:T(8,128)(2,1)S(1)} %shard_map.124.refs_5_.refs_0_, bf16[32,2048]{1,0:T(8,128)(2,1)S(1)} %collective-permute-done.12.refs_1_, bf16[32,2048]{1,0:T(8,128)(2,1)S(1)} %collective-permute-done.13.refs_2_, ...), custom_call_target="tpu_custom_call" | custom-call | flops 603979776 | bytes 4718592 | tf_op jit(solution)/shard_map/pallas_call | solution.py:322
  91.6 4.9 %shard_map.128.after_ref = bf16[32,4,2304]{2,1,0:T(4,128)(2,1)} custom-call(s32[1]{0:T(128)} %bitcast.gy_ref, bf16[32,1280]{1,0:T(8,128)(2,1)S(1)} %shard_map.126.refs_6_.refs_0_, bf16[32,1280]{1,0:T(8,128)(2,1)S(1)} %collective-permute-done.9.refs_1_, bf16[32,1280]{1,0:T(8,128)(2,1)S(1)} %collective-permute-done.10.refs_2_, ...), custom_call_target="tpu_custom_call" | custom-call | flops 377487360 | bytes 2949120 | tf_op jit(solution)/shard_map/pallas_call | solution.py:322
  96.5 4.5 %all-to-all-start.2 = ((bf16[32,4,2304]{2,1,0:T(4,128)(2,1)}), bf16[32,4,2304]{2,1,0:T(4,128)(2,1)S(1)}, u32[]{:S(2)}, u32[]{:S(2)}) async-start(bf16[32,4,2304]{2,1,0:T(4,128)(2,1)} %shard_map.128.after_ref), calls=%async_computation.2 | async-start | bytes 1179648 | tf_op jit(solution)/shard_map/all_to_all | solution.py:462
  101.1 6.3 %shard_map.130 = (f32[4,48,256]{2,1,0:T(8,128)S(1)}, f32[4,48,1]{2,1,0:T(8,128)S(1)}, f32[4,48,1]{2,1,0:T(8,128)S(1)}) custom-call(s32[4]{0:T(128)S(1)} %copy-done.3, bf16[4,48,256]{2,1,0:T(8,128)(2,1)S(1)} %bitcast.20, bf16[4,2048,256]{2,1,0:T(8,128)(2,1)} %key_ref.1, bf16[4,2048,256]{2,1,0:T(8,128)(2,1)} %value_ref.1, ...), custom_call_target="tpu_custom_call" | custom-call | flops 603979776 | bytes 8388608 | tf_op jit(solution)/shard_map/pallas_call | solution.py:416
  108.1 0.7 copy.17
  108.8 9.0 %all-to-all-done.2 = bf16[32,4,2304]{2,1,0:T(4,128)(2,1)S(1)} async-done(((bf16[32,4,2304]{2,1,0:T(4,128)(2,1)}), bf16[32,4,2304]{2,1,0:T(4,128)(2,1)S(1)}, u32[]{:S(2)}, u32[]{:S(2)}) %all-to-all-start.2) | async-done | bytes 589856 | tf_op jit(solution)/shard_map/all_to_all | solution.py:462
  117.8 0.7 shard_map.129
  (44 shorter events, 1.9 us)
Async XLA Ops:
  20.3 14.6 %all-to-all-start = ((bf16[32,4,1280]{2,1,0:T(4,128)(2,1)}), bf16[32,4,1280]{2,1,0:T(4,128)(2,1)S(1)}, u32[]{:S(2)}, u32[]{:S(2)}) async-start(bf16[32,4,1280]{2,1,0:T(4,128)(2,1)} %bitcast.2), calls=%async_computation | async-start | bytes 655360 | tf_op jit(solution)/shard_map/all_to_all | solution.py:462
  34.9 2.3 %copy-start = (f32[2,128,4608]{2,1,0:T(8,128)S(1)}, f32[2,128,4608]{2,1,0:T(8,128)}, u32[]{:S(2)}) copy-start(f32[2,128,4608]{2,1,0:T(8,128)} %shard_map.115.refs_1_.sums_ref) | copy-start | bytes 14155780
  41.4 1.7 %collective-permute-start = (bf16[2,64,1280]{2,1,0:T(8,128)(2,1)S(1)}, bf16[2,64,1280]{2,1,0:T(8,128)(2,1)S(1)}, u32[]{:S(2)}, u32[]{:S(2)}) collective-permute-start(bf16[2,64,1280]{2,1,0:T(8,128)(2,1)S(1)} %get-tuple-element.22), channel_id=1, source_target_pairs={{0,1},{1,0},{2,3},{3,2},{4,5},{5,4},{6,7},{7,6},{8,9},{9,8},{10,11... | collective-permute-start | bytes 983048 | tf_op jit(solution)/shard_map/ppermute | solution.py:50
  48.8 6.7 %collective-permute-start.1 = (bf16[2,64,2048]{2,1,0:T(8,128)(2,1)S(1)}, bf16[2,64,2048]{2,1,0:T(8,128)(2,1)S(1)}, u32[]{:S(2)}, u32[]{:S(2)}) collective-permute-start(bf16[2,64,2048]{2,1,0:T(8,128)(2,1)S(1)} %get-tuple-element.25), channel_id=1, source_target_pairs={{0,1},{1,0},{2,3},{3,2},{4,5},{5,4},{6,7},{7,6},{8,9},{9,8},{10,11... | collective-permute-start | bytes 1572872 | tf_op jit(solution)/shard_map/ppermute | solution.py:50
  49.0 6.5 %collective-permute-start.2 = (bf16[2,32,1280]{2,1,0:T(8,128)(2,1)S(1)}, bf16[2,32,1280]{2,1,0:T(8,128)(2,1)S(1)}, u32[]{:S(2)}, u32[]{:S(2)}) collective-permute-start(bf16[2,32,1280]{2,1,0:T(8,128)(2,1)S(1)} %get-tuple-element.23.refs_0_), channel_id=1, source_target_pairs={{0,2},{1,3},{2,0},{3,1},{4,6},{5,7},{6,4},{7,5},{8,10},{9,11},{10,... | collective-permute-start | bytes 491528 | tf_op jit(solution)/shard_map/ppermute | solution.py:50
  55.6 5.8 %copy-start.2 = (bf16[1,288,512]{2,1,0:T(8,128)(2,1)S(1)}, bf16[1,288,512]{2,1,0:T(8,128)(2,1)}, u32[]{:S(2)}) copy-start(bf16[1,288,512]{2,1,0:T(8,128)(2,1)} %weight_ref.1) | copy-start | bytes 884740
  59.7 1.7 %collective-permute-start.3 = (bf16[2,64,1280]{2,1,0:T(8,128)(2,1)S(1)}, bf16[2,64,1280]{2,1,0:T(8,128)(2,1)S(1)}, u32[]{:S(2)}, u32[]{:S(2)}) collective-permute-start(bf16[2,64,1280]{2,1,0:T(8,128)(2,1)S(1)} %get-tuple-element.29), channel_id=1, source_target_pairs={{0,1},{1,0},{2,3},{3,2},{4,5},{5,4},{6,7},{7,6},{8,9},{9,8},{10,11... | collective-permute-start | bytes 983048 | tf_op jit(solution)/shard_map/ppermute | solution.py:50
  59.8 8.9 %collective-permute-start.8 = (bf16[2,32,2048]{2,1,0:T(8,128)(2,1)S(1)}, bf16[2,32,2048]{2,1,0:T(8,128)(2,1)S(1)}, u32[]{:S(2)}, u32[]{:S(2)}) collective-permute-start(bf16[2,32,2048]{2,1,0:T(8,128)(2,1)S(1)} %get-tuple-element.26.refs_0_), channel_id=1, source_target_pairs={{0,2},{1,3},{2,0},{3,1},{4,6},{5,7},{6,4},{7,5},{8,10},{9,11},{10,... | collective-permute-start | bytes 786440 | tf_op jit(solution)/shard_map/ppermute | solution.py:50
  62.4 34.1 %all-to-all-start.3 = ((f32[32,4,512]{2,1,0:T(4,128)}), f32[32,4,512]{2,1,0:T(4,128)S(1)}, u32[]{:S(2)}, u32[]{:S(2)}) async-start(f32[32,4,512]{2,1,0:T(4,128)} %shard_map.131), calls=%async_computation.3 | async-start | bytes 524288 | tf_op jit(solution)/shard_map/all_to_all | solution.py:462
  67.0 7.1 %collective-permute-start.5 = (bf16[32,1280]{1,0:T(8,128)(2,1)S(1)}, bf16[32,1280]{1,0:T(8,128)(2,1)S(1)}, u32[]{:S(2)}, u32[]{:S(2)}) collective-permute-start(bf16[32,1280]{1,0:T(8,128)(2,1)S(1)} %shard_map.121.refs_1_.refs_0_), channel_id=1, source_target_pairs={{0,2},{1,3},{2,0},{3,1},{4,6},{5,7},{6,4},{7,5},{8,10},{9,11},{10,... | collective-permute-start | bytes 245768 | tf_op jit(solution)/shard_map/ppermute | solution.py:50
  68.7 8.8 %collective-permute-start.12 = (bf16[32,2048]{1,0:T(8,128)(2,1)S(1)}, bf16[32,2048]{1,0:T(8,128)(2,1)S(1)}, u32[]{:S(2)}, u32[]{:S(2)}) collective-permute-start(bf16[32,2048]{1,0:T(8,128)(2,1)S(1)} %shard_map.124.refs_5_.refs_0_), channel_id=1, source_target_pairs={{0,2},{1,3},{2,0},{3,1},{4,6},{5,7},{6,4},{7,5},{8,10},{9,11},{10,... | collective-permute-start | bytes 393224 | tf_op jit(solution)/shard_map/ppermute | solution.py:50
  69.2 12.3 %collective-permute-start.4 = (bf16[2,32,1280]{2,1,0:T(8,128)(2,1)S(1)}, bf16[2,32,1280]{2,1,0:T(8,128)(2,1)S(1)}, u32[]{:S(2)}, u32[]{:S(2)}) collective-permute-start(bf16[2,32,1280]{2,1,0:T(8,128)(2,1)S(1)} %get-tuple-element.31.refs_0_.after_ref), channel_id=1, source_target_pairs={{0,2},{1,3},{2,0},{3,1},{4,6},{5,7},{6,4},{7,5},{8,10},{9,11},{10,... | collective-permute-start | bytes 491528 | tf_op jit(solution)/shard_map/ppermute | solution.py:50
  70.8 6.7 %collective-permute-start.6 = (bf16[32,1280]{1,0:T(8,128)(2,1)S(1)}, bf16[32,1280]{1,0:T(8,128)(2,1)S(1)}, u32[]{:S(2)}, u32[]{:S(2)}) collective-permute-start(bf16[32,1280]{1,0:T(8,128)(2,1)S(1)} %shard_map.121.refs_1_.refs_0_), channel_id=1, source_target_pairs={{0,1},{1,0},{2,3},{3,2},{4,5},{5,4},{6,7},{7,6},{8,9},{9,8},{10,11... | collective-permute-start | bytes 245768 | tf_op jit(solution)/shard_map/ppermute | solution.py:50
  74.0 3.5 %collective-permute-start.7 = (bf16[32,1280]{1,0:T(8,128)(2,1)S(1)}, bf16[32,1280]{1,0:T(8,128)(2,1)S(1)}, u32[]{:S(2)}, u32[]{:S(2)}) collective-permute-start(bf16[32,1280]{1,0:T(8,128)(2,1)S(1)} %collective-permute-done.5.refs_1_), channel_id=1, source_target_pairs={{0,1},{1,0},{2,3},{3,2},{4,5},{5,4},{6,7},{7,6},{8,9},{9,8},{10,11... | collective-permute-start | bytes 245768 | tf_op jit(solution)/shard_map/ppermute | solution.py:50
  74.0 12.5 %collective-permute-start.13 = (bf16[32,2048]{1,0:T(8,128)(2,1)S(1)}, bf16[32,2048]{1,0:T(8,128)(2,1)S(1)}, u32[]{:S(2)}, u32[]{:S(2)}) collective-permute-start(bf16[32,2048]{1,0:T(8,128)(2,1)S(1)} %shard_map.124.refs_5_.refs_0_), channel_id=1, source_target_pairs={{0,1},{1,0},{2,3},{3,2},{4,5},{5,4},{6,7},{7,6},{8,9},{9,8},{10,11... | collective-permute-start | bytes 393224 | tf_op jit(solution)/shard_map/ppermute | solution.py:50
  77.5 9.0 %collective-permute-start.14 = (bf16[32,2048]{1,0:T(8,128)(2,1)S(1)}, bf16[32,2048]{1,0:T(8,128)(2,1)S(1)}, u32[]{:S(2)}, u32[]{:S(2)}) collective-permute-start(bf16[32,2048]{1,0:T(8,128)(2,1)S(1)} %collective-permute-done.12.refs_1_), channel_id=1, source_target_pairs={{0,1},{1,0},{2,3},{3,2},{4,5},{5,4},{6,7},{7,6},{8,9},{9,8},{10,11... | collective-permute-start | bytes 393224 | tf_op jit(solution)/shard_map/ppermute | solution.py:50
  81.6 4.9 %collective-permute-start.9 = (bf16[32,1280]{1,0:T(8,128)(2,1)S(1)}, bf16[32,1280]{1,0:T(8,128)(2,1)S(1)}, u32[]{:S(2)}, u32[]{:S(2)}) collective-permute-start(bf16[32,1280]{1,0:T(8,128)(2,1)S(1)} %shard_map.126.refs_6_.refs_0_), channel_id=1, source_target_pairs={{0,2},{1,3},{2,0},{3,1},{4,6},{5,7},{6,4},{7,5},{8,10},{9,11},{10,... | collective-permute-start | bytes 245768 | tf_op jit(solution)/shard_map/ppermute | solution.py:50
  82.5 9.1 %collective-permute-start.10 = (bf16[32,1280]{1,0:T(8,128)(2,1)S(1)}, bf16[32,1280]{1,0:T(8,128)(2,1)S(1)}, u32[]{:S(2)}, u32[]{:S(2)}) collective-permute-start(bf16[32,1280]{1,0:T(8,128)(2,1)S(1)} %shard_map.126.refs_6_.refs_0_), channel_id=1, source_target_pairs={{0,1},{1,0},{2,3},{3,2},{4,5},{5,4},{6,7},{7,6},{8,9},{9,8},{10,11... | collective-permute-start | bytes 245768 | tf_op jit(solution)/shard_map/ppermute | solution.py:50
  86.5 5.1 %collective-permute-start.11 = (bf16[32,1280]{1,0:T(8,128)(2,1)S(1)}, bf16[32,1280]{1,0:T(8,128)(2,1)S(1)}, u32[]{:S(2)}, u32[]{:S(2)}) collective-permute-start(bf16[32,1280]{1,0:T(8,128)(2,1)S(1)} %collective-permute-done.9.refs_1_), channel_id=1, source_target_pairs={{0,1},{1,0},{2,3},{3,2},{4,5},{5,4},{6,7},{7,6},{8,9},{9,8},{10,11... | collective-permute-start | bytes 245768 | tf_op jit(solution)/shard_map/ppermute | solution.py:50
  91.6 9.5 %copy-start.4 = (bf16[4,12288]{1,0:T(4,128)(2,1)S(1)}, bf16[4,12288]{1,0:T(4,128)(2,1)}, u32[]{:S(2)}) copy-start(bf16[4,12288]{1,0:T(4,128)(2,1)} %param.16) | copy-start | bytes 294916
  91.6 9.5 %copy-start.3 = (s32[4]{0:T(128)S(1)}, s32[4]{0:T(128)}, u32[]{:S(2)}) copy-start(s32[4]{0:T(128)} %lengths_ref.1) | copy-start | bytes 52
  96.5 21.3 %all-to-all-start.2 = ((bf16[32,4,2304]{2,1,0:T(4,128)(2,1)}), bf16[32,4,2304]{2,1,0:T(4,128)(2,1)S(1)}, u32[]{:S(2)}, u32[]{:S(2)}) async-start(bf16[32,4,2304]{2,1,0:T(4,128)(2,1)} %shard_map.128.after_ref), calls=%async_computation.2 | async-start | bytes 1179648 | tf_op jit(solution)/shard_map/all_to_all | solution.py:462
  101.1 16.7 %copy-start.1 = (bf16[4,9216]{1,0:T(4,128)(2,1)S(1)}, bf16[4,9216]{1,0:T(4,128)(2,1)}, u32[]{:S(2)}) copy-start(bf16[4,9216]{1,0:T(4,128)(2,1)} %tokens_ref.1) | copy-start | bytes 221188

commit v6 on v5

--- a/solution.py
+++ b/solution.py
@@ -92,12 +92,8 @@
     )(in_hbm(tokens), in_hbm(gain.reshape(1, -1)))
 
 
-def assemble_kernel(gy_ref, rows_ref, *refs):
-    out_ref = refs[-1]
-    first = 0
-    if len(refs) > 1:
-        first = refs[0].shape[1]
-        out_ref[:, :first] = refs[0][...]
+def assemble_kernel(gy_ref, rows_ref, after_ref, out_ref):
+    del after_ref
     devices, batch, _ = rows_ref.shape
     quarter = devices // 4
     pack = 16 // batch
@@ -108,20 +104,19 @@
                 [rows_ref[base + i + k].astype(F32) for k in range(pack)], axis=0
             )
             start = (at * quarter + i) * batch
-            out_ref[start : start + 16, first:] = tall.astype(BF16)
-
-
-def assemble(gy, rows, before=(), after=()):
+            out_ref[start : start + 16] = tall.astype(BF16)
+
+
+def assemble(gy, rows, after):
     devices, batch, width = rows.shape
-    width += sum(x.shape[1] for x in before)
     return pl.pallas_call(
         assemble_kernel,
-        in_specs=[SCALARS, WHOLE] + [WHOLE] * len(before) + [ANYWHERE] * len(after),
+        in_specs=[SCALARS, WHOLE, ANYWHERE],
         out_specs=WHOLE,
         out_shape=vmem_out((devices * batch, width), BF16),
         compiler_params=params(4),
         cost_estimate=cost(2 * rows.size, 4 * rows.size),
-    )(gy, in_vmem(rows), *[in_vmem(x) for x in before], *after)
+    )(gy, in_vmem(rows), after)
 
 
 def spread_rows(out_ref, value, gy, columns=slice(None)):
@@ -132,6 +127,22 @@
         for i in range(quarter):
             start = (at * quarter + i) * batch
             out_ref[base + i, :, columns] = value[start : start + batch].astype(out_ref.dtype)
+
+
+def tie_kernel(*refs):
+    del refs
+
+
+def tie(x, after):
+    return pl.pallas_call(
+        tie_kernel,
+        in_specs=[ANYWHERE] * (1 + len(after)),
+        out_specs=ANYWHERE,
+        out_shape=jax.ShapeDtypeStruct(x.shape, x.dtype),
+        input_output_aliases={0: 0},
+        compiler_params=params(1),
+        cost_estimate=cost(0, 0),
+    )(x, *after)
 
 
 def in_turn(groups, ahead):
@@ -147,97 +158,44 @@
         yield n
 
 
-def gate_up_first_kernel(tile, x_ref, gate_ref, up_ref, out_ref, slots, sums, sems, out_sems):
-    depth = x_ref.shape[1]
-    groups = []
-    outs = []
-    for n in range(slots.shape[1]):
-        columns = pl.ds(n * tile, tile)
-        groups.append(
-            [
-                pltpu.make_async_copy(
-                    source.at[pl.ds(0, depth), columns], slots.at[k, n], sems.at[k, n]
-                )
-                for k, source in enumerate((gate_ref, up_ref))
-            ]
-        )
-        outs.append(
-            pltpu.make_async_copy(sums.at[n], out_ref.at[:, :, columns], out_sems.at[n])
-        )
-    x = x_ref[...]
-    for n in in_turn(groups, 3):
-        for k in range(2):
-            sums[n, k] = jnp.dot(x, slots[k, n], preferred_element_type=F32)
-        outs[n].start()
-    for out in outs:
-        out.wait()
-
-
-def gate_up_first(x, w_gate, w_up):
-    rows, depth = x.shape
-    width = w_gate.shape[1]
-    tile = tile_of(width, 256)
-    count = width // tile
-    return pl.pallas_call(
-        functools.partial(gate_up_first_kernel, tile),
-        in_specs=[WHOLE, ANYWHERE, ANYWHERE],
-        out_specs=ANYWHERE,
-        out_shape=hbm_out((2, rows, width), F32),
-        scratch_shapes=[
-            pltpu.VMEM((2, count, depth, tile), BF16),
-            pltpu.VMEM((count, 2, rows, tile), F32),
-            pltpu.SemaphoreType.DMA((2, count)),
-            pltpu.SemaphoreType.DMA((count,)),
-        ],
-        compiler_params=params(28),
-        cost_estimate=cost(4 * rows * depth * width, 4 * depth * width),
-    )(in_vmem(x), in_hbm(w_gate), in_hbm(w_up))
-
-
-def gate_up_kernel(start, tile, first, count_after, x_ref, gate_ref, up_ref, sums_ref, *refs):
-    keep_ref, send_ref, slots, sum_slots, sems = refs[count_after:]
+def gate_up_kernel(start, tile, count_after, x_ref, gate_ref, up_ref, *refs):
+    keep_ref, send_ref, slots, sems = refs[count_after:]
     _, half, width = keep_ref.shape
-    depth = slots.shape[2]
     groups = []
     for n in range(width // tile):
         columns = pl.ds(start + n * tile, tile)
         groups.append(
             [
-                pltpu.make_async_copy(
-                    source.at[pl.ds(first, depth), columns], slots.at[k, n], sems.at[k, n]
-                )
+                pltpu.make_async_copy(source.at[:, columns], slots.at[k, n], sems.at[k, n])
                 for k, source in enumerate((gate_ref, up_ref))
             ]
-            + [pltpu.make_async_copy(sums_ref.at[:, :, columns], sum_slots.at[n], sems.at[2, n])]
         )
-    x = x_ref[:, first:]
+    x = x_ref[...]
     for n in in_turn(groups, 3):
         columns = slice(n * tile, (n + 1) * tile)
         for k in range(2):
-            value = jnp.dot(x, slots[k, n], preferred_element_type=F32) + sum_slots[n, k]
+            value = jnp.dot(x, slots[k, n], preferred_element_type=F32)
             keep_ref[k, :, columns] = value[:half]
             send_ref[k, :, columns] = value[half:].astype(BF16)
 
 
-def gate_up(x, w_gate, w_up, sums, first, start, width, after):
-    rows = x.shape[0]
-    depth = x.shape[1] - first
+def gate_up(x, w_gate, w_up, start, width, after):
+    rows, depth = x.shape
     half = rows // 2
     tile = tile_of(width, 256)
     count = width // tile
     return pl.pallas_call(
-        functools.partial(gate_up_kernel, start, tile, first, len(after)),
-        in_specs=[WHOLE] + [ANYWHERE] * (3 + len(after)),
+        functools.partial(gate_up_kernel, start, tile, len(after)),
+        in_specs=[WHOLE] + [ANYWHERE] * (2 + len(after)),
         out_specs=[WHOLE, WHOLE],
         out_shape=[vmem_out((2, half, width), F32), vmem_out((2, half, width), BF16)],
         scratch_shapes=[
             pltpu.VMEM((2, count, depth, tile), BF16),
-            pltpu.VMEM((count, 2, rows, tile), F32),
-            pltpu.SemaphoreType.DMA((3, count)),
+            pltpu.SemaphoreType.DMA((2, count)),
         ],
-        compiler_params=params(20),
+        compiler_params=params(22),
         cost_estimate=cost(rows * depth * width, depth * width),
-    )(in_vmem(x), in_hbm(w_gate), in_hbm(w_up), in_hbm(sums), *after)
+    )(in_vmem(x), in_hbm(w_gate), in_hbm(w_up), *after)
 
 
 def combine_kernel(keep_ref, core_ref, own_ref, across_ref):
@@ -464,52 +422,52 @@
     batch = tokens.shape[0]
     widths = chunk_widths(w_gate.shape[1])
 
-    depth = w_gate.shape[0]
-    unit = 256 if depth % 256 == 0 else 128
-    first = depth // unit // 2 * unit
-
-    normed = norm(tokens, gain, n_gx, n_gy, (first, depth - first))
-    parts = [exchange(part.reshape(devices, batch, -1)) for part in normed]
-    x_first = assemble(gy, parts[0])
-    sums = gate_up_first(x_first, w_gate, w_up)
-    x = assemble(gy, parts[1], [x_first], [sums])
-
-    owns, far, hidden = [], [], []
-    start = 0
-    after = []
-    for c, width in enumerate(widths):
-        keep, send = gate_up(x, w_gate, w_up, sums, first, start, width, after)
-        own, across = combine(keep, swap_gy(send, 1))
-        owns.append(own)
-        far.append(swap_gy(across, 2))
-        after = [across]
-        if c == 1:
-            hidden.append(activate(owns[0], far[0], []))
-            after.append(hidden[0])
-        start += width
-    hidden.append(activate(owns[1], far[1], [across]))
+    (normed,) = norm(tokens, gain, n_gx, n_gy, (w_gate.shape[0],))
+    gathered = exchange(normed.reshape(devices, batch, -1))
+    grouped = queries.reshape(batch, -1, HD)
+    cached = attend_cache(grouped, key_cache, value_cache, lengths, normed)
+    x = assemble(gy, gathered, cached[0])
+
+    starts = [sum(widths[:c]) for c in range(len(widths))]
+
+    def project(c, after):
+        return gate_up(x, w_gate, w_up, starts[c], widths[c], after)
+
+    def back(c, own, after):
+        other = tie(swap_gy(own, 2), after)
+        return own, other, swap_gy(own, 1), swap_gy(other, 1)
+
+    def through(c, pieces, total, after):
+        last = c == len(widths) - 1
+        return down(gy, pieces, w_down, starts[c], total, devices, last, after)
+
+    keep, send = project(0, [])
+    own_0, across_0 = combine(keep, swap_gy(send, 1))
+    far_0 = swap_gy(across_0, 2)
+    keep, send = project(1, [across_0])
+    hidden_0 = activate(own_0, far_0, [send])
+    own_1, across_1 = combine(keep, swap_gy(tie(send, [hidden_0]), 1))
+    far_1 = swap_gy(across_1, 2)
+    keep, send = project(2, [across_1])
+    pieces_0 = back(0, hidden_0, [send])
+    own_2, across_2 = combine(keep, swap_gy(send, 1))
+    far_2 = swap_gy(across_2, 2)
+    hidden_1 = activate(own_1, far_1, [across_2])
 
     slab = w_kv.shape[1]
-    part = fresh_part(gy, lax.dynamic_slice_in_dim(x, gx * slab, slab, 1), w_kv, devices, across)
-    fresh = jnp.sum(exchange(part), axis=0)
+    part = fresh_part(gy, lax.dynamic_slice_in_dim(x, gx * slab, slab, 1), w_kv, devices, send)
+    fresh = jnp.sum(exchange(tie(part, [across_2])), axis=0)
     key_new = fresh[:, :HD].astype(BF16)
     value_new = fresh[:, HD:].astype(BF16)
 
-    total = None
-    start = 0
-    for c, width in enumerate(widths):
-        if c == 1:
-            hidden.append(activate(owns[2], far[2], [total]))
-        own = hidden[c]
-        other = swap_gy(own, 2)
-        pieces = (own, other, swap_gy(own, 1), swap_gy(other, 1))
-        last = c == len(widths) - 1
-        total = down(gy, pieces, w_down, start, total, devices, last, [] if last else [hidden[c + 1]])
-        start += width
+    total = through(0, pieces_0, None, [hidden_1])
+    pieces_1 = back(1, hidden_1, [total])
+    hidden_2 = activate(own_2, far_2, [total])
+    total = through(1, pieces_1, total, [hidden_2])
+    pieces_2 = back(2, hidden_2, [total])
+    total = through(2, pieces_2, total, [])
 
     ffn = exchange(total)
-    grouped = queries.reshape(batch, -1, HD)
-    cached = attend_cache(grouped, key_cache, value_cache, lengths, total)
     context = attend_new(grouped, cached, key_new, value_new)
     mixed = finish(tokens, ffn.reshape(n_gx, n_gy, batch, -1))
     return (mixed, context)

time: 119 us -> 106 us (0.89)
  blocking collectives: 17.7 us -> 0 us
  starting transfers between devices: 18.5 us -> 23.9 us
  Pallas kernels: 48.6 us -> 43.7 us
  waiting for transfers between devices: 28.9 us -> 32.9 us
    all_to_all x1 -> x0, blocking collectives: 17.7 us -> none  [body(): lax.all_to_all(x, ('gx', 'gy'), split_axis=0, concat_axis=0, tiled=True)]
    all_to_all x3, waiting for transfers between devices: 10.5 us -> 23.5 us  [body(): lax.all_to_all(x, ('gx', 'gy'), split_axis=0, concat_axis=0, tiled=True)]
    ppermute x15, waiting for transfers between devices: 18.4 us -> 9.34 us  [swap(): return lax.ppermute(x, axis, [(i, i ^ bits) for i in range(size)])]
    pallas_call x6 -> x9, Pallas kernels: 24.3 us -> 18.4 us  [the longest x3 18.2 us: gate_up(): pl.pallas_call(functools.partial(gate_up_kernel, start, tile, len(after))...]
    all_to_all x3, starting transfers between devices: 11.6 us -> 16 us  [body(): lax.all_to_all(x, ('gx', 'gy'), split_axis=0, concat_axis=0, tiled=True)]
    unnamed x12 -> x14, local copies, waits for them, and re-layouts: 3.07 us -> 2.91 us
  transfers between devices with their start and end apart: 18 -> 18, of which waited for: 8 -> 9; matrix products, arithmetic and copies ran while one was open for 1% -> 2% of each run, Pallas kernels for 27% -> 28%
where the time goes in v6:
time: 106 us; the launch traced here: 105 us
  Pallas kernels  43.7 us (41%)
  waiting for transfers between devices  32.9 us (31%)
  starting transfers between devices  23.9 us (23%)
  local copies, waits for them, and re-layouts  3.13 us (3%)
    all_to_all x3, waiting for transfers between devices, body(): lax.all_to_all(x, ('gx', 'gy'), split_axis=0, concat_axis=0, tiled=True)  23.5 us
    pallas_call x3, Pallas kernels, gate_up(): pl.pallas_call(functools.partial(gate_up_kernel, start, tile, len(after))...  18.2 us
    all_to_all x3, starting transfers between devices, body(): lax.all_to_all(x, ('gx', 'gy'), split_axis=0, concat_axis=0, tiled=True)  16 us
    pallas_call x3, Pallas kernels, down(): pl.pallas_call(functools.partial(down_kernel, start, tile, total is not N...  13.9 us
    ppermute x15, waiting for transfers between devices, swap(): return lax.ppermute(x, axis, [(i, i ^ bits) for i in range(size)])  9.34 us
    ppermute x15, starting transfers between devices, swap(): return lax.ppermute(x, axis, [(i, i ^ bits) for i in range(size)])  7.96 us
    pallas_call x1, Pallas kernels, attend_cache(): pl.pallas_call(functools.partial(cache_kernel, 1.0 / math.sqrt(depth)), i...  6.31 us
    unnamed x14, local copies, waits for them, and re-layouts  2.91 us
  transfers between devices with their start and end apart: 18, of which 9 were waited for; matrix products, arithmetic and copies ran while one was open for 2% of the time, Pallas kernels for 28%

profile of v6, /device:TPU:0, one launch (start us, length us, event | category | flops | bytes accessed | tf_op | source)
XLA Modules:
  0.0 105.1 jit_solution(7749283672908098045)
XLA Ops:
  0.6 2.1 %shard_map.113.after_ref = bf16[8,4,4,2304]{3,2,1,0:T(4,128)(2,1)} custom-call(bf16[4,9216]{1,0:T(4,128)(2,1)} %tokens_ref.1, f32[1,9216]{1,0:T(1,128)} %bitcast.23), custom_call_target="tpu_custom_call" | custom-call | flops 368640 | bytes 589824 | tf_op jit(solution)/shard_map/pallas_call | solution.py:80
  2.7 7.3 %all-to-all-start = ((bf16[32,4,2304]{2,1,0:T(4,128)(2,1)}), bf16[32,4,2304]{2,1,0:T(4,128)(2,1)S(1)}, u32[]{:S(2)}, u32[]{:S(2)}) async-start(bf16[32,4,2304]{2,1,0:T(4,128)(2,1)} %bitcast.2), calls=%async_computation | async-start | bytes 1179648 | tf_op jit(solution)/shard_map/all_to_all | solution.py:420
  10.1 0.9 copy.27
  11.0 0.6 copy-done.4
  11.6 6.3 %shard_map.114 = (f32[4,48,256]{2,1,0:T(8,128)S(1)}, f32[4,48,1]{2,1,0:T(8,128)S(1)}, f32[4,48,1]{2,1,0:T(8,128)S(1)}) custom-call(s32[4]{0:T(128)S(1)} %copy-done.4, bf16[4,48,256]{2,1,0:T(8,128)(2,1)S(1)} %bitcast.19, bf16[4,2048,256]{2,1,0:T(8,128)(2,1)} %key_ref.1, bf16[4,2048,256]{2,1,0:T(8,128)(2,1)} %value_ref.1, ...), custom_call_target="tpu_custom_call" | custom-call | flops 603979776 | bytes 8388608 | tf_op jit(solution)/shard_map/pallas_call | solution.py:374
  18.0 0.6 copy-done.2
  18.6 8.2 %all-to-all-done.rows_ref = bf16[32,4,2304]{2,1,0:T(4,128)(2,1)S(1)} async-done(((bf16[32,4,2304]{2,1,0:T(4,128)(2,1)}), bf16[32,4,2304]{2,1,0:T(4,128)(2,1)S(1)}, u32[]{:S(2)}, u32[]{:S(2)}) %all-to-all-start) | async-done | bytes 589856 | tf_op jit(solution)/shard_map/all_to_all | solution.py:420
  26.9 5.3 %shard_map.116 = (f32[2,64,1280]{2,1,0:T(8,128)S(1)}, bf16[2,64,1280]{2,1,0:T(8,128)(2,1)S(1)}) custom-call(bf16[128,2304]{1,0:T(8,128)(2,1)S(1)} %shard_map.115.x_ref, bf16[2304,4608]{1,0:T(8,128)(2,1)} %gate_ref.5, bf16[2304,4608]{1,0:T(8,128)(2,1)} %up_ref.5), custom_call_target="tpu_custom_call" | custom-call | flops 377487360 | bytes 2949120 | tf_op jit(solution)/shard_map/pallas_call | solution.py:187
  32.3 1.6 %collective-permute-done.core_ref = bf16[2,64,1280]{2,1,0:T(8,128)(2,1)S(1)} collective-permute-done((bf16[2,64,1280]{2,1,0:T(8,128)(2,1)S(1)}, bf16[2,64,1280]{2,1,0:T(8,128)(2,1)S(1)}, u32[]{:S(2)}, u32[]{:S(2)}) %collective-permute-start) | collective-permute-done | bytes 327712 | tf_op jit(solution)/shard_map/ppermute | solution.py:50
  34.0 1.2 %collective-permute-start.1 = (bf16[2,32,1280]{2,1,0:T(8,128)(2,1)S(1)}, bf16[2,32,1280]{2,1,0:T(8,128)(2,1)S(1)}, u32[]{:S(2)}, u32[]{:S(2)}) collective-permute-start(bf16[2,32,1280]{2,1,0:T(8,128)(2,1)S(1)} %get-tuple-element.20.refs_0_), channel_id=1, source_target_pairs={{0,2},{1,3},{2,0},{3,1},{4,6},{5,7},{6,4},{7,5},{8,10},{9,11},{10,... | collective-permute-start | bytes 491528 | tf_op jit(solution)/shard_map/ppermute | solution.py:50
  35.2 7.5 %shard_map.118 = (f32[2,64,2048]{2,1,0:T(8,128)S(1)}, bf16[2,64,2048]{2,1,0:T(8,128)(2,1)S(1)}) custom-call(bf16[128,2304]{1,0:T(8,128)(2,1)S(1)} %shard_map.115.x_ref, bf16[2304,4608]{1,0:T(8,128)(2,1)} %gate_ref.5, bf16[2304,4608]{1,0:T(8,128)(2,1)} %up_ref.5, bf16[2,32,1280]{2,1,0:T(8,128)(2,1)S(1)} %get-tuple-element.20.refs_0_), custom_call_target="tpu_custom_call" | custom-call | flops 603979776 | bytes 4718592 | tf_op jit(solution)/shard_map/pallas_call | solution.py:187
  43.0 1.8 %collective-permute-done.2.core_ref = bf16[2,64,2048]{2,1,0:T(8,128)(2,1)S(1)} collective-permute-done((bf16[2,64,2048]{2,1,0:T(8,128)(2,1)S(1)}, bf16[2,64,2048]{2,1,0:T(8,128)(2,1)S(1)}, u32[]{:S(2)}, u32[]{:S(2)}) %collective-permute-start.2) | collective-permute-done | bytes 524320 | tf_op jit(solution)/shard_map/ppermute | solution.py:50
  44.9 5.4 %shard_map.122 = (f32[2,64,1280]{2,1,0:T(8,128)S(1)}, bf16[2,64,1280]{2,1,0:T(8,128)(2,1)S(1)}) custom-call(bf16[128,2304]{1,0:T(8,128)(2,1)S(1)} %shard_map.115.x_ref, bf16[2304,4608]{1,0:T(8,128)(2,1)} %gate_ref.5, bf16[2304,4608]{1,0:T(8,128)(2,1)} %up_ref.5, bf16[2,32,2048]{2,1,0:T(8,128)(2,1)S(1)} %get-tuple-element.24.refs_0_), custom_call_target="tpu_custom_call" | custom-call | flops 377487360 | bytes 2949120 | tf_op jit(solution)/shard_map/pallas_call | solution.py:187
  50.5 0.9 collective-permute-start.8
  51.5 0.9 shard_map.133.refs_0_
  52.5 3.5 %all-to-all-start.2 = ((f32[32,4,512]{2,1,0:T(4,128)}), f32[32,4,512]{2,1,0:T(4,128)S(1)}, u32[]{:S(2)}, u32[]{:S(2)}) async-start(f32[32,4,512]{2,1,0:T(4,128)} %shard_map.134), calls=%async_computation.2 | async-start | bytes 524288 | tf_op jit(solution)/shard_map/all_to_all | solution.py:420
  56.0 1.7 %collective-permute-start.5 = (bf16[32,1280]{1,0:T(8,128)(2,1)S(1)}, bf16[32,1280]{1,0:T(8,128)(2,1)S(1)}, u32[]{:S(2)}, u32[]{:S(2)}) collective-permute-start(bf16[32,1280]{1,0:T(8,128)(2,1)S(1)} %shard_map.119.refs_1_.refs_0_), channel_id=1, source_target_pairs={{0,2},{1,3},{2,0},{3,1},{4,6},{5,7},{6,4},{7,5},{8,10},{9,11},{10,... | collective-permute-start | bytes 245768 | tf_op jit(solution)/shard_map/ppermute | solution.py:50
  57.7 1.8 %collective-permute-done.8.far_ref = bf16[2,32,2048]{2,1,0:T(8,128)(2,1)} collective-permute-done((bf16[2,32,2048]{2,1,0:T(8,128)(2,1)S(1)}, bf16[2,32,2048]{2,1,0:T(8,128)(2,1)}, u32[]{:S(2)}, u32[]{:S(2)}) %collective-permute-start.8) | collective-permute-done | bytes 262176 | tf_op jit(solution)/shard_map/ppermute | solution.py:50
  59.5 1.0 shard_map.125.refs_5_.refs_0_
  60.5 1.1 %collective-permute-start.10 = (bf16[32,2048]{1,0:T(8,128)(2,1)S(1)}, bf16[32,2048]{1,0:T(8,128)(2,1)S(1)}, u32[]{:S(2)}, u32[]{:S(2)}) collective-permute-start(bf16[32,2048]{1,0:T(8,128)(2,1)S(1)} %shard_map.125.refs_5_.refs_0_), channel_id=1, source_target_pairs={{0,2},{1,3},{2,0},{3,1},{4,6},{5,7},{6,4},{7,5},{8,10},{9,11},{10,... | collective-permute-start | bytes 393224 | tf_op jit(solution)/shard_map/ppermute | solution.py:50
  61.6 1.7 %collective-permute-done.5.refs_0_ = bf16[32,1280]{1,0:T(8,128)(2,1)S(1)} collective-permute-done((bf16[32,1280]{1,0:T(8,128)(2,1)S(1)}, bf16[32,1280]{1,0:T(8,128)(2,1)S(1)}, u32[]{:S(2)}, u32[]{:S(2)}) %collective-permute-start.5) | collective-permute-done | bytes 81952 | tf_op jit(solution)/shard_map/ppermute | solution.py:50
  63.3 0.8 collective-permute-start.4
  64.6 4.0 %shard_map.126.refs_0_.refs_1_.refs_5_ = f32[128,2304]{1,0:T(8,128)S(1)} custom-call(s32[1]{0:T(128)} %bitcast.gy_ref, bf16[32,1280]{1,0:T(8,128)(2,1)S(1)} %shard_map.119.refs_1_.refs_0_, bf16[32,1280]{1,0:T(8,128)(2,1)S(1)} %shard_map.124.refs_1_, bf16[32,1280]{1,0:T(8,128)(2,1)S(1)} %collective-permute-done.6.refs_2_, ...), custom_call_target="tpu_custom_call" | custom-call | flops 377487360 | bytes 2949120 | tf_op jit(solution)/shard_map/pallas_call | solution.py:280
  68.9 1.1 %collective-permute-done.4.far_ref = bf16[2,32,1280]{2,1,0:T(8,128)(2,1)S(1)} collective-permute-done((bf16[2,32,1280]{2,1,0:T(8,128)(2,1)S(1)}, bf16[2,32,1280]{2,1,0:T(8,128)(2,1)S(1)}, u32[]{:S(2)}, u32[]{:S(2)}) %collective-permute-start.4) | collective-permute-done | bytes 163872 | tf_op jit(solution)/shard_map/ppermute | solution.py:50
  70.0 0.9 collective-permute-start.9
  71.0 5.0 %shard_map.129.refs_1_.refs_5_ = f32[128,2304]{1,0:T(8,128)S(1)} custom-call(s32[1]{0:T(128)} %bitcast.gy_ref, bf16[32,2048]{1,0:T(8,128)(2,1)S(1)} %shard_map.125.refs_5_.refs_0_, bf16[32,2048]{1,0:T(8,128)(2,1)S(1)} %shard_map.128.refs_1_, bf16[32,2048]{1,0:T(8,128)(2,1)S(1)} %collective-permute-done.11.refs_2_, ...), custom_call_target="tpu_custom_call" | custom-call | flops 603979776 | bytes 4718592 | tf_op jit(solution)/shard_map/pallas_call | solution.py:280
  76.6 0.9 collective-permute-done.14.refs_3_
  77.6 4.9 %shard_map.131 = bf16[32,4,2304]{2,1,0:T(4,128)(2,1)} custom-call(s32[1]{0:T(128)} %bitcast.gy_ref, bf16[32,1280]{1,0:T(8,128)(2,1)S(1)} %shard_map.127.refs_6_.refs_0_, bf16[32,1280]{1,0:T(8,128)(2,1)S(1)} %shard_map.130.refs_1_, bf16[32,1280]{1,0:T(8,128)(2,1)S(1)} %collective-permute-done.13.refs_2_, ...), custom_call_target="tpu_custom_call" | custom-call | flops 377487360 | bytes 2949120 | tf_op jit(solution)/shard_map/pallas_call | solution.py:280
  82.5 5.2 %all-to-all-start.1 = ((bf16[32,4,2304]{2,1,0:T(4,128)(2,1)}), bf16[32,4,2304]{2,1,0:T(4,128)(2,1)S(1)}, u32[]{:S(2)}, u32[]{:S(2)}) async-start(bf16[32,4,2304]{2,1,0:T(4,128)(2,1)} %shard_map.131), calls=%async_computation.1 | async-start | bytes 1179648 | tf_op jit(solution)/shard_map/all_to_all | solution.py:420
  88.3 0.7 copy.22
  89.0 15.4 %all-to-all-done.1 = bf16[32,4,2304]{2,1,0:T(4,128)(2,1)S(1)} async-done(((bf16[32,4,2304]{2,1,0:T(4,128)(2,1)}), bf16[32,4,2304]{2,1,0:T(4,128)(2,1)S(1)}, u32[]{:S(2)}, u32[]{:S(2)}) %all-to-all-start.1) | async-done | bytes 589856 | tf_op jit(solution)/shard_map/all_to_all | solution.py:420
  104.4 0.7 shard_map.132
  (48 shorter events, 2.9 us)
Async XLA Ops:
  2.7 24.0 %all-to-all-start = ((bf16[32,4,2304]{2,1,0:T(4,128)(2,1)}), bf16[32,4,2304]{2,1,0:T(4,128)(2,1)S(1)}, u32[]{:S(2)}, u32[]{:S(2)}) async-start(bf16[32,4,2304]{2,1,0:T(4,128)(2,1)} %bitcast.2), calls=%async_computation | async-start | bytes 1179648 | tf_op jit(solution)/shard_map/all_to_all | solution.py:420
  11.0 0.7 copy-start.4
  18.0 0.6 copy-start.2
  32.2 1.7 %collective-permute-start = (bf16[2,64,1280]{2,1,0:T(8,128)(2,1)S(1)}, bf16[2,64,1280]{2,1,0:T(8,128)(2,1)S(1)}, u32[]{:S(2)}, u32[]{:S(2)}) collective-permute-start(bf16[2,64,1280]{2,1,0:T(8,128)(2,1)S(1)} %get-tuple-element.19), channel_id=1, source_target_pairs={{0,1},{1,0},{2,3},{3,2},{4,5},{5,4},{6,7},{7,6},{8,9},{9,8},{10,11... | collective-permute-start | bytes 983048 | tf_op jit(solution)/shard_map/ppermute | solution.py:50
  34.0 8.8 %collective-permute-start.1 = (bf16[2,32,1280]{2,1,0:T(8,128)(2,1)S(1)}, bf16[2,32,1280]{2,1,0:T(8,128)(2,1)S(1)}, u32[]{:S(2)}, u32[]{:S(2)}) collective-permute-start(bf16[2,32,1280]{2,1,0:T(8,128)(2,1)S(1)} %get-tuple-element.20.refs_0_), channel_id=1, source_target_pairs={{0,2},{1,3},{2,0},{3,1},{4,6},{5,7},{6,4},{7,5},{8,10},{9,11},{10,... | collective-permute-start | bytes 491528 | tf_op jit(solution)/shard_map/ppermute | solution.py:50
  42.9 2.0 %collective-permute-start.2 = (bf16[2,64,2048]{2,1,0:T(8,128)(2,1)S(1)}, bf16[2,64,2048]{2,1,0:T(8,128)(2,1)S(1)}, u32[]{:S(2)}, u32[]{:S(2)}) collective-permute-start(bf16[2,64,2048]{2,1,0:T(8,128)(2,1)S(1)} %shard_map.120), channel_id=1, source_target_pairs={{0,1},{1,0},{2,3},{3,2},{4,5},{5,4},{6,7},{7,6},{8,9},{9,8},{10,11... | collective-permute-start | bytes 1572872 | tf_op jit(solution)/shard_map/ppermute | solution.py:50
  44.9 6.6 %copy-start = (bf16[1,288,512]{2,1,0:T(8,128)(2,1)S(1)}, bf16[1,288,512]{2,1,0:T(8,128)(2,1)}, u32[]{:S(2)}) copy-start(bf16[1,288,512]{2,1,0:T(8,128)(2,1)} %weight_ref.1) | copy-start | bytes 884740
  50.3 2.1 %collective-permute-start.3 = (bf16[2,64,1280]{2,1,0:T(8,128)(2,1)S(1)}, bf16[2,64,1280]{2,1,0:T(8,128)(2,1)S(1)}, u32[]{:S(2)}, u32[]{:S(2)}) collective-permute-start(bf16[2,64,1280]{2,1,0:T(8,128)(2,1)S(1)} %get-tuple-element.26.refs_1_.after_ref), channel_id=1, source_target_pairs={{0,1},{1,0},{2,3},{3,2},{4,5},{5,4},{6,7},{7,6},{8,9},{9,8},{10,11... | collective-permute-start | bytes 983048 | tf_op jit(solution)/shard_map/ppermute | solution.py:50
  50.5 9.0 %collective-permute-start.8 = (bf16[2,32,2048]{2,1,0:T(8,128)(2,1)S(1)}, bf16[2,32,2048]{2,1,0:T(8,128)(2,1)}, u32[]{:S(2)}, u32[]{:S(2)}) collective-permute-start(bf16[2,32,2048]{2,1,0:T(8,128)(2,1)S(1)} %get-tuple-element.24.refs_0_), channel_id=1, source_target_pairs={{0,2},{1,3},{2,0},{3,1},{4,6},{5,7},{6,4},{7,5},{8,10},{9,11},{10,... | collective-permute-start | bytes 786440 | tf_op jit(solution)/shard_map/ppermute | solution.py:50
  52.5 29.9 %all-to-all-start.2 = ((f32[32,4,512]{2,1,0:T(4,128)}), f32[32,4,512]{2,1,0:T(4,128)S(1)}, u32[]{:S(2)}, u32[]{:S(2)}) async-start(f32[32,4,512]{2,1,0:T(4,128)} %shard_map.134), calls=%async_computation.2 | async-start | bytes 524288 | tf_op jit(solution)/shard_map/all_to_all | solution.py:420
  56.0 7.3 %collective-permute-start.5 = (bf16[32,1280]{1,0:T(8,128)(2,1)S(1)}, bf16[32,1280]{1,0:T(8,128)(2,1)S(1)}, u32[]{:S(2)}, u32[]{:S(2)}) collective-permute-start(bf16[32,1280]{1,0:T(8,128)(2,1)S(1)} %shard_map.119.refs_1_.refs_0_), channel_id=1, source_target_pairs={{0,2},{1,3},{2,0},{3,1},{4,6},{5,7},{6,4},{7,5},{8,10},{9,11},{10,... | collective-permute-start | bytes 245768 | tf_op jit(solution)/shard_map/ppermute | solution.py:50
  60.5 8.1 %collective-permute-start.10 = (bf16[32,2048]{1,0:T(8,128)(2,1)S(1)}, bf16[32,2048]{1,0:T(8,128)(2,1)S(1)}, u32[]{:S(2)}, u32[]{:S(2)}) collective-permute-start(bf16[32,2048]{1,0:T(8,128)(2,1)S(1)} %shard_map.125.refs_5_.refs_0_), channel_id=1, source_target_pairs={{0,2},{1,3},{2,0},{3,1},{4,6},{5,7},{6,4},{7,5},{8,10},{9,11},{10,... | collective-permute-start | bytes 393224 | tf_op jit(solution)/shard_map/ppermute | solution.py:50
  61.6 2.7 %collective-permute-start.6 = (bf16[32,1280]{1,0:T(8,128)(2,1)S(1)}, bf16[32,1280]{1,0:T(8,128)(2,1)S(1)}, u32[]{:S(2)}, u32[]{:S(2)}) collective-permute-start(bf16[32,1280]{1,0:T(8,128)(2,1)S(1)} %shard_map.119.refs_1_.refs_0_), channel_id=1, source_target_pairs={{0,1},{1,0},{2,3},{3,2},{4,5},{5,4},{6,7},{7,6},{8,9},{9,8},{10,11... | collective-permute-start | bytes 245768 | tf_op jit(solution)/shard_map/ppermute | solution.py:50
  63.3 1.3 %collective-permute-start.7 = (bf16[32,1280]{1,0:T(8,128)(2,1)S(1)}, bf16[32,1280]{1,0:T(8,128)(2,1)S(1)}, u32[]{:S(2)}, u32[]{:S(2)}) collective-permute-start(bf16[32,1280]{1,0:T(8,128)(2,1)S(1)} %shard_map.124.refs_1_), channel_id=1, source_target_pairs={{0,1},{1,0},{2,3},{3,2},{4,5},{5,4},{6,7},{7,6},{8,9},{9,8},{10,11... | collective-permute-start | bytes 245768 | tf_op jit(solution)/shard_map/ppermute | solution.py:50
  63.3 6.6 %collective-permute-start.4 = (bf16[2,32,1280]{2,1,0:T(8,128)(2,1)S(1)}, bf16[2,32,1280]{2,1,0:T(8,128)(2,1)S(1)}, u32[]{:S(2)}, u32[]{:S(2)}) collective-permute-start(bf16[2,32,1280]{2,1,0:T(8,128)(2,1)S(1)} %get-tuple-element.28.refs_0_.refs_1_), channel_id=1, source_target_pairs={{0,2},{1,3},{2,0},{3,1},{4,6},{5,7},{6,4},{7,5},{8,10},{9,11},{10,... | collective-permute-start | bytes 491528 | tf_op jit(solution)/shard_map/ppermute | solution.py:50
  64.1 6.9 %collective-permute-start.11 = (bf16[32,2048]{1,0:T(8,128)(2,1)S(1)}, bf16[32,2048]{1,0:T(8,128)(2,1)S(1)}, u32[]{:S(2)}, u32[]{:S(2)}) collective-permute-start(bf16[32,2048]{1,0:T(8,128)(2,1)S(1)} %shard_map.125.refs_5_.refs_0_), channel_id=1, source_target_pairs={{0,1},{1,0},{2,3},{3,2},{4,5},{5,4},{6,7},{7,6},{8,9},{9,8},{10,11... | collective-permute-start | bytes 393224 | tf_op jit(solution)/shard_map/ppermute | solution.py:50
  68.6 2.3 %collective-permute-start.12 = (bf16[32,2048]{1,0:T(8,128)(2,1)S(1)}, bf16[32,2048]{1,0:T(8,128)(2,1)S(1)}, u32[]{:S(2)}, u32[]{:S(2)}) collective-permute-start(bf16[32,2048]{1,0:T(8,128)(2,1)S(1)} %shard_map.128.refs_1_), channel_id=1, source_target_pairs={{0,1},{1,0},{2,3},{3,2},{4,5},{5,4},{6,7},{7,6},{8,9},{9,8},{10,11... | collective-permute-start | bytes 393224 | tf_op jit(solution)/shard_map/ppermute | solution.py:50
  70.0 6.0 %collective-permute-start.9 = (bf16[32,1280]{1,0:T(8,128)(2,1)S(1)}, bf16[32,1280]{1,0:T(8,128)(2,1)S(1)}, u32[]{:S(2)}, u32[]{:S(2)}) collective-permute-start(bf16[32,1280]{1,0:T(8,128)(2,1)S(1)} %shard_map.127.refs_6_.refs_0_), channel_id=1, source_target_pairs={{0,2},{1,3},{2,0},{3,1},{4,6},{5,7},{6,4},{7,5},{8,10},{9,11},{10,... | collective-permute-start | bytes 245768 | tf_op jit(solution)/shard_map/ppermute | solution.py:50
  71.0 5.7 %collective-permute-start.13 = (bf16[32,1280]{1,0:T(8,128)(2,1)S(1)}, bf16[32,1280]{1,0:T(8,128)(2,1)S(1)}, u32[]{:S(2)}, u32[]{:S(2)}) collective-permute-start(bf16[32,1280]{1,0:T(8,128)(2,1)S(1)} %shard_map.127.refs_6_.refs_0_), channel_id=1, source_target_pairs={{0,1},{1,0},{2,3},{3,2},{4,5},{5,4},{6,7},{7,6},{8,9},{9,8},{10,11... | collective-permute-start | bytes 245768 | tf_op jit(solution)/shard_map/ppermute | solution.py:50
  76.0 11.7 %copy-start.5 = (bf16[4,12288]{1,0:T(4,128)(2,1)S(1)}, bf16[4,12288]{1,0:T(4,128)(2,1)}, u32[]{:S(2)}) copy-start(bf16[4,12288]{1,0:T(4,128)(2,1)} %param.16) | copy-start | bytes 294916
  76.1 11.9 %copy-start.3 = (f32[4,48,1]{2,1,0:T(8,128)S(1)}, f32[4,48,1]{2,1,0:T(8,128)}, u32[]{:S(2)}) copy-start(f32[4,48,1]{2,1,0:T(8,128)} %copy-done.2) | copy-start | bytes 2308
  76.1 28.3 %copy-start.1 = (bf16[4,9216]{1,0:T(4,128)(2,1)S(1)}, bf16[4,9216]{1,0:T(4,128)(2,1)}, u32[]{:S(2)}) copy-start(bf16[4,9216]{1,0:T(4,128)(2,1)} %tokens_ref.1) | copy-start | bytes 221188
  76.1 1.5 %collective-permute-start.14 = (bf16[32,1280]{1,0:T(8,128)(2,1)S(1)}, bf16[32,1280]{1,0:T(8,128)(2,1)S(1)}, u32[]{:S(2)}, u32[]{:S(2)}) collective-permute-start(bf16[32,1280]{1,0:T(8,128)(2,1)S(1)} %shard_map.130.refs_1_), channel_id=1, source_target_pairs={{0,1},{1,0},{2,3},{3,2},{4,5},{5,4},{6,7},{7,6},{8,9},{9,8},{10,11... | collective-permute-start | bytes 245768 | tf_op jit(solution)/shard_map/ppermute | solution.py:50
  82.5 21.9 %all-to-all-start.1 = ((bf16[32,4,2304]{2,1,0:T(4,128)(2,1)}), bf16[32,4,2304]{2,1,0:T(4,128)(2,1)S(1)}, u32[]{:S(2)}, u32[]{:S(2)}) async-start(bf16[32,4,2304]{2,1,0:T(4,128)(2,1)} %shard_map.131), calls=%async_computation.1 | async-start | bytes 1179648 | tf_op jit(solution)/shard_map/all_to_all | solution.py:420

commit v7 on v6

--- a/solution.py
+++ b/solution.py
@@ -236,27 +236,17 @@
 
 def down_kernel(start, tile, has_sum, last, gy_ref, *refs):
     hidden, (weight_ref, *refs) = refs[:4], refs[4:]
-    sum_ref = refs.pop(0) if has_sum else None
-    out_ref, slots, sems = refs[-3:]
+    out_ref = refs[-1]
     depth = hidden[0].shape[1]
-    width = weight_ref.shape[1]
-    groups = [
-        [
-            pltpu.make_async_copy(
-                weight_ref.at[pl.ds(start, depth), pl.ds(n * tile, tile)],
-                slots.at[n],
-                sems.at[n],
-            )
-        ]
-        for n in range(width // tile)
-    ]
     x = jnp.concatenate([h[...] for h in hidden], axis=0)
     gy = gy_ref[0]
-    for n in in_turn(groups, 5):
-        columns = slice(n * tile, (n + 1) * tile)
-        value = jnp.dot(x, slots[n], preferred_element_type=F32)
+    for at in range(0, weight_ref.shape[1], tile):
+        columns = slice(at, at + tile)
+        value = jnp.dot(
+            x, weight_ref[start : start + depth, columns], preferred_element_type=F32
+        )
         if has_sum:
-            value = value + sum_ref[:, columns]
+            value = value + refs[0][:, columns]
         if last:
             spread_rows(out_ref, value, gy, columns)
         else:
@@ -267,10 +257,8 @@
     part_rows, depth = hidden[0].shape
     rows = 4 * part_rows
     width = w_down.shape[1]
-    tile = tile_of(width, 256)
-    count = width // tile
-    args = [gy, *[in_vmem(h) for h in hidden], in_hbm(w_down)]
-    in_specs = [SCALARS] + [WHOLE] * 4 + [ANYWHERE]
+    args = [gy, *[in_vmem(h) for h in hidden], in_vmem(w_down)]
+    in_specs = [SCALARS] + [WHOLE] * 5
     if total is not None:
         args.append(in_vmem(total))
         in_specs.append(WHOLE)
@@ -278,15 +266,11 @@
     in_specs.extend([ANYWHERE] * len(after))
     shape = (devices, rows // devices, width) if last else (rows, width)
     return pl.pallas_call(
-        functools.partial(down_kernel, start, tile, total is not None, last),
+        functools.partial(down_kernel, start, tile_of(width, 256), total is not None, last),
         in_specs=in_specs,
         out_specs=WHOLE,
         out_shape=vmem_out(shape, BF16 if last else F32),
-        scratch_shapes=[
-            pltpu.VMEM((count, depth, tile), BF16),
-            pltpu.SemaphoreType.DMA((count,)),
-        ],
-        compiler_params=params(22),
+        compiler_params=params(8),
         cost_estimate=cost(rows * depth * width, depth * width),
     )(*args)
 
@@ -449,20 +433,21 @@
     own_1, across_1 = combine(keep, swap_gy(tie(send, [hidden_0]), 1))
     far_1 = swap_gy(across_1, 2)
     keep, send = project(2, [across_1])
+    hidden_1 = activate(own_1, far_1, [send])
     pieces_0 = back(0, hidden_0, [send])
-    own_2, across_2 = combine(keep, swap_gy(send, 1))
+    own_2, across_2 = combine(keep, swap_gy(tie(send, [hidden_1, pieces_0[1]]), 1))
     far_2 = swap_gy(across_2, 2)
-    hidden_1 = activate(own_1, far_1, [across_2])
+
+    total = through(0, pieces_0, None, [across_2])
+    pieces_1 = back(1, hidden_1, [total])
+    hidden_2 = activate(own_2, far_2, [total])
 
     slab = w_kv.shape[1]
     part = fresh_part(gy, lax.dynamic_slice_in_dim(x, gx * slab, slab, 1), w_kv, devices, send)
-    fresh = jnp.sum(exchange(tie(part, [across_2])), axis=0)
+    fresh = jnp.sum(exchange(tie(part, [hidden_2])), axis=0)
     key_new = fresh[:, :HD].astype(BF16)
     value_new = fresh[:, HD:].astype(BF16)
 
-    total = through(0, pieces_0, None, [hidden_1])
-    pieces_1 = back(1, hidden_1, [total])
-    hidden_2 = activate(own_2, far_2, [total])
     total = through(1, pieces_1, total, [hidden_2])
     pieces_2 = back(2, hidden_2, [total])
     total = through(2, pieces_2, total, [])

time: 106 us -> 118 us (1.11)
  local copies, waits for them, and re-layouts: 3.13 us -> 16.6 us
  Pallas kernels: 43.7 us -> 33.4 us
  waiting for transfers between devices: 32.9 us -> 42.8 us
    unnamed x14 -> x26, local copies, waits for them, and re-layouts: 2.91 us -> 16.4 us
    pallas_call x3, Pallas kernels: 13.9 us -> 4.18 us  [down(): pl.pallas_call(functools.partial(down_kernel, start, tile_of(width, 256),...]
    ppermute x15, waiting for transfers between devices: 9.34 us -> 18.6 us  [swap(): return lax.ppermute(x, axis, [(i, i ^ bits) for i in range(size)])]
  transfers between devices with their start and end apart: 18 -> 18, of which waited for: 9 -> 12; matrix products, arithmetic and copies ran while one was open for 2% -> 2% of each run, Pallas kernels for 28% -> 21%
where the time goes in v7:
time: 118 us
  waiting for transfers between devices  42.8 us (36%)
  Pallas kernels  33.4 us (28%)
  starting transfers between devices  23.6 us (20%)
  local copies, waits for them, and re-layouts  16.6 us (14%)
    all_to_all x3, waiting for transfers between devices, body(): lax.all_to_all(x, ('gx', 'gy'), split_axis=0, concat_axis=0, tiled=True)  24.2 us
    pallas_call x3, Pallas kernels, gate_up(): pl.pallas_call(functools.partial(gate_up_kernel, start, tile, len(after))...  18.6 us
    ppermute x15, waiting for transfers between devices, swap(): return lax.ppermute(x, axis, [(i, i ^ bits) for i in range(size)])  18.6 us
    unnamed x26, local copies, waits for them, and re-layouts  16.4 us
    all_to_all x3, starting transfers between devices, body(): lax.all_to_all(x, ('gx', 'gy'), split_axis=0, concat_axis=0, tiled=True)  15.6 us
    ppermute x15, starting transfers between devices, swap(): return lax.ppermute(x, axis, [(i, i ^ bits) for i in range(size)])  8.02 us
    pallas_call x1, Pallas kernels, attend_cache(): pl.pallas_call(functools.partial(cache_kernel, 1.0 / math.sqrt(depth)), i...  6.31 us
    pallas_call x3, Pallas kernels, down(): pl.pallas_call(functools.partial(down_kernel, start, tile_of(width, 256),...  4.18 us
  transfers between devices with their start and end apart: 18, of which 12 were waited for; matrix products, arithmetic and copies ran while one was open for 2% of the time, Pallas kernels for 21%

profile of v7, /device:TPU:0, one launch (start us, length us, event | category | flops | bytes accessed | tf_op | source)
XLA Modules:
  0.0 117.9 jit_solution(3530387888645050796)
XLA Ops:
  0.6 2.1 %shard_map.113.after_ref = bf16[8,4,4,2304]{3,2,1,0:T(4,128)(2,1)} custom-call(bf16[4,9216]{1,0:T(4,128)(2,1)} %tokens_ref.1, f32[1,9216]{1,0:T(1,128)} %bitcast.25), custom_call_target="tpu_custom_call" | custom-call | flops 368640 | bytes 589824 | tf_op jit(solution)/shard_map/pallas_call | solution.py:80
  2.7 7.3 %all-to-all-start = ((bf16[32,4,2304]{2,1,0:T(4,128)(2,1)}), bf16[32,4,2304]{2,1,0:T(4,128)(2,1)S(1)}, u32[]{:S(2)}, u32[]{:S(2)}) async-start(bf16[32,4,2304]{2,1,0:T(4,128)(2,1)} %bitcast.2), calls=%async_computation | async-start | bytes 1179648 | tf_op jit(solution)/shard_map/all_to_all | solution.py:404
  10.0 0.9 copy.28
  11.6 6.3 %shard_map.114 = (f32[4,48,256]{2,1,0:T(8,128)S(1)}, f32[4,48,1]{2,1,0:T(8,128)S(1)}, f32[4,48,1]{2,1,0:T(8,128)S(1)}) custom-call(s32[4]{0:T(128)S(1)} %copy-done.4, bf16[4,48,256]{2,1,0:T(8,128)(2,1)S(1)} %bitcast.21, bf16[4,2048,256]{2,1,0:T(8,128)(2,1)} %key_ref.1, bf16[4,2048,256]{2,1,0:T(8,128)(2,1)} %value_ref.1, ...), custom_call_target="tpu_custom_call" | custom-call | flops 603979776 | bytes 8388608 | tf_op jit(solution)/shard_map/pallas_call | solution.py:358
  17.9 8.8 %all-to-all-done.rows_ref = bf16[32,4,2304]{2,1,0:T(4,128)(2,1)S(1)} async-done(((bf16[32,4,2304]{2,1,0:T(4,128)(2,1)}), bf16[32,4,2304]{2,1,0:T(4,128)(2,1)S(1)}, u32[]{:S(2)}, u32[]{:S(2)}) %all-to-all-start) | async-done | bytes 589856 | tf_op jit(solution)/shard_map/all_to_all | solution.py:404
  26.9 5.3 %shard_map.116 = (f32[2,64,1280]{2,1,0:T(8,128)S(1)}, bf16[2,64,1280]{2,1,0:T(8,128)(2,1)S(1)}) custom-call(bf16[128,2304]{1,0:T(8,128)(2,1)S(1)} %shard_map.115.x_ref, bf16[2304,4608]{1,0:T(8,128)(2,1)} %gate_ref.5, bf16[2304,4608]{1,0:T(8,128)(2,1)} %up_ref.5), custom_call_target="tpu_custom_call" | custom-call | flops 377487360 | bytes 2949120 | tf_op jit(solution)/shard_map/pallas_call | solution.py:187
  32.3 1.6 %collective-permute-done.core_ref = bf16[2,64,1280]{2,1,0:T(8,128)(2,1)S(1)} collective-permute-done((bf16[2,64,1280]{2,1,0:T(8,128)(2,1)S(1)}, bf16[2,64,1280]{2,1,0:T(8,128)(2,1)S(1)}, u32[]{:S(2)}, u32[]{:S(2)}) %collective-permute-start) | collective-permute-done | bytes 327712 | tf_op jit(solution)/shard_map/ppermute | solution.py:50
  34.0 1.2 %collective-permute-start.1 = (bf16[2,32,1280]{2,1,0:T(8,128)(2,1)S(1)}, bf16[2,32,1280]{2,1,0:T(8,128)(2,1)S(1)}, u32[]{:S(2)}, u32[]{:S(2)}) collective-permute-start(bf16[2,32,1280]{2,1,0:T(8,128)(2,1)S(1)} %get-tuple-element.20.refs_0_), channel_id=1, source_target_pairs={{0,2},{1,3},{2,0},{3,1},{4,6},{5,7},{6,4},{7,5},{8,10},{9,11},{10,... | collective-permute-start | bytes 491528 | tf_op jit(solution)/shard_map/ppermute | solution.py:50
  35.2 7.5 %shard_map.118 = (f32[2,64,2048]{2,1,0:T(8,128)S(1)}, bf16[2,64,2048]{2,1,0:T(8,128)(2,1)S(1)}) custom-call(bf16[128,2304]{1,0:T(8,128)(2,1)S(1)} %shard_map.115.x_ref, bf16[2304,4608]{1,0:T(8,128)(2,1)} %gate_ref.5, bf16[2304,4608]{1,0:T(8,128)(2,1)} %up_ref.5, bf16[2,32,1280]{2,1,0:T(8,128)(2,1)S(1)} %get-tuple-element.20.refs_0_), custom_call_target="tpu_custom_call" | custom-call | flops 603979776 | bytes 4718592 | tf_op jit(solution)/shard_map/pallas_call | solution.py:187
  43.0 1.8 %collective-permute-done.2.core_ref = bf16[2,64,2048]{2,1,0:T(8,128)(2,1)S(1)} collective-permute-done((bf16[2,64,2048]{2,1,0:T(8,128)(2,1)S(1)}, bf16[2,64,2048]{2,1,0:T(8,128)(2,1)S(1)}, u32[]{:S(2)}, u32[]{:S(2)}) %collective-permute-start.2) | collective-permute-done | bytes 524320 | tf_op jit(solution)/shard_map/ppermute | solution.py:50
  44.9 1.0 collective-permute-start.3
  45.8 1.1 collective-permute-start.4
  47.2 5.8 %shard_map.122 = (f32[2,64,1280]{2,1,0:T(8,128)S(1)}, bf16[2,64,1280]{2,1,0:T(8,128)(2,1)S(1)}) custom-call(bf16[128,2304]{1,0:T(8,128)(2,1)S(1)} %shard_map.115.x_ref, bf16[2304,4608]{1,0:T(8,128)(2,1)} %gate_ref.5, bf16[2304,4608]{1,0:T(8,128)(2,1)} %up_ref.5, bf16[2,32,2048]{2,1,0:T(8,128)(2,1)S(1)} %get-tuple-element.24.refs_0_), custom_call_target="tpu_custom_call" | custom-call | flops 377487360 | bytes 2949120 | tf_op jit(solution)/shard_map/pallas_call | solution.py:187
  52.9 2.1 %collective-permute-done.4.refs_0_ = bf16[32,1280]{1,0:T(8,128)(2,1)S(1)} collective-permute-done((bf16[32,1280]{1,0:T(8,128)(2,1)S(1)}, bf16[32,1280]{1,0:T(8,128)(2,1)S(1)}, u32[]{:S(2)}, u32[]{:S(2)}) %collective-permute-start.4) | collective-permute-done | bytes 81952 | tf_op jit(solution)/shard_map/ppermute | solution.py:50
  55.1 0.9 shard_map.134.refs_0_
  56.2 1.6 %collective-permute-done.5.core_ref = bf16[2,64,1280]{2,1,0:T(8,128)(2,1)S(1)} collective-permute-done((bf16[2,64,1280]{2,1,0:T(8,128)(2,1)S(1)}, bf16[2,64,1280]{2,1,0:T(8,128)(2,1)S(1)}, u32[]{:S(2)}, u32[]{:S(2)}) %collective-permute-start.5) | collective-permute-done | bytes 327712 | tf_op jit(solution)/shard_map/ppermute | solution.py:50
  57.9 1.0 collective-permute-start.6
  59.3 0.8 collective-permute-done.7.refs_2_
  60.3 1.0 shard_map.127.refs_0_.refs_1_.refs_5_
  61.3 2.9 %collective-permute-done.6.far_ref = bf16[2,32,1280]{2,1,0:T(8,128)(2,1)S(1)} collective-permute-done((bf16[2,32,1280]{2,1,0:T(8,128)(2,1)S(1)}, bf16[2,32,1280]{2,1,0:T(8,128)(2,1)S(1)}, u32[]{:S(2)}, u32[]{:S(2)}) %collective-permute-start.6) | collective-permute-done | bytes 163872 | tf_op jit(solution)/shard_map/ppermute | solution.py:50
  64.2 2.9 %all-to-all-start.2 = ((f32[32,4,512]{2,1,0:T(4,128)}), f32[32,4,512]{2,1,0:T(4,128)S(1)}, u32[]{:S(2)}, u32[]{:S(2)}) async-start(f32[32,4,512]{2,1,0:T(4,128)} %shard_map.135), calls=%async_computation.2 | async-start | bytes 524288 | tf_op jit(solution)/shard_map/all_to_all | solution.py:404
  67.2 1.7 %collective-permute-start.10 = (bf16[32,2048]{1,0:T(8,128)(2,1)S(1)}, bf16[32,2048]{1,0:T(8,128)(2,1)S(1)}, u32[]{:S(2)}, u32[]{:S(2)}) collective-permute-start(bf16[32,2048]{1,0:T(8,128)(2,1)S(1)} %shard_map.123.refs_1_.refs_0_), channel_id=1, source_target_pairs={{0,2},{1,3},{2,0},{3,1},{4,6},{5,7},{6,4},{7,5},{8,10},{9,11},{10,... | collective-permute-start | bytes 393224 | tf_op jit(solution)/shard_map/ppermute | solution.py:50
  68.8 6.2 %collective-permute-done.10.refs_0_ = bf16[32,2048]{1,0:T(8,128)(2,1)S(1)} collective-permute-done((bf16[32,2048]{1,0:T(8,128)(2,1)S(1)}, bf16[32,2048]{1,0:T(8,128)(2,1)S(1)}, u32[]{:S(2)}, u32[]{:S(2)}) %collective-permute-start.10) | collective-permute-done | bytes 131104 | tf_op jit(solution)/shard_map/ppermute | solution.py:50
  75.0 0.9 collective-permute-start.9
  76.4 7.0 %copy-done = bf16[4608,2304]{1,0:T(8,128)(2,1)S(1)} copy-done((bf16[4608,2304]{1,0:T(8,128)(2,1)S(1)}, bf16[4608,2304]{1,0:T(8,128)(2,1)}, u32[]{:S(2)}) %copy-start) | copy-done | bytes 21233688
  83.4 1.4 %shard_map.130.refs_1_.refs_5_ = f32[128,2304]{1,0:T(8,128)S(1)} custom-call(s32[1]{0:T(128)} %bitcast.gy_ref, bf16[32,2048]{1,0:T(8,128)(2,1)S(1)} %shard_map.123.refs_1_.refs_0_, bf16[32,2048]{1,0:T(8,128)(2,1)S(1)} %shard_map.129.refs_1_, bf16[32,2048]{1,0:T(8,128)(2,1)S(1)} %collective-permute-done.11.refs_2_, ...), custom_call_target="tpu_custom_call" | custom-call | flops 603979776 | bytes 4718592 | tf_op jit(solution)/shard_map/pallas_call | solution.py:268
  85.1 1.1 collective-permute-done.14.refs_3_
  86.2 7.0 %copy-done.1 = bf16[4608,2304]{1,0:T(8,128)(2,1)S(1)} copy-done((bf16[4608,2304]{1,0:T(8,128)(2,1)S(1)}, bf16[4608,2304]{1,0:T(8,128)(2,1)}, u32[]{:S(2)}) %copy-start.1) | copy-done | bytes 21233688
  93.3 1.8 %shard_map.132 = bf16[32,4,2304]{2,1,0:T(4,128)(2,1)} custom-call(s32[1]{0:T(128)} %bitcast.gy_ref, bf16[32,1280]{1,0:T(8,128)(2,1)S(1)} %shard_map.128.refs_6_.refs_0_.refs_1_, bf16[32,1280]{1,0:T(8,128)(2,1)S(1)} %shard_map.131.refs_1_, bf16[32,1280]{1,0:T(8,128)(2,1)S(1)} %collective-permute-done.13.refs_2_, ...), custom_call_target="tpu_custom_call" | custom-call | flops 377487360 | bytes 2949120 | tf_op jit(solution)/shard_map/pallas_call | solution.py:268
  95.1 5.4 %all-to-all-start.1 = ((bf16[32,4,2304]{2,1,0:T(4,128)(2,1)}), bf16[32,4,2304]{2,1,0:T(4,128)(2,1)S(1)}, u32[]{:S(2)}, u32[]{:S(2)}) async-start(bf16[32,4,2304]{2,1,0:T(4,128)(2,1)} %shard_map.132), calls=%async_computation.1 | async-start | bytes 1179648 | tf_op jit(solution)/shard_map/all_to_all | solution.py:404
  101.8 15.4 %all-to-all-done.1 = bf16[32,4,2304]{2,1,0:T(4,128)(2,1)S(1)} async-done(((bf16[32,4,2304]{2,1,0:T(4,128)(2,1)}), bf16[32,4,2304]{2,1,0:T(4,128)(2,1)S(1)}, u32[]{:S(2)}, u32[]{:S(2)}) %all-to-all-start.1) | async-done | bytes 589856 | tf_op jit(solution)/shard_map/all_to_all | solution.py:404
  117.2 0.7 shard_map.133
  (62 shorter events, 4.3 us)
Async XLA Ops:
  2.7 24.0 %all-to-all-start = ((bf16[32,4,2304]{2,1,0:T(4,128)(2,1)}), bf16[32,4,2304]{2,1,0:T(4,128)(2,1)S(1)}, u32[]{:S(2)}, u32[]{:S(2)}) async-start(bf16[32,4,2304]{2,1,0:T(4,128)(2,1)} %bitcast.2), calls=%async_computation | async-start | bytes 1179648 | tf_op jit(solution)/shard_map/all_to_all | solution.py:404
  11.0 0.7 copy-start.4
  32.2 1.7 %collective-permute-start = (bf16[2,64,1280]{2,1,0:T(8,128)(2,1)S(1)}, bf16[2,64,1280]{2,1,0:T(8,128)(2,1)S(1)}, u32[]{:S(2)}, u32[]{:S(2)}) collective-permute-start(bf16[2,64,1280]{2,1,0:T(8,128)(2,1)S(1)} %get-tuple-element.19), channel_id=1, source_target_pairs={{0,1},{1,0},{2,3},{3,2},{4,5},{5,4},{6,7},{7,6},{8,9},{9,8},{10,11... | collective-permute-start | bytes 983048 | tf_op jit(solution)/shard_map/ppermute | solution.py:50
  34.0 8.8 %collective-permute-start.1 = (bf16[2,32,1280]{2,1,0:T(8,128)(2,1)S(1)}, bf16[2,32,1280]{2,1,0:T(8,128)(2,1)S(1)}, u32[]{:S(2)}, u32[]{:S(2)}) collective-permute-start(bf16[2,32,1280]{2,1,0:T(8,128)(2,1)S(1)} %get-tuple-element.20.refs_0_), channel_id=1, source_target_pairs={{0,2},{1,3},{2,0},{3,1},{4,6},{5,7},{6,4},{7,5},{8,10},{9,11},{10,... | collective-permute-start | bytes 491528 | tf_op jit(solution)/shard_map/ppermute | solution.py:50
  42.8 2.0 %collective-permute-start.2 = (bf16[2,64,2048]{2,1,0:T(8,128)(2,1)S(1)}, bf16[2,64,2048]{2,1,0:T(8,128)(2,1)S(1)}, u32[]{:S(2)}, u32[]{:S(2)}) collective-permute-start(bf16[2,64,2048]{2,1,0:T(8,128)(2,1)S(1)} %shard_map.120), channel_id=1, source_target_pairs={{0,1},{1,0},{2,3},{3,2},{4,5},{5,4},{6,7},{7,6},{8,9},{9,8},{10,11... | collective-permute-start | bytes 1572872 | tf_op jit(solution)/shard_map/ppermute | solution.py:50
  44.9 11.1 %collective-permute-start.3 = (bf16[2,32,2048]{2,1,0:T(8,128)(2,1)S(1)}, bf16[2,32,2048]{2,1,0:T(8,128)(2,1)S(1)}, u32[]{:S(2)}, u32[]{:S(2)}) collective-permute-start(bf16[2,32,2048]{2,1,0:T(8,128)(2,1)S(1)} %get-tuple-element.24.refs_0_), channel_id=1, source_target_pairs={{0,2},{1,3},{2,0},{3,1},{4,6},{5,7},{6,4},{7,5},{8,10},{9,11},{10,... | collective-permute-start | bytes 786440 | tf_op jit(solution)/shard_map/ppermute | solution.py:50
  45.8 9.2 %collective-permute-start.4 = (bf16[32,1280]{1,0:T(8,128)(2,1)S(1)}, bf16[32,1280]{1,0:T(8,128)(2,1)S(1)}, u32[]{:S(2)}, u32[]{:S(2)}) collective-permute-start(bf16[32,1280]{1,0:T(8,128)(2,1)S(1)} %shard_map.119.refs_1_.refs_0_), channel_id=1, source_target_pairs={{0,2},{1,3},{2,0},{3,1},{4,6},{5,7},{6,4},{7,5},{8,10},{9,11},{10,... | collective-permute-start | bytes 245768 | tf_op jit(solution)/shard_map/ppermute | solution.py:50
  47.0 13.3 %slice-start = ((s8[21233664]{0:T(1024)(128)(4,1)}), s8[4194304]{0:T(1024)(128)(4,1)S(1)}, s32[]{:S(2)}) async-start(s8[21233664]{0:T(1024)(128)(4,1)} %bitcast.18), calls=%async_computation.3 | async-start | bytes 8388608
  47.1 8.0 %copy-start.2 = (bf16[1,288,512]{2,1,0:T(8,128)(2,1)S(1)}, bf16[1,288,512]{2,1,0:T(8,128)(2,1)}, u32[]{:S(2)}) copy-start(bf16[1,288,512]{2,1,0:T(8,128)(2,1)} %weight_ref.1) | copy-start | bytes 884740
  47.1 13.2 %slice-start.1 = ((s8[21233664]{0:T(1024)(128)(4,1)}), s8[4194304]{0:T(1024)(128)(4,1)S(1)}, s32[]{:S(2)}) async-start(s8[21233664]{0:T(1024)(128)(4,1)} %bitcast.18), calls=%async_computation.4 | async-start | bytes 8388608
  47.1 13.1 %slice-start.2 = ((s8[21233664]{0:T(1024)(128)(4,1)}), s8[4194304]{0:T(1024)(128)(4,1)S(1)}, s32[]{:S(2)}) async-start(s8[21233664]{0:T(1024)(128)(4,1)} %bitcast.18), calls=%async_computation.5 | async-start | bytes 8388608
  47.1 13.1 %slice-start.3 = ((s8[21233664]{0:T(1024)(128)(4,1)}), s8[4194304]{0:T(1024)(128)(4,1)S(1)}, s32[]{:S(2)}) async-start(s8[21233664]{0:T(1024)(128)(4,1)} %bitcast.18), calls=%async_computation.6 | async-start | bytes 8388608
  47.1 13.1 %slice-start.4 = ((s8[21233664]{0:T(1024)(128)(4,1)}), s8[4194304]{0:T(1024)(128)(4,1)S(1)}, s32[]{:S(2)}) async-start(s8[21233664]{0:T(1024)(128)(4,1)} %bitcast.18), calls=%async_computation.7 | async-start | bytes 8388608
  47.1 13.1 %slice-start.5 = ((s8[21233664]{0:T(1024)(128)(4,1)}), s8[262144]{0:T(1024)(128)(4,1)S(1)}, s32[]{:S(2)}) async-start(s8[21233664]{0:T(1024)(128)(4,1)} %bitcast.18), calls=%async_computation.8 | async-start | bytes 524288
  56.1 1.7 %collective-permute-start.5 = (bf16[2,64,1280]{2,1,0:T(8,128)(2,1)S(1)}, bf16[2,64,1280]{2,1,0:T(8,128)(2,1)S(1)}, u32[]{:S(2)}, u32[]{:S(2)}) collective-permute-start(bf16[2,64,1280]{2,1,0:T(8,128)(2,1)S(1)} %shard_map.125), channel_id=1, source_target_pairs={{0,1},{1,0},{2,3},{3,2},{4,5},{5,4},{6,7},{7,6},{8,9},{9,8},{10,11... | collective-permute-start | bytes 983048 | tf_op jit(solution)/shard_map/ppermute | solution.py:50
  57.9 6.3 %collective-permute-start.6 = (bf16[2,32,1280]{2,1,0:T(8,128)(2,1)S(1)}, bf16[2,32,1280]{2,1,0:T(8,128)(2,1)S(1)}, u32[]{:S(2)}, u32[]{:S(2)}) collective-permute-start(bf16[2,32,1280]{2,1,0:T(8,128)(2,1)S(1)} %get-tuple-element.29.refs_5_), channel_id=1, source_target_pairs={{0,2},{1,3},{2,0},{3,1},{4,6},{5,7},{6,4},{7,5},{8,10},{9,11},{10,... | collective-permute-start | bytes 491528 | tf_op jit(solution)/shard_map/ppermute | solution.py:50
  58.8 1.3 %collective-permute-start.7 = (bf16[32,1280]{1,0:T(8,128)(2,1)S(1)}, bf16[32,1280]{1,0:T(8,128)(2,1)S(1)}, u32[]{:S(2)}, u32[]{:S(2)}) collective-permute-start(bf16[32,1280]{1,0:T(8,128)(2,1)S(1)} %shard_map.119.refs_1_.refs_0_), channel_id=1, source_target_pairs={{0,1},{1,0},{2,3},{3,2},{4,5},{5,4},{6,7},{7,6},{8,9},{9,8},{10,11... | collective-permute-start | bytes 245768 | tf_op jit(solution)/shard_map/ppermute | solution.py:50
  58.8 1.4 %collective-permute-start.8 = (bf16[32,1280]{1,0:T(8,128)(2,1)S(1)}, bf16[32,1280]{1,0:T(8,128)(2,1)S(1)}, u32[]{:S(2)}, u32[]{:S(2)}) collective-permute-start(bf16[32,1280]{1,0:T(8,128)(2,1)S(1)} %shard_map.124.refs_2_.refs_1_), channel_id=1, source_target_pairs={{0,1},{1,0},{2,3},{3,2},{4,5},{5,4},{6,7},{7,6},{8,9},{9,8},{10,11... | collective-permute-start | bytes 245768 | tf_op jit(solution)/shard_map/ppermute | solution.py:50
  64.2 30.8 %all-to-all-start.2 = ((f32[32,4,512]{2,1,0:T(4,128)}), f32[32,4,512]{2,1,0:T(4,128)S(1)}, u32[]{:S(2)}, u32[]{:S(2)}) async-start(f32[32,4,512]{2,1,0:T(4,128)} %shard_map.135), calls=%async_computation.2 | async-start | bytes 524288 | tf_op jit(solution)/shard_map/all_to_all | solution.py:404
  67.2 7.8 %collective-permute-start.10 = (bf16[32,2048]{1,0:T(8,128)(2,1)S(1)}, bf16[32,2048]{1,0:T(8,128)(2,1)S(1)}, u32[]{:S(2)}, u32[]{:S(2)}) collective-permute-start(bf16[32,2048]{1,0:T(8,128)(2,1)S(1)} %shard_map.123.refs_1_.refs_0_), channel_id=1, source_target_pairs={{0,2},{1,3},{2,0},{3,1},{4,6},{5,7},{6,4},{7,5},{8,10},{9,11},{10,... | collective-permute-start | bytes 393224 | tf_op jit(solution)/shard_map/ppermute | solution.py:50
  68.8 7.3 %collective-permute-start.11 = (bf16[32,2048]{1,0:T(8,128)(2,1)S(1)}, bf16[32,2048]{1,0:T(8,128)(2,1)S(1)}, u32[]{:S(2)}, u32[]{:S(2)}) collective-permute-start(bf16[32,2048]{1,0:T(8,128)(2,1)S(1)} %shard_map.123.refs_1_.refs_0_), channel_id=1, source_target_pairs={{0,1},{1,0},{2,3},{3,2},{4,5},{5,4},{6,7},{7,6},{8,9},{9,8},{10,11... | collective-permute-start | bytes 393224 | tf_op jit(solution)/shard_map/ppermute | solution.py:50
  75.0 1.3 %collective-permute-start.12 = (bf16[32,2048]{1,0:T(8,128)(2,1)S(1)}, bf16[32,2048]{1,0:T(8,128)(2,1)S(1)}, u32[]{:S(2)}, u32[]{:S(2)}) collective-permute-start(bf16[32,2048]{1,0:T(8,128)(2,1)S(1)} %shard_map.129.refs_1_), channel_id=1, source_target_pairs={{0,1},{1,0},{2,3},{3,2},{4,5},{5,4},{6,7},{7,6},{8,9},{9,8},{10,11... | collective-permute-start | bytes 393224 | tf_op jit(solution)/shard_map/ppermute | solution.py:50
  75.0 9.8 %collective-permute-start.9 = (bf16[32,1280]{1,0:T(8,128)(2,1)S(1)}, bf16[32,1280]{1,0:T(8,128)(2,1)S(1)}, u32[]{:S(2)}, u32[]{:S(2)}) collective-permute-start(bf16[32,1280]{1,0:T(8,128)(2,1)S(1)} %shard_map.128.refs_6_.refs_0_.refs_1_), channel_id=1, source_target_pairs={{0,2},{1,3},{2,0},{3,1},{4,6},{5,7},{6,4},{7,5},{8,10},{9,11},{10,... | collective-permute-start | bytes 245768 | tf_op jit(solution)/shard_map/ppermute | solution.py:50
  75.9 9.2 %collective-permute-start.13 = (bf16[32,1280]{1,0:T(8,128)(2,1)S(1)}, bf16[32,1280]{1,0:T(8,128)(2,1)S(1)}, u32[]{:S(2)}, u32[]{:S(2)}) collective-permute-start(bf16[32,1280]{1,0:T(8,128)(2,1)S(1)} %shard_map.128.refs_6_.refs_0_.refs_1_), channel_id=1, source_target_pairs={{0,1},{1,0},{2,3},{3,2},{4,5},{5,4},{6,7},{7,6},{8,9},{9,8},{10,11... | collective-permute-start | bytes 245768 | tf_op jit(solution)/shard_map/ppermute | solution.py:50
  76.3 7.0 %copy-start = (bf16[4608,2304]{1,0:T(8,128)(2,1)S(1)}, bf16[4608,2304]{1,0:T(8,128)(2,1)}, u32[]{:S(2)}) copy-start(bf16[4608,2304]{1,0:T(8,128)(2,1)} %refs_4_.5) | copy-start | bytes 63700996
  84.9 15.7 %copy-start.5 = (bf16[4,12288]{1,0:T(4,128)(2,1)S(1)}, bf16[4,12288]{1,0:T(4,128)(2,1)}, u32[]{:S(2)}) copy-start(bf16[4,12288]{1,0:T(4,128)(2,1)} %param.16) | copy-start | bytes 294916
  84.9 32.3 %copy-start.3 = (bf16[4,9216]{1,0:T(4,128)(2,1)S(1)}, bf16[4,9216]{1,0:T(4,128)(2,1)}, u32[]{:S(2)}) copy-start(bf16[4,9216]{1,0:T(4,128)(2,1)} %tokens_ref.1) | copy-start | bytes 221188
  84.9 1.3 %collective-permute-start.14 = (bf16[32,1280]{1,0:T(8,128)(2,1)S(1)}, bf16[32,1280]{1,0:T(8,128)(2,1)S(1)}, u32[]{:S(2)}, u32[]{:S(2)}) collective-permute-start(bf16[32,1280]{1,0:T(8,128)(2,1)S(1)} %shard_map.131.refs_1_), channel_id=1, source_target_pairs={{0,1},{1,0},{2,3},{3,2},{4,5},{5,4},{6,7},{7,6},{8,9},{9,8},{10,11... | collective-permute-start | bytes 245768 | tf_op jit(solution)/shard_map/ppermute | solution.py:50
  86.2 7.0 %copy-start.1 = (bf16[4608,2304]{1,0:T(8,128)(2,1)S(1)}, bf16[4608,2304]{1,0:T(8,128)(2,1)}, u32[]{:S(2)}) copy-start(bf16[4608,2304]{1,0:T(8,128)(2,1)} %refs_4_.5) | copy-start | bytes 63700996
  95.1 22.1 %all-to-all-start.1 = ((bf16[32,4,2304]{2,1,0:T(4,128)(2,1)}), bf16[32,4,2304]{2,1,0:T(4,128)(2,1)S(1)}, u32[]{:S(2)}, u32[]{:S(2)}) async-start(bf16[32,4,2304]{2,1,0:T(4,128)(2,1)} %shard_map.132), calls=%async_computation.1 | async-start | bytes 1179648 | tf_op jit(solution)/shard_map/all_to_all | solution.py:404

commit v8 on v7

--- a/solution.py
+++ b/solution.py
@@ -171,7 +171,7 @@
             ]
         )
     x = x_ref[...]
-    for n in in_turn(groups, 3):
+    for n in in_turn(groups, len(groups)):
         columns = slice(n * tile, (n + 1) * tile)
         for k in range(2):
             value = jnp.dot(x, slots[k, n], preferred_element_type=F32)
@@ -296,23 +296,53 @@
     )(in_vmem(tokens), in_vmem(sums))
 
 
-def fresh_kernel(gy_ref, x_ref, weight_ref, after_ref, out_ref):
+def place_of(q, gx, gy, n_gx):
+    blocks = n_gx // 4
+    group = gx ^ q
+    turn = (group // blocks) ^ gy
+    return (((turn & 1) << 1) | (turn >> 1)) * blocks + group % blocks
+
+
+def fresh_kernel(gx_ref, gy_ref, x_ref, weight_ref, after_ref, near_ref, far_ref, rows_ref):
     del after_ref
     value = jnp.dot(x_ref[...], weight_ref[0], preferred_element_type=F32)
-    spread_rows(out_ref, value, gy_ref[0])
-
-
-def fresh_part(gy, x, w_kv, devices, after):
+    rows_ref[...] = value.reshape(rows_ref.shape)
+    n_gx = rows_ref.shape[0]
+    for q in range(n_gx):
+        out_ref = (near_ref, far_ref)[q % 2]
+        out_ref[q // 2] = rows_ref[place_of(q, gx_ref[0], gy_ref[0], n_gx)]
+
+
+def fresh_part(gx, gy, x, w_kv, n_gx, after):
     rows, depth = x.shape
     columns = w_kv.shape[2]
+    shape = (n_gx // 2, rows // n_gx, columns)
     return pl.pallas_call(
         fresh_kernel,
-        in_specs=[SCALARS, WHOLE, WHOLE, ANYWHERE],
-        out_specs=WHOLE,
-        out_shape=vmem_out((devices, rows // devices, columns), F32),
+        in_specs=[SCALARS, SCALARS, WHOLE, WHOLE, ANYWHERE],
+        out_specs=[WHOLE, WHOLE],
+        out_shape=[vmem_out(shape, F32), vmem_out(shape, F32)],
+        scratch_shapes=[pltpu.VMEM((n_gx, rows // n_gx, columns), F32)],
         compiler_params=params(8),
         cost_estimate=cost(2 * rows * depth * columns, 2 * depth * columns),
-    )(gy, in_vmem(x), in_vmem(w_kv), after)
+    )(gx, gy, in_vmem(x), in_vmem(w_kv), after)
+
+
+def own_first_kernel(gy_ref, sums_ref, near_ref, far_ref):
+    for at, turn in enumerate(ORDER):
+        (near_ref, far_ref)[at // 2][at % 2] = sums_ref[gy_ref[0] ^ turn]
+
+
+def own_first(gy, sums):
+    shape = (2, *sums.shape[1:])
+    return pl.pallas_call(
+        own_first_kernel,
+        in_specs=[SCALARS, WHOLE],
+        out_specs=[WHOLE, WHOLE],
+        out_shape=[vmem_out(shape, sums.dtype), vmem_out(shape, sums.dtype)],
+        compiler_params=params(4),
+        cost_estimate=cost(sums.size, 8 * sums.size),
+    )(gy, in_vmem(sums))
 
 
 def cache_kernel(
@@ -400,6 +430,8 @@
 def body(n_gx, n_gy, tokens, gain, w_gate, w_up, w_down, w_kv, queries, key_cache, value_cache, lengths):
     gx = lax.axis_index("gx")
     gy = lax.axis_index("gy").astype(jnp.int32).reshape(1)
+    gx_row = gx.astype(jnp.int32).reshape(1)
+    swap_gx = lambda x, bits: swap(x, "gx", n_gx, bits)
     swap_gy = lambda x, bits: swap(x, "gy", n_gy, bits)
     exchange = lambda x: lax.all_to_all(x, ("gx", "gy"), split_axis=0, concat_axis=0, tiled=True)
     devices = n_gx * n_gy
@@ -426,10 +458,19 @@
         return down(gy, pieces, w_down, starts[c], total, devices, last, after)
 
     keep, send = project(0, [])
+    slab = w_kv.shape[1]
+    near_kv, far_kv = fresh_part(
+        gx_row, gy, lax.dynamic_slice_in_dim(x, gx * slab, slab, 1), w_kv, n_gx, send
+    )
+    far_kv = swap_gx(far_kv, 1)
     own_0, across_0 = combine(keep, swap_gy(send, 1))
     far_0 = swap_gy(across_0, 2)
     keep, send = project(1, [across_0])
     hidden_0 = activate(own_0, far_0, [send])
+    near_kv = near_kv + tie(far_kv, [send])
+    group_kv = near_kv[0]
+    for t in range(1, n_gx // 2):
+        group_kv = group_kv + swap_gx(near_kv[t], 2 * t)
     own_1, across_1 = combine(keep, swap_gy(tie(send, [hidden_0]), 1))
     far_1 = swap_gy(across_1, 2)
     keep, send = project(2, [across_1])
@@ -438,17 +479,17 @@
     own_2, across_2 = combine(keep, swap_gy(tie(send, [hidden_1, pieces_0[1]]), 1))
     far_2 = swap_gy(across_2, 2)
 
-    total = through(0, pieces_0, None, [across_2])
-    pieces_1 = back(1, hidden_1, [total])
-    hidden_2 = activate(own_2, far_2, [total])
-
-    slab = w_kv.shape[1]
-    part = fresh_part(gy, lax.dynamic_slice_in_dim(x, gx * slab, slab, 1), w_kv, devices, send)
-    fresh = jnp.sum(exchange(tie(part, [hidden_2])), axis=0)
+    hidden_2 = activate(own_2, far_2, [])
+    pieces_1 = back(1, tie(hidden_1, [across_2]), [hidden_2])
+
+    own_kv, other_kv = own_first(gy, tie(group_kv, [send]).reshape(n_gy, batch, -1))
+    own_kv = own_kv + swap_gy(other_kv, 1)
+    fresh = own_kv[0] + swap_gy(tie(own_kv[1], [hidden_2]), 2)
     key_new = fresh[:, :HD].astype(BF16)
     value_new = fresh[:, HD:].astype(BF16)
 
-    total = through(1, pieces_1, total, [hidden_2])
+    total = through(0, pieces_0, None, [hidden_2])
+    total = through(1, pieces_1, total, [])
     pieces_2 = back(2, hidden_2, [total])
     total = through(2, pieces_2, total, [])
 

time: 118 us -> 117 us (level)
  waiting for transfers between devices: 42.8 us -> 37.6 us
  local copies, waits for them, and re-layouts: 16.6 us -> 20.8 us
  Pallas kernels: 33.4 us -> 31.9 us
    ppermute x15 -> x21, starting transfers between devices: 8.02 us -> 14.3 us  [swap(): return lax.ppermute(x, axis, [(i, i ^ bits) for i in range(size)])]
    all_to_all x3 -> x2, starting transfers between devices: 15.6 us -> 10.1 us  [body(): lax.all_to_all(x, ('gx', 'gy'), split_axis=0, concat_axis=0, tiled=True)]
    ppermute x15 -> x21, waiting for transfers between devices: 18.6 us -> 13.4 us  [swap(): return lax.ppermute(x, axis, [(i, i ^ bits) for i in range(size)])]
    unnamed x26 -> x16, local copies, waits for them, and re-layouts: 16.4 us -> 20.6 us
    all_to_all x3 -> x2, waiting for transfers between devices: 24.2 us -> 24.2 us  [body(): lax.all_to_all(x, ('gx', 'gy'), split_axis=0, concat_axis=0, tiled=True)]
  transfers between devices with their start and end apart: 18 -> 23, of which waited for: 12 -> 11; matrix products, arithmetic and copies ran while one was open for 2% -> 2% of each run, Pallas kernels for 21% -> 20%
where the time goes in v8:
time: 117 us; the launch traced here: 116 us
  waiting for transfers between devices  37.6 us (32%)
  Pallas kernels  31.9 us (27%)
  starting transfers between devices  24.5 us (21%)
  local copies, waits for them, and re-layouts  20.8 us (18%)
    all_to_all x2, waiting for transfers between devices, body(): lax.all_to_all(x, ('gx', 'gy'), split_axis=0, concat_axis=0, tiled=True)  24.2 us
    unnamed x16, local copies, waits for them, and re-layouts  20.6 us
    pallas_call x3, Pallas kernels, gate_up(): pl.pallas_call(functools.partial(gate_up_kernel, start, tile, len(after))...  17.6 us
    ppermute x21, starting transfers between devices, swap(): return lax.ppermute(x, axis, [(i, i ^ bits) for i in range(size)])  14.3 us
    ppermute x21, waiting for transfers between devices, swap(): return lax.ppermute(x, axis, [(i, i ^ bits) for i in range(size)])  13.4 us
    all_to_all x2, starting transfers between devices, body(): lax.all_to_all(x, ('gx', 'gy'), split_axis=0, concat_axis=0, tiled=True)  10.1 us
    pallas_call x1, Pallas kernels, attend_cache(): pl.pallas_call(functools.partial(cache_kernel, 1.0 / math.sqrt(depth)), i...  6.32 us
    pallas_call x3, Pallas kernels, down(): pl.pallas_call(functools.partial(down_kernel, start, tile_of(width, 256),...  4.36 us
  transfers between devices with their start and end apart: 23, of which 11 were waited for; matrix products, arithmetic and copies ran while one was open for 2% of the time, Pallas kernels for 20%

profile of v8, /device:TPU:0, one launch (start us, length us, event | category | flops | bytes accessed | tf_op | source)
XLA Modules:
  0.0 116.4 jit_solution(11572541143705350539)
XLA Ops:
  0.6 2.1 %shard_map.113.after_ref = bf16[8,4,4,2304]{3,2,1,0:T(4,128)(2,1)} custom-call(bf16[4,9216]{1,0:T(4,128)(2,1)} %tokens_ref.1, f32[1,9216]{1,0:T(1,128)} %bitcast.46), custom_call_target="tpu_custom_call" | custom-call | flops 368640 | bytes 589824 | tf_op jit(solution)/shard_map/pallas_call | solution.py:80
  2.7 7.3 %all-to-all-start = ((bf16[32,4,2304]{2,1,0:T(4,128)(2,1)}), bf16[32,4,2304]{2,1,0:T(4,128)(2,1)S(1)}, u32[]{:S(2)}, u32[]{:S(2)}) async-start(bf16[32,4,2304]{2,1,0:T(4,128)(2,1)} %bitcast.2), calls=%async_computation | async-start | bytes 1179648 | tf_op jit(solution)/shard_map/all_to_all | solution.py:436
  10.0 0.9 copy.31
  11.6 6.3 %shard_map.114 = (f32[4,48,256]{2,1,0:T(8,128)S(1)}, f32[4,48,1]{2,1,0:T(8,128)S(1)}, f32[4,48,1]{2,1,0:T(8,128)S(1)}) custom-call(s32[4]{0:T(128)S(1)} %copy-done.5, bf16[4,48,256]{2,1,0:T(8,128)(2,1)S(1)} %bitcast.42, bf16[4,2048,256]{2,1,0:T(8,128)(2,1)} %key_ref.1, bf16[4,2048,256]{2,1,0:T(8,128)(2,1)} %value_ref.1, ...), custom_call_target="tpu_custom_call" | custom-call | flops 603979776 | bytes 8388608 | tf_op jit(solution)/shard_map/pallas_call | solution.py:388
  17.9 8.8 %all-to-all-done.rows_ref = bf16[32,4,2304]{2,1,0:T(4,128)(2,1)S(1)} async-done(((bf16[32,4,2304]{2,1,0:T(4,128)(2,1)}), bf16[32,4,2304]{2,1,0:T(4,128)(2,1)S(1)}, u32[]{:S(2)}, u32[]{:S(2)}) %all-to-all-start) | async-done | bytes 589856 | tf_op jit(solution)/shard_map/all_to_all | solution.py:436
  26.9 5.2 %shard_map.116 = (f32[2,64,1280]{2,1,0:T(8,128)S(1)}, bf16[2,64,1280]{2,1,0:T(8,128)(2,1)S(1)}) custom-call(bf16[128,2304]{1,0:T(8,128)(2,1)S(1)} %shard_map.115.x_ref, bf16[2304,4608]{1,0:T(8,128)(2,1)} %gate_ref.5, bf16[2304,4608]{1,0:T(8,128)(2,1)} %up_ref.5), custom_call_target="tpu_custom_call" | custom-call | flops 377487360 | bytes 2949120 | tf_op jit(solution)/shard_map/pallas_call | solution.py:187
  32.2 1.6 %collective-permute-done.core_ref = bf16[2,64,1280]{2,1,0:T(8,128)(2,1)S(1)} collective-permute-done((bf16[2,64,1280]{2,1,0:T(8,128)(2,1)S(1)}, bf16[2,64,1280]{2,1,0:T(8,128)(2,1)S(1)}, u32[]{:S(2)}, u32[]{:S(2)}) %collective-permute-start) | collective-permute-done | bytes 327712 | tf_op jit(solution)/shard_map/ppermute | solution.py:50
  33.8 1.2 %collective-permute-start.1 = (bf16[2,32,1280]{2,1,0:T(8,128)(2,1)S(1)}, bf16[2,32,1280]{2,1,0:T(8,128)(2,1)S(1)}, u32[]{:S(2)}, u32[]{:S(2)}) collective-permute-start(bf16[2,32,1280]{2,1,0:T(8,128)(2,1)S(1)} %get-tuple-element.24.refs_0_), channel_id=1, source_target_pairs={{0,2},{1,3},{2,0},{3,1},{4,6},{5,7},{6,4},{7,5},{8,10},{9,11},{10,... | collective-permute-start | bytes 491528 | tf_op jit(solution)/shard_map/ppermute | solution.py:50
  35.4 1.6 %collective-permute-start.15 = (f32[4,16,512]{2,1,0:T(8,128)S(1)}, f32[4,16,512]{2,1,0:T(8,128)S(1)}, u32[]{:S(2)}, u32[]{:S(2)}) collective-permute-start(f32[4,16,512]{2,1,0:T(8,128)S(1)} %get-tuple-element.36), channel_id=1, source_target_pairs={{0,4},{4,0},{8,12},{12,8},{16,20},{20,16},{24,28},{28,24},{1,5},{5... | collective-permute-start | bytes 393224 | tf_op jit(solution)/shard_map/ppermute | solution.py:50
  37.0 7.3 %shard_map.118 = (f32[2,64,2048]{2,1,0:T(8,128)S(1)}, bf16[2,64,2048]{2,1,0:T(8,128)(2,1)S(1)}) custom-call(bf16[128,2304]{1,0:T(8,128)(2,1)S(1)} %shard_map.115.x_ref, bf16[2304,4608]{1,0:T(8,128)(2,1)} %gate_ref.5, bf16[2304,4608]{1,0:T(8,128)(2,1)} %up_ref.5, bf16[2,32,1280]{2,1,0:T(8,128)(2,1)S(1)} %get-tuple-element.24.refs_0_), custom_call_target="tpu_custom_call" | custom-call | flops 603979776 | bytes 4718592 | tf_op jit(solution)/shard_map/pallas_call | solution.py:187
  44.7 1.4 %collective-permute-start.18 = (f32[16,512]{1,0:T(8,128)S(1)}, f32[16,512]{1,0:T(8,128)S(1)}, u32[]{:S(2)}, u32[]{:S(2)}) collective-permute-start(f32[16,512]{1,0:T(8,128)S(1)} %get-tuple-element.44), channel_id=1, source_target_pairs={{0,24},{4,28},{8,16},{12,20},{16,8},{20,12},{24,0},{28,4},{1,25},{... | collective-permute-start | bytes 98312 | tf_op jit(solution)/shard_map/ppermute | solution.py:50
  46.1 2.0 %collective-permute-start.17 = (f32[16,512]{1,0:T(8,128)S(1)}, f32[16,512]{1,0:T(8,128)S(1)}, u32[]{:S(2)}, u32[]{:S(2)}) collective-permute-start(f32[16,512]{1,0:T(8,128)S(1)} %get-tuple-element.45), channel_id=1, source_target_pairs={{0,16},{4,20},{8,24},{12,28},{16,0},{20,4},{24,8},{28,12},{1,17},{... | collective-permute-start | bytes 98312 | tf_op jit(solution)/shard_map/ppermute | solution.py:50
  48.9 1.4 %collective-permute-start.3 = (bf16[2,32,2048]{2,1,0:T(8,128)(2,1)S(1)}, bf16[2,32,2048]{2,1,0:T(8,128)(2,1)S(1)}, u32[]{:S(2)}, u32[]{:S(2)}) collective-permute-start(bf16[2,32,2048]{2,1,0:T(8,128)(2,1)S(1)} %get-tuple-element.28.refs_0_), channel_id=1, source_target_pairs={{0,2},{1,3},{2,0},{3,1},{4,6},{5,7},{6,4},{7,5},{8,10},{9,11},{10,... | collective-permute-start | bytes 786440 | tf_op jit(solution)/shard_map/ppermute | solution.py:50
  50.7 1.3 %collective-permute-done.17 = f32[16,512]{1,0:T(8,128)S(1)} collective-permute-done((f32[16,512]{1,0:T(8,128)S(1)}, f32[16,512]{1,0:T(8,128)S(1)}, u32[]{:S(2)}, u32[]{:S(2)}) %collective-permute-start.17) | collective-permute-done | bytes 32800 | tf_op jit(solution)/shard_map/ppermute | solution.py:50
  52.0 5.1 %shard_map.122 = (f32[2,64,1280]{2,1,0:T(8,128)S(1)}, bf16[2,64,1280]{2,1,0:T(8,128)(2,1)S(1)}) custom-call(bf16[128,2304]{1,0:T(8,128)(2,1)S(1)} %shard_map.115.x_ref, bf16[2304,4608]{1,0:T(8,128)(2,1)} %gate_ref.5, bf16[2304,4608]{1,0:T(8,128)(2,1)} %up_ref.5, bf16[2,32,2048]{2,1,0:T(8,128)(2,1)S(1)} %get-tuple-element.28.refs_0_), custom_call_target="tpu_custom_call" | custom-call | flops 377487360 | bytes 2949120 | tf_op jit(solution)/shard_map/pallas_call | solution.py:187
  57.9 1.6 %collective-permute-done.5.core_ref = bf16[2,64,1280]{2,1,0:T(8,128)(2,1)S(1)} collective-permute-done((bf16[2,64,1280]{2,1,0:T(8,128)(2,1)S(1)}, bf16[2,64,1280]{2,1,0:T(8,128)(2,1)S(1)}, u32[]{:S(2)}, u32[]{:S(2)}) %collective-permute-start.5) | collective-permute-done | bytes 327712 | tf_op jit(solution)/shard_map/ppermute | solution.py:50
  59.5 1.1 collective-permute-start.6
  60.7 1.0 collective-permute-start.8
  61.6 5.0 %collective-permute-done.6.far_ref = bf16[2,32,1280]{2,1,0:T(8,128)(2,1)S(1)} collective-permute-done((bf16[2,32,1280]{2,1,0:T(8,128)(2,1)S(1)}, bf16[2,32,1280]{2,1,0:T(8,128)(2,1)S(1)}, u32[]{:S(2)}, u32[]{:S(2)}) %collective-permute-start.6) | collective-permute-done | bytes 163872 | tf_op jit(solution)/shard_map/ppermute | solution.py:50
  66.7 2.0 %collective-permute-done.8.refs_0_ = bf16[32,2048]{1,0:T(8,128)(2,1)S(1)} collective-permute-done((bf16[32,2048]{1,0:T(8,128)(2,1)S(1)}, bf16[32,2048]{1,0:T(8,128)(2,1)S(1)}, u32[]{:S(2)}, u32[]{:S(2)}) %collective-permute-start.8) | collective-permute-done | bytes 131104 | tf_op jit(solution)/shard_map/ppermute | solution.py:50
  69.8 0.8 collective-permute-done.19
  71.0 1.1 collective-permute-start.7
  72.0 7.0 %copy-done = bf16[4608,2304]{1,0:T(8,128)(2,1)S(1)} copy-done((bf16[4608,2304]{1,0:T(8,128)(2,1)S(1)}, bf16[4608,2304]{1,0:T(8,128)(2,1)}, u32[]{:S(2)}) %copy-start) | copy-done | bytes 21233688
  79.1 1.1 shard_map.130.refs_5_
  80.2 7.0 %copy-done.1 = bf16[4608,2304]{1,0:T(8,128)(2,1)S(1)} copy-done((bf16[4608,2304]{1,0:T(8,128)(2,1)S(1)}, bf16[4608,2304]{1,0:T(8,128)(2,1)}, u32[]{:S(2)}) %copy-start.1) | copy-done | bytes 21233688
  87.3 1.4 %shard_map.131.refs_1_.refs_5_ = f32[128,2304]{1,0:T(8,128)S(1)} custom-call(s32[1]{0:T(128)} %bitcast.gy_ref, bf16[32,2048]{1,0:T(8,128)(2,1)S(1)} %shard_map.128.refs_0_, bf16[32,2048]{1,0:T(8,128)(2,1)S(1)} %shard_map.129.refs_1_, bf16[32,2048]{1,0:T(8,128)(2,1)S(1)} %collective-permute-done.9.refs_2_, ...), custom_call_target="tpu_custom_call" | custom-call | flops 603979776 | bytes 4718592 | tf_op jit(solution)/shard_map/pallas_call | solution.py:268
  88.8 1.1 collective-permute-start.20
  90.1 4.2 %copy-done.2 = bf16[4608,2304]{1,0:T(8,128)(2,1)S(1)} copy-done((bf16[4608,2304]{1,0:T(8,128)(2,1)S(1)}, bf16[4608,2304]{1,0:T(8,128)(2,1)}, u32[]{:S(2)}) %copy-start.2) | copy-done | bytes 21233688
  94.3 1.8 %shard_map.133 = bf16[32,4,2304]{2,1,0:T(4,128)(2,1)} custom-call(s32[1]{0:T(128)} %bitcast.gy_ref, bf16[32,1280]{1,0:T(8,128)(2,1)S(1)} %shard_map.127.refs_1_.refs_5_.refs_0_, bf16[32,1280]{1,0:T(8,128)(2,1)S(1)} %shard_map.132.refs_1_, bf16[32,1280]{1,0:T(8,128)(2,1)S(1)} %collective-permute-done.13.refs_2_, ...), custom_call_target="tpu_custom_call" | custom-call | flops 377487360 | bytes 2949120 | tf_op jit(solution)/shard_map/pallas_call | solution.py:268
  96.1 2.8 %all-to-all-start.1 = ((bf16[32,4,2304]{2,1,0:T(4,128)(2,1)}), bf16[32,4,2304]{2,1,0:T(4,128)(2,1)S(1)}, u32[]{:S(2)}, u32[]{:S(2)}) async-start(bf16[32,4,2304]{2,1,0:T(4,128)(2,1)} %shard_map.133), calls=%async_computation.1 | async-start | bytes 1179648 | tf_op jit(solution)/shard_map/all_to_all | solution.py:436
  100.3 15.4 %all-to-all-done.1 = bf16[32,4,2304]{2,1,0:T(4,128)(2,1)S(1)} async-done(((bf16[32,4,2304]{2,1,0:T(4,128)(2,1)}), bf16[32,4,2304]{2,1,0:T(4,128)(2,1)S(1)}, u32[]{:S(2)}, u32[]{:S(2)}) %all-to-all-start.1) | async-done | bytes 589856 | tf_op jit(solution)/shard_map/all_to_all | solution.py:436
  115.7 0.7 shard_map.134
  (71 shorter events, 6.7 us)
Async XLA Ops:
  2.7 24.0 %all-to-all-start = ((bf16[32,4,2304]{2,1,0:T(4,128)(2,1)}), bf16[32,4,2304]{2,1,0:T(4,128)(2,1)S(1)}, u32[]{:S(2)}, u32[]{:S(2)}) async-start(bf16[32,4,2304]{2,1,0:T(4,128)(2,1)} %bitcast.2), calls=%async_computation | async-start | bytes 1179648 | tf_op jit(solution)/shard_map/all_to_all | solution.py:436
  11.0 0.7 copy-start.5
  26.9 8.3 %copy-start.4 = (bf16[1,288,512]{2,1,0:T(8,128)(2,1)S(1)}, bf16[1,288,512]{2,1,0:T(8,128)(2,1)}, u32[]{:S(2)}) copy-start(bf16[1,288,512]{2,1,0:T(8,128)(2,1)} %weight_ref.1) | copy-start | bytes 884740
  32.1 1.7 %collective-permute-start = (bf16[2,64,1280]{2,1,0:T(8,128)(2,1)S(1)}, bf16[2,64,1280]{2,1,0:T(8,128)(2,1)S(1)}, u32[]{:S(2)}, u32[]{:S(2)}) collective-permute-start(bf16[2,64,1280]{2,1,0:T(8,128)(2,1)S(1)} %get-tuple-element.23.after_ref), channel_id=1, source_target_pairs={{0,1},{1,0},{2,3},{3,2},{4,5},{5,4},{6,7},{7,6},{8,9},{9,8},{10,11... | collective-permute-start | bytes 983048 | tf_op jit(solution)/shard_map/ppermute | solution.py:50
  33.8 10.5 %collective-permute-start.1 = (bf16[2,32,1280]{2,1,0:T(8,128)(2,1)S(1)}, bf16[2,32,1280]{2,1,0:T(8,128)(2,1)S(1)}, u32[]{:S(2)}, u32[]{:S(2)}) collective-permute-start(bf16[2,32,1280]{2,1,0:T(8,128)(2,1)S(1)} %get-tuple-element.24.refs_0_), channel_id=1, source_target_pairs={{0,2},{1,3},{2,0},{3,1},{4,6},{5,7},{6,4},{7,5},{8,10},{9,11},{10,... | collective-permute-start | bytes 491528 | tf_op jit(solution)/shard_map/ppermute | solution.py:50
  35.4 8.9 %collective-permute-start.15 = (f32[4,16,512]{2,1,0:T(8,128)S(1)}, f32[4,16,512]{2,1,0:T(8,128)S(1)}, u32[]{:S(2)}, u32[]{:S(2)}) collective-permute-start(f32[4,16,512]{2,1,0:T(8,128)S(1)} %get-tuple-element.36), channel_id=1, source_target_pairs={{0,4},{4,0},{8,12},{12,8},{16,20},{20,16},{24,28},{28,24},{1,5},{5... | collective-permute-start | bytes 393224 | tf_op jit(solution)/shard_map/ppermute | solution.py:50
  44.4 4.4 %collective-permute-start.2 = (bf16[2,64,2048]{2,1,0:T(8,128)(2,1)S(1)}, bf16[2,64,2048]{2,1,0:T(8,128)(2,1)S(1)}, u32[]{:S(2)}, u32[]{:S(2)}) collective-permute-start(bf16[2,64,2048]{2,1,0:T(8,128)(2,1)S(1)} %shard_map.120), channel_id=1, source_target_pairs={{0,1},{1,0},{2,3},{3,2},{4,5},{5,4},{6,7},{7,6},{8,9},{9,8},{10,11... | collective-permute-start | bytes 1572872 | tf_op jit(solution)/shard_map/ppermute | solution.py:50
  44.5 5.8 %collective-permute-start.16 = (f32[16,512]{1,0:T(8,128)S(1)}, f32[16,512]{1,0:T(8,128)S(1)}, u32[]{:S(2)}, u32[]{:S(2)}) collective-permute-start(f32[16,512]{1,0:T(8,128)S(1)} %get-tuple-element.43), channel_id=1, source_target_pairs={{0,8},{4,12},{8,0},{12,4},{16,24},{20,28},{24,16},{28,20},{1,9},{5... | collective-permute-start | bytes 98312 | tf_op jit(solution)/shard_map/ppermute | solution.py:50
  44.7 6.0 %collective-permute-start.18 = (f32[16,512]{1,0:T(8,128)S(1)}, f32[16,512]{1,0:T(8,128)S(1)}, u32[]{:S(2)}, u32[]{:S(2)}) collective-permute-start(f32[16,512]{1,0:T(8,128)S(1)} %get-tuple-element.44), channel_id=1, source_target_pairs={{0,24},{4,28},{8,16},{12,20},{16,8},{20,12},{24,0},{28,4},{1,25},{... | collective-permute-start | bytes 98312 | tf_op jit(solution)/shard_map/ppermute | solution.py:50
  46.1 5.9 %collective-permute-start.17 = (f32[16,512]{1,0:T(8,128)S(1)}, f32[16,512]{1,0:T(8,128)S(1)}, u32[]{:S(2)}, u32[]{:S(2)}) collective-permute-start(f32[16,512]{1,0:T(8,128)S(1)} %get-tuple-element.45), channel_id=1, source_target_pairs={{0,16},{4,20},{8,24},{12,28},{16,0},{20,4},{24,8},{28,12},{1,17},{... | collective-permute-start | bytes 98312 | tf_op jit(solution)/shard_map/ppermute | solution.py:50
  48.1 9.1 %collective-permute-start.4 = (bf16[32,1280]{1,0:T(8,128)(2,1)S(1)}, bf16[32,1280]{1,0:T(8,128)(2,1)S(1)}, u32[]{:S(2)}, u32[]{:S(2)}) collective-permute-start(bf16[32,1280]{1,0:T(8,128)(2,1)S(1)} %shard_map.119.refs_1_.refs_0_), channel_id=1, source_target_pairs={{0,2},{1,3},{2,0},{3,1},{4,6},{5,7},{6,4},{7,5},{8,10},{9,11},{10,... | collective-permute-start | bytes 245768 | tf_op jit(solution)/shard_map/ppermute | solution.py:50
  48.9 8.8 %collective-permute-start.3 = (bf16[2,32,2048]{2,1,0:T(8,128)(2,1)S(1)}, bf16[2,32,2048]{2,1,0:T(8,128)(2,1)S(1)}, u32[]{:S(2)}, u32[]{:S(2)}) collective-permute-start(bf16[2,32,2048]{2,1,0:T(8,128)(2,1)S(1)} %get-tuple-element.28.refs_0_), channel_id=1, source_target_pairs={{0,2},{1,3},{2,0},{3,1},{4,6},{5,7},{6,4},{7,5},{8,10},{9,11},{10,... | collective-permute-start | bytes 786440 | tf_op jit(solution)/shard_map/ppermute | solution.py:50
  57.8 1.7 %collective-permute-start.5 = (bf16[2,64,1280]{2,1,0:T(8,128)(2,1)S(1)}, bf16[2,64,1280]{2,1,0:T(8,128)(2,1)S(1)}, u32[]{:S(2)}, u32[]{:S(2)}) collective-permute-start(bf16[2,64,1280]{2,1,0:T(8,128)(2,1)S(1)} %shard_map.125), channel_id=1, source_target_pairs={{0,1},{1,0},{2,3},{3,2},{4,5},{5,4},{6,7},{7,6},{8,9},{9,8},{10,11... | collective-permute-start | bytes 983048 | tf_op jit(solution)/shard_map/ppermute | solution.py:50
  59.5 7.1 %collective-permute-start.6 = (bf16[2,32,1280]{2,1,0:T(8,128)(2,1)S(1)}, bf16[2,32,1280]{2,1,0:T(8,128)(2,1)S(1)}, u32[]{:S(2)}, u32[]{:S(2)}) collective-permute-start(bf16[2,32,1280]{2,1,0:T(8,128)(2,1)S(1)} %get-tuple-element.33.refs_1_), channel_id=1, source_target_pairs={{0,2},{1,3},{2,0},{3,1},{4,6},{5,7},{6,4},{7,5},{8,10},{9,11},{10,... | collective-permute-start | bytes 491528 | tf_op jit(solution)/shard_map/ppermute | solution.py:50
  60.7 8.0 %collective-permute-start.8 = (bf16[32,2048]{1,0:T(8,128)(2,1)S(1)}, bf16[32,2048]{1,0:T(8,128)(2,1)S(1)}, u32[]{:S(2)}, u32[]{:S(2)}) collective-permute-start(bf16[32,2048]{1,0:T(8,128)(2,1)S(1)} %shard_map.128.refs_0_), channel_id=1, source_target_pairs={{0,2},{1,3},{2,0},{3,1},{4,6},{5,7},{6,4},{7,5},{8,10},{9,11},{10,... | collective-permute-start | bytes 393224 | tf_op jit(solution)/shard_map/ppermute | solution.py:50
  61.6 18.6 %collective-permute-start.9 = (bf16[32,2048]{1,0:T(8,128)(2,1)S(1)}, bf16[32,2048]{1,0:T(8,128)(2,1)S(1)}, u32[]{:S(2)}, u32[]{:S(2)}) collective-permute-start(bf16[32,2048]{1,0:T(8,128)(2,1)S(1)} %shard_map.128.refs_0_), channel_id=1, source_target_pairs={{0,1},{1,0},{2,3},{3,2},{4,5},{5,4},{6,7},{7,6},{8,9},{9,8},{10,11... | collective-permute-start | bytes 393224 | tf_op jit(solution)/shard_map/ppermute | solution.py:50
  68.6 11.6 %collective-permute-start.10 = (bf16[32,2048]{1,0:T(8,128)(2,1)S(1)}, bf16[32,2048]{1,0:T(8,128)(2,1)S(1)}, u32[]{:S(2)}, u32[]{:S(2)}) collective-permute-start(bf16[32,2048]{1,0:T(8,128)(2,1)S(1)} %shard_map.129.refs_1_), channel_id=1, source_target_pairs={{0,1},{1,0},{2,3},{3,2},{4,5},{5,4},{6,7},{7,6},{8,9},{9,8},{10,11... | collective-permute-start | bytes 393224 | tf_op jit(solution)/shard_map/ppermute | solution.py:50
  68.7 2.3 %collective-permute-start.11 = (bf16[32,1280]{1,0:T(8,128)(2,1)S(1)}, bf16[32,1280]{1,0:T(8,128)(2,1)S(1)}, u32[]{:S(2)}, u32[]{:S(2)}) collective-permute-start(bf16[32,1280]{1,0:T(8,128)(2,1)S(1)} %shard_map.119.refs_1_.refs_0_), channel_id=1, source_target_pairs={{0,1},{1,0},{2,3},{3,2},{4,5},{5,4},{6,7},{7,6},{8,9},{9,8},{10,11... | collective-permute-start | bytes 245768 | tf_op jit(solution)/shard_map/ppermute | solution.py:50
  69.2 2.9 %collective-permute-start.12 = (bf16[32,1280]{1,0:T(8,128)(2,1)S(1)}, bf16[32,1280]{1,0:T(8,128)(2,1)S(1)}, u32[]{:S(2)}, u32[]{:S(2)}) collective-permute-start(bf16[32,1280]{1,0:T(8,128)(2,1)S(1)} %shard_map.124.refs_2_.refs_1_), channel_id=1, source_target_pairs={{0,1},{1,0},{2,3},{3,2},{4,5},{5,4},{6,7},{7,6},{8,9},{9,8},{10,11... | collective-permute-start | bytes 245768 | tf_op jit(solution)/shard_map/ppermute | solution.py:50
  69.2 1.4 %collective-permute-start.19 = (f32[2,4,512]{2,1,0:T(4,128)S(1)}, f32[2,4,512]{2,1,0:T(4,128)S(1)}, u32[]{:S(2)}, u32[]{:S(2)}) collective-permute-start(f32[2,4,512]{2,1,0:T(4,128)S(1)} %get-tuple-element.38), channel_id=1, source_target_pairs={{0,1},{1,0},{2,3},{3,2},{4,5},{5,4},{6,7},{7,6},{8,9},{9,8},{10,11... | collective-permute-start | bytes 49160 | tf_op jit(solution)/shard_map/ppermute | solution.py:50
  70.6 19.3 %collective-permute-start.13 = (bf16[32,1280]{1,0:T(8,128)(2,1)S(1)}, bf16[32,1280]{1,0:T(8,128)(2,1)S(1)}, u32[]{:S(2)}, u32[]{:S(2)}) collective-permute-start(bf16[32,1280]{1,0:T(8,128)(2,1)S(1)} %shard_map.127.refs_1_.refs_5_.refs_0_), channel_id=1, source_target_pairs={{0,1},{1,0},{2,3},{3,2},{4,5},{5,4},{6,7},{7,6},{8,9},{9,8},{10,11... | collective-permute-start | bytes 245768 | tf_op jit(solution)/shard_map/ppermute | solution.py:50
  71.0 17.7 %collective-permute-start.7 = (bf16[32,1280]{1,0:T(8,128)(2,1)S(1)}, bf16[32,1280]{1,0:T(8,128)(2,1)S(1)}, u32[]{:S(2)}, u32[]{:S(2)}) collective-permute-start(bf16[32,1280]{1,0:T(8,128)(2,1)S(1)} %shard_map.127.refs_1_.refs_5_.refs_0_), channel_id=1, source_target_pairs={{0,2},{1,3},{2,0},{3,1},{4,6},{5,7},{6,4},{7,5},{8,10},{9,11},{10,... | collective-permute-start | bytes 245768 | tf_op jit(solution)/shard_map/ppermute | solution.py:50
  72.0 7.0 %copy-start = (bf16[4608,2304]{1,0:T(8,128)(2,1)S(1)}, bf16[4608,2304]{1,0:T(8,128)(2,1)}, u32[]{:S(2)}) copy-start(bf16[4608,2304]{1,0:T(8,128)(2,1)} %refs_4_.5) | copy-start | bytes 63700996
  80.2 7.0 %copy-start.1 = (bf16[4608,2304]{1,0:T(8,128)(2,1)S(1)}, bf16[4608,2304]{1,0:T(8,128)(2,1)}, u32[]{:S(2)}) copy-start(bf16[4608,2304]{1,0:T(8,128)(2,1)} %refs_4_.5) | copy-start | bytes 63700996
  87.3 7.0 %copy-start.2 = (bf16[4608,2304]{1,0:T(8,128)(2,1)S(1)}, bf16[4608,2304]{1,0:T(8,128)(2,1)}, u32[]{:S(2)}) copy-start(bf16[4608,2304]{1,0:T(8,128)(2,1)} %refs_4_.5) | copy-start | bytes 63700996
  88.7 1.3 %collective-permute-start.14 = (bf16[32,1280]{1,0:T(8,128)(2,1)S(1)}, bf16[32,1280]{1,0:T(8,128)(2,1)S(1)}, u32[]{:S(2)}, u32[]{:S(2)}) collective-permute-start(bf16[32,1280]{1,0:T(8,128)(2,1)S(1)} %shard_map.132.refs_1_), channel_id=1, source_target_pairs={{0,1},{1,0},{2,3},{3,2},{4,5},{5,4},{6,7},{7,6},{8,9},{9,8},{10,11... | collective-permute-start | bytes 245768 | tf_op jit(solution)/shard_map/ppermute | solution.py:50
  88.8 10.2 %copy-start.6 = (bf16[4,12288]{1,0:T(4,128)(2,1)S(1)}, bf16[4,12288]{1,0:T(4,128)(2,1)}, u32[]{:S(2)}) copy-start(bf16[4,12288]{1,0:T(4,128)(2,1)} %param.16) | copy-start | bytes 294916
  88.8 26.8 %copy-start.3 = (bf16[4,9216]{1,0:T(4,128)(2,1)S(1)}, bf16[4,9216]{1,0:T(4,128)(2,1)}, u32[]{:S(2)}) copy-start(bf16[4,9216]{1,0:T(4,128)(2,1)} %tokens_ref.1) | copy-start | bytes 221188
  88.8 10.1 %collective-permute-start.20 = (f32[4,512]{1,0:T(4,128)S(1)}, f32[4,512]{1,0:T(4,128)S(1)}, u32[]{:S(2)}, u32[]{:S(2)}) collective-permute-start(f32[4,512]{1,0:T(4,128)S(1)} %shard_map.139), channel_id=1, source_target_pairs={{0,2},{1,3},{2,0},{3,1},{4,6},{5,7},{6,4},{7,5},{8,10},{9,11},{10,... | collective-permute-start | bytes 24584 | tf_op jit(solution)/shard_map/ppermute | solution.py:50
  96.1 19.6 %all-to-all-start.1 = ((bf16[32,4,2304]{2,1,0:T(4,128)(2,1)}), bf16[32,4,2304]{2,1,0:T(4,128)(2,1)S(1)}, u32[]{:S(2)}, u32[]{:S(2)}) async-start(bf16[32,4,2304]{2,1,0:T(4,128)(2,1)} %shard_map.133), calls=%async_computation.1 | async-start | bytes 1179648 | tf_op jit(solution)/shard_map/all_to_all | solution.py:436

commit v9 on v7

--- a/solution.py
+++ b/solution.py
@@ -171,7 +171,7 @@
             ]
         )
     x = x_ref[...]
-    for n in in_turn(groups, 3):
+    for n in in_turn(groups, len(groups)):
         columns = slice(n * tile, (n + 1) * tile)
         for k in range(2):
             value = jnp.dot(x, slots[k, n], preferred_element_type=F32)
@@ -234,45 +234,34 @@
     )(in_vmem(own), in_vmem(far), *after)
 
 
-def down_kernel(start, tile, has_sum, last, gy_ref, *refs):
-    hidden, (weight_ref, *refs) = refs[:4], refs[4:]
-    out_ref = refs[-1]
-    depth = hidden[0].shape[1]
-    x = jnp.concatenate([h[...] for h in hidden], axis=0)
+def down_kernel(tile, gy_ref, weight_ref, *refs):
+    *hidden, out_ref, rows_ref = refs
+    start = 0
+    for n in range(0, len(hidden), 4):
+        depth = hidden[n].shape[1]
+        for k, piece in enumerate(hidden[n : n + 4]):
+            count = piece.shape[0]
+            rows_ref[k * count : (k + 1) * count, start : start + depth] = piece[...]
+        start += depth
     gy = gy_ref[0]
     for at in range(0, weight_ref.shape[1], tile):
         columns = slice(at, at + tile)
-        value = jnp.dot(
-            x, weight_ref[start : start + depth, columns], preferred_element_type=F32
-        )
-        if has_sum:
-            value = value + refs[0][:, columns]
-        if last:
-            spread_rows(out_ref, value, gy, columns)
-        else:
-            out_ref[:, columns] = value
-
-
-def down(gy, hidden, w_down, start, total, devices, last, after):
-    part_rows, depth = hidden[0].shape
-    rows = 4 * part_rows
-    width = w_down.shape[1]
-    args = [gy, *[in_vmem(h) for h in hidden], in_vmem(w_down)]
-    in_specs = [SCALARS] + [WHOLE] * 5
-    if total is not None:
-        args.append(in_vmem(total))
-        in_specs.append(WHOLE)
-    args.extend(after)
-    in_specs.extend([ANYWHERE] * len(after))
-    shape = (devices, rows // devices, width) if last else (rows, width)
-    return pl.pallas_call(
-        functools.partial(down_kernel, start, tile_of(width, 256), total is not None, last),
-        in_specs=in_specs,
+        value = jnp.dot(rows_ref[...], weight_ref[:, columns], preferred_element_type=F32)
+        spread_rows(out_ref, value, gy, columns)
+
+
+def down(gy, hidden, w_down, devices):
+    rows = 4 * hidden[0].shape[0]
+    depth, width = w_down.shape
+    return pl.pallas_call(
+        functools.partial(down_kernel, tile_of(width, 256)),
+        in_specs=[SCALARS, WHOLE] + [WHOLE] * len(hidden),
         out_specs=WHOLE,
-        out_shape=vmem_out(shape, BF16 if last else F32),
-        compiler_params=params(8),
+        out_shape=vmem_out((devices, rows // devices, width), BF16),
+        scratch_shapes=[pltpu.VMEM((rows, depth), BF16)],
+        compiler_params=params(10),
         cost_estimate=cost(rows * depth * width, depth * width),
-    )(*args)
+    )(gy, in_vmem(w_down), *[in_vmem(h) for h in hidden])
 
 
 def finish_kernel(tokens_ref, sums_ref, out_ref):
@@ -421,15 +410,16 @@
         other = tie(swap_gy(own, 2), after)
         return own, other, swap_gy(own, 1), swap_gy(other, 1)
 
-    def through(c, pieces, total, after):
-        last = c == len(widths) - 1
-        return down(gy, pieces, w_down, starts[c], total, devices, last, after)
-
     keep, send = project(0, [])
+    slab = w_kv.shape[1]
+    part = fresh_part(gy, lax.dynamic_slice_in_dim(x, gx * slab, slab, 1), w_kv, devices, send)
     own_0, across_0 = combine(keep, swap_gy(send, 1))
     far_0 = swap_gy(across_0, 2)
     keep, send = project(1, [across_0])
     hidden_0 = activate(own_0, far_0, [send])
+    fresh = jnp.sum(exchange(tie(part, [send])), axis=0)
+    key_new = fresh[:, :HD].astype(BF16)
+    value_new = fresh[:, HD:].astype(BF16)
     own_1, across_1 = combine(keep, swap_gy(tie(send, [hidden_0]), 1))
     far_1 = swap_gy(across_1, 2)
     keep, send = project(2, [across_1])
@@ -437,20 +427,10 @@
     pieces_0 = back(0, hidden_0, [send])
     own_2, across_2 = combine(keep, swap_gy(tie(send, [hidden_1, pieces_0[1]]), 1))
     far_2 = swap_gy(across_2, 2)
-
-    total = through(0, pieces_0, None, [across_2])
-    pieces_1 = back(1, hidden_1, [total])
-    hidden_2 = activate(own_2, far_2, [total])
-
-    slab = w_kv.shape[1]
-    part = fresh_part(gy, lax.dynamic_slice_in_dim(x, gx * slab, slab, 1), w_kv, devices, send)
-    fresh = jnp.sum(exchange(tie(part, [hidden_2])), axis=0)
-    key_new = fresh[:, :HD].astype(BF16)
-    value_new = fresh[:, HD:].astype(BF16)
-
-    total = through(1, pieces_1, total, [hidden_2])
-    pieces_2 = back(2, hidden_2, [total])
-    total = through(2, pieces_2, total, [])
+    hidden_2 = activate(own_2, far_2, [])
+    pieces_1 = back(1, tie(hidden_1, [across_2]), [hidden_2])
+    pieces_2 = back(2, hidden_2, [])
+    total = down(gy, [*pieces_0, *pieces_1, *pieces_2], w_down, devices)
 
     ffn = exchange(total)
     context = attend_new(grouped, cached, key_new, value_new)

time: 118 us -> 108 us (0.915)
  local copies, waits for them, and re-layouts: 16.6 us -> 9.52 us
  waiting for transfers between devices: 42.8 us -> 41.1 us
  Pallas kernels: 33.4 us -> 32.1 us
    unnamed x26 -> x12, local copies, waits for them, and re-layouts: 16.4 us -> 9.31 us
    ppermute x15, waiting for transfers between devices: 18.6 us -> 17 us  [swap(): return lax.ppermute(x, axis, [(i, i ^ bits) for i in range(size)])]
    pallas_call x3 -> x1, Pallas kernels: 4.18 us -> 3.83 us  [down(): pl.pallas_call(functools.partial(down_kernel, tile_of(width, 256)), in_sp...]
  transfers between devices with their start and end apart: 18 -> 18, of which waited for: 12 -> 10; matrix products, arithmetic and copies ran while one was open for 2% -> 2% of each run, Pallas kernels for 21% -> 22%
where the time goes in v9:
time: 108 us; the launch traced here: 107 us
  waiting for transfers between devices  41.1 us (38%)
  Pallas kernels  32.1 us (30%)
  starting transfers between devices  23.1 us (21%)
  local copies, waits for them, and re-layouts  9.52 us (9%)
    all_to_all x3, waiting for transfers between devices, body(): lax.all_to_all(x, ('gx', 'gy'), split_axis=0, concat_axis=0, tiled=True)  24.2 us
    pallas_call x3, Pallas kernels, gate_up(): pl.pallas_call(functools.partial(gate_up_kernel, start, tile, len(after))...  17.6 us
    ppermute x15, waiting for transfers between devices, swap(): return lax.ppermute(x, axis, [(i, i ^ bits) for i in range(size)])  17 us
    all_to_all x3, starting transfers between devices, body(): lax.all_to_all(x, ('gx', 'gy'), split_axis=0, concat_axis=0, tiled=True)  14.8 us
    unnamed x12, local copies, waits for them, and re-layouts  9.31 us
    ppermute x15, starting transfers between devices, swap(): return lax.ppermute(x, axis, [(i, i ^ bits) for i in range(size)])  8.24 us
    pallas_call x1, Pallas kernels, attend_cache(): pl.pallas_call(functools.partial(cache_kernel, 1.0 / math.sqrt(depth)), i...  6.32 us
    pallas_call x1, Pallas kernels, down(): pl.pallas_call(functools.partial(down_kernel, tile_of(width, 256)), in_sp...  3.83 us
  transfers between devices with their start and end apart: 18, of which 10 were waited for; matrix products, arithmetic and copies ran while one was open for 2% of the time, Pallas kernels for 22%

profile of v9, /device:TPU:0, one launch (start us, length us, event | category | flops | bytes accessed | tf_op | source)
XLA Modules:
  0.0 107.2 jit_solution(5832725718458941179)
XLA Ops:
  0.6 2.1 %shard_map.113.after_ref = bf16[8,4,4,2304]{3,2,1,0:T(4,128)(2,1)} custom-call(bf16[4,9216]{1,0:T(4,128)(2,1)} %tokens_ref.1, f32[1,9216]{1,0:T(1,128)} %bitcast.23), custom_call_target="tpu_custom_call" | custom-call | flops 368640 | bytes 589824 | tf_op jit(solution)/shard_map/pallas_call | solution.py:80
  2.7 7.3 %all-to-all-start = ((bf16[32,4,2304]{2,1,0:T(4,128)(2,1)}), bf16[32,4,2304]{2,1,0:T(4,128)(2,1)S(1)}, u32[]{:S(2)}, u32[]{:S(2)}) async-start(bf16[32,4,2304]{2,1,0:T(4,128)(2,1)} %bitcast.2), calls=%async_computation | async-start | bytes 1179648 | tf_op jit(solution)/shard_map/all_to_all | solution.py:393
  10.1 0.9 copy.29
  11.0 0.6 copy-done.3
  11.6 6.3 %shard_map.114 = (f32[4,48,256]{2,1,0:T(8,128)S(1)}, f32[4,48,1]{2,1,0:T(8,128)S(1)}, f32[4,48,1]{2,1,0:T(8,128)S(1)}) custom-call(s32[4]{0:T(128)S(1)} %copy-done.3, bf16[4,48,256]{2,1,0:T(8,128)(2,1)S(1)} %bitcast.19, bf16[4,2048,256]{2,1,0:T(8,128)(2,1)} %key_ref.1, bf16[4,2048,256]{2,1,0:T(8,128)(2,1)} %value_ref.1, ...), custom_call_target="tpu_custom_call" | custom-call | flops 603979776 | bytes 8388608 | tf_op jit(solution)/shard_map/pallas_call | solution.py:347
  18.0 8.8 %all-to-all-done.rows_ref = bf16[32,4,2304]{2,1,0:T(4,128)(2,1)S(1)} async-done(((bf16[32,4,2304]{2,1,0:T(4,128)(2,1)}), bf16[32,4,2304]{2,1,0:T(4,128)(2,1)S(1)}, u32[]{:S(2)}, u32[]{:S(2)}) %all-to-all-start) | async-done | bytes 589856 | tf_op jit(solution)/shard_map/all_to_all | solution.py:393
  26.9 5.2 %shard_map.116 = (f32[2,64,1280]{2,1,0:T(8,128)S(1)}, bf16[2,64,1280]{2,1,0:T(8,128)(2,1)S(1)}) custom-call(bf16[128,2304]{1,0:T(8,128)(2,1)S(1)} %shard_map.115.x_ref, bf16[2304,4608]{1,0:T(8,128)(2,1)} %gate_ref.5, bf16[2304,4608]{1,0:T(8,128)(2,1)} %up_ref.5), custom_call_target="tpu_custom_call" | custom-call | flops 377487360 | bytes 2949120 | tf_op jit(solution)/shard_map/pallas_call | solution.py:187
  32.2 1.6 %collective-permute-done.core_ref = bf16[2,64,1280]{2,1,0:T(8,128)(2,1)S(1)} collective-permute-done((bf16[2,64,1280]{2,1,0:T(8,128)(2,1)S(1)}, bf16[2,64,1280]{2,1,0:T(8,128)(2,1)S(1)}, u32[]{:S(2)}, u32[]{:S(2)}) %collective-permute-start) | collective-permute-done | bytes 327712 | tf_op jit(solution)/shard_map/ppermute | solution.py:50
  33.9 1.2 %collective-permute-start.1 = (bf16[2,32,1280]{2,1,0:T(8,128)(2,1)S(1)}, bf16[2,32,1280]{2,1,0:T(8,128)(2,1)S(1)}, u32[]{:S(2)}, u32[]{:S(2)}) collective-permute-start(bf16[2,32,1280]{2,1,0:T(8,128)(2,1)S(1)} %get-tuple-element.21.refs_0_), channel_id=1, source_target_pairs={{0,2},{1,3},{2,0},{3,1},{4,6},{5,7},{6,4},{7,5},{8,10},{9,11},{10,... | collective-permute-start | bytes 491528 | tf_op jit(solution)/shard_map/ppermute | solution.py:50
  35.2 0.9 shard_map.133.refs_0_
  36.1 7.3 %shard_map.118 = (f32[2,64,2048]{2,1,0:T(8,128)S(1)}, bf16[2,64,2048]{2,1,0:T(8,128)(2,1)S(1)}) custom-call(bf16[128,2304]{1,0:T(8,128)(2,1)S(1)} %shard_map.115.x_ref, bf16[2304,4608]{1,0:T(8,128)(2,1)} %gate_ref.5, bf16[2304,4608]{1,0:T(8,128)(2,1)} %up_ref.5, bf16[2,32,1280]{2,1,0:T(8,128)(2,1)S(1)} %get-tuple-element.21.refs_0_), custom_call_target="tpu_custom_call" | custom-call | flops 603979776 | bytes 4718592 | tf_op jit(solution)/shard_map/pallas_call | solution.py:187
  43.7 1.8 %collective-permute-done.3.core_ref = bf16[2,64,2048]{2,1,0:T(8,128)(2,1)S(1)} collective-permute-done((bf16[2,64,2048]{2,1,0:T(8,128)(2,1)S(1)}, bf16[2,64,2048]{2,1,0:T(8,128)(2,1)S(1)}, u32[]{:S(2)}, u32[]{:S(2)}) %collective-permute-start.3) | collective-permute-done | bytes 524320 | tf_op jit(solution)/shard_map/ppermute | solution.py:50
  45.6 0.9 collective-permute-start.6
  46.5 1.1 %collective-permute-start.2 = (bf16[32,1280]{1,0:T(8,128)(2,1)S(1)}, bf16[32,1280]{1,0:T(8,128)(2,1)S(1)}, u32[]{:S(2)}, u32[]{:S(2)}) collective-permute-start(bf16[32,1280]{1,0:T(8,128)(2,1)S(1)} %shard_map.119.refs_1_.refs_0_), channel_id=1, source_target_pairs={{0,2},{1,3},{2,0},{3,1},{4,6},{5,7},{6,4},{7,5},{8,10},{9,11},{10,... | collective-permute-start | bytes 245768 | tf_op jit(solution)/shard_map/ppermute | solution.py:50
  47.7 5.1 %shard_map.122 = (f32[2,64,1280]{2,1,0:T(8,128)S(1)}, bf16[2,64,1280]{2,1,0:T(8,128)(2,1)S(1)}) custom-call(bf16[128,2304]{1,0:T(8,128)(2,1)S(1)} %shard_map.115.x_ref, bf16[2304,4608]{1,0:T(8,128)(2,1)} %gate_ref.5, bf16[2304,4608]{1,0:T(8,128)(2,1)} %up_ref.5, bf16[2,32,2048]{2,1,0:T(8,128)(2,1)S(1)} %get-tuple-element.24.refs_0_), custom_call_target="tpu_custom_call" | custom-call | flops 377487360 | bytes 2949120 | tf_op jit(solution)/shard_map/pallas_call | solution.py:187
  52.8 2.9 %collective-permute-done.2.refs_0_ = bf16[32,1280]{1,0:T(8,128)(2,1)S(1)} collective-permute-done((bf16[32,1280]{1,0:T(8,128)(2,1)S(1)}, bf16[32,1280]{1,0:T(8,128)(2,1)S(1)}, u32[]{:S(2)}, u32[]{:S(2)}) %collective-permute-start.2) | collective-permute-done | bytes 81952 | tf_op jit(solution)/shard_map/ppermute | solution.py:50
  55.9 3.0 %all-to-all-start.2 = ((f32[32,4,512]{2,1,0:T(4,128)}), f32[32,4,512]{2,1,0:T(4,128)S(1)}, u32[]{:S(2)}, u32[]{:S(2)}) async-start(f32[32,4,512]{2,1,0:T(4,128)} %shard_map.134), calls=%async_computation.2 | async-start | bytes 524288 | tf_op jit(solution)/shard_map/all_to_all | solution.py:393
  59.0 1.7 %collective-permute-start.9 = (bf16[2,32,1280]{2,1,0:T(8,128)(2,1)S(1)}, bf16[2,32,1280]{2,1,0:T(8,128)(2,1)S(1)}, u32[]{:S(2)}, u32[]{:S(2)}) collective-permute-start(bf16[2,32,1280]{2,1,0:T(8,128)(2,1)S(1)} %get-tuple-element.28.refs_1_), channel_id=1, source_target_pairs={{0,2},{1,3},{2,0},{3,1},{4,6},{5,7},{6,4},{7,5},{8,10},{9,11},{10,... | collective-permute-start | bytes 491528 | tf_op jit(solution)/shard_map/ppermute | solution.py:50
  61.1 7.2 %collective-permute-done.9.far_ref = bf16[2,32,1280]{2,1,0:T(8,128)(2,1)S(1)} collective-permute-done((bf16[2,32,1280]{2,1,0:T(8,128)(2,1)S(1)}, bf16[2,32,1280]{2,1,0:T(8,128)(2,1)S(1)}, u32[]{:S(2)}, u32[]{:S(2)}) %collective-permute-start.9) | collective-permute-done | bytes 163872 | tf_op jit(solution)/shard_map/ppermute | solution.py:50
  68.4 1.0 collective-permute-start.12
  69.4 0.5 collective-permute-start.10
  69.9 1.3 %collective-permute-done.8.refs_0_ = bf16[32,2048]{1,0:T(8,128)(2,1)S(1)} collective-permute-done((bf16[32,2048]{1,0:T(8,128)(2,1)S(1)}, bf16[32,2048]{1,0:T(8,128)(2,1)S(1)}, u32[]{:S(2)}, u32[]{:S(2)}) %collective-permute-start.8) | collective-permute-done | bytes 131104 | tf_op jit(solution)/shard_map/ppermute | solution.py:50
  71.2 0.5 collective-permute-start.5
  71.7 1.2 %collective-permute-done.12.refs_0_ = bf16[32,1280]{1,0:T(8,128)(2,1)S(1)} collective-permute-done((bf16[32,1280]{1,0:T(8,128)(2,1)S(1)}, bf16[32,1280]{1,0:T(8,128)(2,1)S(1)}, u32[]{:S(2)}, u32[]{:S(2)}) %collective-permute-start.12) | collective-permute-done | bytes 81952 | tf_op jit(solution)/shard_map/ppermute | solution.py:50
  72.9 0.5 collective-permute-start.14
  73.4 0.8 collective-permute-done.13.refs_10_
  74.3 7.0 %copy-done = bf16[4608,2304]{1,0:T(8,128)(2,1)S(1)} copy-done((bf16[4608,2304]{1,0:T(8,128)(2,1)S(1)}, bf16[4608,2304]{1,0:T(8,128)(2,1)}, u32[]{:S(2)}) %copy-start) | copy-done | bytes 21233688
  81.4 3.8 %shard_map.131 = bf16[32,4,2304]{2,1,0:T(4,128)(2,1)} custom-call(s32[1]{0:T(128)} %bitcast.gy_ref, bf16[4608,2304]{1,0:T(8,128)(2,1)S(1)} %copy-done, bf16[32,1280]{1,0:T(8,128)(2,1)S(1)} %shard_map.119.refs_1_.refs_0_, bf16[32,1280]{1,0:T(8,128)(2,1)S(1)} %shard_map.123.refs_2_.refs_1_, bf16[32,1280]{1,0:T(8,128)(2,1)S(1)} %collective-permute-done.4.refs_2_, ...), custom_call_target="tpu_custom_call" | custom-call | flops 1358954496 | bytes 10616832 | tf_op jit(solution)/shard_map/pallas_call | solution.py:256
  85.2 4.5 %all-to-all-start.1 = ((bf16[32,4,2304]{2,1,0:T(4,128)(2,1)}), bf16[32,4,2304]{2,1,0:T(4,128)(2,1)S(1)}, u32[]{:S(2)}, u32[]{:S(2)}) async-start(bf16[32,4,2304]{2,1,0:T(4,128)(2,1)} %shard_map.131), calls=%async_computation.1 | async-start | bytes 1179648 | tf_op jit(solution)/shard_map/all_to_all | solution.py:393
  90.4 0.7 copy.24
  91.1 15.4 %all-to-all-done.1 = bf16[32,4,2304]{2,1,0:T(4,128)(2,1)S(1)} async-done(((bf16[32,4,2304]{2,1,0:T(4,128)(2,1)}), bf16[32,4,2304]{2,1,0:T(4,128)(2,1)S(1)}, u32[]{:S(2)}, u32[]{:S(2)}) %all-to-all-start.1) | async-done | bytes 589856 | tf_op jit(solution)/shard_map/all_to_all | solution.py:393
  106.5 0.7 shard_map.132
  (46 shorter events, 2.2 us)
Async XLA Ops:
  2.7 24.0 %all-to-all-start = ((bf16[32,4,2304]{2,1,0:T(4,128)(2,1)}), bf16[32,4,2304]{2,1,0:T(4,128)(2,1)S(1)}, u32[]{:S(2)}, u32[]{:S(2)}) async-start(bf16[32,4,2304]{2,1,0:T(4,128)(2,1)} %bitcast.2), calls=%async_computation | async-start | bytes 1179648 | tf_op jit(solution)/shard_map/all_to_all | solution.py:393
  11.0 0.7 copy-start.3
  26.9 8.3 %copy-start.1 = (bf16[1,288,512]{2,1,0:T(8,128)(2,1)S(1)}, bf16[1,288,512]{2,1,0:T(8,128)(2,1)}, u32[]{:S(2)}) copy-start(bf16[1,288,512]{2,1,0:T(8,128)(2,1)} %weight_ref.3) | copy-start | bytes 884740
  32.1 1.7 %collective-permute-start = (bf16[2,64,1280]{2,1,0:T(8,128)(2,1)S(1)}, bf16[2,64,1280]{2,1,0:T(8,128)(2,1)S(1)}, u32[]{:S(2)}, u32[]{:S(2)}) collective-permute-start(bf16[2,64,1280]{2,1,0:T(8,128)(2,1)S(1)} %get-tuple-element.19.after_ref), channel_id=1, source_target_pairs={{0,1},{1,0},{2,3},{3,2},{4,5},{5,4},{6,7},{7,6},{8,9},{9,8},{10,11... | collective-permute-start | bytes 983048 | tf_op jit(solution)/shard_map/ppermute | solution.py:50
  33.9 9.6 %collective-permute-start.1 = (bf16[2,32,1280]{2,1,0:T(8,128)(2,1)S(1)}, bf16[2,32,1280]{2,1,0:T(8,128)(2,1)S(1)}, u32[]{:S(2)}, u32[]{:S(2)}) collective-permute-start(bf16[2,32,1280]{2,1,0:T(8,128)(2,1)S(1)} %get-tuple-element.21.refs_0_), channel_id=1, source_target_pairs={{0,2},{1,3},{2,0},{3,1},{4,6},{5,7},{6,4},{7,5},{8,10},{9,11},{10,... | collective-permute-start | bytes 491528 | tf_op jit(solution)/shard_map/ppermute | solution.py:50
  43.5 2.0 %collective-permute-start.3 = (bf16[2,64,2048]{2,1,0:T(8,128)(2,1)S(1)}, bf16[2,64,2048]{2,1,0:T(8,128)(2,1)S(1)}, u32[]{:S(2)}, u32[]{:S(2)}) collective-permute-start(bf16[2,64,2048]{2,1,0:T(8,128)(2,1)S(1)} %shard_map.120), channel_id=1, source_target_pairs={{0,1},{1,0},{2,3},{3,2},{4,5},{5,4},{6,7},{7,6},{8,9},{9,8},{10,11... | collective-permute-start | bytes 1572872 | tf_op jit(solution)/shard_map/ppermute | solution.py:50
  45.6 10.2 %collective-permute-start.6 = (bf16[2,32,2048]{2,1,0:T(8,128)(2,1)S(1)}, bf16[2,32,2048]{2,1,0:T(8,128)(2,1)S(1)}, u32[]{:S(2)}, u32[]{:S(2)}) collective-permute-start(bf16[2,32,2048]{2,1,0:T(8,128)(2,1)S(1)} %get-tuple-element.24.refs_0_), channel_id=1, source_target_pairs={{0,2},{1,3},{2,0},{3,1},{4,6},{5,7},{6,4},{7,5},{8,10},{9,11},{10,... | collective-permute-start | bytes 786440 | tf_op jit(solution)/shard_map/ppermute | solution.py:50
  46.5 9.2 %collective-permute-start.2 = (bf16[32,1280]{1,0:T(8,128)(2,1)S(1)}, bf16[32,1280]{1,0:T(8,128)(2,1)S(1)}, u32[]{:S(2)}, u32[]{:S(2)}) collective-permute-start(bf16[32,1280]{1,0:T(8,128)(2,1)S(1)} %shard_map.119.refs_1_.refs_0_), channel_id=1, source_target_pairs={{0,2},{1,3},{2,0},{3,1},{4,6},{5,7},{6,4},{7,5},{8,10},{9,11},{10,... | collective-permute-start | bytes 245768 | tf_op jit(solution)/shard_map/ppermute | solution.py:50
  52.8 37.0 %copy-start.4 = (bf16[4,12288]{1,0:T(4,128)(2,1)S(1)}, bf16[4,12288]{1,0:T(4,128)(2,1)}, u32[]{:S(2)}) copy-start(bf16[4,12288]{1,0:T(4,128)(2,1)} %param.16) | copy-start | bytes 294916
  52.8 53.6 %copy-start.2 = (bf16[4,9216]{1,0:T(4,128)(2,1)S(1)}, bf16[4,9216]{1,0:T(4,128)(2,1)}, u32[]{:S(2)}) copy-start(bf16[4,9216]{1,0:T(4,128)(2,1)} %tokens_ref.1) | copy-start | bytes 221188
  55.8 3.1 %collective-permute-start.7 = (bf16[2,64,1280]{2,1,0:T(8,128)(2,1)S(1)}, bf16[2,64,1280]{2,1,0:T(8,128)(2,1)S(1)}, u32[]{:S(2)}, u32[]{:S(2)}) collective-permute-start(bf16[2,64,1280]{2,1,0:T(8,128)(2,1)S(1)} %shard_map.125), channel_id=1, source_target_pairs={{0,1},{1,0},{2,3},{3,2},{4,5},{5,4},{6,7},{7,6},{8,9},{9,8},{10,11... | collective-permute-start | bytes 983048 | tf_op jit(solution)/shard_map/ppermute | solution.py:50
  55.9 29.3 %all-to-all-start.2 = ((f32[32,4,512]{2,1,0:T(4,128)}), f32[32,4,512]{2,1,0:T(4,128)S(1)}, u32[]{:S(2)}, u32[]{:S(2)}) async-start(f32[32,4,512]{2,1,0:T(4,128)} %shard_map.134), calls=%async_computation.2 | async-start | bytes 524288 | tf_op jit(solution)/shard_map/all_to_all | solution.py:393
  59.0 9.3 %collective-permute-start.9 = (bf16[2,32,1280]{2,1,0:T(8,128)(2,1)S(1)}, bf16[2,32,1280]{2,1,0:T(8,128)(2,1)S(1)}, u32[]{:S(2)}, u32[]{:S(2)}) collective-permute-start(bf16[2,32,1280]{2,1,0:T(8,128)(2,1)S(1)} %get-tuple-element.28.refs_1_), channel_id=1, source_target_pairs={{0,2},{1,3},{2,0},{3,1},{4,6},{5,7},{6,4},{7,5},{8,10},{9,11},{10,... | collective-permute-start | bytes 491528 | tf_op jit(solution)/shard_map/ppermute | solution.py:50
  60.7 10.5 %collective-permute-start.8 = (bf16[32,2048]{1,0:T(8,128)(2,1)S(1)}, bf16[32,2048]{1,0:T(8,128)(2,1)S(1)}, u32[]{:S(2)}, u32[]{:S(2)}) collective-permute-start(bf16[32,2048]{1,0:T(8,128)(2,1)S(1)} %shard_map.127.refs_4_), channel_id=1, source_target_pairs={{0,2},{1,3},{2,0},{3,1},{4,6},{5,7},{6,4},{7,5},{8,10},{9,11},{10,... | collective-permute-start | bytes 393224 | tf_op jit(solution)/shard_map/ppermute | solution.py:50
  68.4 4.5 %collective-permute-start.12 = (bf16[32,1280]{1,0:T(8,128)(2,1)S(1)}, bf16[32,1280]{1,0:T(8,128)(2,1)S(1)}, u32[]{:S(2)}, u32[]{:S(2)}) collective-permute-start(bf16[32,1280]{1,0:T(8,128)(2,1)S(1)} %shard_map.128.refs_1_.refs_8_), channel_id=1, source_target_pairs={{0,2},{1,3},{2,0},{3,1},{4,6},{5,7},{6,4},{7,5},{8,10},{9,11},{10,... | collective-permute-start | bytes 245768 | tf_op jit(solution)/shard_map/ppermute | solution.py:50
  69.4 3.5 %collective-permute-start.4 = (bf16[32,1280]{1,0:T(8,128)(2,1)S(1)}, bf16[32,1280]{1,0:T(8,128)(2,1)S(1)}, u32[]{:S(2)}, u32[]{:S(2)}) collective-permute-start(bf16[32,1280]{1,0:T(8,128)(2,1)S(1)} %shard_map.119.refs_1_.refs_0_), channel_id=1, source_target_pairs={{0,1},{1,0},{2,3},{3,2},{4,5},{5,4},{6,7},{7,6},{8,9},{9,8},{10,11... | collective-permute-start | bytes 245768 | tf_op jit(solution)/shard_map/ppermute | solution.py:50
  69.4 4.0 %collective-permute-start.10 = (bf16[32,2048]{1,0:T(8,128)(2,1)S(1)}, bf16[32,2048]{1,0:T(8,128)(2,1)S(1)}, u32[]{:S(2)}, u32[]{:S(2)}) collective-permute-start(bf16[32,2048]{1,0:T(8,128)(2,1)S(1)} %shard_map.127.refs_4_), channel_id=1, source_target_pairs={{0,1},{1,0},{2,3},{3,2},{4,5},{5,4},{6,7},{7,6},{8,9},{9,8},{10,11... | collective-permute-start | bytes 393224 | tf_op jit(solution)/shard_map/ppermute | solution.py:50
  71.2 2.9 %collective-permute-start.11 = (bf16[32,2048]{1,0:T(8,128)(2,1)S(1)}, bf16[32,2048]{1,0:T(8,128)(2,1)S(1)}, u32[]{:S(2)}, u32[]{:S(2)}) collective-permute-start(bf16[32,2048]{1,0:T(8,128)(2,1)S(1)} %shard_map.129.refs_5_), channel_id=1, source_target_pairs={{0,1},{1,0},{2,3},{3,2},{4,5},{5,4},{6,7},{7,6},{8,9},{9,8},{10,11... | collective-permute-start | bytes 393224 | tf_op jit(solution)/shard_map/ppermute | solution.py:50
  71.2 2.2 %collective-permute-start.5 = (bf16[32,1280]{1,0:T(8,128)(2,1)S(1)}, bf16[32,1280]{1,0:T(8,128)(2,1)S(1)}, u32[]{:S(2)}, u32[]{:S(2)}) collective-permute-start(bf16[32,1280]{1,0:T(8,128)(2,1)S(1)} %shard_map.123.refs_2_.refs_1_), channel_id=1, source_target_pairs={{0,1},{1,0},{2,3},{3,2},{4,5},{5,4},{6,7},{7,6},{8,9},{9,8},{10,11... | collective-permute-start | bytes 245768 | tf_op jit(solution)/shard_map/ppermute | solution.py:50
  72.9 1.3 %collective-permute-start.13 = (bf16[32,1280]{1,0:T(8,128)(2,1)S(1)}, bf16[32,1280]{1,0:T(8,128)(2,1)S(1)}, u32[]{:S(2)}, u32[]{:S(2)}) collective-permute-start(bf16[32,1280]{1,0:T(8,128)(2,1)S(1)} %shard_map.128.refs_1_.refs_8_), channel_id=1, source_target_pairs={{0,1},{1,0},{2,3},{3,2},{4,5},{5,4},{6,7},{7,6},{8,9},{9,8},{10,11... | collective-permute-start | bytes 245768 | tf_op jit(solution)/shard_map/ppermute | solution.py:50
  72.9 1.4 %collective-permute-start.14 = (bf16[32,1280]{1,0:T(8,128)(2,1)S(1)}, bf16[32,1280]{1,0:T(8,128)(2,1)S(1)}, u32[]{:S(2)}, u32[]{:S(2)}) collective-permute-start(bf16[32,1280]{1,0:T(8,128)(2,1)S(1)} %shard_map.130.refs_9_), channel_id=1, source_target_pairs={{0,1},{1,0},{2,3},{3,2},{4,5},{5,4},{6,7},{7,6},{8,9},{9,8},{10,11... | collective-permute-start | bytes 245768 | tf_op jit(solution)/shard_map/ppermute | solution.py:50
  74.3 7.0 %copy-start = (bf16[4608,2304]{1,0:T(8,128)(2,1)S(1)}, bf16[4608,2304]{1,0:T(8,128)(2,1)}, u32[]{:S(2)}) copy-start(bf16[4608,2304]{1,0:T(8,128)(2,1)} %weight_ref.2) | copy-start | bytes 63700996
  85.2 21.3 %all-to-all-start.1 = ((bf16[32,4,2304]{2,1,0:T(4,128)(2,1)}), bf16[32,4,2304]{2,1,0:T(4,128)(2,1)S(1)}, u32[]{:S(2)}, u32[]{:S(2)}) async-start(bf16[32,4,2304]{2,1,0:T(4,128)(2,1)} %shard_map.131), calls=%async_computation.1 | async-start | bytes 1179648 | tf_op jit(solution)/shard_map/all_to_all | solution.py:393

commit v10 on v6

--- a/solution.py
+++ b/solution.py
@@ -171,7 +171,7 @@
             ]
         )
     x = x_ref[...]
-    for n in in_turn(groups, 3):
+    for n in in_turn(groups, len(groups)):
         columns = slice(n * tile, (n + 1) * tile)
         for k in range(2):
             value = jnp.dot(x, slots[k, n], preferred_element_type=F32)
@@ -252,7 +252,7 @@
     ]
     x = jnp.concatenate([h[...] for h in hidden], axis=0)
     gy = gy_ref[0]
-    for n in in_turn(groups, 5):
+    for n in in_turn(groups, len(groups)):
         columns = slice(n * tile, (n + 1) * tile)
         value = jnp.dot(x, slots[n], preferred_element_type=F32)
         if has_sum:
@@ -442,29 +442,27 @@
         return down(gy, pieces, w_down, starts[c], total, devices, last, after)
 
     keep, send = project(0, [])
+    slab = w_kv.shape[1]
+    part = fresh_part(gy, lax.dynamic_slice_in_dim(x, gx * slab, slab, 1), w_kv, devices, send)
     own_0, across_0 = combine(keep, swap_gy(send, 1))
     far_0 = swap_gy(across_0, 2)
     keep, send = project(1, [across_0])
     hidden_0 = activate(own_0, far_0, [send])
+    fresh = jnp.sum(exchange(tie(part, [send])), axis=0)
+    key_new = fresh[:, :HD].astype(BF16)
+    value_new = fresh[:, HD:].astype(BF16)
     own_1, across_1 = combine(keep, swap_gy(tie(send, [hidden_0]), 1))
     far_1 = swap_gy(across_1, 2)
     keep, send = project(2, [across_1])
+    hidden_1 = activate(own_1, far_1, [send])
     pieces_0 = back(0, hidden_0, [send])
-    own_2, across_2 = combine(keep, swap_gy(send, 1))
+    own_2, across_2 = combine(keep, swap_gy(tie(send, [hidden_1, pieces_0[1]]), 1))
     far_2 = swap_gy(across_2, 2)
-    hidden_1 = activate(own_1, far_1, [across_2])
-
-    slab = w_kv.shape[1]
-    part = fresh_part(gy, lax.dynamic_slice_in_dim(x, gx * slab, slab, 1), w_kv, devices, send)
-    fresh = jnp.sum(exchange(tie(part, [across_2])), axis=0)
-    key_new = fresh[:, :HD].astype(BF16)
-    value_new = fresh[:, HD:].astype(BF16)
-
-    total = through(0, pieces_0, None, [hidden_1])
-    pieces_1 = back(1, hidden_1, [total])
+    total = through(0, pieces_0, None, [across_2])
+    pieces_1 = back(1, hidden_1, [across_2])
+    total = through(1, pieces_1, total, [])
     hidden_2 = activate(own_2, far_2, [total])
-    total = through(1, pieces_1, total, [hidden_2])
-    pieces_2 = back(2, hidden_2, [total])
+    pieces_2 = back(2, hidden_2, [])
     total = through(2, pieces_2, total, [])
 
     ffn = exchange(total)

time: 106 us -> 106 us (level)
  waiting for transfers between devices: 32.9 us -> 37.1 us
  Pallas kernels: 43.7 us -> 42.1 us
  starting transfers between devices: 23.9 us -> 22.6 us
    ppermute x15, waiting for transfers between devices: 9.34 us -> 12.9 us  [swap(): return lax.ppermute(x, axis, [(i, i ^ bits) for i in range(size)])]
    unnamed x14 -> x10, local copies, waits for them, and re-layouts: 2.91 us -> 2.26 us
  transfers between devices with their start and end apart: 18 -> 18, of which waited for: 9 -> 10; matrix products, arithmetic and copies ran while one was open for 2% -> 2% of each run, Pallas kernels for 28% -> 32%
where the time goes in v10:
time: 106 us
  Pallas kernels  42.1 us (40%)
  waiting for transfers between devices  37.1 us (35%)
  starting transfers between devices  22.6 us (21%)
  local copies, waits for them, and re-layouts  2.48 us (2%)
    all_to_all x3, waiting for transfers between devices, body(): lax.all_to_all(x, ('gx', 'gy'), split_axis=0, concat_axis=0, tiled=True)  24.2 us
    pallas_call x3, Pallas kernels, gate_up(): pl.pallas_call(functools.partial(gate_up_kernel, start, tile, len(after))...  17.6 us
    all_to_all x3, starting transfers between devices, body(): lax.all_to_all(x, ('gx', 'gy'), split_axis=0, concat_axis=0, tiled=True)  15.5 us
    pallas_call x3, Pallas kernels, down(): pl.pallas_call(functools.partial(down_kernel, start, tile, total is not N...  13.9 us
    ppermute x15, waiting for transfers between devices, swap(): return lax.ppermute(x, axis, [(i, i ^ bits) for i in range(size)])  12.9 us
    ppermute x15, starting transfers between devices, swap(): return lax.ppermute(x, axis, [(i, i ^ bits) for i in range(size)])  7.02 us
    pallas_call x1, Pallas kernels, attend_cache(): pl.pallas_call(functools.partial(cache_kernel, 1.0 / math.sqrt(depth)), i...  6.32 us
    unnamed x10, local copies, waits for them, and re-layouts  2.26 us
  transfers between devices with their start and end apart: 18, of which 10 were waited for; matrix products, arithmetic and copies ran while one was open for 2% of the time, Pallas kernels for 32%

profile of v10, /device:TPU:0, one launch (start us, length us, event | category | flops | bytes accessed | tf_op | source)
XLA Modules:
  0.0 105.7 jit_solution(11725495155226142128)
XLA Ops:
  0.6 2.1 %shard_map.113.after_ref = bf16[8,4,4,2304]{3,2,1,0:T(4,128)(2,1)} custom-call(bf16[4,9216]{1,0:T(4,128)(2,1)} %tokens_ref.1, f32[1,9216]{1,0:T(1,128)} %bitcast.23), custom_call_target="tpu_custom_call" | custom-call | flops 368640 | bytes 589824 | tf_op jit(solution)/shard_map/pallas_call | solution.py:80
  2.7 7.3 %all-to-all-start = ((bf16[32,4,2304]{2,1,0:T(4,128)(2,1)}), bf16[32,4,2304]{2,1,0:T(4,128)(2,1)S(1)}, u32[]{:S(2)}, u32[]{:S(2)}) async-start(bf16[32,4,2304]{2,1,0:T(4,128)(2,1)} %bitcast.2), calls=%async_computation | async-start | bytes 1179648 | tf_op jit(solution)/shard_map/all_to_all | solution.py:420
  10.0 0.9 copy.28
  11.0 0.6 copy-done.2
  11.6 6.3 %shard_map.114 = (f32[4,48,256]{2,1,0:T(8,128)S(1)}, f32[4,48,1]{2,1,0:T(8,128)S(1)}, f32[4,48,1]{2,1,0:T(8,128)S(1)}) custom-call(s32[4]{0:T(128)S(1)} %copy-done.2, bf16[4,48,256]{2,1,0:T(8,128)(2,1)S(1)} %bitcast.19, bf16[4,2048,256]{2,1,0:T(8,128)(2,1)} %key_ref.1, bf16[4,2048,256]{2,1,0:T(8,128)(2,1)} %value_ref.1, ...), custom_call_target="tpu_custom_call" | custom-call | flops 603979776 | bytes 8388608 | tf_op jit(solution)/shard_map/pallas_call | solution.py:374
  17.9 8.8 %all-to-all-done.rows_ref = bf16[32,4,2304]{2,1,0:T(4,128)(2,1)S(1)} async-done(((bf16[32,4,2304]{2,1,0:T(4,128)(2,1)}), bf16[32,4,2304]{2,1,0:T(4,128)(2,1)S(1)}, u32[]{:S(2)}, u32[]{:S(2)}) %all-to-all-start) | async-done | bytes 589856 | tf_op jit(solution)/shard_map/all_to_all | solution.py:420
  26.9 5.2 %shard_map.116 = (f32[2,64,1280]{2,1,0:T(8,128)S(1)}, bf16[2,64,1280]{2,1,0:T(8,128)(2,1)S(1)}) custom-call(bf16[128,2304]{1,0:T(8,128)(2,1)S(1)} %shard_map.115.x_ref, bf16[2304,4608]{1,0:T(8,128)(2,1)} %gate_ref.5, bf16[2304,4608]{1,0:T(8,128)(2,1)} %up_ref.5), custom_call_target="tpu_custom_call" | custom-call | flops 377487360 | bytes 2949120 | tf_op jit(solution)/shard_map/pallas_call | solution.py:187
  32.2 1.6 %collective-permute-done.core_ref = bf16[2,64,1280]{2,1,0:T(8,128)(2,1)S(1)} collective-permute-done((bf16[2,64,1280]{2,1,0:T(8,128)(2,1)S(1)}, bf16[2,64,1280]{2,1,0:T(8,128)(2,1)S(1)}, u32[]{:S(2)}, u32[]{:S(2)}) %collective-permute-start) | collective-permute-done | bytes 327712 | tf_op jit(solution)/shard_map/ppermute | solution.py:50
  33.9 1.2 %collective-permute-start.1 = (bf16[2,32,1280]{2,1,0:T(8,128)(2,1)S(1)}, bf16[2,32,1280]{2,1,0:T(8,128)(2,1)S(1)}, u32[]{:S(2)}, u32[]{:S(2)}) collective-permute-start(bf16[2,32,1280]{2,1,0:T(8,128)(2,1)S(1)} %get-tuple-element.20.refs_0_), channel_id=1, source_target_pairs={{0,2},{1,3},{2,0},{3,1},{4,6},{5,7},{6,4},{7,5},{8,10},{9,11},{10,... | collective-permute-start | bytes 491528 | tf_op jit(solution)/shard_map/ppermute | solution.py:50
  35.2 0.9 shard_map.134.refs_0_
  36.1 7.3 %shard_map.118 = (f32[2,64,2048]{2,1,0:T(8,128)S(1)}, bf16[2,64,2048]{2,1,0:T(8,128)(2,1)S(1)}) custom-call(bf16[128,2304]{1,0:T(8,128)(2,1)S(1)} %shard_map.115.x_ref, bf16[2304,4608]{1,0:T(8,128)(2,1)} %gate_ref.5, bf16[2304,4608]{1,0:T(8,128)(2,1)} %up_ref.5, bf16[2,32,1280]{2,1,0:T(8,128)(2,1)S(1)} %get-tuple-element.20.refs_0_), custom_call_target="tpu_custom_call" | custom-call | flops 603979776 | bytes 4718592 | tf_op jit(solution)/shard_map/pallas_call | solution.py:187
  43.6 1.8 %collective-permute-done.2.core_ref = bf16[2,64,2048]{2,1,0:T(8,128)(2,1)S(1)} collective-permute-done((bf16[2,64,2048]{2,1,0:T(8,128)(2,1)S(1)}, bf16[2,64,2048]{2,1,0:T(8,128)(2,1)S(1)}, u32[]{:S(2)}, u32[]{:S(2)}) %collective-permute-start.2) | collective-permute-done | bytes 524320 | tf_op jit(solution)/shard_map/ppermute | solution.py:50
  45.6 0.9 collective-permute-start.3
  46.5 1.1 %collective-permute-start.4 = (bf16[32,1280]{1,0:T(8,128)(2,1)S(1)}, bf16[32,1280]{1,0:T(8,128)(2,1)S(1)}, u32[]{:S(2)}, u32[]{:S(2)}) collective-permute-start(bf16[32,1280]{1,0:T(8,128)(2,1)S(1)} %shard_map.119.refs_1_.refs_0_), channel_id=1, source_target_pairs={{0,2},{1,3},{2,0},{3,1},{4,6},{5,7},{6,4},{7,5},{8,10},{9,11},{10,... | collective-permute-start | bytes 245768 | tf_op jit(solution)/shard_map/ppermute | solution.py:50
  47.7 5.1 %shard_map.122 = (f32[2,64,1280]{2,1,0:T(8,128)S(1)}, bf16[2,64,1280]{2,1,0:T(8,128)(2,1)S(1)}) custom-call(bf16[128,2304]{1,0:T(8,128)(2,1)S(1)} %shard_map.115.x_ref, bf16[2304,4608]{1,0:T(8,128)(2,1)} %gate_ref.5, bf16[2304,4608]{1,0:T(8,128)(2,1)} %up_ref.5, bf16[2,32,2048]{2,1,0:T(8,128)(2,1)S(1)} %get-tuple-element.24.refs_0_), custom_call_target="tpu_custom_call" | custom-call | flops 377487360 | bytes 2949120 | tf_op jit(solution)/shard_map/pallas_call | solution.py:187
  52.8 2.9 %collective-permute-done.4.refs_0_ = bf16[32,1280]{1,0:T(8,128)(2,1)S(1)} collective-permute-done((bf16[32,1280]{1,0:T(8,128)(2,1)S(1)}, bf16[32,1280]{1,0:T(8,128)(2,1)S(1)}, u32[]{:S(2)}, u32[]{:S(2)}) %collective-permute-start.4) | collective-permute-done | bytes 81952 | tf_op jit(solution)/shard_map/ppermute | solution.py:50
  55.9 0.9 collective-permute-start.7
  56.9 3.5 %all-to-all-start.2 = ((f32[32,4,512]{2,1,0:T(4,128)}), f32[32,4,512]{2,1,0:T(4,128)S(1)}, u32[]{:S(2)}, u32[]{:S(2)}) async-start(f32[32,4,512]{2,1,0:T(4,128)} %shard_map.135), calls=%async_computation.2 | async-start | bytes 524288 | tf_op jit(solution)/shard_map/all_to_all | solution.py:420
  60.6 1.3 %collective-permute-done.7.refs_0_ = bf16[32,2048]{1,0:T(8,128)(2,1)S(1)} collective-permute-done((bf16[32,2048]{1,0:T(8,128)(2,1)S(1)}, bf16[32,2048]{1,0:T(8,128)(2,1)S(1)}, u32[]{:S(2)}, u32[]{:S(2)}) %collective-permute-start.7) | collective-permute-done | bytes 131104 | tf_op jit(solution)/shard_map/ppermute | solution.py:50
  61.8 0.5 collective-permute-start.10
  62.3 0.9 collective-permute-start.6
  63.3 0.3 collective-permute-done.11.refs_3_
  63.6 4.0 %shard_map.128.refs_5_ = f32[128,2304]{1,0:T(8,128)S(1)} custom-call(s32[1]{0:T(128)} %bitcast.gy_ref, bf16[32,1280]{1,0:T(8,128)(2,1)S(1)} %shard_map.119.refs_1_.refs_0_, bf16[32,1280]{1,0:T(8,128)(2,1)S(1)} %shard_map.124.refs_2_.refs_1_, bf16[32,1280]{1,0:T(8,128)(2,1)S(1)} %collective-permute-done.10.refs_2_, ...), custom_call_target="tpu_custom_call" | custom-call | flops 377487360 | bytes 2949120 | tf_op jit(solution)/shard_map/pallas_call | solution.py:280
  67.6 5.0 %shard_map.129.refs_0_.refs_5_ = f32[128,2304]{1,0:T(8,128)S(1)} custom-call(s32[1]{0:T(128)} %bitcast.gy_ref, bf16[32,2048]{1,0:T(8,128)(2,1)S(1)} %shard_map.123.refs_1_.refs_0_, bf16[32,2048]{1,0:T(8,128)(2,1)S(1)} %shard_map.127.refs_1_, bf16[32,2048]{1,0:T(8,128)(2,1)S(1)} %collective-permute-done.8.refs_2_, ...), custom_call_target="tpu_custom_call" | custom-call | flops 603979776 | bytes 4718592 | tf_op jit(solution)/shard_map/pallas_call | solution.py:280
  72.8 0.9 collective-permute-start.12
  73.7 3.6 %collective-permute-done.12.refs_0_ = bf16[32,1280]{1,0:T(8,128)(2,1)S(1)} collective-permute-done((bf16[32,1280]{1,0:T(8,128)(2,1)S(1)}, bf16[32,1280]{1,0:T(8,128)(2,1)S(1)}, u32[]{:S(2)}, u32[]{:S(2)}) %collective-permute-start.12) | collective-permute-done | bytes 81952 | tf_op jit(solution)/shard_map/ppermute | solution.py:50
  77.4 1.3 %collective-permute-done.14.refs_3_ = bf16[32,1280]{1,0:T(8,128)(2,1)S(1)} collective-permute-done((bf16[32,1280]{1,0:T(8,128)(2,1)S(1)}, bf16[32,1280]{1,0:T(8,128)(2,1)S(1)}, u32[]{:S(2)}, u32[]{:S(2)}) %collective-permute-start.14) | collective-permute-done | bytes 81952 | tf_op jit(solution)/shard_map/ppermute | solution.py:50
  78.6 4.9 %shard_map.132 = bf16[32,4,2304]{2,1,0:T(4,128)(2,1)} custom-call(s32[1]{0:T(128)} %bitcast.gy_ref, bf16[32,1280]{1,0:T(8,128)(2,1)S(1)} %shard_map.130.refs_0_, bf16[32,1280]{1,0:T(8,128)(2,1)S(1)} %shard_map.131.refs_1_, bf16[32,1280]{1,0:T(8,128)(2,1)S(1)} %collective-permute-done.13.refs_2_, bf16[32,1280]{1,0:T(8,128)(2,1)S(1)} %collective-permute-done.14.refs_3_, ...), custom_call_target="tpu_custom_call" | custom-call | flops 377487360 | bytes 2949120 | tf_op jit(solution)/shard_map/pallas_call | solution.py:280
  83.5 4.8 %all-to-all-start.1 = ((bf16[32,4,2304]{2,1,0:T(4,128)(2,1)}), bf16[32,4,2304]{2,1,0:T(4,128)(2,1)S(1)}, u32[]{:S(2)}, u32[]{:S(2)}) async-start(bf16[32,4,2304]{2,1,0:T(4,128)(2,1)} %shard_map.132), calls=%async_computation.1 | async-start | bytes 1179648 | tf_op jit(solution)/shard_map/all_to_all | solution.py:420
  88.9 0.7 copy.23
  89.6 15.4 %all-to-all-done.1 = bf16[32,4,2304]{2,1,0:T(4,128)(2,1)S(1)} async-done(((bf16[32,4,2304]{2,1,0:T(4,128)(2,1)}), bf16[32,4,2304]{2,1,0:T(4,128)(2,1)S(1)}, u32[]{:S(2)}, u32[]{:S(2)}) %all-to-all-start.1) | async-done | bytes 589856 | tf_op jit(solution)/shard_map/all_to_all | solution.py:420
  105.0 0.7 shard_map.133
  (45 shorter events, 1.8 us)
Async XLA Ops:
  2.7 24.0 %all-to-all-start = ((bf16[32,4,2304]{2,1,0:T(4,128)(2,1)}), bf16[32,4,2304]{2,1,0:T(4,128)(2,1)S(1)}, u32[]{:S(2)}, u32[]{:S(2)}) async-start(bf16[32,4,2304]{2,1,0:T(4,128)(2,1)} %bitcast.2), calls=%async_computation | async-start | bytes 1179648 | tf_op jit(solution)/shard_map/all_to_all | solution.py:420
  11.0 0.7 copy-start.2
  26.9 8.3 %copy-start = (bf16[1,288,512]{2,1,0:T(8,128)(2,1)S(1)}, bf16[1,288,512]{2,1,0:T(8,128)(2,1)}, u32[]{:S(2)}) copy-start(bf16[1,288,512]{2,1,0:T(8,128)(2,1)} %weight_ref.1) | copy-start | bytes 884740
  32.1 1.7 %collective-permute-start = (bf16[2,64,1280]{2,1,0:T(8,128)(2,1)S(1)}, bf16[2,64,1280]{2,1,0:T(8,128)(2,1)S(1)}, u32[]{:S(2)}, u32[]{:S(2)}) collective-permute-start(bf16[2,64,1280]{2,1,0:T(8,128)(2,1)S(1)} %get-tuple-element.19.after_ref), channel_id=1, source_target_pairs={{0,1},{1,0},{2,3},{3,2},{4,5},{5,4},{6,7},{7,6},{8,9},{9,8},{10,11... | collective-permute-start | bytes 983048 | tf_op jit(solution)/shard_map/ppermute | solution.py:50
  33.9 9.6 %collective-permute-start.1 = (bf16[2,32,1280]{2,1,0:T(8,128)(2,1)S(1)}, bf16[2,32,1280]{2,1,0:T(8,128)(2,1)S(1)}, u32[]{:S(2)}, u32[]{:S(2)}) collective-permute-start(bf16[2,32,1280]{2,1,0:T(8,128)(2,1)S(1)} %get-tuple-element.20.refs_0_), channel_id=1, source_target_pairs={{0,2},{1,3},{2,0},{3,1},{4,6},{5,7},{6,4},{7,5},{8,10},{9,11},{10,... | collective-permute-start | bytes 491528 | tf_op jit(solution)/shard_map/ppermute | solution.py:50
  43.5 2.0 %collective-permute-start.2 = (bf16[2,64,2048]{2,1,0:T(8,128)(2,1)S(1)}, bf16[2,64,2048]{2,1,0:T(8,128)(2,1)S(1)}, u32[]{:S(2)}, u32[]{:S(2)}) collective-permute-start(bf16[2,64,2048]{2,1,0:T(8,128)(2,1)S(1)} %shard_map.120), channel_id=1, source_target_pairs={{0,1},{1,0},{2,3},{3,2},{4,5},{5,4},{6,7},{7,6},{8,9},{9,8},{10,11... | collective-permute-start | bytes 1572872 | tf_op jit(solution)/shard_map/ppermute | solution.py:50
  45.6 10.2 %collective-permute-start.3 = (bf16[2,32,2048]{2,1,0:T(8,128)(2,1)S(1)}, bf16[2,32,2048]{2,1,0:T(8,128)(2,1)S(1)}, u32[]{:S(2)}, u32[]{:S(2)}) collective-permute-start(bf16[2,32,2048]{2,1,0:T(8,128)(2,1)S(1)} %get-tuple-element.24.refs_0_), channel_id=1, source_target_pairs={{0,2},{1,3},{2,0},{3,1},{4,6},{5,7},{6,4},{7,5},{8,10},{9,11},{10,... | collective-permute-start | bytes 786440 | tf_op jit(solution)/shard_map/ppermute | solution.py:50
  46.5 9.2 %collective-permute-start.4 = (bf16[32,1280]{1,0:T(8,128)(2,1)S(1)}, bf16[32,1280]{1,0:T(8,128)(2,1)S(1)}, u32[]{:S(2)}, u32[]{:S(2)}) collective-permute-start(bf16[32,1280]{1,0:T(8,128)(2,1)S(1)} %shard_map.119.refs_1_.refs_0_), channel_id=1, source_target_pairs={{0,2},{1,3},{2,0},{3,1},{4,6},{5,7},{6,4},{7,5},{8,10},{9,11},{10,... | collective-permute-start | bytes 245768 | tf_op jit(solution)/shard_map/ppermute | solution.py:50
  55.8 4.7 %collective-permute-start.5 = (bf16[2,64,1280]{2,1,0:T(8,128)(2,1)S(1)}, bf16[2,64,1280]{2,1,0:T(8,128)(2,1)S(1)}, u32[]{:S(2)}, u32[]{:S(2)}) collective-permute-start(bf16[2,64,1280]{2,1,0:T(8,128)(2,1)S(1)} %shard_map.125), channel_id=1, source_target_pairs={{0,1},{1,0},{2,3},{3,2},{4,5},{5,4},{6,7},{7,6},{8,9},{9,8},{10,11... | collective-permute-start | bytes 983048 | tf_op jit(solution)/shard_map/ppermute | solution.py:50
  55.9 5.9 %collective-permute-start.7 = (bf16[32,2048]{1,0:T(8,128)(2,1)S(1)}, bf16[32,2048]{1,0:T(8,128)(2,1)S(1)}, u32[]{:S(2)}, u32[]{:S(2)}) collective-permute-start(bf16[32,2048]{1,0:T(8,128)(2,1)S(1)} %shard_map.123.refs_1_.refs_0_), channel_id=1, source_target_pairs={{0,2},{1,3},{2,0},{3,1},{4,6},{5,7},{6,4},{7,5},{8,10},{9,11},{10,... | collective-permute-start | bytes 393224 | tf_op jit(solution)/shard_map/ppermute | solution.py:50
  56.9 26.6 %all-to-all-start.2 = ((f32[32,4,512]{2,1,0:T(4,128)}), f32[32,4,512]{2,1,0:T(4,128)S(1)}, u32[]{:S(2)}, u32[]{:S(2)}) async-start(f32[32,4,512]{2,1,0:T(4,128)} %shard_map.135), calls=%async_computation.2 | async-start | bytes 524288 | tf_op jit(solution)/shard_map/all_to_all | solution.py:420
  60.3 7.3 %collective-permute-start.8 = (bf16[32,2048]{1,0:T(8,128)(2,1)S(1)}, bf16[32,2048]{1,0:T(8,128)(2,1)S(1)}, u32[]{:S(2)}, u32[]{:S(2)}) collective-permute-start(bf16[32,2048]{1,0:T(8,128)(2,1)S(1)} %shard_map.123.refs_1_.refs_0_), channel_id=1, source_target_pairs={{0,1},{1,0},{2,3},{3,2},{4,5},{5,4},{6,7},{7,6},{8,9},{9,8},{10,11... | collective-permute-start | bytes 393224 | tf_op jit(solution)/shard_map/ppermute | solution.py:50
  61.8 5.8 %collective-permute-start.9 = (bf16[32,2048]{1,0:T(8,128)(2,1)S(1)}, bf16[32,2048]{1,0:T(8,128)(2,1)S(1)}, u32[]{:S(2)}, u32[]{:S(2)}) collective-permute-start(bf16[32,2048]{1,0:T(8,128)(2,1)S(1)} %shard_map.127.refs_1_), channel_id=1, source_target_pairs={{0,1},{1,0},{2,3},{3,2},{4,5},{5,4},{6,7},{7,6},{8,9},{9,8},{10,11... | collective-permute-start | bytes 393224 | tf_op jit(solution)/shard_map/ppermute | solution.py:50
  61.8 1.5 %collective-permute-start.10 = (bf16[32,1280]{1,0:T(8,128)(2,1)S(1)}, bf16[32,1280]{1,0:T(8,128)(2,1)S(1)}, u32[]{:S(2)}, u32[]{:S(2)}) collective-permute-start(bf16[32,1280]{1,0:T(8,128)(2,1)S(1)} %shard_map.119.refs_1_.refs_0_), channel_id=1, source_target_pairs={{0,1},{1,0},{2,3},{3,2},{4,5},{5,4},{6,7},{7,6},{8,9},{9,8},{10,11... | collective-permute-start | bytes 245768 | tf_op jit(solution)/shard_map/ppermute | solution.py:50
  62.3 1.3 %collective-permute-start.11 = (bf16[32,1280]{1,0:T(8,128)(2,1)S(1)}, bf16[32,1280]{1,0:T(8,128)(2,1)S(1)}, u32[]{:S(2)}, u32[]{:S(2)}) collective-permute-start(bf16[32,1280]{1,0:T(8,128)(2,1)S(1)} %shard_map.124.refs_2_.refs_1_), channel_id=1, source_target_pairs={{0,1},{1,0},{2,3},{3,2},{4,5},{5,4},{6,7},{7,6},{8,9},{9,8},{10,11... | collective-permute-start | bytes 245768 | tf_op jit(solution)/shard_map/ppermute | solution.py:50
  62.3 10.4 %collective-permute-start.6 = (bf16[2,32,1280]{2,1,0:T(8,128)(2,1)S(1)}, bf16[2,32,1280]{2,1,0:T(8,128)(2,1)S(1)}, u32[]{:S(2)}, u32[]{:S(2)}) collective-permute-start(bf16[2,32,1280]{2,1,0:T(8,128)(2,1)S(1)} %get-tuple-element.29.refs_1_.refs_5_), channel_id=1, source_target_pairs={{0,2},{1,3},{2,0},{3,1},{4,6},{5,7},{6,4},{7,5},{8,10},{9,11},{10,... | collective-permute-start | bytes 491528 | tf_op jit(solution)/shard_map/ppermute | solution.py:50
  72.8 4.6 %collective-permute-start.12 = (bf16[32,1280]{1,0:T(8,128)(2,1)S(1)}, bf16[32,1280]{1,0:T(8,128)(2,1)S(1)}, u32[]{:S(2)}, u32[]{:S(2)}) collective-permute-start(bf16[32,1280]{1,0:T(8,128)(2,1)S(1)} %shard_map.130.refs_0_), channel_id=1, source_target_pairs={{0,2},{1,3},{2,0},{3,1},{4,6},{5,7},{6,4},{7,5},{8,10},{9,11},{10,... | collective-permute-start | bytes 245768 | tf_op jit(solution)/shard_map/ppermute | solution.py:50
  73.7 3.6 %collective-permute-start.13 = (bf16[32,1280]{1,0:T(8,128)(2,1)S(1)}, bf16[32,1280]{1,0:T(8,128)(2,1)S(1)}, u32[]{:S(2)}, u32[]{:S(2)}) collective-permute-start(bf16[32,1280]{1,0:T(8,128)(2,1)S(1)} %shard_map.130.refs_0_), channel_id=1, source_target_pairs={{0,1},{1,0},{2,3},{3,2},{4,5},{5,4},{6,7},{7,6},{8,9},{9,8},{10,11... | collective-permute-start | bytes 245768 | tf_op jit(solution)/shard_map/ppermute | solution.py:50
  77.3 11.0 %copy-start.3 = (bf16[4,12288]{1,0:T(4,128)(2,1)S(1)}, bf16[4,12288]{1,0:T(4,128)(2,1)}, u32[]{:S(2)}) copy-start(bf16[4,12288]{1,0:T(4,128)(2,1)} %param.16) | copy-start | bytes 294916
  77.3 27.7 %copy-start.1 = (bf16[4,9216]{1,0:T(4,128)(2,1)S(1)}, bf16[4,9216]{1,0:T(4,128)(2,1)}, u32[]{:S(2)}) copy-start(bf16[4,9216]{1,0:T(4,128)(2,1)} %tokens_ref.1) | copy-start | bytes 221188
  77.3 1.3 %collective-permute-start.14 = (bf16[32,1280]{1,0:T(8,128)(2,1)S(1)}, bf16[32,1280]{1,0:T(8,128)(2,1)S(1)}, u32[]{:S(2)}, u32[]{:S(2)}) collective-permute-start(bf16[32,1280]{1,0:T(8,128)(2,1)S(1)} %shard_map.131.refs_1_), channel_id=1, source_target_pairs={{0,1},{1,0},{2,3},{3,2},{4,5},{5,4},{6,7},{7,6},{8,9},{9,8},{10,11... | collective-permute-start | bytes 245768 | tf_op jit(solution)/shard_map/ppermute | solution.py:50
  83.5 21.5 %all-to-all-start.1 = ((bf16[32,4,2304]{2,1,0:T(4,128)(2,1)}), bf16[32,4,2304]{2,1,0:T(4,128)(2,1)S(1)}, u32[]{:S(2)}, u32[]{:S(2)}) async-start(bf16[32,4,2304]{2,1,0:T(4,128)(2,1)} %shard_map.132), calls=%async_computation.1 | async-start | bytes 1179648 | tf_op jit(solution)/shard_map/all_to_all | solution.py:420
